TPU v7x, 32 devices: a whole 2x2x4 slice. The times are simulated.
32 devices in a mesh: clip: 2 (over core), ctx: 4 (over z), head: 4 (over y, x).
Axes of the slice: x: 2, y: 2, z: 4, core: 2. Of those that a mesh axis runs over, the one named last changes fastest.
Arguments:
- queries: bfloat16 [1792, 5120], P(('clip', 'ctx', 'head')), parts along dimension 0, may hold values from -6 to 6
- keys_in: bfloat16 [1792, 5120], P(('clip', 'ctx', 'head')), parts along dimension 0, may hold values from -6 to 6
- values_in: bfloat16 [1792, 5120], P(('clip', 'ctx', 'head')), parts along dimension 0, may hold values from -6 to 6
- attn_out: bfloat16 [1792, 5120], P(('clip', 'ctx', 'head')), parts along dimension 0, may hold values from -6 to 6
- out_grad: bfloat16 [1792, 5120], P(('clip', 'ctx', 'head')), parts along dimension 0, may hold values from -192 to 192
- log_norm: float32 [1792, 40], P(('clip', 'ctx'), 'head'), parts along dimension 0, may hold values from -1 to 12
- span_id: int32 [1792], P(('clip', 'ctx', 'head')), parts along dimension 0, may hold values from 0 to 11, as said below
Outputs:
- query_grad: bfloat16 [1792, 5120], P(('clip', 'ctx', 'head')), parts along dimension 0
- key_grad: bfloat16 [1792, 5120], P(('clip', 'ctx', 'head')), parts along dimension 0
- value_grad: bfloat16 [1792, 5120], P(('clip', 'ctx', 'head')), parts along dimension 0
There are 2 independent parts, one for each index of `clip`. A program takes and returns all parts, laid end to end along the dimension named above; each array names one. Nothing has to cross between parts.
Inputs may be any that keep to these rules, and one draw needn't show every extreme that they name: span_id[i] = (i + o) // 75 for one offset o per clip, 0 <= o <= 4: spans of 75 tokens, the first one entered partway.
All inputs are finite; a program needn't handle non-finite values.
Results may differ from a plain program's by a relative error of at most 0.007.
Values may be sent and summed in bfloat16 or wider, within the bound.
No kernel may reach another device: no remote copies, remote signals or barrier semaphores. Data moves between devices by JAX's collectives and lax.ppermute only.
A program may use at most 128 MiB of HBM per device.

v0:
```python
import math

import jax
import jax.numpy as jnp
from jax import lax
from jax.sharding import PartitionSpec as P


def tile_terms(query_blk, grad_blk, norm_blk, delta_blk, query_ids, key_blk, value_blk, key_ids):
    row_count = query_blk.shape[0]
    key_count = key_blk.shape[0]
    head_count = norm_blk.shape[1]
    head_width = query_blk.shape[1] // head_count
    scale = 1.0 / math.sqrt(head_width)
    query3 = query_blk.reshape(row_count, head_count, head_width)
    grad3 = grad_blk.reshape(row_count, head_count, head_width)
    key3 = key_blk.reshape(key_count, head_count, head_width)
    value3 = value_blk.reshape(key_count, head_count, head_width)
    scores = jnp.einsum("rhd,khd->hrk", query3, key3, preferred_element_type=jnp.float32)
    visible = key_ids[None, :] <= query_ids[:, None]
    weight = jnp.where(visible[None], jnp.exp(scores * scale - norm_blk.T[:, :, None]), 0.0)
    weight_low = weight.astype(jnp.bfloat16)
    dweight = jnp.einsum("rhd,khd->hrk", grad3, value3, preferred_element_type=jnp.float32)
    dscore = (weight * (dweight - delta_blk.T[:, :, None]) * scale).astype(jnp.bfloat16)
    query_term = jnp.einsum("hrk,khd->rhd", dscore, key3, preferred_element_type=jnp.float32)
    key_term = jnp.einsum("hrk,rhd->khd", dscore, query3, preferred_element_type=jnp.float32)
    value_term = jnp.einsum("hrk,rhd->khd", weight_low, grad3, preferred_element_type=jnp.float32)
    return (
        query_term.reshape(row_count, -1),
        key_term.reshape(key_count, -1),
        value_term.reshape(key_count, -1),
    )


def rounded(term):
    return lax.optimization_barrier(term.astype(jnp.bfloat16)).astype(jnp.float32)


def local(queries, keys_in, values_in, attn_out, out_grad, log_norm, span_id):
    local_q, local_k, local_v, local_out, local_grad = (
        lax.all_to_all(queries, "head", split_axis=1, concat_axis=0, tiled=True),
        lax.all_to_all(keys_in, "head", split_axis=1, concat_axis=0, tiled=True),
        lax.all_to_all(values_in, "head", split_axis=1, concat_axis=0, tiled=True),
        lax.all_to_all(attn_out, "head", split_axis=1, concat_axis=0, tiled=True),
        lax.all_to_all(out_grad, "head", split_axis=1, concat_axis=0, tiled=True),
    )
    all_ids = lax.all_gather(span_id, ("ctx", "head"), axis=0, tiled=True)
    seg_rows = local_q.shape[0]
    block_count = lax.axis_size("ctx")
    head_count = log_norm.shape[1]
    head_width = local_q.shape[1] // head_count
    my_block = lax.axis_index("ctx")
    own_ids = lax.dynamic_slice_in_dim(all_ids, my_block * seg_rows, seg_rows)
    id_blocks = all_ids.reshape(block_count, seg_rows)
    deltas = jnp.sum(
        (local_grad.astype(jnp.float32) * local_out.astype(jnp.float32)).reshape(
            seg_rows, head_count, head_width
        ),
        axis=2,
    )
    far_queries, far_grads = (
        lax.all_gather(local_q, "ctx", axis=0, tiled=True),
        lax.all_gather(local_grad, "ctx", axis=0, tiled=True),
    )
    far_norms, far_deltas = (
        lax.all_gather(log_norm, "ctx", axis=0, tiled=True),
        lax.all_gather(deltas, "ctx", axis=0, tiled=True),
    )

    def query_step(totals, piece):
        query_blk, grad_blk, norm_blk, delta_blk, query_ids = piece
        query_term, key_term, value_term = tile_terms(
            query_blk, grad_blk, norm_blk, delta_blk, query_ids, local_k, local_v, own_ids
        )
        return ((totals[0] + rounded(key_term), totals[1] + rounded(value_term)), query_term)

    zero_block = jnp.zeros(local_k.shape, jnp.float32)
    (dk_total, dv_total), query_terms = lax.scan(
        query_step,
        (zero_block, zero_block),
        (
            far_queries.reshape(block_count, seg_rows, -1),
            far_grads.reshape(block_count, seg_rows, -1),
            far_norms.reshape(block_count, seg_rows, -1),
            far_deltas.reshape(block_count, seg_rows, -1),
            id_blocks,
        ),
    )
    query_sum = lax.psum_scatter(
        query_terms.reshape(block_count * seg_rows, -1).astype(jnp.bfloat16),
        "ctx",
        scatter_dimension=0,
        tiled=True,
    )
    dk_local = dk_total.astype(jnp.bfloat16)
    dv_local = dv_total.astype(jnp.bfloat16)
    query_grad, key_grad, value_grad = (
        lax.all_to_all(query_sum, "head", split_axis=0, concat_axis=1, tiled=True),
        lax.all_to_all(dk_local, "head", split_axis=0, concat_axis=1, tiled=True),
        lax.all_to_all(dv_local, "head", split_axis=0, concat_axis=1, tiled=True),
    )
    return (query_grad, key_grad, value_grad)


def solution(mesh):
    placed = (
        P(("clip", "ctx", "head"), None),
        P(("clip", "ctx", "head"), None),
        P(("clip", "ctx", "head"), None),
        P(("clip", "ctx", "head"), None),
        P(("clip", "ctx", "head"), None),
        P(("clip", "ctx"), "head"),
        P(("clip", "ctx", "head")),
    )
    return jax.shard_map(
        local,
        mesh=mesh,
        in_specs=placed,
        out_specs=(
            P(("clip", "ctx", "head"), None),
            P(("clip", "ctx", "head"), None),
            P(("clip", "ctx", "head"), None),
        ),
        check_vma=False,
    )
```

profile of v0, /device:TPU:0, one launch (start us, length us, event | category | flops | bytes accessed | tf_op | source)
XLA Modules:
  0.0 272.2 jit_solution(13044754273349177607)
XLA Ops:
  8.4 14.5 %all_to_all.146 = bf16[56,4,1280]{2,0,1:T(8,128)(2,1)} all-to-all(bf16[56,4,1280]{2,0,1:T(8,128)(2,1)S(1)} %bitcast.147), channel_id=1, replica_groups=mesh['clip'=2,'ctx'=4,'head'=4] {'head'}, dimensions={1} | all-to-all | bytes 1146880 | tf_op jit(solution)/shard_map/all_to_all | solution.py:45
  23.0 11.5 %all_to_all.147 = bf16[56,4,1280]{2,0,1:T(8,128)(2,1)} all-to-all(bf16[56,4,1280]{2,0,1:T(8,128)(2,1)S(1)} %bitcast.148), channel_id=1, replica_groups=mesh['clip'=2,'ctx'=4,'head'=4] {'head'}, dimensions={1} | all-to-all | bytes 1146880 | tf_op jit(solution)/shard_map/all_to_all | solution.py:41
  35.4 3.6 %all-to-all-start.4 = ((bf16[56,4,1280]{2,0,1:T(8,128)(2,1)}), bf16[56,4,1280]{2,0,1:T(8,128)(2,1)S(1)}, u32[]{:S(2)}, u32[]{:S(2)}) async-start(bf16[56,4,1280]{2,0,1:T(8,128)(2,1)} %bitcast.79), calls=%async_computation.4 | async-start | bytes 1146880 | tf_op jit(solution)/shard_map/all_to_all | solution.py:44
  39.9 6.0 %all-to-all-done.4 = bf16[56,4,1280]{2,0,1:T(8,128)(2,1)S(1)} async-done(((bf16[56,4,1280]{2,0,1:T(8,128)(2,1)}), bf16[56,4,1280]{2,0,1:T(8,128)(2,1)S(1)}, u32[]{:S(2)}, u32[]{:S(2)}) %all-to-all-start.4) | async-done | bytes 573472 | tf_op jit(solution)/shard_map/all_to_all | solution.py:44
  45.8 3.5 %all-to-all-start.1 = ((bf16[56,4,1280]{2,0,1:T(8,128)(2,1)}), bf16[56,4,1280]{2,0,1:T(8,128)(2,1)S(1)}, u32[]{:S(2)}, u32[]{:S(2)}) async-start(bf16[56,4,1280]{2,0,1:T(8,128)(2,1)} %bitcast.82), calls=%async_computation.1 | async-start | bytes 1146880 | tf_op jit(solution)/shard_map/all_to_all | solution.py:42
  50.9 16.9 %all-reduce = s32[896]{0:T(1024)S(1)} all-reduce(s32[896]{0:T(1024)S(1)} %dynamic-update-slice), channel_id=1, replica_groups=mesh['clip'=2,'ctx'=4,'head'=4] {'ctx','head'}, use_global_device_ids=true, to_apply=%add | all-reduce | flops 896 | bytes 7168
  70.0 13.9 %all-gather = f32[4,224,10]{1,2,0:T(8,128)} all-gather(f32[1,224,10]{1,2,0:T(8,128)S(1)} %bitcast.161), channel_id=1, replica_groups=mesh['clip'=2,'ctx'=4,'head'=4] {'ctx'}, dimensions={0}, use_global_device_ids=true | all-gather | bytes 44800 | tf_op jit(solution)/shard_map/all_gather | solution.py:66
  83.9 4.2 %all-to-all-start.3 = ((bf16[56,4,1280]{2,0,1:T(8,128)(2,1)}), bf16[56,4,1280]{2,0,1:T(8,128)(2,1)}, u32[]{:S(2)}, u32[]{:S(2)}) async-start(bf16[56,4,1280]{2,0,1:T(8,128)(2,1)} %bitcast.80), calls=%async_computation.3 | async-start | bytes 1146880 | tf_op jit(solution)/shard_map/all_to_all | solution.py:43
  89.6 5.4 %all-to-all-done.3 = bf16[56,4,1280]{2,0,1:T(8,128)(2,1)} async-done(((bf16[56,4,1280]{2,0,1:T(8,128)(2,1)}), bf16[56,4,1280]{2,0,1:T(8,128)(2,1)}, u32[]{:S(2)}, u32[]{:S(2)}) %all-to-all-start.3) | async-done | bytes 573472 | tf_op jit(solution)/shard_map/all_to_all | solution.py:43
  95.0 2.2 copy.110
  97.2 13.6 %all-gather.1 = f32[4,224,10]{1,2,0:T(8,128)S(1)} all-gather(f32[1,224,10]{1,2,0:T(8,128)S(1)} %copy.106), channel_id=1, replica_groups=mesh['clip'=2,'ctx'=4,'head'=4] {'ctx'}, dimensions={0}, use_global_device_ids=true | all-gather | bytes 44800 | tf_op jit(solution)/shard_map/all_gather | solution.py:67
  110.8 12.4 %all-gather.5.cloned.1.call-done = bf16[896,1280]{1,0:T(8,128)(2,1)} async-done(((bf16[224,1280]{1,0:T(8,128)(2,1)}), bf16[896,1280]{1,0:T(8,128)(2,1)}) %all-gather.5.cloned.1.call-update) | async-done | bytes 2293776 | tf_op jit(solution)/shard_map/all_gather | solution.py:62
  123.2 79.2 %while.15 = (s32[]{:T(128)}, f32[224,1280]{0,1:T(8,128)}, f32[224,1280]{0,1:T(8,128)}, bf16[4,224,1280]{1,2,0:T(8,128)(2,1)}, bf16[4,224,1280]{2,1,0:T(8,128)(2,...) while((s32[]{:T(128)}, f32[224,1280]{0,1:T(8,128)}, ...), condition=%wide.region_2.3_spmd.clone, body=%wide.region_1.2_spmd.clone.sunk | while | flops 650116096 | bytes 32268732 | solution.py:78
  124.5 2.0 fusion.43
  129.5 2.8 %multiply_convert_fusion.2 = bf16[10,224,224]{2,1,0:T(8,128)(2,1)S(1)} fusion(f32[10,224,224]{2,1,0:T(8,128)} %fusion.43, bf16[224,10,128]{0,2,1:T(8,128)(2,1)S(1)} %bitcast.135, bf16[224,10,128]{0,2,1:T(8,128)(2,1)} %bitcast.149, f32[10,224]{1,0:T(8,128)S(1)} %dynamic-slice_bitcast_fusion.5, f32[10,224]{1,0:T(8,128)S(1)} %dynamic-slice_bitcast_fusion.4, ...), kind=kOutput, calls=%fused_computation.clone.1 | convolution fusion | flops 131962880 | bytes 4225536 | tf_op jit(solution)/shard_map/while/body/eval_jaxpr/rhd,khd->hrk/dot_general | solution.py:23
  133.2 3.8 %fusion.44 = bf16[224,10,128]{2,0,1:T(8,128)(2,1)} fusion(bf16[224,10,128]{0,2,1:T(8,128)(2,1)} %bitcast.136, f32[10,224,224]{2,1,0:T(8,128)} %fusion.43, f32[10,224]{1,0:T(8,128)S(1)} %dynamic-slice_bitcast_fusion.4, pred[224,224]{1,0:T(8,128)(4,1)S(1)} %broadcast_compare_fusion.2), kind=kOutput, calls=%fused_computation.9.clone.1 | convolution fusion | flops 130744320 | bytes 3213056 | tf_op jit(solution)/shard_map/while/body/eval_jaxpr/hrk,rhd->khd/dot_general | solution.py:27
  148.1 2.8 %multiply_convert_fusion.2 = bf16[10,224,224]{2,1,0:T(8,128)(2,1)S(1)} fusion(f32[10,224,224]{2,1,0:T(8,128)} %fusion.43, bf16[224,10,128]{0,2,1:T(8,128)(2,1)S(1)} %bitcast.135, bf16[224,10,128]{0,2,1:T(8,128)(2,1)} %bitcast.149, f32[10,224]{1,0:T(8,128)S(1)} %dynamic-slice_bitcast_fusion.5, f32[10,224]{1,0:T(8,128)S(1)} %dynamic-slice_bitcast_fusion.4, ...), kind=kOutput, calls=%fused_computation.clone.1 | convolution fusion | flops 131962880 | bytes 4225536 | tf_op jit(solution)/shard_map/while/body/eval_jaxpr/rhd,khd->hrk/dot_general | solution.py:23
  151.7 3.8 %fusion.44 = bf16[224,10,128]{2,0,1:T(8,128)(2,1)} fusion(bf16[224,10,128]{0,2,1:T(8,128)(2,1)} %bitcast.136, f32[10,224,224]{2,1,0:T(8,128)} %fusion.43, f32[10,224]{1,0:T(8,128)S(1)} %dynamic-slice_bitcast_fusion.4, pred[224,224]{1,0:T(8,128)(4,1)S(1)} %broadcast_compare_fusion.2), kind=kOutput, calls=%fused_computation.9.clone.1 | convolution fusion | flops 130744320 | bytes 3213056 | tf_op jit(solution)/shard_map/while/body/eval_jaxpr/hrk,rhd->khd/dot_general | solution.py:27
  156.8 3.5 %select_add_fusion.3 = (f32[224,1280]{0,1:T(8,128)}, f32[224,1280]{0,1:T(8,128)}) fusion(f32[224,1280]{0,1:T(8,128)} %get-tuple-element.264, bf16[224,1280]{0,1:T(8,128)(2,1)S(1)} %bitcast.134, pred[]{:T(512)S(6)} %compare.3, bf16[224,1280]{0,1:T(8,128)(2,1)S(1)} %bitcast.133, f32[224,1280]{0,1:T(8,128)} %get-tuple-element.263), kind=kLoop, calls=%fused_computation.6.clone.1 | loop fusion | flops 1720320 | bytes 5734401 | tf_op jit(solution)/shard_map/while/body/eval_jaxpr/add | solution.py:75
  168.3 2.8 %multiply_convert_fusion.2 = bf16[10,224,224]{2,1,0:T(8,128)(2,1)S(1)} fusion(f32[10,224,224]{2,1,0:T(8,128)} %fusion.43, bf16[224,10,128]{0,2,1:T(8,128)(2,1)S(1)} %bitcast.135, bf16[224,10,128]{0,2,1:T(8,128)(2,1)} %bitcast.149, f32[10,224]{1,0:T(8,128)S(1)} %dynamic-slice_bitcast_fusion.5, f32[10,224]{1,0:T(8,128)S(1)} %dynamic-slice_bitcast_fusion.4, ...), kind=kOutput, calls=%fused_computation.clone.1 | convolution fusion | flops 131962880 | bytes 4225536 | tf_op jit(solution)/shard_map/while/body/eval_jaxpr/rhd,khd->hrk/dot_general | solution.py:23
  171.9 3.8 %fusion.44 = bf16[224,10,128]{2,0,1:T(8,128)(2,1)} fusion(bf16[224,10,128]{0,2,1:T(8,128)(2,1)} %bitcast.136, f32[10,224,224]{2,1,0:T(8,128)} %fusion.43, f32[10,224]{1,0:T(8,128)S(1)} %dynamic-slice_bitcast_fusion.4, pred[224,224]{1,0:T(8,128)(4,1)S(1)} %broadcast_compare_fusion.2), kind=kOutput, calls=%fused_computation.9.clone.1 | convolution fusion | flops 130744320 | bytes 3213056 | tf_op jit(solution)/shard_map/while/body/eval_jaxpr/hrk,rhd->khd/dot_general | solution.py:27
  177.1 3.5 %select_add_fusion.3 = (f32[224,1280]{0,1:T(8,128)}, f32[224,1280]{0,1:T(8,128)}) fusion(f32[224,1280]{0,1:T(8,128)} %get-tuple-element.264, bf16[224,1280]{0,1:T(8,128)(2,1)S(1)} %bitcast.134, pred[]{:T(512)S(6)} %compare.3, bf16[224,1280]{0,1:T(8,128)(2,1)S(1)} %bitcast.133, f32[224,1280]{0,1:T(8,128)} %get-tuple-element.263), kind=kLoop, calls=%fused_computation.6.clone.1 | loop fusion | flops 1720320 | bytes 5734401 | tf_op jit(solution)/shard_map/while/body/eval_jaxpr/add | solution.py:75
  188.5 2.8 %multiply_convert_fusion.2 = bf16[10,224,224]{2,1,0:T(8,128)(2,1)S(1)} fusion(f32[10,224,224]{2,1,0:T(8,128)} %fusion.43, bf16[224,10,128]{0,2,1:T(8,128)(2,1)S(1)} %bitcast.135, bf16[224,10,128]{0,2,1:T(8,128)(2,1)} %bitcast.149, f32[10,224]{1,0:T(8,128)S(1)} %dynamic-slice_bitcast_fusion.5, f32[10,224]{1,0:T(8,128)S(1)} %dynamic-slice_bitcast_fusion.4, ...), kind=kOutput, calls=%fused_computation.clone.1 | convolution fusion | flops 131962880 | bytes 4225536 | tf_op jit(solution)/shard_map/while/body/eval_jaxpr/rhd,khd->hrk/dot_general | solution.py:23
  192.1 3.8 %fusion.44 = bf16[224,10,128]{2,0,1:T(8,128)(2,1)} fusion(bf16[224,10,128]{0,2,1:T(8,128)(2,1)} %bitcast.136, f32[10,224,224]{2,1,0:T(8,128)} %fusion.43, f32[10,224]{1,0:T(8,128)S(1)} %dynamic-slice_bitcast_fusion.4, pred[224,224]{1,0:T(8,128)(4,1)S(1)} %broadcast_compare_fusion.2), kind=kOutput, calls=%fused_computation.9.clone.1 | convolution fusion | flops 130744320 | bytes 3213056 | tf_op jit(solution)/shard_map/while/body/eval_jaxpr/hrk,rhd->khd/dot_general | solution.py:27
  197.3 3.5 %select_add_fusion.3 = (f32[224,1280]{0,1:T(8,128)}, f32[224,1280]{0,1:T(8,128)}) fusion(f32[224,1280]{0,1:T(8,128)} %get-tuple-element.264, bf16[224,1280]{0,1:T(8,128)(2,1)S(1)} %bitcast.134, pred[]{:T(512)S(6)} %compare.3, bf16[224,1280]{0,1:T(8,128)(2,1)S(1)} %bitcast.133, f32[224,1280]{0,1:T(8,128)} %get-tuple-element.263), kind=kLoop, calls=%fused_computation.6.clone.1 | loop fusion | flops 1720320 | bytes 5734401 | tf_op jit(solution)/shard_map/while/body/eval_jaxpr/add | solution.py:75
  202.4 4.3 %copy.111 = bf16[4,224,1280]{2,1,0:T(8,128)(2,1)} copy(bf16[4,224,1280]{1,2,0:T(8,128)(2,1)} %get-tuple-element.67) | data formatting | bytes 4587520 | tf_op jit(solution)/shard_map/convert_element_type | solution.py:90
  209.0 3.6 %all-to-all-start.6 = ((bf16[4,56,1280]{2,1,0:T(8,128)(2,1)}), bf16[4,56,1280]{2,1,0:T(8,128)(2,1)S(1)}, u32[]{:S(2)}, u32[]{:S(2)}) async-start(bf16[4,56,1280]{2,1,0:T(8,128)(2,1)} %bitcast.17), calls=%async_computation.7 | async-start | bytes 1146880 | tf_op jit(solution)/shard_map/all_to_all | solution.py:99
  212.9 8.4 %all-to-all-done.6 = bf16[4,56,1280]{2,1,0:T(8,128)(2,1)S(1)} async-done(((bf16[4,56,1280]{2,1,0:T(8,128)(2,1)}), bf16[4,56,1280]{2,1,0:T(8,128)(2,1)S(1)}, u32[]{:S(2)}, u32[]{:S(2)}) %all-to-all-start.6) | async-done | bytes 573472 | tf_op jit(solution)/shard_map/all_to_all | solution.py:99
  221.3 11.0 %all_to_all.148 = bf16[4,56,1280]{2,1,0:T(8,128)(2,1)S(1)} all-to-all(bf16[4,56,1280]{2,1,0:T(8,128)(2,1)S(1)} %bitcast.141), channel_id=1, replica_groups=mesh['clip'=2,'ctx'=4,'head'=4] {'head'}, dimensions={0} | all-to-all | bytes 1146880 | tf_op jit(solution)/shard_map/all_to_all | solution.py:100
  232.2 20.4 %reduce-scatter.2.cloned.1.call-done = bf16[224,1280]{1,0:T(8,128)(2,1)} async-done(((bf16[896,1280]{1,0:T(8,128)(2,1)}), bf16[224,1280]{1,0:T(8,128)(2,1)}) %reduce-scatter.2.cloned.1.call-update) | async-done | bytes 573456 | tf_op jit(solution)/shard_map/reduce_scatter | solution.py:89
  252.7 3.6 %all-to-all-start.5 = ((bf16[4,56,1280]{2,1,0:T(8,128)(2,1)}), bf16[4,56,1280]{2,1,0:T(8,128)(2,1)S(1)}, u32[]{:S(2)}, u32[]{:S(2)}) async-start(bf16[4,56,1280]{2,1,0:T(8,128)(2,1)} %bitcast.155), calls=%async_computation.6 | async-start | bytes 1146880 | tf_op jit(solution)/shard_map/all_to_all | solution.py:98
  258.0 6.8 %all-to-all-done.5 = bf16[4,56,1280]{2,1,0:T(8,128)(2,1)S(1)} async-done(((bf16[4,56,1280]{2,1,0:T(8,128)(2,1)}), bf16[4,56,1280]{2,1,0:T(8,128)(2,1)S(1)}, u32[]{:S(2)}, u32[]{:S(2)}) %all-to-all-start.5) | async-done | bytes 573472 | tf_op jit(solution)/shard_map/all_to_all | solution.py:98
  (125 shorter events, 52.5 us)
Async XLA Ops:
  7.2 15.8 %copy-start.6 = (bf16[56,5120]{1,0:T(8,128)(2,1)S(1)}, bf16[56,5120]{1,0:T(8,128)(2,1)}, u32[]{:S(2)}) copy-start(bf16[56,5120]{1,0:T(8,128)(2,1)} %param.9) | copy-start | bytes 1720324
  7.2 103.6 %all-gather.7.cloned.1.call-start = ((), (), s32[]{:S(2)}) async-start(), calls=%async_computation.10 | async-start | bytes 2867200 | tf_op jit(solution)/shard_map/all_gather | solution.py:63
  8.4 26.1 %copy-start.7 = (bf16[56,5120]{1,0:T(8,128)(2,1)S(1)}, bf16[56,5120]{1,0:T(8,128)(2,1)}, u32[]{:S(2)}) copy-start(bf16[56,5120]{1,0:T(8,128)(2,1)} %param.12) | copy-start | bytes 1720324
  22.9 100.3 %all-gather.5.cloned.1.call-start = ((), (), s32[]{:S(2)}) async-start(), calls=%async_computation.9 | async-start | bytes 2867200 | tf_op jit(solution)/shard_map/all_gather | solution.py:62
  23.0 16.0 %copy-start.8 = (bf16[56,5120]{1,0:T(8,128)(2,1)S(1)}, bf16[56,5120]{1,0:T(8,128)(2,1)}, u32[]{:S(2)}) copy-start(bf16[56,5120]{1,0:T(8,128)(2,1)} %param.10) | copy-start | bytes 1720324
  34.5 14.9 %copy-start.13 = (u32[32]{0:T(128)S(1)}, u32[32]{0:T(128)}, u32[]{:S(2)}) copy-start(u32[32]{0:T(128)} %constant.43) | copy-start | bytes 388
  34.5 16.1 %copy-start.12 = (s32[56]{0:T(128)S(1)}, s32[56]{0:T(128)}, u32[]{:S(2)}) copy-start(s32[56]{0:T(128)} %param.15) | copy-start | bytes 676
  34.5 34.7 %copy-start.9 = (bf16[56,5120]{1,0:T(8,128)(2,1)S(1)}, bf16[56,5120]{1,0:T(8,128)(2,1)}, u32[]{:S(2)}) copy-start(bf16[56,5120]{1,0:T(8,128)(2,1)} %param.11) | copy-start | bytes 1720324
  35.4 34.7 %copy-start.11 = (f32[224,10]{0,1:T(8,128)S(1)}, f32[224,10]{0,1:T(8,128)}, u32[]{:S(2)}) copy-start(f32[224,10]{0,1:T(8,128)} %param.14) | copy-start | bytes 26884
  35.4 10.5 %all-to-all-start.4 = ((bf16[56,4,1280]{2,0,1:T(8,128)(2,1)}), bf16[56,4,1280]{2,0,1:T(8,128)(2,1)S(1)}, u32[]{:S(2)}, u32[]{:S(2)}) async-start(bf16[56,4,1280]{2,0,1:T(8,128)(2,1)} %bitcast.79), calls=%async_computation.4 | async-start | bytes 1146880 | tf_op jit(solution)/shard_map/all_to_all | solution.py:44
  39.0 49.1 %copy-start.3 = (bf16[56,4,1280]{2,0,1:T(8,128)(2,1)S(1)}, bf16[56,4,1280]{2,0,1:T(8,128)(2,1)}, u32[]{:S(2)}) copy-start(bf16[56,4,1280]{2,0,1:T(8,128)(2,1)} %all_to_all.146) | copy-start | bytes 1720324
  45.8 38.0 %all-to-all-start.1 = ((bf16[56,4,1280]{2,0,1:T(8,128)(2,1)}), bf16[56,4,1280]{2,0,1:T(8,128)(2,1)S(1)}, u32[]{:S(2)}, u32[]{:S(2)}) async-start(bf16[56,4,1280]{2,0,1:T(8,128)(2,1)} %bitcast.82), calls=%async_computation.1 | async-start | bytes 1146880 | tf_op jit(solution)/shard_map/all_to_all | solution.py:42
  83.9 4.2 %copy-start.4 = (bf16[56,4,1280]{2,0,1:T(8,128)(2,1)}, bf16[56,4,1280]{2,0,1:T(8,128)(2,1)S(1)}, u32[]{:S(2)}) copy-start(bf16[56,4,1280]{2,0,1:T(8,128)(2,1)S(1)} %all-to-all-done.1) | copy-start | bytes 1720324
  83.9 11.1 %all-to-all-start.3 = ((bf16[56,4,1280]{2,0,1:T(8,128)(2,1)}), bf16[56,4,1280]{2,0,1:T(8,128)(2,1)}, u32[]{:S(2)}, u32[]{:S(2)}) async-start(bf16[56,4,1280]{2,0,1:T(8,128)(2,1)} %bitcast.80), calls=%async_computation.3 | async-start | bytes 1146880 | tf_op jit(solution)/shard_map/all_to_all | solution.py:43
  88.1 164.6 %reduce-scatter.2.cloned.1.call-start = ((), (), s32[]{:S(2)}) async-start(), calls=%async_computation.11 | async-start | bytes 2867200 | tf_op jit(solution)/shard_map/reduce_scatter | solution.py:89
  88.3 1.1 copy-start.5
  88.5 34.7 %copy-start.10 = (s32[224]{0:T(256)S(1)}, s32[224]{0:T(256)}, u32[]{:S(2)}) copy-start(s32[224]{0:T(256)} %dynamic_slice.21) | copy-start | bytes 2692
  128.7 0.9 copy-start.2
  147.2 0.9 copy-start.2
  167.4 0.9 copy-start.2
  187.6 0.9 copy-start.2
  206.7 1.3 copy-start
  206.7 5.9 %copy-start.1 = (f32[224,1280]{0,1:T(8,128)S(1)}, f32[224,1280]{0,1:T(8,128)}, u32[]{:S(2)}) copy-start(f32[224,1280]{0,1:T(8,128)} %get-tuple-element.69) | copy-start | bytes 3440644
  209.0 12.2 %all-to-all-start.6 = ((bf16[4,56,1280]{2,1,0:T(8,128)(2,1)}), bf16[4,56,1280]{2,1,0:T(8,128)(2,1)S(1)}, u32[]{:S(2)}, u32[]{:S(2)}) async-start(bf16[4,56,1280]{2,1,0:T(8,128)(2,1)} %bitcast.17), calls=%async_computation.7 | async-start | bytes 1146880 | tf_op jit(solution)/shard_map/all_to_all | solution.py:99
  252.7 12.1 %all-to-all-start.5 = ((bf16[4,56,1280]{2,1,0:T(8,128)(2,1)}), bf16[4,56,1280]{2,1,0:T(8,128)(2,1)S(1)}, u32[]{:S(2)}, u32[]{:S(2)}) async-start(bf16[4,56,1280]{2,1,0:T(8,128)(2,1)} %bitcast.155), calls=%async_computation.6 | async-start | bytes 1146880 | tf_op jit(solution)/shard_map/all_to_all | solution.py:98
Sparse Core Ops, SparseCore 0:
  23.0 49.3 all-gather.6
  73.9 49.2 all-gather.4
  206.8 45.7 reduce-scatter.1
where the time goes:
time: 274 us; the launch traced here: 272 us
  blocking collectives  81.4 us (30%)
  waiting for transfers between devices  59.5 us (22%)
  local copies, waits for them, and re-layouts  46 us (17%)
  matrix products  38.6 us (14%)
  starting transfers between devices  18.6 us (7%)
  between operations  14.7 us (5%)
  other arithmetic  13.3 us (5%)
    reduce_scatter x1, waiting for transfers between devices, local(): lax.psum_scatter(query_terms.reshape(block_count * seg_rows, -1).astype(j...  20.4 us
    unnamed x1, blocking collectives  16.9 us
    dot_general x4, matrix products, tile_terms(): jnp.einsum('hrk,rhd->khd', weight_low, grad3, preferred_element_type=jnp....  15.3 us
    all_to_all x1, blocking collectives, local(): lax.all_to_all(out_grad, 'head', split_axis=1, concat_axis=0, tiled=True)  14.5 us
    all_gather x1, blocking collectives, local(): lax.all_gather(log_norm, 'ctx', axis=0, tiled=True)  13.9 us
    all_gather x1, blocking collectives, local(): lax.all_gather(deltas, 'ctx', axis=0, tiled=True)  13.6 us
    dynamic_slice x20, local copies, waits for them, and re-layouts, local(): lax.scan(query_step, (zero_block, zero_block), (far_queries.reshape(block...  13.5 us
    all_gather x1, waiting for transfers between devices, local(): lax.all_gather(local_q, 'ctx', axis=0, tiled=True)  12.4 us
  transfers between devices with their start and end apart: 8, of which 6 were waited for; matrix products, arithmetic and copies ran while one was open for 4% of the time, Pallas kernels for 0%

commit v1 on v0

--- a/solution.py
+++ b/solution.py
@@ -3,7 +3,21 @@
 import jax
 import jax.numpy as jnp
 from jax import lax
+from jax.experimental import pallas as pl
+from jax.experimental.pallas import tpu as pltpu
 from jax.sharding import PartitionSpec as P
+
+SPANS = 12
+EDGE = 16
+LANES = 128
+BF16 = jnp.bfloat16
+F32 = jnp.float32
+
+INWARD = ((0, 1), (3, 2))
+SWAP = ((1, 2), (2, 1))
+OUTWARD = ((1, 0), (2, 3))
+DOWN = ((1, 0), (2, 1), (3, 2))
+UP = ((0, 1), (1, 2), (2, 3))
 
 
 def tile_terms(query_blk, grad_blk, norm_blk, delta_blk, query_ids, key_blk, value_blk, key_ids):
@@ -36,7 +50,7 @@
     return lax.optimization_barrier(term.astype(jnp.bfloat16)).astype(jnp.float32)
 
 
-def local(queries, keys_in, values_in, attn_out, out_grad, log_norm, span_id):
+def local_plain(queries, keys_in, values_in, attn_out, out_grad, log_norm, span_id):
     local_q, local_k, local_v, local_out, local_grad = (
         lax.all_to_all(queries, "head", split_axis=1, concat_axis=0, tiled=True),
         lax.all_to_all(keys_in, "head", split_axis=1, concat_axis=0, tiled=True),
@@ -102,6 +116,576 @@
     return (query_grad, key_grad, value_grad)
 
 
+def nt(a, b):
+    return lax.dot_general(a, b, (((1,), (1,)), ((), ())), preferred_element_type=F32)
+
+
+def tn(a, b):
+    return lax.dot_general(a, b, (((0,), (0,)), ((), ())), preferred_element_type=F32)
+
+
+def pieces(value):
+    high = value.astype(BF16)
+    rest = value - high.astype(F32)
+    middle = rest.astype(BF16)
+    low = (rest - middle.astype(F32)).astype(BF16)
+    return high, middle, low
+
+
+def run_copies(pairs, sems, first=0):
+    made = [pltpu.make_async_copy(src, dst, sems.at[first + i]) for i, (src, dst) in enumerate(pairs)]
+    for copy in made:
+        copy.start()
+    return made
+
+
+def wait_all(made):
+    for copy in made:
+        copy.wait()
+
+
+def anywhere(count):
+    return [pl.BlockSpec(memory_space=pl.ANY)] * count
+
+
+def pack(queries, keys_in, values_in, attn_out, out_grad, span_row, groups, width):
+    rows = queries.shape[0]
+    heads = width // LANES
+    half = width // 2
+
+    def body(q, k, v, o, g, ids, x1, x2, x3, o_v, g_v, meta, sems):
+        low = lax.axis_index("ctx") < 2
+        loads = run_copies([(o, o_v), (g, g_v)], sems)
+
+        def moves(first, second, third, fourth, near, far):
+            todo = []
+            for h in range(groups):
+                base = h * width
+                todo.append((first.at[:, pl.ds(base + near, half)], x1.at[h, :, pl.ds(0, half)]))
+                todo.append((second.at[:, pl.ds(base + near, half)], x1.at[h, :, pl.ds(half, half)]))
+                todo.append((first.at[:, pl.ds(base + far, half)], x2.at[h, :, pl.ds(0, half)]))
+                todo.append((second.at[:, pl.ds(base + far, half)], x2.at[h, :, pl.ds(half, half)]))
+                todo.append((third.at[:, pl.ds(base, width)], x3.at[h, :, pl.ds(0, width)]))
+                todo.append((fourth.at[:, pl.ds(base, width)], x3.at[h, :, pl.ds(width, width)]))
+            return todo
+
+        count = 6 * groups
+
+        @pl.when(low)
+        def _():
+            run_copies(moves(k, v, q, g, half, 0), sems, 2)
+
+        @pl.when(jnp.logical_not(low))
+        def _():
+            run_copies(moves(q, g, k, v, 0, half), sems, 2)
+
+        wait_all(loads)
+        lane = lax.broadcasted_iota(jnp.int32, (rows, LANES), 1)
+        slot = jnp.where(lane < 3 * heads, lane % heads, -1)
+        at_row = lax.broadcasted_iota(jnp.int32, (rows, rows), 0)
+        at_col = lax.broadcasted_iota(jnp.int32, (rows, rows), 1)
+        own = jnp.sum(jnp.where(at_row == at_col, ids[...].astype(F32), 0.0), axis=1, keepdims=True)
+        for h in range(groups):
+            total = jnp.zeros((rows, LANES), F32)
+            for c in range(heads):
+                cols = pl.ds(h * width + c * LANES, LANES)
+                delta = jnp.sum(o_v[:, cols].astype(F32) * g_v[:, cols].astype(F32), axis=1, keepdims=True)
+                total = jnp.where(slot == c, delta, total)
+            high, middle, lowest = pieces(total)
+            kept = jnp.where(lane < heads, high, jnp.where(lane < 2 * heads, middle, lowest))
+            meta[h] = jnp.where(lane < 3 * heads, kept, jnp.where(lane == 3 * heads, own.astype(BF16), 0.0).astype(BF16))
+        last = run_copies([(meta, x1.at[:, :, pl.ds(width, LANES)])], sems, 2 + count)
+
+        @pl.when(low)
+        def _():
+            wait_all(
+                [
+                    pltpu.make_async_copy(src, dst, sems.at[2 + i])
+                    for i, (src, dst) in enumerate(moves(k, v, q, g, half, 0))
+                ]
+            )
+
+        @pl.when(jnp.logical_not(low))
+        def _():
+            wait_all(
+                [
+                    pltpu.make_async_copy(src, dst, sems.at[2 + i])
+                    for i, (src, dst) in enumerate(moves(q, g, k, v, 0, half))
+                ]
+            )
+
+        wait_all(last)
+
+    return pl.pallas_call(
+        body,
+        out_shape=[
+            jax.ShapeDtypeStruct((groups, rows, width + LANES), BF16),
+            jax.ShapeDtypeStruct((groups, rows, width), BF16),
+            jax.ShapeDtypeStruct((groups, rows, 2 * width), BF16),
+        ],
+        in_specs=anywhere(5) + [pl.BlockSpec(memory_space=pltpu.VMEM)],
+        out_specs=anywhere(3),
+        scratch_shapes=[
+            pltpu.VMEM((rows, groups * width), BF16),
+            pltpu.VMEM((rows, groups * width), BF16),
+            pltpu.VMEM((groups, rows, LANES), BF16),
+            pltpu.SemaphoreType.DMA((3 + 6 * groups,)),
+        ],
+        cost_estimate=pl.CostEstimate(flops=0, bytes_accessed=10 * rows * groups * width * 2, transcendentals=0),
+        name="pack",
+    )(queries, keys_in, values_in, attn_out, out_grad, span_row)
+
+
+def add_norm(payload, norm_rows):
+    rows, width = payload.shape
+    heads = norm_rows.shape[0]
+    block = pl.BlockSpec((rows, LANES), lambda i: (0, width // LANES - 1))
+
+    def body(x, norm, y):
+        at_row = lax.broadcasted_iota(jnp.int32, (heads, LANES), 0)
+        at_lane = lax.broadcasted_iota(jnp.int32, (heads, LANES), 1)
+        total = x[...].astype(F32)
+        for i, piece in enumerate(pieces(norm[...])):
+            place = jnp.where(at_lane == at_row + (3 * heads + 1 + i * heads), 1.0, 0.0).astype(BF16)
+            total += tn(piece, place)
+        y[...] = total.astype(BF16)
+
+    return pl.pallas_call(
+        body,
+        grid=(1,),
+        out_shape=jax.ShapeDtypeStruct(payload.shape, BF16),
+        in_specs=[block, pl.BlockSpec((heads, rows), lambda i: (0, 0))],
+        out_specs=block,
+        input_output_aliases={0: 0},
+        cost_estimate=pl.CostEstimate(flops=0, bytes_accessed=4 * rows * LANES, transcendentals=0),
+        name="add_norm",
+    )(payload, norm_rows)
+
+
+def token_rows(meta, heads):
+    at_row = lax.broadcasted_iota(jnp.int32, (32, LANES), 0)
+    at_lane = lax.broadcasted_iota(jnp.int32, (32, LANES), 1)
+    norm_lane = at_lane - (3 * heads + 1)
+    is_norm = (norm_lane >= 0) & (norm_lane < 3 * heads) & (norm_lane % heads == at_row) & (at_row < heads)
+    is_delta = (at_lane < 3 * heads) & (at_lane % heads == at_row - heads) & (at_row >= heads)
+    is_id = (at_lane == 3 * heads) & (at_row == 2 * heads)
+    chosen = jnp.where(is_norm | is_delta | is_id, 1.0, 0.0).astype(BF16)
+    return nt(chosen, meta)
+
+
+def pair_terms(query, grad, key, value, norm, delta, visible=None):
+    scale = 1.0 / math.sqrt(query.shape[1])
+    weight = jnp.exp(nt(key, query) * scale - norm)
+    if visible is not None:
+        weight = jnp.where(visible, weight, 0.0)
+    dscore = (weight * (nt(value, grad) - delta) * scale).astype(BF16)
+    value_term = jnp.dot(weight.astype(BF16), grad, preferred_element_type=F32)
+    key_term = jnp.dot(dscore, query, preferred_element_type=F32)
+    query_term = tn(dscore, key)
+    return query_term, key_term, value_term
+
+
+def far_pairs(y1, y2, w, r1, r2, s1, s2):
+    rows, width = y2.shape
+    half = width // 2
+    count = half // LANES
+    heads = 2 * count
+
+    def body(y1, y2, w, r1, r2, s1, s2, swap1, out1, swap2, l1, l2, l3, buf, grads, meta, info, sems):
+        z = lax.axis_index("ctx")
+        one = z == 1
+
+        def pick(a, b):
+            return jnp.where(one, a, b)
+
+        @pl.when((z == 1) | (z == 2))
+        def _():
+            near = pl.multiple_of(pick(0, half), LANES)
+            other = pl.multiple_of(pick(half, 0), LANES)
+            main = pl.ds(0, width)
+            tail = pl.ds(width, LANES)
+            left, right = pl.ds(0, half), pl.ds(half, half)
+            made = run_copies(
+                [
+                    (y1.at[:, tail], meta.at[pick(2, 0)]),
+                    (s1.at[:, tail], meta.at[pick(0, 3)]),
+                    (s2.at[:, tail], meta.at[pick(1, 4)]),
+                    (r1.at[:, tail], meta.at[pick(3, 1)]),
+                    (s1.at[:, main], buf.at[pick(0, 3)]),
+                    (s2.at[:, main], buf.at[pick(1, 2)]),
+                    (r2, buf.at[pick(2, 1)]),
+                    (y2, buf.at[pick(3, 0)]),
+                    (w.at[:, pl.ds(near, half)], buf.at[4, :, left]),
+                    (w.at[:, pl.ds(width + near, half)], buf.at[4, :, right]),
+                    (w.at[:, pl.ds(other, half)], buf.at[5, :, left]),
+                    (w.at[:, pl.ds(width + other, half)], buf.at[5, :, right]),
+                    (r1.at[:, main], buf.at[6]),
+                ],
+                sems,
+            )
+            wait_all(made)
+            for i in range(3):
+                info[i] = token_rows(meta[i], heads)
+            first_active = pick(0, count)
+            first_other = pick(count, 0)
+            zero = jnp.zeros((rows, LANES), BF16)
+
+            def single(q_slot, k_slot, c, head):
+                a = pl.ds(pl.multiple_of(c * LANES, LANES), LANES)
+                b = pl.ds(pl.multiple_of(half + c * LANES, LANES), LANES)
+                own = pick(2, 1)
+                return pair_terms(
+                    buf[q_slot, :, a],
+                    buf[q_slot, :, b],
+                    buf[k_slot, :, a],
+                    buf[k_slot, :, b],
+                    info[own, pl.ds(head, 1), :],
+                    info[own, pl.ds(heads + head, 1), :],
+                )
+
+            def step(c, carry):
+                a = pl.ds(pl.multiple_of(c * LANES, LANES), LANES)
+                b = pl.ds(pl.multiple_of(half + c * LANES, LANES), LANES)
+                head = first_active + c
+                extra_q, extra_k, extra_v = single(pick(4, 1), pick(2, 4), c, head)
+                key = buf[2:4, :, a].reshape(2 * rows, LANES)
+                value = buf[2:4, :, b].reshape(2 * rows, LANES)
+                key_sum, value_sum = None, None
+                for i in range(2):
+                    query_term, key_term, value_term = pair_terms(
+                        buf[i, :, a],
+                        buf[i, :, b],
+                        key,
+                        value,
+                        info[i, pl.ds(head, 1), :],
+                        info[i, pl.ds(heads + head, 1), :],
+                    )
+                    if i == 1:
+                        query_term += jnp.where(one, 0.0, extra_q)
+                    grads[i, :, a] = query_term.astype(BF16)
+                    grads[i, :, b] = zero
+                    key_sum = key_term if i == 0 else key_sum + key_term
+                    value_sum = value_term if i == 0 else value_sum + value_term
+                grads[2, :, a] = (key_sum[:rows] + jnp.where(one, extra_k, 0.0)).astype(BF16)
+                grads[2, :, b] = (value_sum[:rows] + jnp.where(one, extra_v, 0.0)).astype(BF16)
+                grads[3, :, a] = key_sum[rows:].astype(BF16)
+                grads[3, :, b] = value_sum[rows:].astype(BF16)
+                grads[4, :, a] = jnp.where(one, extra_q, extra_k).astype(BF16)
+                grads[4, :, b] = jnp.where(one, 0.0, extra_v).astype(BF16)
+                extra_q, extra_k, extra_v = single(pick(5, 6), pick(6, 5), c, first_other + c)
+                grads[5, :, a] = jnp.where(one, extra_q, extra_k).astype(BF16)
+                grads[5, :, b] = jnp.where(one, 0.0, extra_v).astype(BF16)
+                grads[6, :, a] = jnp.where(one, extra_k, extra_q).astype(BF16)
+                grads[6, :, b] = jnp.where(one, extra_v, 0.0).astype(BF16)
+                return carry
+
+            lax.fori_loop(0, count, step, 0)
+            made = run_copies(
+                [
+                    (grads.at[pick(1, 2)], swap1),
+                    (grads.at[pick(2, 1)], out1),
+                    (grads.at[pick(0, 3)], swap2),
+                    (grads.at[pick(3, 0)], l2),
+                    (grads.at[6], l3),
+                    (grads.at[4, :, left], l1.at[:, pl.ds(near, half)]),
+                    (grads.at[4, :, right], l1.at[:, pl.ds(width + near, half)]),
+                    (grads.at[5, :, left], l1.at[:, pl.ds(other, half)]),
+                    (grads.at[5, :, right], l1.at[:, pl.ds(width + other, half)]),
+                ],
+                sems,
+            )
+            wait_all(made)
+
+    single_shape = jax.ShapeDtypeStruct((rows, width), BF16)
+    return pl.pallas_call(
+        body,
+        out_shape=[
+            single_shape,
+            single_shape,
+            single_shape,
+            jax.ShapeDtypeStruct((rows, 2 * width), BF16),
+            single_shape,
+            single_shape,
+        ],
+        in_specs=anywhere(7),
+        out_specs=anywhere(6),
+        scratch_shapes=[
+            pltpu.VMEM((7, rows, width), BF16),
+            pltpu.VMEM((7, rows, width), BF16),
+            pltpu.VMEM((5, rows, LANES), BF16),
+            pltpu.VMEM((3, 32, rows), F32),
+            pltpu.SemaphoreType.DMA((13,)),
+        ],
+        compiler_params=pltpu.CompilerParams(vmem_limit_bytes=40 * 2**20),
+        cost_estimate=pl.CostEstimate(
+            flops=30 * 10 * rows * rows * LANES, bytes_accessed=30 * rows * width, transcendentals=30 * rows * rows
+        ),
+        name="far_pairs",
+    )(y1, y2, w, r1, r2, s1, s2)
+
+
+def near_pairs(y1, y2, w, key_edge, query_edge):
+    rows, width = y2.shape
+    half = width // 2
+    count = half // LANES
+    heads = 2 * count
+    total = rows + EDGE
+
+    def body(y1, y2, w, kedge, qedge, dw, dy1, dy2, dkedge, dqedge, qbuf, kbuf, dq, dk, kmeta, qmeta, info, sems):
+        low = lax.axis_index("ctx") < 2
+        left, right = pl.ds(0, half), pl.ds(half, half)
+        own, past = pl.ds(0, rows), pl.ds(rows, EDGE)
+        main = pl.ds(0, width)
+
+        def halves(array, there, back=False):
+            todo = []
+            for i in range(2):
+                for j in range(array.shape[1] // width):
+                    wide = array.at[:, pl.ds(j * width + i * half, half)]
+                    narrow = there(i, right if j else left)
+                    todo.append((narrow, wide) if back else (wide, narrow))
+            return todo
+
+        shared = run_copies(
+            [
+                (y1.at[:, pl.ds(width, LANES)], kmeta.at[own]),
+                (y1.at[:, pl.ds(width, LANES)], qmeta.at[own]),
+                (kedge.at[:, pl.ds(2 * width, LANES)], kmeta.at[past]),
+                (qedge.at[:, pl.ds(2 * width, LANES)], qmeta.at[past]),
+            ]
+            + halves(kedge, lambda i, cols: kbuf.at[i, past, cols])
+            + halves(qedge, lambda i, cols: qbuf.at[i, past, cols]),
+            sems,
+        )
+
+        @pl.when(low)
+        def _():
+            todo = halves(w, lambda i, cols: qbuf.at[i, own, cols])
+            todo += [(y2, kbuf.at[0, own]), (y1.at[:, main], kbuf.at[1, own])]
+            wait_all(run_copies(todo, sems, 12))
+
+        @pl.when(jnp.logical_not(low))
+        def _():
+            todo = halves(w, lambda i, cols: kbuf.at[i, own, cols])
+            todo += [(y1.at[:, main], qbuf.at[0, own]), (y2, qbuf.at[1, own])]
+            wait_all(run_copies(todo, sems, 12))
+
+        wait_all(shared)
+        info[...] = token_rows(qmeta[...], heads)
+        id_lane = lax.broadcasted_iota(jnp.int32, (total, LANES), 1) == 3 * heads
+        key_ids = jnp.sum(jnp.where(id_lane, kmeta[...].astype(F32), 0.0), axis=1, keepdims=True)
+        at_key = lax.broadcasted_iota(jnp.int32, (total, total), 0)
+        at_query = lax.broadcasted_iota(jnp.int32, (total, total), 1)
+        visible = (key_ids <= info[2 * heads : 2 * heads + 1, :]) & ((at_key < rows) | (at_query < rows - EDGE))
+        for i in range(2):
+
+            def step(c, carry, i=i):
+                a = pl.ds(pl.multiple_of(c * LANES, LANES), LANES)
+                b = pl.ds(pl.multiple_of(half + c * LANES, LANES), LANES)
+                head = i * count + c
+                query_term, key_term, value_term = pair_terms(
+                    qbuf[i, :, a],
+                    qbuf[i, :, b],
+                    kbuf[i, :, a],
+                    kbuf[i, :, b],
+                    info[pl.ds(head, 1), :],
+                    info[pl.ds(heads + head, 1), :],
+                    visible,
+                )
+                dq[i, :, a] = query_term.astype(BF16)
+                dk[i, :, a] = key_term.astype(BF16)
+                dk[i, :, b] = value_term.astype(BF16)
+                return carry
+
+            lax.fori_loop(0, count, step, 0)
+
+        made = run_copies(
+            halves(dkedge, lambda i, cols: dk.at[i, past, cols], back=True)
+            + halves(dqedge, lambda i, cols: dq.at[i, past, cols], back=True),
+            sems,
+        )
+
+        @pl.when(low)
+        def _():
+            todo = [(dq.at[0, own], dw.at[:, left]), (dq.at[1, own], dw.at[:, right])]
+            todo += [(dk.at[0, own], dy2), (dk.at[1, own], dy1)]
+            wait_all(run_copies(todo, sems, 12))
+
+        @pl.when(jnp.logical_not(low))
+        def _():
+            todo = halves(dw, lambda i, cols: dk.at[i, own, cols], back=True)
+            todo += [(dq.at[0, own], dy1.at[:, left]), (dq.at[1, own], dy2.at[:, left])]
+            wait_all(run_copies(todo, sems, 12))
+
+        wait_all(made)
+
+    return pl.pallas_call(
+        body,
+        out_shape=[
+            jax.ShapeDtypeStruct((rows, 2 * width), BF16),
+            jax.ShapeDtypeStruct((rows, width), BF16),
+            jax.ShapeDtypeStruct((rows, width), BF16),
+            jax.ShapeDtypeStruct((EDGE, 2 * width), BF16),
+            jax.ShapeDtypeStruct((EDGE, width), BF16),
+        ],
+        in_specs=anywhere(5),
+        out_specs=anywhere(5),
+        scratch_shapes=[
+            pltpu.VMEM((2, total, width), BF16),
+            pltpu.VMEM((2, total, width), BF16),
+            pltpu.VMEM((2, total, half), BF16),
+            pltpu.VMEM((2, total, width), BF16),
+            pltpu.VMEM((total, LANES), BF16),
+            pltpu.VMEM((total, LANES), BF16),
+            pltpu.VMEM((32, total), F32),
+            pltpu.SemaphoreType.DMA((18,)),
+        ],
+        compiler_params=pltpu.CompilerParams(vmem_limit_bytes=32 * 2**20),
+        cost_estimate=pl.CostEstimate(
+            flops=10 * 10 * rows * rows * LANES, bytes_accessed=16 * rows * width, transcendentals=10 * rows * rows
+        ),
+        name="near_pairs",
+    )(y1, y2, w, key_edge, query_edge)
+
+
+def unpack(e1, e2, e3):
+    groups, rows, width = e1.shape
+    half = width // 2
+
+    def body(e1, e2, e3, dq, dk, dv, sems):
+        low = lax.axis_index("ctx") < 2
+        left, right = pl.ds(0, half), pl.ds(half, half)
+
+        def moves(first, far_dst, second_dst, near):
+            todo = []
+            far = half - near
+            for h in range(groups):
+                base = h * width
+                todo.append((e1.at[h], first.at[:, pl.ds(base, width)]))
+                todo.append((e2.at[h, :, left], far_dst.at[:, pl.ds(base + far, half)]))
+                todo.append((e3.at[h, :, left], far_dst.at[:, pl.ds(base + near, half)]))
+                spot = 0 if second_dst is None else 1
+                if spot:
+                    todo.append((e2.at[h, :, right], second_dst[0].at[:, pl.ds(base + second_dst[1], half)]))
+                    todo.append((e3.at[h, :, right], second_dst[0].at[:, pl.ds(base + second_dst[2], half)]))
+            return todo
+
+        @pl.when(low)
+        def _():
+            wait_all(run_copies(moves(dq, dk, (dv, 0, half), half), sems))
+
+        @pl.when(jnp.logical_not(low))
+        def _():
+            wait_all(run_copies(moves(dk, dq, (dv, 0, half), 0), sems))
+
+    shape = jax.ShapeDtypeStruct((rows, groups * width), BF16)
+    return pl.pallas_call(
+        body,
+        out_shape=[shape] * 3,
+        in_specs=anywhere(3),
+        out_specs=anywhere(3),
+        scratch_shapes=[pltpu.SemaphoreType.DMA((5 * groups,))],
+        cost_estimate=pl.CostEstimate(flops=0, bytes_accessed=6 * rows * groups * width * 2, transcendentals=0),
+        name="unpack",
+    )(e1, e2, e3)
+
+
+def local_split(queries, keys_in, values_in, attn_out, out_grad, log_norm, span_id):
+    groups = lax.axis_size("head")
+    width = queries.shape[1] // groups
+    half = width // 2
+    z = lax.axis_index("ctx")
+    low = z < 2
+    middle = (z == 1) | (z == 2)
+
+    def to_heads(x):
+        y = lax.all_to_all(x, "head", split_axis=0, concat_axis=0, tiled=True)
+        return y.reshape(-1, y.shape[2])
+
+    def to_tokens(x):
+        x = x.reshape(groups, -1, x.shape[1])
+        return lax.all_to_all(x, "head", split_axis=0, concat_axis=0, tiled=True)
+
+    x1, x2, x3 = pack(queries, keys_in, values_in, attn_out, out_grad, span_id.reshape(1, -1), groups, width)
+    y1 = add_norm(to_heads(x1), log_norm.T)
+    r1 = lax.ppermute(y1, "ctx", INWARD)
+    s1 = lax.ppermute(y1, "ctx", SWAP)
+    y2 = to_heads(x2)
+    r2 = lax.ppermute(y2, "ctx", INWARD)
+    s2 = lax.ppermute(r1, "ctx", SWAP)
+    w = to_heads(x3)
+
+    def joined(first, second, at):
+        return jnp.concatenate([first[at, :half], second[at, :half], first[at, half:width], second[at, half:width]], axis=1)
+
+    top, bottom = slice(0, EDGE), slice(y2.shape[0] - EDGE, None)
+    key_edge = jnp.where(low, joined(y2, y1, top), w[top])
+    query_edge = jnp.where(low, w[bottom], joined(y1, y2, bottom))
+    key_edge = lax.ppermute(jnp.concatenate([key_edge, y1[top, width:]], axis=1), "ctx", DOWN)
+    query_edge = lax.ppermute(jnp.concatenate([query_edge, y1[bottom, width:]], axis=1), "ctx", UP)
+
+    swap1, out1, swap2, l1, l2, l3 = far_pairs(y1, y2, w, r1, r2, s1, s2)
+    swap1 = lax.ppermute(swap1, "ctx", SWAP)
+    out1 = lax.ppermute(out1, "ctx", OUTWARD)
+    swap2 = lax.ppermute(swap2, "ctx", SWAP)
+    dw, dy1, dy2, dkedge, dqedge = near_pairs(y1, y2, w, key_edge, query_edge)
+    dkedge = lax.ppermute(dkedge, "ctx", UP)
+    dqedge = lax.ppermute(dqedge, "ctx", DOWN)
+    out2 = (swap1.astype(F32) + l3.astype(F32)).astype(BF16)
+    out2 = lax.ppermute(out2, "ctx", OUTWARD)
+
+    def wide(x):
+        return x.astype(F32)
+
+    def kept(x):
+        return jnp.where(middle, x.astype(F32), 0.0)
+
+    def edged(total, first, last):
+        return jnp.concatenate([total[:EDGE] + first, total[EDGE:-EDGE], total[-EDGE:] + last], axis=0).astype(BF16)
+
+    def sides(x):
+        parts = jnp.split(x, x.shape[1] // half, axis=1)
+        return jnp.concatenate(parts[0::2], axis=1), jnp.concatenate(parts[1::2], axis=1)
+
+    dk_low, dk_high = jnp.where(low, wide(dkedge), 0.0), jnp.where(low, 0.0, wide(dkedge))
+    dq_low, dq_high = jnp.where(low, wide(dqedge), 0.0), jnp.where(low, 0.0, wide(dqedge))
+    dq_low, dq_high = (jnp.concatenate([x, jnp.zeros_like(x)], axis=1) for x in (dq_low, dq_high))
+    gw = edged(wide(dw) + kept(l1), dk_high, dq_low)
+    first_k, second_k = sides(dk_low)
+    first_q, second_q = sides(dq_high)
+    g2 = edged(wide(dy2) + kept(l2) + wide(out1), first_k, second_q)
+    g1 = edged(wide(dy1) + wide(swap2) + wide(out2), second_k, first_q)
+    e1 = to_tokens(gw[:, :width])
+    e2 = to_tokens(
+        jnp.concatenate([g2[:, :half], jnp.where(low, g2[:, half:], gw[:, width : width + half])], axis=1)
+    )
+    e3 = to_tokens(jnp.concatenate([g1[:, :half], jnp.where(low, g1[:, half:], gw[:, width + half :])], axis=1))
+    return tuple(unpack(e1, e2, e3))
+
+
+def splits(tokens, blocks, head_width, heads):
+    if blocks != 4 or heads % 2 or head_width != LANES or 6 * heads + 1 > LANES:
+        return False
+    block = tokens // blocks
+    span = -(-tokens // SPANS)
+    for offset in range(SPANS * span - tokens + 1):
+        for end in range(block, tokens, block):
+            start = (end - 1 + offset) // span * span - offset
+            if min(end - start, start + span - end) > EDGE or max(end - start, span) > block:
+                return False
+    return block % EDGE == 0
+
+
+def local(queries, keys_in, values_in, attn_out, out_grad, log_norm, span_id):
+    blocks, groups = lax.axis_size("ctx"), lax.axis_size("head")
+    heads = log_norm.shape[1]
+    tokens = queries.shape[0] * blocks * groups
+    plan = local_plain
+    if splits(tokens, blocks, queries.shape[1] // (heads * groups), heads):
+        plan = local_split
+    return plan(queries, keys_in, values_in, attn_out, out_grad, log_norm, span_id)
+
+
 def solution(mesh):
     placed = (
         P(("clip", "ctx", "head"), None),

time: 274 us -> 286 us (1.044)
  Pallas kernels: 0 us -> 133 us
  blocking collectives: 81.4 us -> 37.1 us
  local copies, waits for them, and re-layouts: 46 us -> 5.91 us
  matrix products: 38.6 us -> 0 us
  starting transfers between devices: 18.6 us -> 41.6 us
  between operations: 14.7 us -> 1 us
  other arithmetic: 13.3 us -> 6.19 us
    pallas_call x0 -> x5, Pallas kernels: none -> 133 us  [the longest x1 71.5 us: pack(): pl.pallas_call(body, out_shape=[jax.ShapeDtypeStruct((groups, rows, width...]
    ppermute x0 -> x12, waiting for transfers between devices: none -> 48.7 us  [the longest x1 26.6 us: local_split(): out2 = lax.ppermute(out2, 'ctx', OUTWARD)]
    dot_general x20 -> x0, matrix products: 38.6 us -> none  [the longest x4 15.3 us: tile_terms(): jnp.einsum('hrk,rhd->khd', weight_low, grad3, preferred_element_type=jnp....]
    ppermute x0 -> x12, starting transfers between devices: none -> 31.1 us  [the longest x1 7.18 us: local_split(): r2 = lax.ppermute(y2, 'ctx', INWARD)]
    all_gather x2 -> x0, blocking collectives: 27.5 us -> none  [the longest x1 13.9 us: local(): lax.all_gather(log_norm, 'ctx', axis=0, tiled=True)]
    reduce_scatter x1 -> x0, waiting for transfers between devices: 20.4 us -> none  [local(): lax.psum_scatter(query_terms.reshape(block_count * seg_rows, -1).astype(j...]
    unnamed x1 -> x0, blocking collectives: 16.9 us -> none
    all_to_all x5 -> x3, waiting for transfers between devices: 26.6 us -> 11.3 us  [the longest x2 6.79 us: to_tokens(): return lax.all_to_all(x, 'head', split_axis=0, concat_axis=0, tiled=True)]
  transfers between devices with their start and end apart: 8 -> 15, of which waited for: 6 -> 5; matrix products, arithmetic and copies ran while one was open for 4% -> 3% of each run, Pallas kernels for 0% -> 3%
where the time goes in v1:
time: 286 us; the launch traced here: 285 us
  Pallas kernels  133 us (47%)
  waiting for transfers between devices  60 us (21%)
  starting transfers between devices  41.6 us (15%)
  blocking collectives  37.1 us (13%)
  other arithmetic  6.19 us (2%)
  local copies, waits for them, and re-layouts  5.91 us (2%)
    pallas_call x1, Pallas kernels, pack(): pl.pallas_call(body, out_shape=[jax.ShapeDtypeStruct((groups, rows, width...  71.5 us
    pallas_call x1, Pallas kernels, unpack(): pl.pallas_call(body, out_shape=[shape] * 3, in_specs=anywhere(3), out_spe...  53.4 us
    ppermute x1, waiting for transfers between devices, local_split(): out2 = lax.ppermute(out2, 'ctx', OUTWARD)  26.6 us
    all_to_all x2, blocking collectives, to_heads(): y = lax.all_to_all(x, 'head', split_axis=0, concat_axis=0, tiled=True)  26.4 us
    ppermute x1, waiting for transfers between devices, local_split(): out1 = lax.ppermute(out1, 'ctx', OUTWARD)  22 us
    all_to_all x1, blocking collectives, to_tokens(): return lax.all_to_all(x, 'head', split_axis=0, concat_axis=0, tiled=True)  10.7 us
    ppermute x1, starting transfers between devices, local_split(): r2 = lax.ppermute(y2, 'ctx', INWARD)  7.18 us
    all_to_all x2, starting transfers between devices, to_tokens(): return lax.all_to_all(x, 'head', split_axis=0, concat_axis=0, tiled=True)  6.95 us
  transfers between devices with their start and end apart: 15, of which 5 were waited for; matrix products, arithmetic and copies ran while one was open for 3% of the time, Pallas kernels for 3%

profile of v1, /device:TPU:0, one launch (start us, length us, event | category | flops | bytes accessed | tf_op | source)
XLA Modules:
  0.0 284.5 jit_solution(17459850009399342977)
XLA Ops:
  0.6 71.5 %pack.1 = (bf16[4,56,1408]{2,1,0:T(8,128)(2,1)}, bf16[4,56,1280]{2,1,0:T(8,128)(2,1)}, bf16[4,56,2560]{2,1,0:T(8,128)(2,1)}) custom-call(bf16[56,5120]{1,0:T(8,128)(2,1)} %q.1, bf16[56,5120]{1,0:T(8,128)(2,1)} %k.1, bf16[56,5120]{1,0:T(8,128)(2,1)} %v.1, bf16[56,5120]{1,0:T(8,128)(2,1)} %o.1, bf16[56,5120]{1,0:T(8,128)(2,1)} %g.1, s32[1,56]{1,0:T(1,128)} %bitcast.18), custom_call_target="tpu_custom_call" | custom-call | bytes 5734400 | tf_op jit(solution)/shard_map/pack/pallas_call | solution.py:219
  72.1 14.6 %all_to_all.30 = bf16[4,56,1280]{2,1,0:T(8,128)(2,1)S(1)} all-to-all(bf16[4,56,1280]{2,1,0:T(8,128)(2,1)} %get-tuple-element.18), channel_id=1, replica_groups=mesh['clip'=2,'ctx'=4,'head'=4] {'head'}, dimensions={0} | all-to-all | bytes 1146880 | tf_op jit(solution)/shard_map/all_to_all | solution.py:602
  86.7 11.8 %all_to_all.31 = bf16[4,56,1408]{2,1,0:T(8,128)(2,1)} all-to-all(bf16[4,56,1408]{2,1,0:T(8,128)(2,1)S(1)} %copy-done.10), channel_id=1, replica_groups=mesh['clip'=2,'ctx'=4,'head'=4] {'head'}, dimensions={0} | all-to-all | bytes 1261568 | tf_op jit(solution)/shard_map/all_to_all | solution.py:602
  98.5 3.5 %all-to-all-start.2 = ((bf16[4,56,2560]{2,1,0:T(8,128)(2,1)}), bf16[4,56,2560]{2,1,0:T(8,128)(2,1)S(1)}, u32[]{:S(2)}, u32[]{:S(2)}) async-start(bf16[4,56,2560]{2,1,0:T(8,128)(2,1)} %get-tuple-element.19), calls=%async_computation.2 | async-start | bytes 2293760 | tf_op jit(solution)/shard_map/all_to_all | solution.py:602
  102.1 1.7 add_norm.1.y1
  103.8 4.5 %collective-permute-start.2 = (bf16[224,1408]{1,0:T(8,128)(2,1)}, bf16[224,1408]{1,0:T(8,128)(2,1)}, u32[]{:S(2)}, u32[]{:S(2)}) collective-permute-start(bf16[224,1408]{1,0:T(8,128)(2,1)} %add_norm.1.y1), channel_id=1, source_target_pairs={{0,4},{12,8},{1,5},{13,9},{2,6},{14,10},{3,7},{15,11},{16,20},{28,... | collective-permute-start | bytes 1892360 | tf_op jit(solution)/shard_map/ppermute | solution.py:611
  109.7 4.5 %all-to-all-done.2 = bf16[4,56,2560]{2,1,0:T(8,128)(2,1)S(1)} async-done(((bf16[4,56,2560]{2,1,0:T(8,128)(2,1)}), bf16[4,56,2560]{2,1,0:T(8,128)(2,1)S(1)}, u32[]{:S(2)}, u32[]{:S(2)}) %all-to-all-start.2) | async-done | bytes 1146912 | tf_op jit(solution)/shard_map/all_to_all | solution.py:602
  114.2 1.3 collective-permute-start
  115.5 4.6 %collective-permute-start.1 = (bf16[16,2688]{1,0:T(8,128)(2,1)S(1)}, bf16[16,2688]{1,0:T(8,128)(2,1)S(1)}, u32[]{:S(2)}, u32[]{:S(2)}) collective-permute-start(bf16[16,2688]{1,0:T(8,128)(2,1)S(1)} %pad_maximum_fusion.6), channel_id=1, source_target_pairs={{0,4},{4,8},{8,12},{1,5},{5,9},{9,13},{2,6},{6,10},{10,14},{3,7},{... | collective-permute-start | bytes 258056 | tf_op jit(solution)/shard_map/ppermute | solution.py:625
  120.1 1.5 collective-permute-start.4
  121.6 1.5 collective-permute-start.5
  123.1 7.2 %collective-permute-start.3 = (bf16[224,1280]{1,0:T(8,128)(2,1)S(1)}, bf16[224,1280]{1,0:T(8,128)(2,1)}, u32[]{:S(2)}, u32[]{:S(2)}) collective-permute-start(bf16[224,1280]{1,0:T(8,128)(2,1)S(1)} %bitcast.13), channel_id=1, source_target_pairs={{0,4},{12,8},{1,5},{13,9},{2,6},{14,10},{3,7},{15,11},{16,20},{28,... | collective-permute-start | bytes 1720328 | tf_op jit(solution)/shard_map/ppermute | solution.py:614
  130.3 6.1 %near_pairs.1 = (bf16[224,2560]{1,0:T(8,128)(2,1)S(1)}, bf16[224,1280]{1,0:T(8,128)(2,1)S(1)}, bf16[224,1280]{1,0:T(8,128)(2,1)S(1)}, bf16[16,2560]{1,0:T(8,128)(2,1)S(1)}, bf16[16,1280]{1,0:T(8,128)(2,1)S(1)}) custom-call(bf16[224,1408]{1,0:T(8,128)(2,1)S(1)} %copy-done, bf16[224,1280]{1,0:T(8,128)(2,1)S(1)} %bitcast.14, bf16[224,2560]{1,0:T(8,128)(2,1)S(1)} %bitcast.10, ...), custom_call_target="tpu_custom_call" | custom-call | flops 642252800 | bytes 4587520 | tf_op jit(solution)/shard_map/near_pairs/pallas_call | solution.py:522
  136.4 0.8 copy-done.1
  137.2 0.8 copy-done.3
  138.7 1.3 collective-permute-start.7
  140.0 4.6 %collective-permute-start.6 = (bf16[16,2560]{1,0:T(8,128)(2,1)}, bf16[16,2560]{1,0:T(8,128)(2,1)S(1)}, u32[]{:S(2)}, u32[]{:S(2)}) collective-permute-start(bf16[16,2560]{1,0:T(8,128)(2,1)} %copy-done.7), channel_id=1, source_target_pairs={{0,4},{4,8},{8,12},{1,5},{5,9},{9,13},{2,6},{6,10},{10,14},{3,7},{... | collective-permute-start | bytes 245768 | tf_op jit(solution)/shard_map/ppermute | solution.py:632
  146.6 1.3 collective-permute-start.8
  147.9 1.5 collective-permute-start.9
  150.3 1.3 collective-permute-start.11
  152.3 0.8 slice.131
  153.1 3.5 %all-to-all-start.3 = ((bf16[4,56,1280]{2,1,0:T(8,128)(2,1)}), bf16[4,56,1280]{2,1,0:T(8,128)(2,1)S(1)}, u32[]{:S(2)}, u32[]{:S(2)}) async-start(bf16[4,56,1280]{2,1,0:T(8,128)(2,1)} %bitcast.5), calls=%async_computation.3 | async-start | bytes 1146880 | tf_op jit(solution)/shard_map/all_to_all | solution.py:607
  156.6 22.0 %collective-permute-done.8 = bf16[224,1280]{1,0:T(8,128)(2,1)} collective-permute-done((bf16[224,1280]{1,0:T(8,128)(2,1)}, bf16[224,1280]{1,0:T(8,128)(2,1)}, u32[]{:S(2)}, u32[]{:S(2)}) %collective-permute-start.8) | collective-permute-done | bytes 573472 | tf_op jit(solution)/shard_map/ppermute | solution.py:629
  178.6 1.3 convert_add_fusion.1
  180.0 26.6 %collective-permute-done.11 = bf16[224,1280]{1,0:T(8,128)(2,1)} collective-permute-done((bf16[224,1280]{1,0:T(8,128)(2,1)S(1)}, bf16[224,1280]{1,0:T(8,128)(2,1)}, u32[]{:S(2)}, u32[]{:S(2)}) %collective-permute-start.11) | collective-permute-done | bytes 573472 | tf_op jit(solution)/shard_map/ppermute | solution.py:635
  206.6 1.4 convert_add_fusion
  208.1 0.8 fusion.4
  209.2 0.9 pad_maximum_fusion.4
  210.1 3.5 %all-to-all-start.5 = ((bf16[4,56,1280]{2,1,0:T(8,128)(2,1)}), bf16[4,56,1280]{2,1,0:T(8,128)(2,1)S(1)}, u32[]{:S(2)}, u32[]{:S(2)}) async-start(bf16[4,56,1280]{2,1,0:T(8,128)(2,1)} %bitcast.7), calls=%async_computation.5 | async-start | bytes 1146880 | tf_op jit(solution)/shard_map/all_to_all | solution.py:607
  213.7 6.8 %all-to-all-done.5.e3 = bf16[4,56,1280]{2,1,0:T(8,128)(2,1)S(1)} async-done(((bf16[4,56,1280]{2,1,0:T(8,128)(2,1)}), bf16[4,56,1280]{2,1,0:T(8,128)(2,1)S(1)}, u32[]{:S(2)}, u32[]{:S(2)}) %all-to-all-start.5) | async-done | bytes 573472 | tf_op jit(solution)/shard_map/all_to_all | solution.py:607
  220.4 10.7 %all_to_all.32.e2 = bf16[4,56,1280]{2,1,0:T(8,128)(2,1)} all-to-all(bf16[4,56,1280]{2,1,0:T(8,128)(2,1)S(1)} %bitcast.16), channel_id=1, replica_groups=mesh['clip'=2,'ctx'=4,'head'=4] {'head'}, dimensions={0} | all-to-all | bytes 1146880 | tf_op jit(solution)/shard_map/all_to_all | solution.py:607
  231.1 53.4 %unpack.1 = (bf16[56,5120]{1,0:T(8,128)(2,1)}, bf16[56,5120]{1,0:T(8,128)(2,1)}, bf16[56,5120]{1,0:T(8,128)(2,1)}) custom-call(bf16[4,56,1280]{2,1,0:T(8,128)(2,1)} %copy-done.8, bf16[4,56,1280]{2,1,0:T(8,128)(2,1)} %all_to_all.32.e2, bf16[4,56,1280]{2,1,0:T(8,128)(2,1)} %copy-done.9), custom_call_target="tpu_custom_call" | custom-call | bytes 3440640 | tf_op jit(solution)/shard_map/unpack/pallas_call | solution.py:582
  (59 shorter events, 6.2 us)
Async XLA Ops:
  72.1 14.6 %copy-start.10 = (bf16[4,56,1408]{2,1,0:T(8,128)(2,1)S(1)}, bf16[4,56,1408]{2,1,0:T(8,128)(2,1)}, u32[]{:S(2)}) copy-start(bf16[4,56,1408]{2,1,0:T(8,128)(2,1)} %get-tuple-element.17) | copy-start | bytes 1892356
  98.5 15.6 %all-to-all-start.2 = ((bf16[4,56,2560]{2,1,0:T(8,128)(2,1)}), bf16[4,56,2560]{2,1,0:T(8,128)(2,1)S(1)}, u32[]{:S(2)}, u32[]{:S(2)}) async-start(bf16[4,56,2560]{2,1,0:T(8,128)(2,1)} %get-tuple-element.19), calls=%async_computation.2 | async-start | bytes 2293760 | tf_op jit(solution)/shard_map/all_to_all | solution.py:602
  103.8 26.5 %copy-start = (bf16[224,1408]{1,0:T(8,128)(2,1)S(1)}, bf16[224,1408]{1,0:T(8,128)(2,1)}, u32[]{:S(2)}) copy-start(bf16[224,1408]{1,0:T(8,128)(2,1)} %add_norm.1.y1) | copy-start | bytes 1892356
  103.8 17.8 %collective-permute-start.2 = (bf16[224,1408]{1,0:T(8,128)(2,1)}, bf16[224,1408]{1,0:T(8,128)(2,1)}, u32[]{:S(2)}, u32[]{:S(2)}) collective-permute-start(bf16[224,1408]{1,0:T(8,128)(2,1)} %add_norm.1.y1), channel_id=1, source_target_pairs={{0,4},{12,8},{1,5},{13,9},{2,6},{14,10},{3,7},{15,11},{16,20},{28,... | collective-permute-start | bytes 1892360 | tf_op jit(solution)/shard_map/ppermute | solution.py:611
  114.2 16.1 %collective-permute-start = (bf16[16,2688]{1,0:T(8,128)(2,1)S(1)}, bf16[16,2688]{1,0:T(8,128)(2,1)S(1)}, u32[]{:S(2)}, u32[]{:S(2)}) collective-permute-start(bf16[16,2688]{1,0:T(8,128)(2,1)S(1)} %pad_maximum_fusion.5), channel_id=1, source_target_pairs={{4,0},{8,4},{12,8},{5,1},{9,5},{13,9},{6,2},{10,6},{14,10},{7,3},{... | collective-permute-start | bytes 258056 | tf_op jit(solution)/shard_map/ppermute | solution.py:624
  115.5 14.8 %collective-permute-start.1 = (bf16[16,2688]{1,0:T(8,128)(2,1)S(1)}, bf16[16,2688]{1,0:T(8,128)(2,1)S(1)}, u32[]{:S(2)}, u32[]{:S(2)}) collective-permute-start(bf16[16,2688]{1,0:T(8,128)(2,1)S(1)} %pad_maximum_fusion.6), channel_id=1, source_target_pairs={{0,4},{4,8},{8,12},{1,5},{5,9},{9,13},{2,6},{6,10},{10,14},{3,7},{... | collective-permute-start | bytes 258056 | tf_op jit(solution)/shard_map/ppermute | solution.py:625
  120.1 25.4 %collective-permute-start.4 = (bf16[224,1408]{1,0:T(8,128)(2,1)}, bf16[224,1408]{1,0:T(8,128)(2,1)}, u32[]{:S(2)}, u32[]{:S(2)}) collective-permute-start(bf16[224,1408]{1,0:T(8,128)(2,1)} %add_norm.1.y1), channel_id=1, source_target_pairs={{4,8},{8,4},{5,9},{9,5},{6,10},{10,6},{7,11},{11,7},{20,24},{24,20... | collective-permute-start | bytes 1892360 | tf_op jit(solution)/shard_map/ppermute | solution.py:612
  121.6 23.9 %collective-permute-start.5 = (bf16[224,1408]{1,0:T(8,128)(2,1)}, bf16[224,1408]{1,0:T(8,128)(2,1)}, u32[]{:S(2)}, u32[]{:S(2)}) collective-permute-start(bf16[224,1408]{1,0:T(8,128)(2,1)} %collective-permute-done.2.r1), channel_id=1, source_target_pairs={{4,8},{8,4},{5,9},{9,5},{6,10},{10,6},{7,11},{11,7},{20,24},{24,20... | collective-permute-start | bytes 1892360 | tf_op jit(solution)/shard_map/ppermute | solution.py:615
  123.1 22.4 %collective-permute-start.3 = (bf16[224,1280]{1,0:T(8,128)(2,1)S(1)}, bf16[224,1280]{1,0:T(8,128)(2,1)}, u32[]{:S(2)}, u32[]{:S(2)}) collective-permute-start(bf16[224,1280]{1,0:T(8,128)(2,1)S(1)} %bitcast.13), channel_id=1, source_target_pairs={{0,4},{12,8},{1,5},{13,9},{2,6},{14,10},{3,7},{15,11},{16,20},{28,... | collective-permute-start | bytes 1720328 | tf_op jit(solution)/shard_map/ppermute | solution.py:614
  136.4 0.8 copy-start.1
  137.2 0.8 copy-start.3
  138.1 0.6 copy-start.7
  138.7 6.0 %collective-permute-start.7 = (bf16[16,1280]{1,0:T(8,128)(2,1)S(1)}, bf16[16,1280]{1,0:T(8,128)(2,1)}, u32[]{:S(2)}, u32[]{:S(2)}) collective-permute-start(bf16[16,1280]{1,0:T(8,128)(2,1)S(1)} %get-tuple-element.23), channel_id=1, source_target_pairs={{4,0},{8,4},{12,8},{5,1},{9,5},{13,9},{6,2},{10,6},{14,10},{7,3},{... | collective-permute-start | bytes 122888 | tf_op jit(solution)/shard_map/ppermute | solution.py:633
  140.0 10.0 %collective-permute-start.6 = (bf16[16,2560]{1,0:T(8,128)(2,1)}, bf16[16,2560]{1,0:T(8,128)(2,1)S(1)}, u32[]{:S(2)}, u32[]{:S(2)}) collective-permute-start(bf16[16,2560]{1,0:T(8,128)(2,1)} %copy-done.7), channel_id=1, source_target_pairs={{0,4},{4,8},{8,12},{1,5},{5,9},{9,13},{2,6},{6,10},{10,14},{3,7},{... | collective-permute-start | bytes 245768 | tf_op jit(solution)/shard_map/ppermute | solution.py:632
  145.7 0.8 copy-start.5
  146.6 32.0 %collective-permute-start.8 = (bf16[224,1280]{1,0:T(8,128)(2,1)}, bf16[224,1280]{1,0:T(8,128)(2,1)}, u32[]{:S(2)}, u32[]{:S(2)}) collective-permute-start(bf16[224,1280]{1,0:T(8,128)(2,1)} %get-tuple-element.26), channel_id=1, source_target_pairs={{4,0},{8,12},{5,1},{9,13},{6,2},{10,14},{7,3},{11,15},{20,16},{24,... | collective-permute-start | bytes 1720328 | tf_op jit(solution)/shard_map/ppermute | solution.py:629
  147.9 32.1 %collective-permute-start.9 = (bf16[224,1280]{1,0:T(8,128)(2,1)}, bf16[224,1280]{1,0:T(8,128)(2,1)}, u32[]{:S(2)}, u32[]{:S(2)}) collective-permute-start(bf16[224,1280]{1,0:T(8,128)(2,1)} %get-tuple-element.28), channel_id=1, source_target_pairs={{4,8},{8,4},{5,9},{9,5},{6,10},{10,6},{7,11},{11,7},{20,24},{24,20... | collective-permute-start | bytes 1720328 | tf_op jit(solution)/shard_map/ppermute | solution.py:630
  149.3 0.8 collective-permute-start.10
  150.3 56.2 %collective-permute-start.11 = (bf16[224,1280]{1,0:T(8,128)(2,1)S(1)}, bf16[224,1280]{1,0:T(8,128)(2,1)}, u32[]{:S(2)}, u32[]{:S(2)}) collective-permute-start(bf16[224,1280]{1,0:T(8,128)(2,1)S(1)} %add_convert_fusion), channel_id=1, source_target_pairs={{4,0},{8,12},{5,1},{9,13},{6,2},{10,14},{7,3},{11,15},{20,16},{24,... | collective-permute-start | bytes 1720328 | tf_op jit(solution)/shard_map/ppermute | solution.py:635
  152.3 26.3 %copy-start.4 = (bf16[224,1280]{1,0:T(8,128)(2,1)S(1)}, bf16[224,1280]{1,0:T(8,128)(2,1)}, u32[]{:S(2)}) copy-start(bf16[224,1280]{1,0:T(8,128)(2,1)} %copy-done.3) | copy-start | bytes 1720324
  152.3 26.3 %copy-start.6 = (bf16[224,1280]{1,0:T(8,128)(2,1)S(1)}, bf16[224,1280]{1,0:T(8,128)(2,1)}, u32[]{:S(2)}) copy-start(bf16[224,1280]{1,0:T(8,128)(2,1)} %copy-done.5) | copy-start | bytes 1720324
  153.1 57.0 %all-to-all-start.3 = ((bf16[4,56,1280]{2,1,0:T(8,128)(2,1)}), bf16[4,56,1280]{2,1,0:T(8,128)(2,1)S(1)}, u32[]{:S(2)}, u32[]{:S(2)}) async-start(bf16[4,56,1280]{2,1,0:T(8,128)(2,1)} %bitcast.5), calls=%async_computation.3 | async-start | bytes 1146880 | tf_op jit(solution)/shard_map/all_to_all | solution.py:607
  179.9 26.7 %copy-start.2 = (bf16[224,1280]{1,0:T(8,128)(2,1)S(1)}, bf16[224,1280]{1,0:T(8,128)(2,1)}, u32[]{:S(2)}) copy-start(bf16[224,1280]{1,0:T(8,128)(2,1)} %copy-done.1) | copy-start | bytes 1720324
  206.6 1.5 copy-start.11
  206.6 1.5 copy-start.12
  206.6 1.5 copy-start.13
  210.1 3.5 %copy-start.8 = (bf16[4,56,1280]{2,1,0:T(8,128)(2,1)}, bf16[4,56,1280]{2,1,0:T(8,128)(2,1)S(1)}, u32[]{:S(2)}) copy-start(bf16[4,56,1280]{2,1,0:T(8,128)(2,1)S(1)} %all-to-all-done.3.e1) | copy-start | bytes 1720324
  210.1 10.3 %all-to-all-start.5 = ((bf16[4,56,1280]{2,1,0:T(8,128)(2,1)}), bf16[4,56,1280]{2,1,0:T(8,128)(2,1)S(1)}, u32[]{:S(2)}, u32[]{:S(2)}) async-start(bf16[4,56,1280]{2,1,0:T(8,128)(2,1)} %bitcast.7), calls=%async_computation.5 | async-start | bytes 1146880 | tf_op jit(solution)/shard_map/all_to_all | solution.py:607
  220.4 10.7 %copy-start.9 = (bf16[4,56,1280]{2,1,0:T(8,128)(2,1)}, bf16[4,56,1280]{2,1,0:T(8,128)(2,1)S(1)}, u32[]{:S(2)}) copy-start(bf16[4,56,1280]{2,1,0:T(8,128)(2,1)S(1)} %all-to-all-done.5.e3) | copy-start | bytes 1720324

commit v2 on v1

--- a/solution.py
+++ b/solution.py
@@ -153,9 +153,9 @@
     heads = width // LANES
     half = width // 2
 
-    def body(q, k, v, o, g, ids, x1, x2, x3, o_v, g_v, meta, sems):
+    def body(q, k, v, o, g, ids, x1, x2, x3, q_v, k_v, v_v, o_v, g_v, meta, sems):
         low = lax.axis_index("ctx") < 2
-        loads = run_copies([(o, o_v), (g, g_v)], sems)
+        loads = run_copies([(k, k_v), (v, v_v), (q, q_v), (g, g_v), (o, o_v)], sems)
 
         def moves(first, second, third, fourth, near, far):
             todo = []
@@ -163,23 +163,29 @@
                 base = h * width
                 todo.append((first.at[:, pl.ds(base + near, half)], x1.at[h, :, pl.ds(0, half)]))
                 todo.append((second.at[:, pl.ds(base + near, half)], x1.at[h, :, pl.ds(half, half)]))
+            for h in range(groups):
+                base = h * width
                 todo.append((first.at[:, pl.ds(base + far, half)], x2.at[h, :, pl.ds(0, half)]))
                 todo.append((second.at[:, pl.ds(base + far, half)], x2.at[h, :, pl.ds(half, half)]))
                 todo.append((third.at[:, pl.ds(base, width)], x3.at[h, :, pl.ds(0, width)]))
                 todo.append((fourth.at[:, pl.ds(base, width)], x3.at[h, :, pl.ds(width, width)]))
-            return todo
-
-        count = 6 * groups
+            return [pltpu.make_async_copy(src, dst, sems.at[5 + i]) for i, (src, dst) in enumerate(todo)]
+
+        low_moves = (k_v, v_v, q_v, g_v, half, 0)
+        high_moves = (q_v, g_v, k_v, v_v, 0, half)
+        wait_all(loads[:4])
 
         @pl.when(low)
         def _():
-            run_copies(moves(k, v, q, g, half, 0), sems, 2)
+            for copy in moves(*low_moves):
+                copy.start()
 
         @pl.when(jnp.logical_not(low))
         def _():
-            run_copies(moves(q, g, k, v, 0, half), sems, 2)
-
-        wait_all(loads)
+            for copy in moves(*high_moves):
+                copy.start()
+
+        wait_all(loads[4:])
         lane = lax.broadcasted_iota(jnp.int32, (rows, LANES), 1)
         slot = jnp.where(lane < 3 * heads, lane % heads, -1)
         at_row = lax.broadcasted_iota(jnp.int32, (rows, rows), 0)
@@ -194,28 +200,19 @@
             high, middle, lowest = pieces(total)
             kept = jnp.where(lane < heads, high, jnp.where(lane < 2 * heads, middle, lowest))
             meta[h] = jnp.where(lane < 3 * heads, kept, jnp.where(lane == 3 * heads, own.astype(BF16), 0.0).astype(BF16))
-        last = run_copies([(meta, x1.at[:, :, pl.ds(width, LANES)])], sems, 2 + count)
+        last = run_copies([(meta, x1.at[:, :, pl.ds(width, LANES)])], sems, 5 + 6 * groups)
 
         @pl.when(low)
         def _():
-            wait_all(
-                [
-                    pltpu.make_async_copy(src, dst, sems.at[2 + i])
-                    for i, (src, dst) in enumerate(moves(k, v, q, g, half, 0))
-                ]
-            )
+            wait_all(moves(*low_moves))
 
         @pl.when(jnp.logical_not(low))
         def _():
-            wait_all(
-                [
-                    pltpu.make_async_copy(src, dst, sems.at[2 + i])
-                    for i, (src, dst) in enumerate(moves(q, g, k, v, 0, half))
-                ]
-            )
+            wait_all(moves(*high_moves))
 
         wait_all(last)
 
+    whole = pltpu.VMEM((rows, groups * width), BF16)
     return pl.pallas_call(
         body,
         out_shape=[
@@ -225,12 +222,8 @@
         ],
         in_specs=anywhere(5) + [pl.BlockSpec(memory_space=pltpu.VMEM)],
         out_specs=anywhere(3),
-        scratch_shapes=[
-            pltpu.VMEM((rows, groups * width), BF16),
-            pltpu.VMEM((rows, groups * width), BF16),
-            pltpu.VMEM((groups, rows, LANES), BF16),
-            pltpu.SemaphoreType.DMA((3 + 6 * groups,)),
-        ],
+        scratch_shapes=[whole] * 5
+        + [pltpu.VMEM((groups, rows, LANES), BF16), pltpu.SemaphoreType.DMA((6 + 6 * groups,))],
         cost_estimate=pl.CostEstimate(flops=0, bytes_accessed=10 * rows * groups * width * 2, transcendentals=0),
         name="pack",
     )(queries, keys_in, values_in, attn_out, out_grad, span_row)
@@ -552,31 +545,52 @@
     groups, rows, width = e1.shape
     half = width // 2
 
-    def body(e1, e2, e3, dq, dk, dv, sems):
+    def body(e1, e2, e3, dq, dk, dv, first, second, third, sems):
         low = lax.axis_index("ctx") < 2
         left, right = pl.ds(0, half), pl.ds(half, half)
-
-        def moves(first, far_dst, second_dst, near):
-            todo = []
-            far = half - near
+        todo = []
+        for h in range(groups):
+            todo.append((e1.at[h], first.at[:, pl.ds(h * width, width)]))
+        for h in range(groups):
+            todo.append((e2.at[h, :, right], third.at[:, pl.ds(h * width, half)]))
+            todo.append((e3.at[h, :, right], third.at[:, pl.ds(h * width + half, half)]))
+        for e, near in ((e2, jnp.where(low, 0, half)), (e3, jnp.where(low, half, 0))):
             for h in range(groups):
-                base = h * width
-                todo.append((e1.at[h], first.at[:, pl.ds(base, width)]))
-                todo.append((e2.at[h, :, left], far_dst.at[:, pl.ds(base + far, half)]))
-                todo.append((e3.at[h, :, left], far_dst.at[:, pl.ds(base + near, half)]))
-                spot = 0 if second_dst is None else 1
-                if spot:
-                    todo.append((e2.at[h, :, right], second_dst[0].at[:, pl.ds(base + second_dst[1], half)]))
-                    todo.append((e3.at[h, :, right], second_dst[0].at[:, pl.ds(base + second_dst[2], half)]))
-            return todo
+                at = pl.multiple_of(h * width + near, LANES)
+                todo.append((e.at[h, :, left], second.at[:, pl.ds(at, half)]))
+        loads = run_copies(todo, sems)
+        count = len(loads)
+        wait_all(loads[:groups])
+
+        def stores(near, far):
+            return [
+                pltpu.make_async_copy(src, dst, sems.at[count + i])
+                for i, (src, dst) in enumerate([(first, near), (third, dv), (second, far)])
+            ]
 
         @pl.when(low)
         def _():
-            wait_all(run_copies(moves(dq, dk, (dv, 0, half), half), sems))
+            stores(dq, dk)[0].start()
 
         @pl.when(jnp.logical_not(low))
         def _():
-            wait_all(run_copies(moves(dk, dq, (dv, 0, half), 0), sems))
+            stores(dk, dq)[0].start()
+
+        wait_all(loads[groups:])
+
+        @pl.when(low)
+        def _():
+            made = stores(dq, dk)
+            made[1].start()
+            made[2].start()
+            wait_all(made)
+
+        @pl.when(jnp.logical_not(low))
+        def _():
+            made = stores(dk, dq)
+            made[1].start()
+            made[2].start()
+            wait_all(made)
 
     shape = jax.ShapeDtypeStruct((rows, groups * width), BF16)
     return pl.pallas_call(
@@ -584,7 +598,7 @@
         out_shape=[shape] * 3,
         in_specs=anywhere(3),
         out_specs=anywhere(3),
-        scratch_shapes=[pltpu.SemaphoreType.DMA((5 * groups,))],
+        scratch_shapes=[pltpu.VMEM((rows, groups * width), BF16)] * 3 + [pltpu.SemaphoreType.DMA((3 + 5 * groups,))],
         cost_estimate=pl.CostEstimate(flops=0, bytes_accessed=6 * rows * groups * width * 2, transcendentals=0),
         name="unpack",
     )(e1, e2, e3)
@@ -610,7 +624,9 @@
     y1 = add_norm(to_heads(x1), log_norm.T)
     r1 = lax.ppermute(y1, "ctx", INWARD)
     s1 = lax.ppermute(y1, "ctx", SWAP)
+    x2, y1 = lax.optimization_barrier((x2, y1))
     y2 = to_heads(x2)
+    x3, y2 = lax.optimization_barrier((x3, y2))
     r2 = lax.ppermute(y2, "ctx", INWARD)
     s2 = lax.ppermute(r1, "ctx", SWAP)
     w = to_heads(x3)

time: 286 us -> 154 us (0.54)
  Pallas kernels: 133 us -> 14.5 us
  waiting for transfers between devices: 60 us -> 26.5 us
  starting transfers between devices: 41.6 us -> 56.3 us
    pallas_call x1, Pallas kernels: 71.5 us -> 3.92 us  [pack(): pl.pallas_call(body, out_shape=[jax.ShapeDtypeStruct((groups, rows, width...]
    pallas_call x1, Pallas kernels: 53.4 us -> 2.69 us  [unpack(): pl.pallas_call(body, out_shape=[shape] * 3, in_specs=anywhere(3), out_spe...]
    ppermute x1, waiting for transfers between devices: 22 us -> 0.01 us  [local_split(): out1 = lax.ppermute(out1, 'ctx', OUTWARD)]
    ppermute x1, waiting for transfers between devices: 26.6 us -> 6.39 us  [local_split(): out2 = lax.ppermute(out2, 'ctx', OUTWARD)]
    ppermute x1, starting transfers between devices: 4.55 us -> 21.4 us  [local_split(): dkedge = lax.ppermute(dkedge, 'ctx', UP)]
    ppermute x1, waiting for transfers between devices: 0.01 us -> 10.6 us  [local_split(): r1 = lax.ppermute(y1, 'ctx', INWARD)]
    ppermute x1, starting transfers between devices: 7.18 us -> 1.31 us  [local_split(): r2 = lax.ppermute(y2, 'ctx', INWARD)]
    all_to_all x1, waiting for transfers between devices: 4.47 us -> 0.01 us  [to_heads(): y = lax.all_to_all(x, 'head', split_axis=0, concat_axis=0, tiled=True)]
  transfers between devices with their start and end apart: 15 -> 15, of which waited for: 5 -> 4; matrix products, arithmetic and copies ran while one was open for 3% -> 7% of each run, Pallas kernels for 3% -> 4%
where the time goes in v2:
time: 154 us; the launch traced here: 151 us
  starting transfers between devices  56.3 us (37%)
  blocking collectives  37.4 us (24%)
  waiting for transfers between devices  26.5 us (17%)
  Pallas kernels  14.5 us (9%)
  local copies, waits for them, and re-layouts  7.99 us (5%)
  other arithmetic  7.73 us (5%)
    all_to_all x2, blocking collectives, to_heads(): y = lax.all_to_all(x, 'head', split_axis=0, concat_axis=0, tiled=True)  26.6 us
    ppermute x1, starting transfers between devices, local_split(): dkedge = lax.ppermute(dkedge, 'ctx', UP)  21.4 us
    all_to_all x1, blocking collectives, to_tokens(): return lax.all_to_all(x, 'head', split_axis=0, concat_axis=0, tiled=True)  10.7 us
    ppermute x1, waiting for transfers between devices, local_split(): r1 = lax.ppermute(y1, 'ctx', INWARD)  10.6 us
    all_to_all x2, waiting for transfers between devices, to_tokens(): return lax.all_to_all(x, 'head', split_axis=0, concat_axis=0, tiled=True)  8.44 us
    all_to_all x2, starting transfers between devices, to_tokens(): return lax.all_to_all(x, 'head', split_axis=0, concat_axis=0, tiled=True)  7.73 us
    ppermute x1, starting transfers between devices, local_split(): r1 = lax.ppermute(y1, 'ctx', INWARD)  6.73 us
    ppermute x1, waiting for transfers between devices, local_split(): out2 = lax.ppermute(out2, 'ctx', OUTWARD)  6.39 us
  transfers between devices with their start and end apart: 15, of which 4 were waited for; matrix products, arithmetic and copies ran while one was open for 7% of the time, Pallas kernels for 4%

profile of v2, /device:TPU:0, one launch (start us, length us, event | category | flops | bytes accessed | tf_op | source)
XLA Modules:
  0.0 151.4 jit_solution(4075246578695070655)
XLA Ops:
  0.6 3.9 %pack.1 = (bf16[4,56,1408]{2,1,0:T(8,128)(2,1)}, bf16[4,56,1280]{2,1,0:T(8,128)(2,1)}, bf16[4,56,2560]{2,1,0:T(8,128)(2,1)}) custom-call(bf16[56,5120]{1,0:T(8,128)(2,1)} %q.1, bf16[56,5120]{1,0:T(8,128)(2,1)} %k.1, bf16[56,5120]{1,0:T(8,128)(2,1)} %v.1, bf16[56,5120]{1,0:T(8,128)(2,1)} %o.1, bf16[56,5120]{1,0:T(8,128)(2,1)} %g.1, s32[1,56]{1,0:T(1,128)} %bitcast.18), custom_call_target="tpu_custom_call" | custom-call | bytes 5734400 | tf_op jit(solution)/shard_map/pack/pallas_call | solution.py:216
  4.6 15.6 %all_to_all.30 = bf16[4,56,1408]{2,1,0:T(8,128)(2,1)} all-to-all(bf16[4,56,1408]{2,1,0:T(8,128)(2,1)} %get-tuple-element.22), channel_id=1, replica_groups=mesh['clip'=2,'ctx'=4,'head'=4] {'head'}, dimensions={0} | all-to-all | bytes 1261568 | tf_op jit(solution)/shard_map/all_to_all | solution.py:616
  20.2 1.7 %add_norm.1.y1 = bf16[224,1408]{1,0:T(8,128)(2,1)} custom-call(bf16[224,1408]{1,0:T(8,128)(2,1)} %bitcast.8, f32[10,224]{1,0:T(8,128)} %bitcast.17), custom_call_target="tpu_custom_call", output_to_operand_aliasing={{}: (0, {})} | custom-call | bytes 114688 | tf_op jit(solution)/shard_map/add_norm/pallas_call | solution.py:246
  21.9 11.0 %all_to_all.31 = bf16[4,56,1280]{2,1,0:T(8,128)(2,1)S(1)} all-to-all(bf16[4,56,1280]{2,1,0:T(8,128)(2,1)S(1)} %copy-done.10), channel_id=1, replica_groups=mesh['clip'=2,'ctx'=4,'head'=4] {'head'}, dimensions={0} | all-to-all | bytes 1146880 | tf_op jit(solution)/shard_map/all_to_all | solution.py:616
  32.9 3.7 %all-to-all-start.2 = ((bf16[4,56,2560]{2,1,0:T(8,128)(2,1)}), bf16[4,56,2560]{2,1,0:T(8,128)(2,1)S(1)}, u32[]{:S(2)}, u32[]{:S(2)}) async-start(bf16[4,56,2560]{2,1,0:T(8,128)(2,1)} %get-tuple-element.27), calls=%async_computation.2 | async-start | bytes 2293760 | tf_op jit(solution)/shard_map/all_to_all | solution.py:616
  37.3 6.7 %collective-permute-start.2 = (bf16[224,1408]{1,0:T(8,128)(2,1)S(1)}, bf16[224,1408]{1,0:T(8,128)(2,1)}, u32[]{:S(2)}, u32[]{:S(2)}) collective-permute-start(bf16[224,1408]{1,0:T(8,128)(2,1)S(1)} %copy-done), channel_id=1, source_target_pairs={{0,4},{12,8},{1,5},{13,9},{2,6},{14,10},{3,7},{15,11},{16,20},{28,... | collective-permute-start | bytes 1892360 | tf_op jit(solution)/shard_map/ppermute | solution.py:625
  45.3 1.3 collective-permute-start.3
  47.2 10.6 %collective-permute-done.2.r1 = bf16[224,1408]{1,0:T(8,128)(2,1)} collective-permute-done((bf16[224,1408]{1,0:T(8,128)(2,1)S(1)}, bf16[224,1408]{1,0:T(8,128)(2,1)}, u32[]{:S(2)}, u32[]{:S(2)}) %collective-permute-start.2) | collective-permute-done | bytes 630816 | tf_op jit(solution)/shard_map/ppermute | solution.py:625
  57.9 1.5 collective-permute-start.5
  59.4 0.9 slice_select_fusion
  61.0 1.3 collective-permute-start
  62.9 6.0 %collective-permute-start.1 = (bf16[16,2688]{1,0:T(8,128)(2,1)S(1)}, bf16[16,2688]{1,0:T(8,128)(2,1)S(1)}, u32[]{:S(2)}, u32[]{:S(2)}) collective-permute-start(bf16[16,2688]{1,0:T(8,128)(2,1)S(1)} %pad_maximum_fusion.6), channel_id=1, source_target_pairs={{0,4},{4,8},{8,12},{1,5},{5,9},{9,13},{2,6},{6,10},{10,14},{3,7},{... | collective-permute-start | bytes 258056 | tf_op jit(solution)/shard_map/ppermute | solution.py:641
  68.9 0.8 copy-done.3
  69.8 1.1 copy-done.4
  70.9 1.3 collective-permute-start.8
  72.2 1.5 collective-permute-start.9
  74.5 6.1 %near_pairs.1 = (bf16[224,2560]{1,0:T(8,128)(2,1)S(1)}, bf16[224,1280]{1,0:T(8,128)(2,1)S(1)}, bf16[224,1280]{1,0:T(8,128)(2,1)S(1)}, bf16[16,2560]{1,0:T(8,128)(2,1)S(1)}, bf16[16,1280]{1,0:T(8,128)(2,1)S(1)}) custom-call(bf16[224,1408]{1,0:T(8,128)(2,1)S(1)} %copy-done, bf16[224,1280]{1,0:T(8,128)(2,1)S(1)} %bitcast.15, bf16[224,2560]{1,0:T(8,128)(2,1)S(1)} %bitcast.11, ...), custom_call_target="tpu_custom_call" | custom-call | flops 642252800 | bytes 4587520 | tf_op jit(solution)/shard_map/near_pairs/pallas_call | solution.py:515
  80.6 1.3 collective-permute-start.7
  81.9 21.4 %collective-permute-start.6 = (bf16[16,2560]{1,0:T(8,128)(2,1)S(1)}, bf16[16,2560]{1,0:T(8,128)(2,1)S(1)}, u32[]{:S(2)}, u32[]{:S(2)}) collective-permute-start(bf16[16,2560]{1,0:T(8,128)(2,1)S(1)} %get-tuple-element.30), channel_id=1, source_target_pairs={{0,4},{4,8},{8,12},{1,5},{5,9},{9,13},{2,6},{6,10},{10,14},{3,7},{... | collective-permute-start | bytes 245768 | tf_op jit(solution)/shard_map/ppermute | solution.py:648
  104.4 0.9 collective-permute-done.6
  106.0 0.9 add_convert_fusion
  107.0 1.3 collective-permute-start.11
  108.9 0.8 slice.121
  109.8 4.2 %all-to-all-start.3 = ((bf16[4,56,1280]{2,1,0:T(8,128)(2,1)}), bf16[4,56,1280]{2,1,0:T(8,128)(2,1)}, u32[]{:S(2)}, u32[]{:S(2)}) async-start(bf16[4,56,1280]{2,1,0:T(8,128)(2,1)} %bitcast.5), calls=%async_computation.3 | async-start | bytes 1146880 | tf_op jit(solution)/shard_map/all_to_all | solution.py:621
  114.0 1.3 convert_add_fusion.1
  115.4 6.4 %collective-permute-done.11 = bf16[224,1280]{1,0:T(8,128)(2,1)} collective-permute-done((bf16[224,1280]{1,0:T(8,128)(2,1)}, bf16[224,1280]{1,0:T(8,128)(2,1)}, u32[]{:S(2)}, u32[]{:S(2)}) %collective-permute-start.11) | collective-permute-done | bytes 573472 | tf_op jit(solution)/shard_map/ppermute | solution.py:651
  121.8 1.5 convert_add_fusion
  125.1 0.9 pad_maximum_fusion.4
  126.0 3.6 %all-to-all-start.5 = ((bf16[4,56,1280]{2,1,0:T(8,128)(2,1)}), bf16[4,56,1280]{2,1,0:T(8,128)(2,1)S(1)}, u32[]{:S(2)}, u32[]{:S(2)}) async-start(bf16[4,56,1280]{2,1,0:T(8,128)(2,1)} %bitcast.7), calls=%async_computation.5 | async-start | bytes 1146880 | tf_op jit(solution)/shard_map/all_to_all | solution.py:621
  129.6 8.4 %all-to-all-done.5.e3 = bf16[4,56,1280]{2,1,0:T(8,128)(2,1)S(1)} async-done(((bf16[4,56,1280]{2,1,0:T(8,128)(2,1)}), bf16[4,56,1280]{2,1,0:T(8,128)(2,1)S(1)}, u32[]{:S(2)}, u32[]{:S(2)}) %all-to-all-start.5) | async-done | bytes 573472 | tf_op jit(solution)/shard_map/all_to_all | solution.py:621
  138.1 10.7 %all_to_all.32.e2 = bf16[4,56,1280]{2,1,0:T(8,128)(2,1)} all-to-all(bf16[4,56,1280]{2,1,0:T(8,128)(2,1)S(1)} %bitcast.16), channel_id=1, replica_groups=mesh['clip'=2,'ctx'=4,'head'=4] {'head'}, dimensions={0} | all-to-all | bytes 1146880 | tf_op jit(solution)/shard_map/all_to_all | solution.py:621
  148.8 2.7 %unpack.1 = (bf16[56,5120]{1,0:T(8,128)(2,1)}, bf16[56,5120]{1,0:T(8,128)(2,1)}, bf16[56,5120]{1,0:T(8,128)(2,1)}) custom-call(bf16[4,56,1280]{2,1,0:T(8,128)(2,1)} %all-to-all-done.3.e1, bf16[4,56,1280]{2,1,0:T(8,128)(2,1)} %all_to_all.32.e2, bf16[4,56,1280]{2,1,0:T(8,128)(2,1)} %copy-done.5), custom_call_target="tpu_custom_call" | custom-call | bytes 3440640 | tf_op jit(solution)/shard_map/unpack/pallas_call | solution.py:596
  (65 shorter events, 9.1 us)
Async XLA Ops:
  4.6 17.4 %copy-start.10 = (bf16[4,56,1280]{2,1,0:T(8,128)(2,1)S(1)}, bf16[4,56,1280]{2,1,0:T(8,128)(2,1)}, u32[]{:S(2)}) copy-start(bf16[4,56,1280]{2,1,0:T(8,128)(2,1)} %get-tuple-element.25) | copy-start | bytes 1720324
  32.9 3.7 %copy-start = (bf16[224,1408]{1,0:T(8,128)(2,1)S(1)}, bf16[224,1408]{1,0:T(8,128)(2,1)}, u32[]{:S(2)}) copy-start(bf16[224,1408]{1,0:T(8,128)(2,1)} %add_norm.1.y1) | copy-start | bytes 1892356
  32.9 26.4 %all-to-all-start.2 = ((bf16[4,56,2560]{2,1,0:T(8,128)(2,1)}), bf16[4,56,2560]{2,1,0:T(8,128)(2,1)S(1)}, u32[]{:S(2)}, u32[]{:S(2)}) async-start(bf16[4,56,2560]{2,1,0:T(8,128)(2,1)} %get-tuple-element.27), calls=%async_computation.2 | async-start | bytes 2293760 | tf_op jit(solution)/shard_map/all_to_all | solution.py:616
  36.6 32.3 %collective-permute-start.4 = (bf16[224,1408]{1,0:T(8,128)(2,1)S(1)}, bf16[224,1408]{1,0:T(8,128)(2,1)S(1)}, u32[]{:S(2)}, u32[]{:S(2)}) collective-permute-start(bf16[224,1408]{1,0:T(8,128)(2,1)S(1)} %copy-done), channel_id=1, source_target_pairs={{4,8},{8,4},{5,9},{9,5},{6,10},{10,6},{7,11},{11,7},{20,24},{24,20... | collective-permute-start | bytes 1892360 | tf_op jit(solution)/shard_map/ppermute | solution.py:626
  37.3 20.6 %collective-permute-start.2 = (bf16[224,1408]{1,0:T(8,128)(2,1)S(1)}, bf16[224,1408]{1,0:T(8,128)(2,1)}, u32[]{:S(2)}, u32[]{:S(2)}) collective-permute-start(bf16[224,1408]{1,0:T(8,128)(2,1)S(1)} %copy-done), channel_id=1, source_target_pairs={{0,4},{12,8},{1,5},{13,9},{2,6},{14,10},{3,7},{15,11},{16,20},{28,... | collective-permute-start | bytes 1892360 | tf_op jit(solution)/shard_map/ppermute | solution.py:625
  45.3 23.6 %collective-permute-start.3 = (bf16[224,1280]{1,0:T(8,128)(2,1)S(1)}, bf16[224,1280]{1,0:T(8,128)(2,1)S(1)}, u32[]{:S(2)}, u32[]{:S(2)}) collective-permute-start(bf16[224,1280]{1,0:T(8,128)(2,1)S(1)} %bitcast.12), channel_id=1, source_target_pairs={{0,4},{12,8},{1,5},{13,9},{2,6},{14,10},{3,7},{15,11},{16,20},{28,... | collective-permute-start | bytes 1720328 | tf_op jit(solution)/shard_map/ppermute | solution.py:630
  57.9 11.9 %collective-permute-start.5 = (bf16[224,1408]{1,0:T(8,128)(2,1)}, bf16[224,1408]{1,0:T(8,128)(2,1)}, u32[]{:S(2)}, u32[]{:S(2)}) collective-permute-start(bf16[224,1408]{1,0:T(8,128)(2,1)} %collective-permute-done.2.r1), channel_id=1, source_target_pairs={{4,8},{8,4},{5,9},{9,5},{6,10},{10,6},{7,11},{11,7},{20,24},{24,20... | collective-permute-start | bytes 1892360 | tf_op jit(solution)/shard_map/ppermute | solution.py:631
  61.0 13.5 %collective-permute-start = (bf16[16,2688]{1,0:T(8,128)(2,1)S(1)}, bf16[16,2688]{1,0:T(8,128)(2,1)S(1)}, u32[]{:S(2)}, u32[]{:S(2)}) collective-permute-start(bf16[16,2688]{1,0:T(8,128)(2,1)S(1)} %pad_maximum_fusion.5), channel_id=1, source_target_pairs={{4,0},{8,4},{12,8},{5,1},{9,5},{13,9},{6,2},{10,6},{14,10},{7,3},{... | collective-permute-start | bytes 258056 | tf_op jit(solution)/shard_map/ppermute | solution.py:640
  62.9 11.5 %collective-permute-start.1 = (bf16[16,2688]{1,0:T(8,128)(2,1)S(1)}, bf16[16,2688]{1,0:T(8,128)(2,1)S(1)}, u32[]{:S(2)}, u32[]{:S(2)}) collective-permute-start(bf16[16,2688]{1,0:T(8,128)(2,1)S(1)} %pad_maximum_fusion.6), channel_id=1, source_target_pairs={{0,4},{4,8},{8,12},{1,5},{5,9},{9,13},{2,6},{6,10},{10,14},{3,7},{... | collective-permute-start | bytes 258056 | tf_op jit(solution)/shard_map/ppermute | solution.py:641
  68.9 0.8 copy-start.3
  69.8 1.1 copy-start.4
  70.9 43.0 %collective-permute-start.8 = (bf16[224,1280]{1,0:T(8,128)(2,1)}, bf16[224,1280]{1,0:T(8,128)(2,1)}, u32[]{:S(2)}, u32[]{:S(2)}) collective-permute-start(bf16[224,1280]{1,0:T(8,128)(2,1)} %get-tuple-element.34), channel_id=1, source_target_pairs={{4,0},{8,12},{5,1},{9,13},{6,2},{10,14},{7,3},{11,15},{20,16},{24,... | collective-permute-start | bytes 1720328 | tf_op jit(solution)/shard_map/ppermute | solution.py:645
  72.2 43.1 %collective-permute-start.9 = (bf16[224,1280]{1,0:T(8,128)(2,1)}, bf16[224,1280]{1,0:T(8,128)(2,1)}, u32[]{:S(2)}, u32[]{:S(2)}) collective-permute-start(bf16[224,1280]{1,0:T(8,128)(2,1)} %get-tuple-element.36), channel_id=1, source_target_pairs={{4,8},{8,4},{5,9},{9,5},{6,10},{10,6},{7,11},{11,7},{20,24},{24,20... | collective-permute-start | bytes 1720328 | tf_op jit(solution)/shard_map/ppermute | solution.py:646
  73.7 32.3 %collective-permute-start.10 = (bf16[224,1280]{1,0:T(8,128)(2,1)S(1)}, bf16[224,1280]{1,0:T(8,128)(2,1)S(1)}, u32[]{:S(2)}, u32[]{:S(2)}) collective-permute-start(bf16[224,1280]{1,0:T(8,128)(2,1)S(1)} %get-tuple-element.37), channel_id=1, source_target_pairs={{4,8},{8,4},{5,9},{9,5},{6,10},{10,6},{7,11},{11,7},{20,24},{24,20... | collective-permute-start | bytes 1720328 | tf_op jit(solution)/shard_map/ppermute | solution.py:644
  80.6 23.1 %copy-start.1 = (bf16[224,1280]{1,0:T(8,128)(2,1)}, bf16[224,1280]{1,0:T(8,128)(2,1)S(1)}, u32[]{:S(2)}) copy-start(bf16[224,1280]{1,0:T(8,128)(2,1)S(1)} %get-tuple-element.32) | copy-start | bytes 1720324
  80.6 23.2 %collective-permute-start.7 = (bf16[16,1280]{1,0:T(8,128)(2,1)S(1)}, bf16[16,1280]{1,0:T(8,128)(2,1)S(1)}, u32[]{:S(2)}, u32[]{:S(2)}) collective-permute-start(bf16[16,1280]{1,0:T(8,128)(2,1)S(1)} %get-tuple-element.31), channel_id=1, source_target_pairs={{4,0},{8,4},{12,8},{5,1},{9,5},{13,9},{6,2},{10,6},{14,10},{7,3},{... | collective-permute-start | bytes 122888 | tf_op jit(solution)/shard_map/ppermute | solution.py:649
  81.9 23.4 %collective-permute-start.6 = (bf16[16,2560]{1,0:T(8,128)(2,1)S(1)}, bf16[16,2560]{1,0:T(8,128)(2,1)S(1)}, u32[]{:S(2)}, u32[]{:S(2)}) collective-permute-start(bf16[16,2560]{1,0:T(8,128)(2,1)S(1)} %get-tuple-element.30), channel_id=1, source_target_pairs={{0,4},{4,8},{8,12},{1,5},{5,9},{9,13},{2,6},{6,10},{10,14},{3,7},{... | collective-permute-start | bytes 245768 | tf_op jit(solution)/shard_map/ppermute | solution.py:648
  103.8 0.6 copy-start.14
  105.4 0.6 copy-start.6
  105.4 0.7 copy-start.8
  107.0 14.8 %collective-permute-start.11 = (bf16[224,1280]{1,0:T(8,128)(2,1)}, bf16[224,1280]{1,0:T(8,128)(2,1)}, u32[]{:S(2)}, u32[]{:S(2)}) collective-permute-start(bf16[224,1280]{1,0:T(8,128)(2,1)} %add_convert_fusion), channel_id=1, source_target_pairs={{4,0},{8,12},{5,1},{9,13},{6,2},{10,14},{7,3},{11,15},{20,16},{24,... | collective-permute-start | bytes 1720328 | tf_op jit(solution)/shard_map/ppermute | solution.py:651
  108.9 5.0 %copy-start.2 = (bf16[224,1280]{1,0:T(8,128)(2,1)S(1)}, bf16[224,1280]{1,0:T(8,128)(2,1)}, u32[]{:S(2)}) copy-start(bf16[224,1280]{1,0:T(8,128)(2,1)} %copy-done.1) | copy-start | bytes 1720324
  109.8 16.2 %all-to-all-start.3 = ((bf16[4,56,1280]{2,1,0:T(8,128)(2,1)}), bf16[4,56,1280]{2,1,0:T(8,128)(2,1)}, u32[]{:S(2)}, u32[]{:S(2)}) async-start(bf16[4,56,1280]{2,1,0:T(8,128)(2,1)} %bitcast.5), calls=%async_computation.3 | async-start | bytes 1146880 | tf_op jit(solution)/shard_map/all_to_all | solution.py:621
  121.8 1.5 %copy-start.12 = (f32[16,640]{1,0:T(8,128)S(1)}, f32[16,640]{1,0:T(8,128)}, u32[]{:S(2)}) copy-start(f32[16,640]{1,0:T(8,128)} %get-tuple-element.61) | copy-start | bytes 122884
  121.8 1.5 %copy-start.13 = (f32[16,640]{1,0:T(8,128)S(1)}, f32[16,640]{1,0:T(8,128)}, u32[]{:S(2)}) copy-start(f32[16,640]{1,0:T(8,128)} %get-tuple-element.62) | copy-start | bytes 122884
  121.8 1.6 %copy-start.15 = (bf16[16,1280]{1,0:T(8,128)(2,1)S(1)}, bf16[16,1280]{1,0:T(8,128)(2,1)}, u32[]{:S(2)}) copy-start(bf16[16,1280]{1,0:T(8,128)(2,1)} %copy-done.14) | copy-start | bytes 122884
  121.8 1.6 %copy-start.16 = (pred[1280]{0:T(1024)(128)(4,1)S(1)}, pred[1280]{0:T(1024)(128)(4,1)}, u32[]{:S(2)}) copy-start(pred[1280]{0:T(1024)(128)(4,1)} %constant.14.clone.1) | copy-start | bytes 3844
  123.2 0.8 copy-start.11
  124.0 0.9 copy-start.7
  124.0 0.9 copy-start.9
  126.0 12.1 %all-to-all-start.5 = ((bf16[4,56,1280]{2,1,0:T(8,128)(2,1)}), bf16[4,56,1280]{2,1,0:T(8,128)(2,1)S(1)}, u32[]{:S(2)}, u32[]{:S(2)}) async-start(bf16[4,56,1280]{2,1,0:T(8,128)(2,1)} %bitcast.7), calls=%async_computation.5 | async-start | bytes 1146880 | tf_op jit(solution)/shard_map/all_to_all | solution.py:621
  138.0 10.7 %copy-start.5 = (bf16[4,56,1280]{2,1,0:T(8,128)(2,1)}, bf16[4,56,1280]{2,1,0:T(8,128)(2,1)S(1)}, u32[]{:S(2)}) copy-start(bf16[4,56,1280]{2,1,0:T(8,128)(2,1)S(1)} %all-to-all-done.5.e3) | copy-start | bytes 1720324

commit v3 on v2

--- a/solution.py
+++ b/solution.py
@@ -9,6 +9,7 @@
 
 SPANS = 12
 EDGE = 16
+VMEM_LIMIT = 32 * 2**20
 LANES = 128
 BF16 = jnp.bfloat16
 F32 = jnp.float32
@@ -153,7 +154,7 @@
     heads = width // LANES
     half = width // 2
 
-    def body(q, k, v, o, g, ids, x1, x2, x3, q_v, k_v, v_v, o_v, g_v, meta, sems):
+    def body(q, k, v, o, g, ids, x1, rest, q_v, k_v, v_v, o_v, g_v, meta, sems):
         low = lax.axis_index("ctx") < 2
         loads = run_copies([(k, k_v), (v, v_v), (q, q_v), (g, g_v), (o, o_v)], sems)
 
@@ -165,10 +166,10 @@
                 todo.append((second.at[:, pl.ds(base + near, half)], x1.at[h, :, pl.ds(half, half)]))
             for h in range(groups):
                 base = h * width
-                todo.append((first.at[:, pl.ds(base + far, half)], x2.at[h, :, pl.ds(0, half)]))
-                todo.append((second.at[:, pl.ds(base + far, half)], x2.at[h, :, pl.ds(half, half)]))
-                todo.append((third.at[:, pl.ds(base, width)], x3.at[h, :, pl.ds(0, width)]))
-                todo.append((fourth.at[:, pl.ds(base, width)], x3.at[h, :, pl.ds(width, width)]))
+                todo.append((first.at[:, pl.ds(base + far, half)], rest.at[h, :, pl.ds(0, half)]))
+                todo.append((second.at[:, pl.ds(base + far, half)], rest.at[h, :, pl.ds(half, half)]))
+                todo.append((third.at[:, pl.ds(base, width)], rest.at[h, :, pl.ds(width, width)]))
+                todo.append((fourth.at[:, pl.ds(base, width)], rest.at[h, :, pl.ds(2 * width, width)]))
             return [pltpu.make_async_copy(src, dst, sems.at[5 + i]) for i, (src, dst) in enumerate(todo)]
 
         low_moves = (k_v, v_v, q_v, g_v, half, 0)
@@ -217,11 +218,10 @@
         body,
         out_shape=[
             jax.ShapeDtypeStruct((groups, rows, width + LANES), BF16),
-            jax.ShapeDtypeStruct((groups, rows, width), BF16),
-            jax.ShapeDtypeStruct((groups, rows, 2 * width), BF16),
+            jax.ShapeDtypeStruct((groups, rows, 3 * width), BF16),
         ],
         in_specs=anywhere(5) + [pl.BlockSpec(memory_space=pltpu.VMEM)],
-        out_specs=anywhere(3),
+        out_specs=anywhere(2),
         scratch_shapes=[whole] * 5
         + [pltpu.VMEM((groups, rows, LANES), BF16), pltpu.SemaphoreType.DMA((6 + 6 * groups,))],
         cost_estimate=pl.CostEstimate(flops=0, bytes_accessed=10 * rows * groups * width * 2, transcendentals=0),
@@ -278,13 +278,65 @@
     return query_term, key_term, value_term
 
 
-def far_pairs(y1, y2, w, r1, r2, s1, s2):
-    rows, width = y2.shape
+def cut(y1, rest):
+    rows = rest.shape[0]
+    width = rest.shape[1] // 3
+    half = width // 2
+
+    def body(y1, rest, y2, kedge, qedge, sems):
+        low = lax.axis_index("ctx") < 2
+        top, bottom, tail = pl.ds(0, EDGE), pl.ds(rows - EDGE, EDGE), pl.ds(width, LANES)
+        end = pl.ds(2 * width, LANES)
+        made = run_copies(
+            [
+                (y1.at[top, tail], kedge.at[:, end]),
+                (y1.at[bottom, tail], qedge.at[:, end]),
+                (rest.at[:, pl.ds(0, width)], y2),
+            ],
+            sems,
+        )
+
+        def joined(first, second, at, edge):
+            todo = []
+            for i in range(2):
+                for j, part in enumerate((first, second)):
+                    todo.append((part.at[at, pl.ds(i * half, half)], edge.at[:, pl.ds(i * width + j * half, half)]))
+            return todo
+
+        whole = pl.ds(width, 2 * width)
+
+        @pl.when(low)
+        def _():
+            todo = joined(rest, y1, top, kedge) + [(rest.at[bottom, whole], qedge.at[:, pl.ds(0, 2 * width)])]
+            wait_all(run_copies(todo, sems, 3))
+
+        @pl.when(jnp.logical_not(low))
+        def _():
+            todo = joined(y1, rest, bottom, qedge) + [(rest.at[top, whole], kedge.at[:, pl.ds(0, 2 * width)])]
+            wait_all(run_copies(todo, sems, 3))
+
+        wait_all(made)
+
+    edge = jax.ShapeDtypeStruct((EDGE, 2 * width + LANES), BF16)
+    return pl.pallas_call(
+        body,
+        out_shape=[jax.ShapeDtypeStruct((rows, width), BF16), edge, edge],
+        in_specs=anywhere(2),
+        out_specs=[pl.BlockSpec(memory_space=pltpu.VMEM)] * 3,
+        scratch_shapes=[pltpu.SemaphoreType.DMA((8,))],
+        compiler_params=pltpu.CompilerParams(vmem_limit_bytes=60 * 2**20),
+        cost_estimate=pl.CostEstimate(flops=0, bytes_accessed=4 * rows * width, transcendentals=0),
+        name="cut",
+    )(y1, rest)
+
+
+def far_pairs(y1, rest, r1, r2, s1, s2):
+    rows, width = r2.shape
     half = width // 2
     count = half // LANES
     heads = 2 * count
 
-    def body(y1, y2, w, r1, r2, s1, s2, swap1, out1, swap2, l1, l2, l3, buf, grads, meta, info, sems):
+    def body(y1, rest, r1, r2, s1, s2, swap1, out1, swap2, l1, l2, l3, buf, grads, meta, info, sems):
         z = lax.axis_index("ctx")
         one = z == 1
 
@@ -307,11 +359,11 @@
                     (s1.at[:, main], buf.at[pick(0, 3)]),
                     (s2.at[:, main], buf.at[pick(1, 2)]),
                     (r2, buf.at[pick(2, 1)]),
-                    (y2, buf.at[pick(3, 0)]),
-                    (w.at[:, pl.ds(near, half)], buf.at[4, :, left]),
-                    (w.at[:, pl.ds(width + near, half)], buf.at[4, :, right]),
-                    (w.at[:, pl.ds(other, half)], buf.at[5, :, left]),
-                    (w.at[:, pl.ds(width + other, half)], buf.at[5, :, right]),
+                    (rest.at[:, main], buf.at[pick(3, 0)]),
+                    (rest.at[:, pl.ds(width + near, half)], buf.at[4, :, left]),
+                    (rest.at[:, pl.ds(2 * width + near, half)], buf.at[4, :, right]),
+                    (rest.at[:, pl.ds(width + other, half)], buf.at[5, :, left]),
+                    (rest.at[:, pl.ds(2 * width + other, half)], buf.at[5, :, right]),
                     (r1.at[:, main], buf.at[6]),
                 ],
                 sems,
@@ -372,7 +424,7 @@
                 grads[6, :, b] = jnp.where(one, extra_v, 0.0).astype(BF16)
                 return carry
 
-            lax.fori_loop(0, count, step, 0)
+            lax.fori_loop(0, count, step, 0, unroll=True)
             made = run_copies(
                 [
                     (grads.at[pick(1, 2)], swap1),
@@ -400,7 +452,7 @@
             single_shape,
             single_shape,
         ],
-        in_specs=anywhere(7),
+        in_specs=anywhere(6),
         out_specs=anywhere(6),
         scratch_shapes=[
             pltpu.VMEM((7, rows, width), BF16),
@@ -409,32 +461,33 @@
             pltpu.VMEM((3, 32, rows), F32),
             pltpu.SemaphoreType.DMA((13,)),
         ],
-        compiler_params=pltpu.CompilerParams(vmem_limit_bytes=40 * 2**20),
+        compiler_params=pltpu.CompilerParams(vmem_limit_bytes=VMEM_LIMIT),
         cost_estimate=pl.CostEstimate(
             flops=30 * 10 * rows * rows * LANES, bytes_accessed=30 * rows * width, transcendentals=30 * rows * rows
         ),
         name="far_pairs",
-    )(y1, y2, w, r1, r2, s1, s2)
-
-
-def near_pairs(y1, y2, w, key_edge, query_edge):
-    rows, width = y2.shape
+    )(y1, rest, r1, r2, s1, s2)
+
+
+def near_pairs(y1, rest, key_edge, query_edge):
+    rows = rest.shape[0]
+    width = rest.shape[1] // 3
     half = width // 2
     count = half // LANES
     heads = 2 * count
     total = rows + EDGE
 
-    def body(y1, y2, w, kedge, qedge, dw, dy1, dy2, dkedge, dqedge, qbuf, kbuf, dq, dk, kmeta, qmeta, info, sems):
+    def body(y1, rest, kedge, qedge, dw, dy1, dy2, dkedge, dqedge, qbuf, kbuf, dq, dk, kmeta, qmeta, info, sems):
         low = lax.axis_index("ctx") < 2
         left, right = pl.ds(0, half), pl.ds(half, half)
         own, past = pl.ds(0, rows), pl.ds(rows, EDGE)
         main = pl.ds(0, width)
 
-        def halves(array, there, back=False):
+        def halves(array, there, back=False, start=0, parts=2):
             todo = []
             for i in range(2):
-                for j in range(array.shape[1] // width):
-                    wide = array.at[:, pl.ds(j * width + i * half, half)]
+                for j in range(parts):
+                    wide = array.at[:, pl.ds(start + j * width + i * half, half)]
                     narrow = there(i, right if j else left)
                     todo.append((narrow, wide) if back else (wide, narrow))
             return todo
@@ -453,14 +506,14 @@
 
         @pl.when(low)
         def _():
-            todo = halves(w, lambda i, cols: qbuf.at[i, own, cols])
-            todo += [(y2, kbuf.at[0, own]), (y1.at[:, main], kbuf.at[1, own])]
+            todo = halves(rest, lambda i, cols: qbuf.at[i, own, cols], start=width)
+            todo += [(rest.at[:, main], kbuf.at[0, own]), (y1.at[:, main], kbuf.at[1, own])]
             wait_all(run_copies(todo, sems, 12))
 
         @pl.when(jnp.logical_not(low))
         def _():
-            todo = halves(w, lambda i, cols: kbuf.at[i, own, cols])
-            todo += [(y1.at[:, main], qbuf.at[0, own]), (y2, qbuf.at[1, own])]
+            todo = halves(rest, lambda i, cols: kbuf.at[i, own, cols], start=width)
+            todo += [(y1.at[:, main], qbuf.at[0, own]), (rest.at[:, main], qbuf.at[1, own])]
             wait_all(run_copies(todo, sems, 12))
 
         wait_all(shared)
@@ -490,11 +543,11 @@
                 dk[i, :, b] = value_term.astype(BF16)
                 return carry
 
-            lax.fori_loop(0, count, step, 0)
+            lax.fori_loop(0, count, step, 0, unroll=True)
 
         made = run_copies(
             halves(dkedge, lambda i, cols: dk.at[i, past, cols], back=True)
-            + halves(dqedge, lambda i, cols: dq.at[i, past, cols], back=True),
+            + halves(dqedge, lambda i, cols: dq.at[i, past, cols], back=True, parts=1),
             sems,
         )
 
@@ -521,7 +574,7 @@
             jax.ShapeDtypeStruct((EDGE, 2 * width), BF16),
             jax.ShapeDtypeStruct((EDGE, width), BF16),
         ],
-        in_specs=anywhere(5),
+        in_specs=anywhere(4),
         out_specs=anywhere(5),
         scratch_shapes=[
             pltpu.VMEM((2, total, width), BF16),
@@ -533,84 +586,153 @@
             pltpu.VMEM((32, total), F32),
             pltpu.SemaphoreType.DMA((18,)),
         ],
-        compiler_params=pltpu.CompilerParams(vmem_limit_bytes=32 * 2**20),
+        compiler_params=pltpu.CompilerParams(vmem_limit_bytes=VMEM_LIMIT),
         cost_estimate=pl.CostEstimate(
             flops=10 * 10 * rows * rows * LANES, bytes_accessed=16 * rows * width, transcendentals=10 * rows * rows
         ),
         name="near_pairs",
-    )(y1, y2, w, key_edge, query_edge)
-
-
-def unpack(e1, e2, e3):
-    groups, rows, width = e1.shape
+    )(y1, rest, key_edge, query_edge)
+
+
+def finish_first(dw, l1, dy2, l2, out1, dkedge, dqedge):
+    rows, width = dy2.shape
     half = width // 2
 
-    def body(e1, e2, e3, dq, dk, dv, first, second, third, sems):
+    def body(dw, l1, dy2, l2, out1, dk, dq, e, v):
+        z = lax.axis_index("ctx")
+        low, middle = z < 2, (z == 1) | (z == 2)
+
+        def own(cols):
+            return dw[:, cols].astype(F32) + jnp.where(middle, l1[:, cols].astype(F32), 0.0)
+
+        def second(cols):
+            return dy2[:, cols].astype(F32) + jnp.where(middle, l2[:, cols].astype(F32), 0.0) + out1[:, cols].astype(F32)
+
+        def put(dst, cols, total, first, last=None):
+            end = total[rows - EDGE :] if last is None else total[rows - EDGE :] + last
+            total = jnp.concatenate([total[:EDGE] + first, total[EDGE : rows - EDGE], end], axis=0)
+            dst[:, cols] = total.astype(BF16)
+
+        def key_edge(cols):
+            return dk[:, cols].astype(F32)
+
+        def query_edge(cols):
+            return dq[:, cols].astype(F32)
+
+        a, b = pl.ds(0, half), pl.ds(half, half)
+        c, d = pl.ds(width, half), pl.ds(width + half, half)
+        for cols in (a, b):
+            put(e, cols, own(cols), jnp.where(low, 0.0, key_edge(cols)), jnp.where(low, query_edge(cols), 0.0))
+        put(e, c, second(a), jnp.where(low, key_edge(a), 0.0), jnp.where(low, 0.0, query_edge(b)))
+        put(e, d, jnp.where(low, second(b), own(c)), key_edge(c))
+        put(v, pl.ds(0, half), own(d), key_edge(d))
+
+    return pl.pallas_call(
+        body,
+        out_shape=[jax.ShapeDtypeStruct((rows, 2 * width), BF16), jax.ShapeDtypeStruct((rows, half), BF16)],
+        in_specs=[pl.BlockSpec(memory_space=pltpu.VMEM)] * 7,
+        out_specs=[pl.BlockSpec(memory_space=pltpu.VMEM)] * 2,
+        compiler_params=pltpu.CompilerParams(vmem_limit_bytes=32 * 2**20),
+        cost_estimate=pl.CostEstimate(flops=0, bytes_accessed=16 * rows * width, transcendentals=0),
+        name="finish_first",
+    )(dw, l1, dy2, l2, out1, dkedge, dqedge)
+
+
+def finish_second(dy1, swap2, out2, v, dkedge, dqedge):
+    rows, width = dy1.shape
+    half = width // 2
+
+    def body(dy1, swap2, out2, v, dk, dq, e):
         low = lax.axis_index("ctx") < 2
-        left, right = pl.ds(0, half), pl.ds(half, half)
+        a, b = pl.ds(0, half), pl.ds(half, half)
+        end = pl.ds(width + half, half)
+
+        def total(cols):
+            return dy1[:, cols].astype(F32) + swap2[:, cols].astype(F32) + out2[:, cols].astype(F32)
+
+        left = total(a)
+        first = left[:EDGE] + jnp.where(low, dk[:, b].astype(F32), 0.0)
+        last = left[rows - EDGE :] + jnp.where(low, 0.0, dq[:, a].astype(F32))
+        e[:, a] = jnp.concatenate([first, left[EDGE : rows - EDGE], last], axis=0).astype(BF16)
+        right = total(b)
+        right = jnp.concatenate([right[:EDGE] + dk[:, end].astype(F32), right[EDGE:]], axis=0)
+        e[:, b] = jnp.where(low, right.astype(BF16), v[...])
+
+    return pl.pallas_call(
+        body,
+        out_shape=jax.ShapeDtypeStruct((rows, width), BF16),
+        in_specs=[pl.BlockSpec(memory_space=pltpu.VMEM)] * 6,
+        out_specs=pl.BlockSpec(memory_space=pltpu.VMEM),
+        compiler_params=pltpu.CompilerParams(vmem_limit_bytes=32 * 2**20),
+        cost_estimate=pl.CostEstimate(flops=0, bytes_accessed=9 * rows * width, transcendentals=0),
+        name="finish_second",
+    )(dy1, swap2, out2, v, dkedge, dqedge)
+
+
+def unpack(early, late):
+    groups, rows, width = late.shape
+    half = width // 2
+
+    def body(early, late, dq, dk, dv, first, second, third, sems):
+        low = lax.axis_index("ctx") < 2
         todo = []
         for h in range(groups):
-            todo.append((e1.at[h], first.at[:, pl.ds(h * width, width)]))
+            todo.append((early.at[h, :, pl.ds(0, width)], first.at[:, pl.ds(h * width, width)]))
         for h in range(groups):
-            todo.append((e2.at[h, :, right], third.at[:, pl.ds(h * width, half)]))
-            todo.append((e3.at[h, :, right], third.at[:, pl.ds(h * width + half, half)]))
-        for e, near in ((e2, jnp.where(low, 0, half)), (e3, jnp.where(low, half, 0))):
-            for h in range(groups):
-                at = pl.multiple_of(h * width + near, LANES)
-                todo.append((e.at[h, :, left], second.at[:, pl.ds(at, half)]))
+            todo.append((early.at[h, :, pl.ds(width + half, half)], third.at[:, pl.ds(h * width, half)]))
+            todo.append((late.at[h, :, pl.ds(half, half)], third.at[:, pl.ds(h * width + half, half)]))
+        for h in range(groups):
+            here = pl.multiple_of(h * width + jnp.where(low, 0, half), LANES)
+            there = pl.multiple_of(h * width + jnp.where(low, half, 0), LANES)
+            todo.append((early.at[h, :, pl.ds(width, half)], second.at[:, pl.ds(here, half)]))
+            todo.append((late.at[h, :, pl.ds(0, half)], second.at[:, pl.ds(there, half)]))
         loads = run_copies(todo, sems)
         count = len(loads)
         wait_all(loads[:groups])
 
-        def stores(near, far):
-            return [
-                pltpu.make_async_copy(src, dst, sems.at[count + i])
-                for i, (src, dst) in enumerate([(first, near), (third, dv), (second, far)])
-            ]
-
         @pl.when(low)
         def _():
-            stores(dq, dk)[0].start()
+            run_copies([(first, dq)], sems, count)
 
         @pl.when(jnp.logical_not(low))
         def _():
-            stores(dk, dq)[0].start()
-
-        wait_all(loads[groups:])
+            run_copies([(first, dk)], sems, count)
+
+        wait_all(loads[groups : 3 * groups])
+        run_copies([(third, dv)], sems, count + 1)
+        wait_all(loads[3 * groups :])
 
         @pl.when(low)
         def _():
-            made = stores(dq, dk)
-            made[1].start()
-            made[2].start()
-            wait_all(made)
+            wait_all(run_copies([(second, dk)], sems, count + 2))
+            pltpu.make_async_copy(first, dq, sems.at[count]).wait()
 
         @pl.when(jnp.logical_not(low))
         def _():
-            made = stores(dk, dq)
-            made[1].start()
-            made[2].start()
-            wait_all(made)
+            wait_all(run_copies([(second, dq)], sems, count + 2))
+            pltpu.make_async_copy(first, dk, sems.at[count]).wait()
+
+        pltpu.make_async_copy(third, dv, sems.at[count + 1]).wait()
 
     shape = jax.ShapeDtypeStruct((rows, groups * width), BF16)
     return pl.pallas_call(
         body,
         out_shape=[shape] * 3,
-        in_specs=anywhere(3),
+        in_specs=anywhere(2),
         out_specs=anywhere(3),
         scratch_shapes=[pltpu.VMEM((rows, groups * width), BF16)] * 3 + [pltpu.SemaphoreType.DMA((3 + 5 * groups,))],
         cost_estimate=pl.CostEstimate(flops=0, bytes_accessed=6 * rows * groups * width * 2, transcendentals=0),
         name="unpack",
-    )(e1, e2, e3)
+    )(early, late)
+
+
+def after(array, other):
+    return lax.optimization_barrier((array, other))[0]
 
 
 def local_split(queries, keys_in, values_in, attn_out, out_grad, log_norm, span_id):
     groups = lax.axis_size("head")
     width = queries.shape[1] // groups
-    half = width // 2
-    z = lax.axis_index("ctx")
-    low = z < 2
-    middle = (z == 1) | (z == 2)
 
     def to_heads(x):
         y = lax.all_to_all(x, "head", split_axis=0, concat_axis=0, tiled=True)
@@ -620,63 +742,31 @@
         x = x.reshape(groups, -1, x.shape[1])
         return lax.all_to_all(x, "head", split_axis=0, concat_axis=0, tiled=True)
 
-    x1, x2, x3 = pack(queries, keys_in, values_in, attn_out, out_grad, span_id.reshape(1, -1), groups, width)
+    x1, rest = pack(queries, keys_in, values_in, attn_out, out_grad, span_id.reshape(1, -1), groups, width)
     y1 = add_norm(to_heads(x1), log_norm.T)
     r1 = lax.ppermute(y1, "ctx", INWARD)
     s1 = lax.ppermute(y1, "ctx", SWAP)
-    x2, y1 = lax.optimization_barrier((x2, y1))
-    y2 = to_heads(x2)
-    x3, y2 = lax.optimization_barrier((x3, y2))
+    rest = to_heads(after(rest, y1))
+    y2, key_edge, query_edge = cut(y1, rest)
+    y2, r1, s1 = lax.optimization_barrier((y2, r1, s1))
     r2 = lax.ppermute(y2, "ctx", INWARD)
     s2 = lax.ppermute(r1, "ctx", SWAP)
-    w = to_heads(x3)
-
-    def joined(first, second, at):
-        return jnp.concatenate([first[at, :half], second[at, :half], first[at, half:width], second[at, half:width]], axis=1)
-
-    top, bottom = slice(0, EDGE), slice(y2.shape[0] - EDGE, None)
-    key_edge = jnp.where(low, joined(y2, y1, top), w[top])
-    query_edge = jnp.where(low, w[bottom], joined(y1, y2, bottom))
-    key_edge = lax.ppermute(jnp.concatenate([key_edge, y1[top, width:]], axis=1), "ctx", DOWN)
-    query_edge = lax.ppermute(jnp.concatenate([query_edge, y1[bottom, width:]], axis=1), "ctx", UP)
-
-    swap1, out1, swap2, l1, l2, l3 = far_pairs(y1, y2, w, r1, r2, s1, s2)
+    key_edge = lax.ppermute(key_edge, "ctx", DOWN)
+    query_edge = lax.ppermute(query_edge, "ctx", UP)
+    rest, key_edge, query_edge = lax.optimization_barrier((rest, key_edge, query_edge))
+    swap1, out1, swap2, l1, l2, l3 = far_pairs(y1, rest, r1, r2, s1, s2)
+    dw, dy1, dy2, dkedge, dqedge = near_pairs(y1, rest, after(key_edge, l3), query_edge)
     swap1 = lax.ppermute(swap1, "ctx", SWAP)
     out1 = lax.ppermute(out1, "ctx", OUTWARD)
-    swap2 = lax.ppermute(swap2, "ctx", SWAP)
-    dw, dy1, dy2, dkedge, dqedge = near_pairs(y1, y2, w, key_edge, query_edge)
     dkedge = lax.ppermute(dkedge, "ctx", UP)
     dqedge = lax.ppermute(dqedge, "ctx", DOWN)
-    out2 = (swap1.astype(F32) + l3.astype(F32)).astype(BF16)
-    out2 = lax.ppermute(out2, "ctx", OUTWARD)
-
-    def wide(x):
-        return x.astype(F32)
-
-    def kept(x):
-        return jnp.where(middle, x.astype(F32), 0.0)
-
-    def edged(total, first, last):
-        return jnp.concatenate([total[:EDGE] + first, total[EDGE:-EDGE], total[-EDGE:] + last], axis=0).astype(BF16)
-
-    def sides(x):
-        parts = jnp.split(x, x.shape[1] // half, axis=1)
-        return jnp.concatenate(parts[0::2], axis=1), jnp.concatenate(parts[1::2], axis=1)
-
-    dk_low, dk_high = jnp.where(low, wide(dkedge), 0.0), jnp.where(low, 0.0, wide(dkedge))
-    dq_low, dq_high = jnp.where(low, wide(dqedge), 0.0), jnp.where(low, 0.0, wide(dqedge))
-    dq_low, dq_high = (jnp.concatenate([x, jnp.zeros_like(x)], axis=1) for x in (dq_low, dq_high))
-    gw = edged(wide(dw) + kept(l1), dk_high, dq_low)
-    first_k, second_k = sides(dk_low)
-    first_q, second_q = sides(dq_high)
-    g2 = edged(wide(dy2) + kept(l2) + wide(out1), first_k, second_q)
-    g1 = edged(wide(dy1) + wide(swap2) + wide(out2), second_k, first_q)
-    e1 = to_tokens(gw[:, :width])
-    e2 = to_tokens(
-        jnp.concatenate([g2[:, :half], jnp.where(low, g2[:, half:], gw[:, width : width + half])], axis=1)
-    )
-    e3 = to_tokens(jnp.concatenate([g1[:, :half], jnp.where(low, g1[:, half:], gw[:, width + half :])], axis=1))
-    return tuple(unpack(e1, e2, e3))
+    sum1 = (swap1.astype(F32) + l3.astype(F32)).astype(BF16)
+    swap2 = lax.ppermute(after(swap2, swap1), "ctx", SWAP)
+    out2 = lax.ppermute(sum1, "ctx", OUTWARD)
+    dkedge, dqedge, out1 = after((dkedge, dqedge, out1), sum1)
+    early, kept = finish_first(dw, l1, dy2, l2, out1, dkedge, dqedge)
+    late = finish_second(dy1, swap2, out2, kept, dkedge, dqedge)
+    return tuple(unpack(to_tokens(early), to_tokens(late)))
 
 
 def splits(tokens, blocks, head_width, heads):

time: 154 us -> 134 us (0.87); the launches traced: 151 us -> 133 us
  waiting for transfers between devices: 26.5 us -> 37.6 us
  blocking collectives: 37.4 us -> 26.9 us
  starting transfers between devices: 56.3 us -> 47.7 us
  other arithmetic: 7.73 us -> 0.13 us
  local copies, waits for them, and re-layouts: 7.99 us -> 2.7 us
  Pallas kernels: 14.5 us -> 17.2 us
    ppermute x4, waiting for transfers between devices: 6.4 us -> 22.2 us  [the longest x1 14.9 us: local_split(): out2 = lax.ppermute(sum1, 'ctx', OUTWARD)]
    all_to_all x1, waiting for transfers between devices: 0.01 us -> 12.9 us  [to_heads(): y = lax.all_to_all(x, 'head', split_axis=0, concat_axis=0, tiled=True)]
    all_to_all x2 -> x1, blocking collectives: 26.6 us -> 15.5 us  [to_heads(): y = lax.all_to_all(x, 'head', split_axis=0, concat_axis=0, tiled=True)]
    ppermute x1, waiting for transfers between devices: 10.6 us -> 0.01 us  [local_split(): r1 = lax.ppermute(y1, 'ctx', INWARD)]
    all_to_all x2 -> x1, waiting for transfers between devices: 8.44 us -> 0.01 us  [to_tokens(): return lax.all_to_all(x, 'head', split_axis=0, concat_axis=0, tiled=True)]
    ppermute x1, starting transfers between devices: 21.4 us -> 15.6 us  [local_split(): dkedge = lax.ppermute(dkedge, 'ctx', UP)]
    ppermute x1, starting transfers between devices: 1.31 us -> 5.98 us  [local_split(): r2 = lax.ppermute(y2, 'ctx', INWARD)]
    all_to_all x2 -> x1, starting transfers between devices: 7.73 us -> 3.52 us  [to_tokens(): return lax.all_to_all(x, 'head', split_axis=0, concat_axis=0, tiled=True)]
  transfers between devices with their start and end apart: 15 -> 14, of which waited for: 4 -> 5; matrix products, arithmetic and copies ran while one was open for 7% -> 0% of each run, Pallas kernels for 4% -> 6%
where the time goes in v3:
time: 134 us; the launch traced here: 133 us
  starting transfers between devices  47.7 us (36%)
  waiting for transfers between devices  37.6 us (28%)
  blocking collectives  26.9 us (20%)
  Pallas kernels  17.2 us (13%)
  local copies, waits for them, and re-layouts  2.7 us (2%)
    ppermute x1, starting transfers between devices, local_split(): dkedge = lax.ppermute(dkedge, 'ctx', UP)  15.6 us
    all_to_all x1, blocking collectives, to_heads(): y = lax.all_to_all(x, 'head', split_axis=0, concat_axis=0, tiled=True)  15.5 us
    ppermute x1, waiting for transfers between devices, local_split(): out2 = lax.ppermute(sum1, 'ctx', OUTWARD)  14.9 us
    all_to_all x1, waiting for transfers between devices, to_heads(): y = lax.all_to_all(x, 'head', split_axis=0, concat_axis=0, tiled=True)  12.9 us
    all_to_all x1, blocking collectives, to_tokens(): return lax.all_to_all(x, 'head', split_axis=0, concat_axis=0, tiled=True)  11.4 us
    ppermute x1, waiting for transfers between devices, local_split(): query_edge = lax.ppermute(query_edge, 'ctx', UP)  6.64 us
    ppermute x1, starting transfers between devices, local_split(): r1 = lax.ppermute(y1, 'ctx', INWARD)  6.51 us
    ppermute x1, starting transfers between devices, local_split(): r2 = lax.ppermute(y2, 'ctx', INWARD)  5.98 us
  transfers between devices with their start and end apart: 14, of which 5 were waited for; matrix products, arithmetic and copies ran while one was open for 0% of the time, Pallas kernels for 6%

profile of v3, /device:TPU:0, one launch (start us, length us, event | category | flops | bytes accessed | tf_op | source)
XLA Modules:
  0.0 133.3 jit_solution(6862407961575387387)
XLA Ops:
  0.6 3.9 %pack.1 = (bf16[4,56,1408]{2,1,0:T(8,128)(2,1)}, bf16[4,56,3840]{2,1,0:T(8,128)(2,1)}) custom-call(bf16[56,5120]{1,0:T(8,128)(2,1)} %q.1, bf16[56,5120]{1,0:T(8,128)(2,1)} %k.1, bf16[56,5120]{1,0:T(8,128)(2,1)} %v.1, bf16[56,5120]{1,0:T(8,128)(2,1)} %o.1, bf16[56,5120]{1,0:T(8,128)(2,1)} %g.1, s32[1,56]{1,0:T(1,128)} %bitcast.11), custom_call_target="tpu_custom_call" | custom-call | bytes 5734400 | tf_op jit(solution)/shard_map/pack/pallas_call | solution.py:217
  4.6 15.5 %all_to_all.20 = bf16[4,56,1408]{2,1,0:T(8,128)(2,1)} all-to-all(bf16[4,56,1408]{2,1,0:T(8,128)(2,1)} %get-tuple-element.33), channel_id=1, replica_groups=mesh['clip'=2,'ctx'=4,'head'=4] {'head'}, dimensions={0} | all-to-all | bytes 1261568 | tf_op jit(solution)/shard_map/all_to_all | solution.py:738
  20.1 1.7 %add_norm.1.y1 = bf16[224,1408]{1,0:T(8,128)(2,1)} custom-call(bf16[224,1408]{1,0:T(8,128)(2,1)} %bitcast.1.x, f32[10,224]{1,0:T(8,128)} %bitcast.10), custom_call_target="tpu_custom_call", output_to_operand_aliasing={{}: (0, {})} | custom-call | bytes 114688 | tf_op jit(solution)/shard_map/add_norm/pallas_call | solution.py:246
  21.8 3.6 %all-to-all-start.1 = ((bf16[4,56,3840]{2,1,0:T(8,128)(2,1)}), bf16[4,56,3840]{2,1,0:T(8,128)(2,1)S(1)}, u32[]{:S(2)}, u32[]{:S(2)}) async-start(bf16[4,56,3840]{2,1,0:T(8,128)(2,1)} %get-tuple-element.35), calls=%async_computation.1 | async-start | bytes 3440640 | tf_op jit(solution)/shard_map/all_to_all | solution.py:738
  25.4 0.7 collective-permute-start.3
  26.1 6.5 %collective-permute-start.2 = (bf16[224,1408]{1,0:T(8,128)(2,1)}, bf16[224,1408]{1,0:T(8,128)(2,1)S(1)}, u32[]{:S(2)}, u32[]{:S(2)}) collective-permute-start(bf16[224,1408]{1,0:T(8,128)(2,1)} %add_norm.1.y1), channel_id=1, source_target_pairs={{0,4},{12,8},{1,5},{13,9},{2,6},{14,10},{3,7},{15,11},{16,20},{28,... | collective-permute-start | bytes 1892360 | tf_op jit(solution)/shard_map/ppermute | solution.py:747
  32.6 12.9 %all-to-all-done.1 = bf16[4,56,3840]{2,1,0:T(8,128)(2,1)S(1)} async-done(((bf16[4,56,3840]{2,1,0:T(8,128)(2,1)}), bf16[4,56,3840]{2,1,0:T(8,128)(2,1)S(1)}, u32[]{:S(2)}, u32[]{:S(2)}) %all-to-all-start.1) | async-done | bytes 1720352 | tf_op jit(solution)/shard_map/all_to_all | solution.py:738
  45.5 1.2 copy-done
  46.8 2.1 %cut.1 = (bf16[224,1280]{1,0:T(8,128)(2,1)}, bf16[16,2688]{1,0:T(8,128)(2,1)}, bf16[16,2688]{1,0:T(8,128)(2,1)}) custom-call(bf16[224,1408]{1,0:T(8,128)(2,1)} %add_norm.1.y1, bf16[224,3840]{1,0:T(8,128)(2,1)} %bitcast.6), custom_call_target="tpu_custom_call" | custom-call | bytes 1146880 | tf_op jit(solution)/shard_map/cut/pallas_call | solution.py:321
  48.8 0.7 collective-permute-start.5
  49.5 6.0 %collective-permute-start.4 = (bf16[224,1280]{1,0:T(8,128)(2,1)}, bf16[224,1280]{1,0:T(8,128)(2,1)S(1)}, u32[]{:S(2)}, u32[]{:S(2)}) collective-permute-start(bf16[224,1280]{1,0:T(8,128)(2,1)} %get-tuple-element.42), channel_id=1, source_target_pairs={{0,4},{12,8},{1,5},{13,9},{2,6},{14,10},{3,7},{15,11},{16,20},{28,... | collective-permute-start | bytes 1720328 | tf_op jit(solution)/shard_map/ppermute | solution.py:752
  55.5 1.3 collective-permute-start
  56.8 4.5 %collective-permute-start.1 = (bf16[16,2688]{1,0:T(8,128)(2,1)}, bf16[16,2688]{1,0:T(8,128)(2,1)S(1)}, u32[]{:S(2)}, u32[]{:S(2)}) collective-permute-start(bf16[16,2688]{1,0:T(8,128)(2,1)} %get-tuple-element.37), channel_id=1, source_target_pairs={{0,4},{4,8},{8,12},{1,5},{5,9},{9,13},{2,6},{6,10},{10,14},{3,7},{... | collective-permute-start | bytes 258056 | tf_op jit(solution)/shard_map/ppermute | solution.py:755
  61.4 0.7 collective-permute-done.kedge
  62.1 6.6 %collective-permute-done.1.qedge = bf16[16,2688]{1,0:T(8,128)(2,1)S(1)} collective-permute-done((bf16[16,2688]{1,0:T(8,128)(2,1)}, bf16[16,2688]{1,0:T(8,128)(2,1)S(1)}, u32[]{:S(2)}, u32[]{:S(2)}) %collective-permute-start.1) | collective-permute-done | bytes 86048 | tf_op jit(solution)/shard_map/ppermute | solution.py:755
  68.8 1.5 %copy-done.1 = bf16[4,56,3840]{2,1,0:T(8,128)(2,1)S(1)} copy-done((bf16[4,56,3840]{2,1,0:T(8,128)(2,1)S(1)}, bf16[4,56,3840]{2,1,0:T(8,128)(2,1)}, u32[]{:S(2)}) %copy-start.1) | copy-done | bytes 1720344
  70.2 0.1 far_pairs.1
  70.4 0.7 collective-permute-start.9
  71.1 1.3 collective-permute-start.8
  72.4 5.0 %near_pairs.1 = (bf16[224,2560]{1,0:T(8,128)(2,1)S(1)}, bf16[224,1280]{1,0:T(8,128)(2,1)S(1)}, bf16[224,1280]{1,0:T(8,128)(2,1)S(1)}, bf16[16,2560]{1,0:T(8,128)(2,1)S(1)}, bf16[16,1280]{1,0:T(8,128)(2,1)S(1)}) custom-call(bf16[224,1408]{1,0:T(8,128)(2,1)} %add_norm.1.y1, bf16[224,3840]{1,0:T(8,128)(2,1)S(1)} %bitcast.8, ...), custom_call_target="tpu_custom_call" | custom-call | flops 642252800 | bytes 4587520 | tf_op jit(solution)/shard_map/near_pairs/pallas_call | solution.py:568
  77.4 1.3 collective-permute-start.7
  78.7 15.6 %collective-permute-start.6 = (bf16[16,2560]{1,0:T(8,128)(2,1)S(1)}, bf16[16,2560]{1,0:T(8,128)(2,1)S(1)}, u32[]{:S(2)}, u32[]{:S(2)}) collective-permute-start(bf16[16,2560]{1,0:T(8,128)(2,1)S(1)} %get-tuple-element.51), channel_id=1, source_target_pairs={{0,4},{4,8},{8,12},{1,5},{5,9},{9,13},{2,6},{6,10},{10,14},{3,7},{... | collective-permute-start | bytes 245768 | tf_op jit(solution)/shard_map/ppermute | solution.py:761
  94.4 0.1 add_convert_fusion
  94.5 2.4 %collective-permute-done.7.dq = bf16[16,1280]{1,0:T(8,128)(2,1)S(1)} collective-permute-done((bf16[16,1280]{1,0:T(8,128)(2,1)S(1)}, bf16[16,1280]{1,0:T(8,128)(2,1)S(1)}, u32[]{:S(2)}, u32[]{:S(2)}) %collective-permute-start.7) | collective-permute-done | bytes 40992 | tf_op jit(solution)/shard_map/ppermute | solution.py:762
  96.9 1.6 %finish_first.1 = (bf16[224,2560]{1,0:T(8,128)(2,1)}, bf16[224,640]{1,0:T(8,128)(2,1)S(1)}) custom-call(bf16[224,2560]{1,0:T(8,128)(2,1)S(1)} %get-tuple-element.47.dw, bf16[224,2560]{1,0:T(8,128)(2,1)S(1)} %get-tuple-element.48.l1, bf16[224,1280]{1,0:T(8,128)(2,1)S(1)} %get-tuple-element.49.dy2, bf16[224,1280]{1,0:T(8,128)(2,1)S(1)} %get-tuple-element.50.l2, ...), custom_call_target="tpu_custom_call" | custom-call | bytes 4587520 | tf_op jit(solution)/shard_map/finish_first/pallas_call | solution.py:630
  98.5 3.5 %all-to-all-start.2 = ((bf16[4,56,2560]{2,1,0:T(8,128)(2,1)}), bf16[4,56,2560]{2,1,0:T(8,128)(2,1)S(1)}, u32[]{:S(2)}, u32[]{:S(2)}) async-start(bf16[4,56,2560]{2,1,0:T(8,128)(2,1)} %bitcast.4), calls=%async_computation.2 | async-start | bytes 2293760 | tf_op jit(solution)/shard_map/all_to_all | solution.py:743
  102.1 0.7 collective-permute-start.10
  102.8 1.3 collective-permute-start.11
  104.1 14.9 %collective-permute-done.11.out2 = bf16[224,1280]{1,0:T(8,128)(2,1)S(1)} collective-permute-done((bf16[224,1280]{1,0:T(8,128)(2,1)S(1)}, bf16[224,1280]{1,0:T(8,128)(2,1)S(1)}, u32[]{:S(2)}, u32[]{:S(2)}) %collective-permute-start.11) | collective-permute-done | bytes 573472 | tf_op jit(solution)/shard_map/ppermute | solution.py:765
  119.0 0.2 finish_second.1
  119.2 11.4 %all_to_all.21.late = bf16[4,56,1280]{2,1,0:T(8,128)(2,1)} all-to-all(bf16[4,56,1280]{2,1,0:T(8,128)(2,1)S(1)} %bitcast.9), channel_id=1, replica_groups=mesh['clip'=2,'ctx'=4,'head'=4] {'head'}, dimensions={0} | all-to-all | bytes 1146880 | tf_op jit(solution)/shard_map/all_to_all | solution.py:743
  130.6 2.5 %unpack.1 = (bf16[56,5120]{1,0:T(8,128)(2,1)}, bf16[56,5120]{1,0:T(8,128)(2,1)}, bf16[56,5120]{1,0:T(8,128)(2,1)}) custom-call(bf16[4,56,2560]{2,1,0:T(8,128)(2,1)} %copy-done.2, bf16[4,56,1280]{2,1,0:T(8,128)(2,1)} %all_to_all.21.late), custom_call_target="tpu_custom_call" | custom-call | bytes 3440640 | tf_op jit(solution)/shard_map/unpack/pallas_call | solution.py:718
  (13 shorter events, 0.0 us)
Async XLA Ops:
  21.8 23.7 %all-to-all-start.1 = ((bf16[4,56,3840]{2,1,0:T(8,128)(2,1)}), bf16[4,56,3840]{2,1,0:T(8,128)(2,1)S(1)}, u32[]{:S(2)}, u32[]{:S(2)}) async-start(bf16[4,56,3840]{2,1,0:T(8,128)(2,1)} %get-tuple-element.35), calls=%async_computation.1 | async-start | bytes 3440640 | tf_op jit(solution)/shard_map/all_to_all | solution.py:738
  25.4 23.5 %collective-permute-start.3 = (bf16[224,1408]{1,0:T(8,128)(2,1)}, bf16[224,1408]{1,0:T(8,128)(2,1)S(1)}, u32[]{:S(2)}, u32[]{:S(2)}) collective-permute-start(bf16[224,1408]{1,0:T(8,128)(2,1)} %add_norm.1.y1), channel_id=1, source_target_pairs={{4,8},{8,4},{5,9},{9,5},{6,10},{10,6},{7,11},{11,7},{20,24},{24,20... | collective-permute-start | bytes 1892360 | tf_op jit(solution)/shard_map/ppermute | solution.py:748
  26.1 22.8 %collective-permute-start.2 = (bf16[224,1408]{1,0:T(8,128)(2,1)}, bf16[224,1408]{1,0:T(8,128)(2,1)S(1)}, u32[]{:S(2)}, u32[]{:S(2)}) collective-permute-start(bf16[224,1408]{1,0:T(8,128)(2,1)} %add_norm.1.y1), channel_id=1, source_target_pairs={{0,4},{12,8},{1,5},{13,9},{2,6},{14,10},{3,7},{15,11},{16,20},{28,... | collective-permute-start | bytes 1892360 | tf_op jit(solution)/shard_map/ppermute | solution.py:747
  45.5 1.2 copy-start
  48.8 19.9 %collective-permute-start.5 = (bf16[224,1408]{1,0:T(8,128)(2,1)S(1)}, bf16[224,1408]{1,0:T(8,128)(2,1)S(1)}, u32[]{:S(2)}, u32[]{:S(2)}) collective-permute-start(bf16[224,1408]{1,0:T(8,128)(2,1)S(1)} %collective-permute-done.2.r1), channel_id=1, source_target_pairs={{4,8},{8,4},{5,9},{9,5},{6,10},{10,6},{7,11},{11,7},{20,24},{24,20... | collective-permute-start | bytes 1892360 | tf_op jit(solution)/shard_map/ppermute | solution.py:753
  49.5 19.2 %collective-permute-start.4 = (bf16[224,1280]{1,0:T(8,128)(2,1)}, bf16[224,1280]{1,0:T(8,128)(2,1)S(1)}, u32[]{:S(2)}, u32[]{:S(2)}) collective-permute-start(bf16[224,1280]{1,0:T(8,128)(2,1)} %get-tuple-element.42), channel_id=1, source_target_pairs={{0,4},{12,8},{1,5},{13,9},{2,6},{14,10},{3,7},{15,11},{16,20},{28,... | collective-permute-start | bytes 1720328 | tf_op jit(solution)/shard_map/ppermute | solution.py:752
  55.5 6.6 %collective-permute-start = (bf16[16,2688]{1,0:T(8,128)(2,1)}, bf16[16,2688]{1,0:T(8,128)(2,1)S(1)}, u32[]{:S(2)}, u32[]{:S(2)}) collective-permute-start(bf16[16,2688]{1,0:T(8,128)(2,1)} %get-tuple-element.36), channel_id=1, source_target_pairs={{4,0},{8,4},{12,8},{5,1},{9,5},{13,9},{6,2},{10,6},{14,10},{7,3},{... | collective-permute-start | bytes 258056 | tf_op jit(solution)/shard_map/ppermute | solution.py:754
  56.8 11.9 %collective-permute-start.1 = (bf16[16,2688]{1,0:T(8,128)(2,1)}, bf16[16,2688]{1,0:T(8,128)(2,1)S(1)}, u32[]{:S(2)}, u32[]{:S(2)}) collective-permute-start(bf16[16,2688]{1,0:T(8,128)(2,1)} %get-tuple-element.37), channel_id=1, source_target_pairs={{0,4},{4,8},{8,12},{1,5},{5,9},{9,13},{2,6},{6,10},{10,14},{3,7},{... | collective-permute-start | bytes 258056 | tf_op jit(solution)/shard_map/ppermute | solution.py:755
  68.8 1.5 %copy-start.1 = (bf16[4,56,3840]{2,1,0:T(8,128)(2,1)S(1)}, bf16[4,56,3840]{2,1,0:T(8,128)(2,1)}, u32[]{:S(2)}) copy-start(bf16[4,56,3840]{2,1,0:T(8,128)(2,1)} %copy-done) | copy-start | bytes 5160964
  70.4 24.0 %collective-permute-start.9 = (bf16[224,1280]{1,0:T(8,128)(2,1)S(1)}, bf16[224,1280]{1,0:T(8,128)(2,1)S(1)}, u32[]{:S(2)}, u32[]{:S(2)}) collective-permute-start(bf16[224,1280]{1,0:T(8,128)(2,1)S(1)} %get-tuple-element.54), channel_id=1, source_target_pairs={{4,8},{8,4},{5,9},{9,5},{6,10},{10,6},{7,11},{11,7},{20,24},{24,20... | collective-permute-start | bytes 1720328 | tf_op jit(solution)/shard_map/ppermute | solution.py:759
  71.1 25.9 %collective-permute-start.8 = (bf16[224,1280]{1,0:T(8,128)(2,1)S(1)}, bf16[224,1280]{1,0:T(8,128)(2,1)S(1)}, u32[]{:S(2)}, u32[]{:S(2)}) collective-permute-start(bf16[224,1280]{1,0:T(8,128)(2,1)S(1)} %get-tuple-element.53), channel_id=1, source_target_pairs={{4,0},{8,12},{5,1},{9,13},{6,2},{10,14},{7,3},{11,15},{20,16},{24,... | collective-permute-start | bytes 1720328 | tf_op jit(solution)/shard_map/ppermute | solution.py:760
  77.4 19.5 %collective-permute-start.7 = (bf16[16,1280]{1,0:T(8,128)(2,1)S(1)}, bf16[16,1280]{1,0:T(8,128)(2,1)S(1)}, u32[]{:S(2)}, u32[]{:S(2)}) collective-permute-start(bf16[16,1280]{1,0:T(8,128)(2,1)S(1)} %get-tuple-element.52), channel_id=1, source_target_pairs={{4,0},{8,4},{12,8},{5,1},{9,5},{13,9},{6,2},{10,6},{14,10},{7,3},{... | collective-permute-start | bytes 122888 | tf_op jit(solution)/shard_map/ppermute | solution.py:762
  78.7 18.2 %collective-permute-start.6 = (bf16[16,2560]{1,0:T(8,128)(2,1)S(1)}, bf16[16,2560]{1,0:T(8,128)(2,1)S(1)}, u32[]{:S(2)}, u32[]{:S(2)}) collective-permute-start(bf16[16,2560]{1,0:T(8,128)(2,1)S(1)} %get-tuple-element.51), channel_id=1, source_target_pairs={{0,4},{4,8},{8,12},{1,5},{5,9},{9,13},{2,6},{6,10},{10,14},{3,7},{... | collective-permute-start | bytes 245768 | tf_op jit(solution)/shard_map/ppermute | solution.py:761
  98.5 20.7 %all-to-all-start.2 = ((bf16[4,56,2560]{2,1,0:T(8,128)(2,1)}), bf16[4,56,2560]{2,1,0:T(8,128)(2,1)S(1)}, u32[]{:S(2)}, u32[]{:S(2)}) async-start(bf16[4,56,2560]{2,1,0:T(8,128)(2,1)} %bitcast.4), calls=%async_computation.2 | async-start | bytes 2293760 | tf_op jit(solution)/shard_map/all_to_all | solution.py:743
  102.1 2.0 %collective-permute-start.10 = (bf16[224,1280]{1,0:T(8,128)(2,1)S(1)}, bf16[224,1280]{1,0:T(8,128)(2,1)S(1)}, u32[]{:S(2)}, u32[]{:S(2)}) collective-permute-start(bf16[224,1280]{1,0:T(8,128)(2,1)S(1)} %get-tuple-element.61), channel_id=1, source_target_pairs={{4,8},{8,4},{5,9},{9,5},{6,10},{10,6},{7,11},{11,7},{20,24},{24,20... | collective-permute-start | bytes 1720328 | tf_op jit(solution)/shard_map/ppermute | solution.py:764
  102.8 16.2 %collective-permute-start.11 = (bf16[224,1280]{1,0:T(8,128)(2,1)S(1)}, bf16[224,1280]{1,0:T(8,128)(2,1)S(1)}, u32[]{:S(2)}, u32[]{:S(2)}) collective-permute-start(bf16[224,1280]{1,0:T(8,128)(2,1)S(1)} %add_convert_fusion), channel_id=1, source_target_pairs={{4,0},{8,12},{5,1},{9,13},{6,2},{10,14},{7,3},{11,15},{20,16},{24,... | collective-permute-start | bytes 1720328 | tf_op jit(solution)/shard_map/ppermute | solution.py:765
  119.2 11.4 %copy-start.2 = (bf16[4,56,2560]{2,1,0:T(8,128)(2,1)}, bf16[4,56,2560]{2,1,0:T(8,128)(2,1)S(1)}, u32[]{:S(2)}) copy-start(bf16[4,56,2560]{2,1,0:T(8,128)(2,1)S(1)} %all-to-all-done.2.early) | copy-start | bytes 3440644

commit v4 on v3

--- a/solution.py
+++ b/solution.py
@@ -10,6 +10,8 @@
 SPANS = 12
 EDGE = 16
 VMEM_LIMIT = 32 * 2**20
+VMEM_SMALL = 16 * 2**20
+VMEM_WHOLE = 60 * 2**20
 LANES = 128
 BF16 = jnp.bfloat16
 F32 = jnp.float32
@@ -154,22 +156,25 @@
     heads = width // LANES
     half = width // 2
 
-    def body(q, k, v, o, g, ids, x1, rest, q_v, k_v, v_v, o_v, g_v, meta, sems):
+    def body(q, k, v, o, g, ids, *refs):
+        x1, x2, x3 = refs[:groups], refs[groups : 2 * groups], refs[2 * groups : 3 * groups]
+        q_v, k_v, v_v, o_v, g_v, meta, sems = refs[3 * groups :]
+        here = lax.axis_index("head")
         low = lax.axis_index("ctx") < 2
         loads = run_copies([(k, k_v), (v, v_v), (q, q_v), (g, g_v), (o, o_v)], sems)
 
         def moves(first, second, third, fourth, near, far):
             todo = []
-            for h in range(groups):
-                base = h * width
-                todo.append((first.at[:, pl.ds(base + near, half)], x1.at[h, :, pl.ds(0, half)]))
-                todo.append((second.at[:, pl.ds(base + near, half)], x1.at[h, :, pl.ds(half, half)]))
-            for h in range(groups):
-                base = h * width
-                todo.append((first.at[:, pl.ds(base + far, half)], rest.at[h, :, pl.ds(0, half)]))
-                todo.append((second.at[:, pl.ds(base + far, half)], rest.at[h, :, pl.ds(half, half)]))
-                todo.append((third.at[:, pl.ds(base, width)], rest.at[h, :, pl.ds(width, width)]))
-                todo.append((fourth.at[:, pl.ds(base, width)], rest.at[h, :, pl.ds(2 * width, width)]))
+            for m in range(groups):
+                base = pl.multiple_of((here ^ m) * width, LANES)
+                todo.append((first.at[:, pl.ds(base + near, half)], x1[m].at[:, pl.ds(0, half)]))
+                todo.append((second.at[:, pl.ds(base + near, half)], x1[m].at[:, pl.ds(half, half)]))
+            for m in range(groups):
+                base = pl.multiple_of((here ^ m) * width, LANES)
+                todo.append((first.at[:, pl.ds(base + far, half)], x2[m].at[:, pl.ds(0, half)]))
+                todo.append((second.at[:, pl.ds(base + far, half)], x2[m].at[:, pl.ds(half, half)]))
+                todo.append((third.at[:, pl.ds(base, width)], x3[m].at[:, pl.ds(0, width)]))
+                todo.append((fourth.at[:, pl.ds(base, width)], x3[m].at[:, pl.ds(width, width)]))
             return [pltpu.make_async_copy(src, dst, sems.at[5 + i]) for i, (src, dst) in enumerate(todo)]
 
         low_moves = (k_v, v_v, q_v, g_v, half, 0)
@@ -201,7 +206,9 @@
             high, middle, lowest = pieces(total)
             kept = jnp.where(lane < heads, high, jnp.where(lane < 2 * heads, middle, lowest))
             meta[h] = jnp.where(lane < 3 * heads, kept, jnp.where(lane == 3 * heads, own.astype(BF16), 0.0).astype(BF16))
-        last = run_copies([(meta, x1.at[:, :, pl.ds(width, LANES)])], sems, 5 + 6 * groups)
+        last = run_copies(
+            [(meta.at[here ^ m], x1[m].at[:, pl.ds(width, LANES)]) for m in range(groups)], sems, 5 + 6 * groups
+        )
 
         @pl.when(low)
         def _():
@@ -214,45 +221,75 @@
         wait_all(last)
 
     whole = pltpu.VMEM((rows, groups * width), BF16)
-    return pl.pallas_call(
+    made = pl.pallas_call(
         body,
         out_shape=[
-            jax.ShapeDtypeStruct((groups, rows, width + LANES), BF16),
-            jax.ShapeDtypeStruct((groups, rows, 3 * width), BF16),
+            jax.ShapeDtypeStruct((rows, size), BF16)
+            for size in (width + LANES, width, 2 * width)
+            for _ in range(groups)
         ],
         in_specs=anywhere(5) + [pl.BlockSpec(memory_space=pltpu.VMEM)],
-        out_specs=anywhere(2),
+        out_specs=anywhere(3 * groups),
         scratch_shapes=[whole] * 5
-        + [pltpu.VMEM((groups, rows, LANES), BF16), pltpu.SemaphoreType.DMA((6 + 6 * groups,))],
+        + [pltpu.VMEM((groups, rows, LANES), BF16), pltpu.SemaphoreType.DMA((5 + 7 * groups,))],
         cost_estimate=pl.CostEstimate(flops=0, bytes_accessed=10 * rows * groups * width * 2, transcendentals=0),
+        compiler_params=pltpu.CompilerParams(vmem_limit_bytes=VMEM_WHOLE),
         name="pack",
     )(queries, keys_in, values_in, attn_out, out_grad, span_row)
-
-
-def add_norm(payload, norm_rows):
-    rows, width = payload.shape
+    return made[:groups], made[groups : 2 * groups], made[2 * groups :]
+
+
+def join_first(parts, norm_rows):
+    groups = len(parts)
+    rows, width = parts[0].shape
     heads = norm_rows.shape[0]
-    block = pl.BlockSpec((rows, LANES), lambda i: (0, width // LANES - 1))
-
-    def body(x, norm, y):
+
+    def body(*refs):
+        norm, y, sems = refs[groups:]
+        here = lax.axis_index("head")
+        made = run_copies([(refs[m], y.at[here ^ m]) for m in range(groups)], sems)
         at_row = lax.broadcasted_iota(jnp.int32, (heads, LANES), 0)
         at_lane = lax.broadcasted_iota(jnp.int32, (heads, LANES), 1)
-        total = x[...].astype(F32)
+        total = jnp.zeros((groups * rows, LANES), F32)
         for i, piece in enumerate(pieces(norm[...])):
             place = jnp.where(at_lane == at_row + (3 * heads + 1 + i * heads), 1.0, 0.0).astype(BF16)
             total += tn(piece, place)
-        y[...] = total.astype(BF16)
+        wait_all(made)
+        tail = pl.ds(width - LANES, LANES)
+        for h in range(groups):
+            y[h, :, tail] = (y[h, :, tail].astype(F32) + total[h * rows : (h + 1) * rows]).astype(BF16)
 
     return pl.pallas_call(
         body,
-        grid=(1,),
-        out_shape=jax.ShapeDtypeStruct(payload.shape, BF16),
-        in_specs=[block, pl.BlockSpec((heads, rows), lambda i: (0, 0))],
-        out_specs=block,
-        input_output_aliases={0: 0},
-        cost_estimate=pl.CostEstimate(flops=0, bytes_accessed=4 * rows * LANES, transcendentals=0),
-        name="add_norm",
-    )(payload, norm_rows)
+        out_shape=jax.ShapeDtypeStruct((groups, rows, width), BF16),
+        in_specs=anywhere(groups) + [pl.BlockSpec(memory_space=pltpu.VMEM)],
+        out_specs=pl.BlockSpec(memory_space=pltpu.VMEM),
+        scratch_shapes=[pltpu.SemaphoreType.DMA((groups,))],
+        cost_estimate=pl.CostEstimate(flops=0, bytes_accessed=4 * groups * rows * width, transcendentals=0),
+        compiler_params=pltpu.CompilerParams(vmem_limit_bytes=VMEM_SMALL),
+        name="join_first",
+    )(*parts, norm_rows).reshape(groups * rows, width)
+
+
+def join(parts):
+    groups = len(parts)
+    rows, width = parts[0].shape
+
+    def body(*refs):
+        y, sems = refs[groups:]
+        here = lax.axis_index("head")
+        wait_all(run_copies([(refs[m], y.at[here ^ m]) for m in range(groups)], sems))
+
+    return pl.pallas_call(
+        body,
+        out_shape=jax.ShapeDtypeStruct((groups, rows, width), BF16),
+        in_specs=anywhere(groups),
+        out_specs=pl.BlockSpec(memory_space=pltpu.VMEM),
+        scratch_shapes=[pltpu.SemaphoreType.DMA((groups,))],
+        cost_estimate=pl.CostEstimate(flops=0, bytes_accessed=4 * groups * rows * width, transcendentals=0),
+        compiler_params=pltpu.CompilerParams(vmem_limit_bytes=VMEM_SMALL),
+        name="join",
+    )(*parts).reshape(groups * rows, width)
 
 
 def token_rows(meta, heads):
@@ -278,23 +315,19 @@
     return query_term, key_term, value_term
 
 
-def cut(y1, rest):
-    rows = rest.shape[0]
-    width = rest.shape[1] // 3
+def join_last(parts, y1, y2):
+    groups = len(parts)
+    share = parts[0].shape[0]
+    rows, width = y2.shape
     half = width // 2
 
-    def body(y1, rest, y2, kedge, qedge, sems):
-        low = lax.axis_index("ctx") < 2
+    def body(*refs):
+        y1, y2, w, kedge, qedge, sems = refs[groups:]
+        here, low = lax.axis_index("head"), lax.axis_index("ctx") < 2
         top, bottom, tail = pl.ds(0, EDGE), pl.ds(rows - EDGE, EDGE), pl.ds(width, LANES)
-        end = pl.ds(2 * width, LANES)
-        made = run_copies(
-            [
-                (y1.at[top, tail], kedge.at[:, end]),
-                (y1.at[bottom, tail], qedge.at[:, end]),
-                (rest.at[:, pl.ds(0, width)], y2),
-            ],
-            sems,
-        )
+        whole, end = pl.ds(0, 2 * width), pl.ds(2 * width, LANES)
+        made = run_copies([(y1.at[top, tail], kedge.at[:, end]), (y1.at[bottom, tail], qedge.at[:, end])], sems)
+        loads = run_copies([(refs[m], w.at[here ^ m]) for m in range(groups)], sems, 2)
 
         def joined(first, second, at, edge):
             todo = []
@@ -303,40 +336,47 @@
                     todo.append((part.at[at, pl.ds(i * half, half)], edge.at[:, pl.ds(i * width + j * half, half)]))
             return todo
 
-        whole = pl.ds(width, 2 * width)
-
         @pl.when(low)
         def _():
-            todo = joined(rest, y1, top, kedge) + [(rest.at[bottom, whole], qedge.at[:, pl.ds(0, 2 * width)])]
-            wait_all(run_copies(todo, sems, 3))
+            wait_all(run_copies(joined(y2, y1, top, kedge), sems, 2 + groups))
 
         @pl.when(jnp.logical_not(low))
         def _():
-            todo = joined(y1, rest, bottom, qedge) + [(rest.at[top, whole], kedge.at[:, pl.ds(0, 2 * width)])]
-            wait_all(run_copies(todo, sems, 3))
+            wait_all(run_copies(joined(y1, y2, bottom, qedge), sems, 2 + groups))
+
+        wait_all(loads)
+
+        @pl.when(low)
+        def _():
+            qedge[:, whole] = w[groups - 1, share - EDGE :, :]
+
+        @pl.when(jnp.logical_not(low))
+        def _():
+            kedge[:, whole] = w[0, :EDGE, :]
 
         wait_all(made)
 
     edge = jax.ShapeDtypeStruct((EDGE, 2 * width + LANES), BF16)
-    return pl.pallas_call(
-        body,
-        out_shape=[jax.ShapeDtypeStruct((rows, width), BF16), edge, edge],
-        in_specs=anywhere(2),
+    w, key_edge, query_edge = pl.pallas_call(
+        body,
+        out_shape=[jax.ShapeDtypeStruct((groups, share, 2 * width), BF16), edge, edge],
+        in_specs=anywhere(groups + 2),
         out_specs=[pl.BlockSpec(memory_space=pltpu.VMEM)] * 3,
-        scratch_shapes=[pltpu.SemaphoreType.DMA((8,))],
-        compiler_params=pltpu.CompilerParams(vmem_limit_bytes=60 * 2**20),
-        cost_estimate=pl.CostEstimate(flops=0, bytes_accessed=4 * rows * width, transcendentals=0),
-        name="cut",
-    )(y1, rest)
-
-
-def far_pairs(y1, rest, r1, r2, s1, s2):
+        scratch_shapes=[pltpu.SemaphoreType.DMA((6 + groups,))],
+        compiler_params=pltpu.CompilerParams(vmem_limit_bytes=VMEM_SMALL),
+        cost_estimate=pl.CostEstimate(flops=0, bytes_accessed=8 * rows * width, transcendentals=0),
+        name="join_last",
+    )(*parts, y1, y2)
+    return w.reshape(rows, 2 * width), key_edge, query_edge
+
+
+def far_pairs(y1, y2, w, r1, r2, s1, s2):
     rows, width = r2.shape
     half = width // 2
     count = half // LANES
     heads = 2 * count
 
-    def body(y1, rest, r1, r2, s1, s2, swap1, out1, swap2, l1, l2, l3, buf, grads, meta, info, sems):
+    def body(y1, y2, w, r1, r2, s1, s2, swap1, out1, swap2, l1, l2, l3, buf, grads, meta, info, sems):
         z = lax.axis_index("ctx")
         one = z == 1
 
@@ -359,11 +399,11 @@
                     (s1.at[:, main], buf.at[pick(0, 3)]),
                     (s2.at[:, main], buf.at[pick(1, 2)]),
                     (r2, buf.at[pick(2, 1)]),
-                    (rest.at[:, main], buf.at[pick(3, 0)]),
-                    (rest.at[:, pl.ds(width + near, half)], buf.at[4, :, left]),
-                    (rest.at[:, pl.ds(2 * width + near, half)], buf.at[4, :, right]),
-                    (rest.at[:, pl.ds(width + other, half)], buf.at[5, :, left]),
-                    (rest.at[:, pl.ds(2 * width + other, half)], buf.at[5, :, right]),
+                    (y2, buf.at[pick(3, 0)]),
+                    (w.at[:, pl.ds(near, half)], buf.at[4, :, left]),
+                    (w.at[:, pl.ds(width + near, half)], buf.at[4, :, right]),
+                    (w.at[:, pl.ds(other, half)], buf.at[5, :, left]),
+                    (w.at[:, pl.ds(width + other, half)], buf.at[5, :, right]),
                     (r1.at[:, main], buf.at[6]),
                 ],
                 sems,
@@ -452,7 +492,7 @@
             single_shape,
             single_shape,
         ],
-        in_specs=anywhere(6),
+        in_specs=anywhere(7),
         out_specs=anywhere(6),
         scratch_shapes=[
             pltpu.VMEM((7, rows, width), BF16),
@@ -466,28 +506,27 @@
             flops=30 * 10 * rows * rows * LANES, bytes_accessed=30 * rows * width, transcendentals=30 * rows * rows
         ),
         name="far_pairs",
-    )(y1, rest, r1, r2, s1, s2)
-
-
-def near_pairs(y1, rest, key_edge, query_edge):
-    rows = rest.shape[0]
-    width = rest.shape[1] // 3
+    )(y1, y2, w, r1, r2, s1, s2)
+
+
+def near_pairs(y1, y2, w, key_edge, query_edge):
+    rows, width = y2.shape
     half = width // 2
     count = half // LANES
     heads = 2 * count
     total = rows + EDGE
 
-    def body(y1, rest, kedge, qedge, dw, dy1, dy2, dkedge, dqedge, qbuf, kbuf, dq, dk, kmeta, qmeta, info, sems):
+    def body(y1, y2, w, kedge, qedge, dw, dy1, dy2, dkedge, dqedge, qbuf, kbuf, dq, dk, kmeta, qmeta, info, sems):
         low = lax.axis_index("ctx") < 2
         left, right = pl.ds(0, half), pl.ds(half, half)
         own, past = pl.ds(0, rows), pl.ds(rows, EDGE)
         main = pl.ds(0, width)
 
-        def halves(array, there, back=False, start=0, parts=2):
+        def halves(array, there, back=False, parts=2):
             todo = []
             for i in range(2):
                 for j in range(parts):
-                    wide = array.at[:, pl.ds(start + j * width + i * half, half)]
+                    wide = array.at[:, pl.ds(j * width + i * half, half)]
                     narrow = there(i, right if j else left)
                     todo.append((narrow, wide) if back else (wide, narrow))
             return todo
@@ -506,14 +545,14 @@
 
         @pl.when(low)
         def _():
-            todo = halves(rest, lambda i, cols: qbuf.at[i, own, cols], start=width)
-            todo += [(rest.at[:, main], kbuf.at[0, own]), (y1.at[:, main], kbuf.at[1, own])]
+            todo = halves(w, lambda i, cols: qbuf.at[i, own, cols])
+            todo += [(y2, kbuf.at[0, own]), (y1.at[:, main], kbuf.at[1, own])]
             wait_all(run_copies(todo, sems, 12))
 
         @pl.when(jnp.logical_not(low))
         def _():
-            todo = halves(rest, lambda i, cols: kbuf.at[i, own, cols], start=width)
-            todo += [(y1.at[:, main], qbuf.at[0, own]), (rest.at[:, main], qbuf.at[1, own])]
+            todo = halves(w, lambda i, cols: kbuf.at[i, own, cols])
+            todo += [(y1.at[:, main], qbuf.at[0, own]), (y2, qbuf.at[1, own])]
             wait_all(run_copies(todo, sems, 12))
 
         wait_all(shared)
@@ -574,7 +613,7 @@
             jax.ShapeDtypeStruct((EDGE, 2 * width), BF16),
             jax.ShapeDtypeStruct((EDGE, width), BF16),
         ],
-        in_specs=anywhere(4),
+        in_specs=anywhere(5),
         out_specs=anywhere(5),
         scratch_shapes=[
             pltpu.VMEM((2, total, width), BF16),
@@ -591,14 +630,17 @@
             flops=10 * 10 * rows * rows * LANES, bytes_accessed=16 * rows * width, transcendentals=10 * rows * rows
         ),
         name="near_pairs",
-    )(y1, rest, key_edge, query_edge)
-
-
-def finish_first(dw, l1, dy2, l2, out1, dkedge, dqedge):
+    )(y1, y2, w, key_edge, query_edge)
+
+
+def finish_first(dw, l1, dy2, l2, out1, dkedge, dqedge, groups):
     rows, width = dy2.shape
     half = width // 2
-
-    def body(dw, l1, dy2, l2, out1, dk, dq, e, v):
+    share = rows // groups
+
+    def body(dw, l1, dy2, l2, out1, dk, dq, *refs):
+        outs, v, e, sems = refs[:groups], *refs[groups:]
+        here = lax.axis_index("head")
         z = lax.axis_index("ctx")
         low, middle = z < 2, (z == 1) | (z == 2)
 
@@ -611,7 +653,8 @@
         def put(dst, cols, total, first, last=None):
             end = total[rows - EDGE :] if last is None else total[rows - EDGE :] + last
             total = jnp.concatenate([total[:EDGE] + first, total[EDGE : rows - EDGE], end], axis=0)
-            dst[:, cols] = total.astype(BF16)
+            for h in range(groups):
+                dst[h, :, cols] = total[h * share : (h + 1) * share].astype(BF16)
 
         def key_edge(cols):
             return dk[:, cols].astype(F32)
@@ -625,25 +668,37 @@
             put(e, cols, own(cols), jnp.where(low, 0.0, key_edge(cols)), jnp.where(low, query_edge(cols), 0.0))
         put(e, c, second(a), jnp.where(low, key_edge(a), 0.0), jnp.where(low, 0.0, query_edge(b)))
         put(e, d, jnp.where(low, second(b), own(c)), key_edge(c))
-        put(v, pl.ds(0, half), own(d), key_edge(d))
+        made = run_copies([(e.at[here ^ m], outs[m]) for m in range(groups)], sems)
+        left_over = own(d)
+        left_over = jnp.concatenate([left_over[:EDGE] + key_edge(d), left_over[EDGE:]], axis=0)
+        v[...] = left_over.astype(BF16)
+        wait_all(made)
 
     return pl.pallas_call(
         body,
-        out_shape=[jax.ShapeDtypeStruct((rows, 2 * width), BF16), jax.ShapeDtypeStruct((rows, half), BF16)],
+        out_shape=[jax.ShapeDtypeStruct((share, 2 * width), BF16)] * groups + [jax.ShapeDtypeStruct((rows, half), BF16)],
         in_specs=[pl.BlockSpec(memory_space=pltpu.VMEM)] * 7,
-        out_specs=[pl.BlockSpec(memory_space=pltpu.VMEM)] * 2,
-        compiler_params=pltpu.CompilerParams(vmem_limit_bytes=32 * 2**20),
+        out_specs=anywhere(groups) + [pl.BlockSpec(memory_space=pltpu.VMEM)],
+        scratch_shapes=[pltpu.VMEM((groups, share, 2 * width), BF16), pltpu.SemaphoreType.DMA((groups,))],
+        compiler_params=pltpu.CompilerParams(vmem_limit_bytes=VMEM_SMALL),
         cost_estimate=pl.CostEstimate(flops=0, bytes_accessed=16 * rows * width, transcendentals=0),
         name="finish_first",
     )(dw, l1, dy2, l2, out1, dkedge, dqedge)
 
 
-def finish_second(dy1, swap2, out2, v, dkedge, dqedge):
+def finish_second(dy1, swap2, out2, v, dkedge, dqedge, groups):
     rows, width = dy1.shape
     half = width // 2
-
-    def body(dy1, swap2, out2, v, dk, dq, e):
-        low = lax.axis_index("ctx") < 2
+    share = rows // groups
+
+    def body(dy1, swap2, out2, v, dk, dq, *refs):
+        outs, e, sems = refs[:groups], *refs[groups:]
+        here, low = lax.axis_index("head"), lax.axis_index("ctx") < 2
+
+        def put(cols, whole):
+            for h in range(groups):
+                e[h, :, cols] = whole[h * share : (h + 1) * share].astype(BF16)
+
         a, b = pl.ds(0, half), pl.ds(half, half)
         end = pl.ds(width + half, half)
 
@@ -653,77 +708,103 @@
         left = total(a)
         first = left[:EDGE] + jnp.where(low, dk[:, b].astype(F32), 0.0)
         last = left[rows - EDGE :] + jnp.where(low, 0.0, dq[:, a].astype(F32))
-        e[:, a] = jnp.concatenate([first, left[EDGE : rows - EDGE], last], axis=0).astype(BF16)
+        put(a, jnp.concatenate([first, left[EDGE : rows - EDGE], last], axis=0))
         right = total(b)
         right = jnp.concatenate([right[:EDGE] + dk[:, end].astype(F32), right[EDGE:]], axis=0)
-        e[:, b] = jnp.where(low, right.astype(BF16), v[...])
+        put(b, jnp.where(low, right, v[...].astype(F32)))
+        wait_all(run_copies([(e.at[here ^ m], outs[m]) for m in range(groups)], sems))
 
     return pl.pallas_call(
         body,
-        out_shape=jax.ShapeDtypeStruct((rows, width), BF16),
+        out_shape=[jax.ShapeDtypeStruct((share, width), BF16)] * groups,
         in_specs=[pl.BlockSpec(memory_space=pltpu.VMEM)] * 6,
-        out_specs=pl.BlockSpec(memory_space=pltpu.VMEM),
-        compiler_params=pltpu.CompilerParams(vmem_limit_bytes=32 * 2**20),
+        out_specs=anywhere(groups),
+        scratch_shapes=[pltpu.VMEM((groups, share, width), BF16), pltpu.SemaphoreType.DMA((groups,))],
+        compiler_params=pltpu.CompilerParams(vmem_limit_bytes=VMEM_SMALL),
         cost_estimate=pl.CostEstimate(flops=0, bytes_accessed=9 * rows * width, transcendentals=0),
         name="finish_second",
     )(dy1, swap2, out2, v, dkedge, dqedge)
 
 
-def unpack(early, late):
-    groups, rows, width = late.shape
+def unpack_early(parts):
+    groups = len(parts)
+    rows = parts[0].shape[0]
+    width = parts[0].shape[1] // 2
     half = width // 2
 
-    def body(early, late, dq, dk, dv, first, second, third, sems):
-        low = lax.axis_index("ctx") < 2
+    def body(*refs):
+        dq, dk, dv, first, second, third, sems = refs[groups:]
+        here, low = lax.axis_index("head"), lax.axis_index("ctx") < 2
         todo = []
-        for h in range(groups):
-            todo.append((early.at[h, :, pl.ds(0, width)], first.at[:, pl.ds(h * width, width)]))
-        for h in range(groups):
-            todo.append((early.at[h, :, pl.ds(width + half, half)], third.at[:, pl.ds(h * width, half)]))
-            todo.append((late.at[h, :, pl.ds(half, half)], third.at[:, pl.ds(h * width + half, half)]))
-        for h in range(groups):
-            here = pl.multiple_of(h * width + jnp.where(low, 0, half), LANES)
-            there = pl.multiple_of(h * width + jnp.where(low, half, 0), LANES)
-            todo.append((early.at[h, :, pl.ds(width, half)], second.at[:, pl.ds(here, half)]))
-            todo.append((late.at[h, :, pl.ds(0, half)], second.at[:, pl.ds(there, half)]))
-        loads = run_copies(todo, sems)
-        count = len(loads)
-        wait_all(loads[:groups])
+        for m in range(groups):
+            base = pl.multiple_of((here ^ m) * width, LANES)
+            place = pl.multiple_of(base + jnp.where(low, 0, half), LANES)
+            todo.append((refs[m].at[:, pl.ds(0, width)], first.at[:, pl.ds(base, width)]))
+            todo.append((refs[m].at[:, pl.ds(width, half)], second.at[:, pl.ds(place, half)]))
+            todo.append((refs[m].at[:, pl.ds(width + half, half)], third.at[:, pl.ds(base, half)]))
+        wait_all(run_copies(todo, sems))
 
         @pl.when(low)
         def _():
-            run_copies([(first, dq)], sems, count)
+            wait_all(run_copies([(first, dq), (second, dk), (third, dv)], sems))
 
         @pl.when(jnp.logical_not(low))
         def _():
-            run_copies([(first, dk)], sems, count)
-
-        wait_all(loads[groups : 3 * groups])
-        run_copies([(third, dv)], sems, count + 1)
-        wait_all(loads[3 * groups :])
-
-        @pl.when(low)
-        def _():
-            wait_all(run_copies([(second, dk)], sems, count + 2))
-            pltpu.make_async_copy(first, dq, sems.at[count]).wait()
-
-        @pl.when(jnp.logical_not(low))
-        def _():
-            wait_all(run_copies([(second, dq)], sems, count + 2))
-            pltpu.make_async_copy(first, dk, sems.at[count]).wait()
-
-        pltpu.make_async_copy(third, dv, sems.at[count + 1]).wait()
+            wait_all(run_copies([(first, dk), (second, dq), (third, dv)], sems))
 
     shape = jax.ShapeDtypeStruct((rows, groups * width), BF16)
     return pl.pallas_call(
         body,
         out_shape=[shape] * 3,
-        in_specs=anywhere(2),
+        in_specs=anywhere(groups),
         out_specs=anywhere(3),
-        scratch_shapes=[pltpu.VMEM((rows, groups * width), BF16)] * 3 + [pltpu.SemaphoreType.DMA((3 + 5 * groups,))],
-        cost_estimate=pl.CostEstimate(flops=0, bytes_accessed=6 * rows * groups * width * 2, transcendentals=0),
-        name="unpack",
-    )(early, late)
+        scratch_shapes=[pltpu.VMEM(shape.shape, BF16)] * 3 + [pltpu.SemaphoreType.DMA((3 * groups,))],
+        cost_estimate=pl.CostEstimate(flops=0, bytes_accessed=10 * rows * groups * width, transcendentals=0),
+        compiler_params=pltpu.CompilerParams(vmem_limit_bytes=VMEM_SMALL),
+        name="unpack_early",
+    )(*parts)
+
+
+def unpack_late(parts, dq, dk, dv):
+    groups = len(parts)
+    rows, width = parts[0].shape
+    half = width // 2
+
+    def body(*refs):
+        dq, dk, dv, held, sems = refs[groups + 3 :]
+        here, low = lax.axis_index("head"), lax.axis_index("ctx") < 2
+        loads = run_copies([(refs[m], held.at[m]) for m in range(groups)], sems)
+
+        def moves(far, near):
+            todo = []
+            for m in range(groups):
+                base = pl.multiple_of((here ^ m) * width, LANES)
+                todo.append((held.at[m, :, pl.ds(0, half)], far.at[:, pl.ds(base + near, half)]))
+                todo.append((held.at[m, :, pl.ds(half, half)], dv.at[:, pl.ds(base + half, half)]))
+            return todo
+
+        wait_all(loads)
+
+        @pl.when(low)
+        def _():
+            wait_all(run_copies(moves(dk, half), sems))
+
+        @pl.when(jnp.logical_not(low))
+        def _():
+            wait_all(run_copies(moves(dq, 0), sems))
+
+    shape = jax.ShapeDtypeStruct(dq.shape, BF16)
+    return pl.pallas_call(
+        body,
+        out_shape=[shape] * 3,
+        in_specs=anywhere(groups + 3),
+        out_specs=anywhere(3),
+        scratch_shapes=[pltpu.VMEM((groups, rows, width), BF16), pltpu.SemaphoreType.DMA((2 * groups,))],
+        input_output_aliases={groups: 0, groups + 1: 1, groups + 2: 2},
+        compiler_params=pltpu.CompilerParams(vmem_limit_bytes=VMEM_SMALL),
+        cost_estimate=pl.CostEstimate(flops=0, bytes_accessed=8 * rows * groups * width, transcendentals=0),
+        name="unpack_late",
+    )(*parts, dq, dk, dv)
 
 
 def after(array, other):
@@ -734,39 +815,39 @@
     groups = lax.axis_size("head")
     width = queries.shape[1] // groups
 
-    def to_heads(x):
-        y = lax.all_to_all(x, "head", split_axis=0, concat_axis=0, tiled=True)
-        return y.reshape(-1, y.shape[2])
-
-    def to_tokens(x):
-        x = x.reshape(groups, -1, x.shape[1])
-        return lax.all_to_all(x, "head", split_axis=0, concat_axis=0, tiled=True)
-
-    x1, rest = pack(queries, keys_in, values_in, attn_out, out_grad, span_id.reshape(1, -1), groups, width)
-    y1 = add_norm(to_heads(x1), log_norm.T)
+    def swapped(parts):
+        return [parts[0]] + [
+            lax.ppermute(parts[m], "head", [(i, i ^ m) for i in range(groups)]) for m in range(1, groups)
+        ]
+
+    x1, x2, x3 = pack(queries, keys_in, values_in, attn_out, out_grad, span_id.reshape(1, -1), groups, width)
+    x1 = swapped(x1)
+    y1 = join_first(x1, log_norm.T)
     r1 = lax.ppermute(y1, "ctx", INWARD)
     s1 = lax.ppermute(y1, "ctx", SWAP)
-    rest = to_heads(after(rest, y1))
-    y2, key_edge, query_edge = cut(y1, rest)
-    y2, r1, s1 = lax.optimization_barrier((y2, r1, s1))
+    x2 = swapped(x2)
+    x3 = swapped(x3)
+    y2 = join(x2)
+    y2, r1, s1, x3 = lax.optimization_barrier((y2, r1, s1, x3))
     r2 = lax.ppermute(y2, "ctx", INWARD)
     s2 = lax.ppermute(r1, "ctx", SWAP)
+    w, key_edge, query_edge = join_last(x3, y1, y2)
     key_edge = lax.ppermute(key_edge, "ctx", DOWN)
     query_edge = lax.ppermute(query_edge, "ctx", UP)
-    rest, key_edge, query_edge = lax.optimization_barrier((rest, key_edge, query_edge))
-    swap1, out1, swap2, l1, l2, l3 = far_pairs(y1, rest, r1, r2, s1, s2)
-    dw, dy1, dy2, dkedge, dqedge = near_pairs(y1, rest, after(key_edge, l3), query_edge)
+    w, key_edge, query_edge = lax.optimization_barrier((w, key_edge, query_edge))
+    swap1, out1, swap2, l1, l2, l3 = far_pairs(y1, y2, w, r1, r2, s1, s2)
+    dw, dy1, dy2, dkedge, dqedge = near_pairs(y1, y2, w, after(key_edge, l3), query_edge)
     swap1 = lax.ppermute(swap1, "ctx", SWAP)
     out1 = lax.ppermute(out1, "ctx", OUTWARD)
     dkedge = lax.ppermute(dkedge, "ctx", UP)
     dqedge = lax.ppermute(dqedge, "ctx", DOWN)
-    sum1 = (swap1.astype(F32) + l3.astype(F32)).astype(BF16)
-    swap2 = lax.ppermute(after(swap2, swap1), "ctx", SWAP)
-    out2 = lax.ppermute(sum1, "ctx", OUTWARD)
-    dkedge, dqedge, out1 = after((dkedge, dqedge, out1), sum1)
-    early, kept = finish_first(dw, l1, dy2, l2, out1, dkedge, dqedge)
-    late = finish_second(dy1, swap2, out2, kept, dkedge, dqedge)
-    return tuple(unpack(to_tokens(early), to_tokens(late)))
+    swap1, swap2, out1, dkedge, dqedge = lax.optimization_barrier((swap1, swap2, out1, dkedge, dqedge))
+    swap2 = lax.ppermute(swap2, "ctx", SWAP)
+    out2 = lax.ppermute((swap1.astype(F32) + l3.astype(F32)).astype(BF16), "ctx", OUTWARD)
+    *early, kept = finish_first(dw, l1, dy2, l2, out1, dkedge, dqedge, groups)
+    early = swapped(early)
+    late = swapped(finish_second(dy1, swap2, out2, kept, dkedge, dqedge, groups))
+    return tuple(unpack_late(late, *unpack_early(early)))
 
 
 def splits(tokens, blocks, head_width, heads):
@@ -787,7 +868,7 @@
     heads = log_norm.shape[1]
     tokens = queries.shape[0] * blocks * groups
     plan = local_plain
-    if splits(tokens, blocks, queries.shape[1] // (heads * groups), heads):
+    if groups & (groups - 1) == 0 and splits(tokens, blocks, queries.shape[1] // (heads * groups), heads):
         plan = local_split
     return plan(queries, keys_in, values_in, attn_out, out_grad, log_norm, span_id)
 

time: 134 us -> 114 us (0.85)
  blocking collectives: 26.9 us -> 0 us
  starting transfers between devices: 47.7 us -> 55.4 us
  waiting for transfers between devices: 37.6 us -> 40.1 us
  local copies, waits for them, and re-layouts: 2.7 us -> 0.94 us
  Pallas kernels: 17.2 us -> 15.6 us
    all_to_all x2 -> x0, blocking collectives: 26.9 us -> none  [the longest x1 15.5 us: to_heads(): y = lax.all_to_all(x, 'head', split_axis=0, concat_axis=0, tiled=True)]
    ppermute x2 -> x17, starting transfers between devices: 1.99 us -> 19.5 us  [the longest x15 17.5 us: swapped(): lax.ppermute(parts[m], 'head', [(i, i ^ m) for i in range(groups)])]
    ppermute x2 -> x17, waiting for transfers between devices: 14.9 us -> 31.6 us  [the longest x15 26.4 us: swapped(): lax.ppermute(parts[m], 'head', [(i, i ^ m) for i in range(groups)])]
    all_to_all x2 -> x0, waiting for transfers between devices: 12.9 us -> none  [the longest x1 12.9 us: to_heads(): y = lax.all_to_all(x, 'head', split_axis=0, concat_axis=0, tiled=True)]
    all_to_all x2 -> x0, starting transfers between devices: 7.1 us -> none  [the longest x1 3.57 us: to_heads(): y = lax.all_to_all(x, 'head', split_axis=0, concat_axis=0, tiled=True)]
    ppermute x1, waiting for transfers between devices: 6.64 us -> 2.95 us  [local_split(): query_edge = lax.ppermute(query_edge, 'ctx', UP)]
    ppermute x1, starting transfers between devices: 5.98 us -> 3.11 us  [local_split(): r2 = lax.ppermute(y2, 'ctx', INWARD)]
    ppermute x1, waiting for transfers between devices: 2.44 us -> 5.06 us  [local_split(): dqedge = lax.ppermute(dqedge, 'ctx', DOWN)]
  transfers between devices with their start and end apart: 14 -> 27, of which waited for: 5 -> 13; matrix products, arithmetic and copies ran while one was open for 0% -> 0% of each run, Pallas kernels for 6% -> 8%
where the time goes in v4:
time: 114 us; the launch traced here: 113 us
  starting transfers between devices  55.4 us (49%)
  waiting for transfers between devices  40.1 us (35%)
  Pallas kernels  15.6 us (14%)
    ppermute x15, waiting for transfers between devices, swapped(): lax.ppermute(parts[m], 'head', [(i, i ^ m) for i in range(groups)])  26.4 us
    ppermute x15, starting transfers between devices, swapped(): lax.ppermute(parts[m], 'head', [(i, i ^ m) for i in range(groups)])  17.5 us
    ppermute x1, starting transfers between devices, local_split(): dkedge = lax.ppermute(dkedge, 'ctx', UP)  15.9 us
    ppermute x1, starting transfers between devices, local_split(): r1 = lax.ppermute(y1, 'ctx', INWARD)  6.3 us
    ppermute x1, waiting for transfers between devices, local_split(): lax.ppermute((swap1.astype(F32) + l3.astype(F32)).astype(BF16), 'ctx', OU...  5.15 us
    ppermute x1, waiting for transfers between devices, local_split(): dqedge = lax.ppermute(dqedge, 'ctx', DOWN)  5.06 us
    ppermute x1, starting transfers between devices, local_split(): query_edge = lax.ppermute(query_edge, 'ctx', UP)  4.55 us
    pallas_call x1, Pallas kernels, near_pairs(): pl.pallas_call(body, out_shape=[jax.ShapeDtypeStruct((rows, 2 * width), B...  4.28 us
  transfers between devices with their start and end apart: 27, of which 13 were waited for; matrix products, arithmetic and copies ran while one was open for 0% of the time, Pallas kernels for 8%

profile of v4, /device:TPU:0, one launch (start us, length us, event | category | flops | bytes accessed | tf_op | source)
XLA Modules:
  0.0 113.2 jit_solution(15367394500767038462)
XLA Ops:
  0.6 3.9 %pack.1 = (bf16[56,1408]{1,0:T(8,128)(2,1)}, bf16[56,1408]{1,0:T(8,128)(2,1)}, bf16[56,1408]{1,0:T(8,128)(2,1)}, bf16[56,1408]{1,0:T(8,128)(2,1)}, bf16[56,1280]...) custom-call(bf16[56,5120]{1,0:T(8,128)(2,1)} %q.1, ...), custom_call_target="tpu_custom_call" | custom-call | bytes 5734400 | tf_op jit(solution)/shard_map/pack/pallas_call | solution.py:224
  4.6 3.0 %collective-permute-start = (bf16[56,1408]{1,0:T(8,128)(2,1)}, bf16[56,1408]{1,0:T(8,128)(2,1)S(1)}, u32[]{:S(2)}, u32[]{:S(2)}) collective-permute-start(bf16[56,1408]{1,0:T(8,128)(2,1)} %get-tuple-element.58), channel_id=1, source_target_pairs={{0,1},{1,0},{2,3},{3,2},{4,5},{5,4},{6,7},{7,6},{8,9},{9,8},{10,11... | collective-permute-start | bytes 473096 | tf_op jit(solution)/shard_map/ppermute | solution.py:820
  7.6 1.5 %collective-permute-start.1 = (bf16[56,1408]{1,0:T(8,128)(2,1)}, bf16[56,1408]{1,0:T(8,128)(2,1)S(1)}, u32[]{:S(2)}, u32[]{:S(2)}) collective-permute-start(bf16[56,1408]{1,0:T(8,128)(2,1)} %get-tuple-element.59), channel_id=1, source_target_pairs={{0,2},{1,3},{2,0},{3,1},{4,6},{5,7},{6,4},{7,5},{8,10},{9,11},{10,... | collective-permute-start | bytes 473096 | tf_op jit(solution)/shard_map/ppermute | solution.py:820
  9.1 3.4 %collective-permute-done.refs_1_ = bf16[56,1408]{1,0:T(8,128)(2,1)S(1)} collective-permute-done((bf16[56,1408]{1,0:T(8,128)(2,1)}, bf16[56,1408]{1,0:T(8,128)(2,1)S(1)}, u32[]{:S(2)}, u32[]{:S(2)}) %collective-permute-start) | collective-permute-done | bytes 157728 | tf_op jit(solution)/shard_map/ppermute | solution.py:820
  12.5 4.2 %collective-permute-done.1.refs_2_ = bf16[56,1408]{1,0:T(8,128)(2,1)S(1)} collective-permute-done((bf16[56,1408]{1,0:T(8,128)(2,1)}, bf16[56,1408]{1,0:T(8,128)(2,1)S(1)}, u32[]{:S(2)}, u32[]{:S(2)}) %collective-permute-start.1) | collective-permute-done | bytes 157728 | tf_op jit(solution)/shard_map/ppermute | solution.py:820
  17.6 1.1 join_first.1
  19.4 6.3 %collective-permute-start.6 = (bf16[224,1408]{1,0:T(8,128)(2,1)S(1)}, bf16[224,1408]{1,0:T(8,128)(2,1)S(1)}, u32[]{:S(2)}, u32[]{:S(2)}) collective-permute-start(bf16[224,1408]{1,0:T(8,128)(2,1)S(1)} %bitcast.6), channel_id=1, source_target_pairs={{0,4},{12,8},{1,5},{13,9},{2,6},{14,10},{3,7},{15,11},{16,20},{28,... | collective-permute-start | bytes 1892360 | tf_op jit(solution)/shard_map/ppermute | solution.py:826
  25.7 1.3 %collective-permute-start.3 = (bf16[56,1280]{1,0:T(8,128)(2,1)}, bf16[56,1280]{1,0:T(8,128)(2,1)S(1)}, u32[]{:S(2)}, u32[]{:S(2)}) collective-permute-start(bf16[56,1280]{1,0:T(8,128)(2,1)} %get-tuple-element.62), channel_id=1, source_target_pairs={{0,1},{1,0},{2,3},{3,2},{4,5},{5,4},{6,7},{7,6},{8,9},{9,8},{10,11... | collective-permute-start | bytes 430088 | tf_op jit(solution)/shard_map/ppermute | solution.py:820
  27.9 1.4 %collective-permute-start.5 = (bf16[56,1280]{1,0:T(8,128)(2,1)S(1)}, bf16[56,1280]{1,0:T(8,128)(2,1)S(1)}, u32[]{:S(2)}, u32[]{:S(2)}) collective-permute-start(bf16[56,1280]{1,0:T(8,128)(2,1)S(1)} %copy-done.6), channel_id=1, source_target_pairs={{0,3},{1,2},{2,1},{3,0},{4,7},{5,6},{6,5},{7,4},{8,11},{9,10},{10,... | collective-permute-start | bytes 430088 | tf_op jit(solution)/shard_map/ppermute | solution.py:820
  29.3 3.3 %collective-permute-done.3.refs_1_ = bf16[56,1280]{1,0:T(8,128)(2,1)S(1)} collective-permute-done((bf16[56,1280]{1,0:T(8,128)(2,1)}, bf16[56,1280]{1,0:T(8,128)(2,1)S(1)}, u32[]{:S(2)}, u32[]{:S(2)}) %collective-permute-start.3) | collective-permute-done | bytes 143392 | tf_op jit(solution)/shard_map/ppermute | solution.py:820
  33.9 2.3 %collective-permute-done.5.refs_3_ = bf16[56,1280]{1,0:T(8,128)(2,1)S(1)} collective-permute-done((bf16[56,1280]{1,0:T(8,128)(2,1)S(1)}, bf16[56,1280]{1,0:T(8,128)(2,1)S(1)}, u32[]{:S(2)}, u32[]{:S(2)}) %collective-permute-start.5) | collective-permute-done | bytes 143392 | tf_op jit(solution)/shard_map/ppermute | solution.py:820
  38.0 4.6 %collective-permute-done.8.refs_1_ = bf16[56,2560]{1,0:T(8,128)(2,1)S(1)} collective-permute-done((bf16[56,2560]{1,0:T(8,128)(2,1)}, bf16[56,2560]{1,0:T(8,128)(2,1)S(1)}, u32[]{:S(2)}, u32[]{:S(2)}) %collective-permute-start.8) | collective-permute-done | bytes 286752 | tf_op jit(solution)/shard_map/ppermute | solution.py:820
  42.6 4.8 %collective-permute-done.9.refs_2_ = bf16[56,2560]{1,0:T(8,128)(2,1)S(1)} collective-permute-done((bf16[56,2560]{1,0:T(8,128)(2,1)S(1)}, bf16[56,2560]{1,0:T(8,128)(2,1)S(1)}, u32[]{:S(2)}, u32[]{:S(2)}) %collective-permute-start.9) | collective-permute-done | bytes 286752 | tf_op jit(solution)/shard_map/ppermute | solution.py:820
  48.1 3.1 %collective-permute-start.13 = (bf16[224,1280]{1,0:T(8,128)(2,1)S(1)}, bf16[224,1280]{1,0:T(8,128)(2,1)S(1)}, u32[]{:S(2)}, u32[]{:S(2)}) collective-permute-start(bf16[224,1280]{1,0:T(8,128)(2,1)S(1)} %bitcast.10), channel_id=1, source_target_pairs={{0,4},{12,8},{1,5},{13,9},{2,6},{14,10},{3,7},{15,11},{16,20},{28,... | collective-permute-start | bytes 1720328 | tf_op jit(solution)/shard_map/ppermute | solution.py:832
  51.6 1.3 %collective-permute-start.11 = (bf16[16,2688]{1,0:T(8,128)(2,1)S(1)}, bf16[16,2688]{1,0:T(8,128)(2,1)S(1)}, u32[]{:S(2)}, u32[]{:S(2)}) collective-permute-start(bf16[16,2688]{1,0:T(8,128)(2,1)S(1)} %get-tuple-element.75), channel_id=1, source_target_pairs={{4,0},{8,4},{12,8},{5,1},{9,5},{13,9},{6,2},{10,6},{14,10},{7,3},{... | collective-permute-start | bytes 258056 | tf_op jit(solution)/shard_map/ppermute | solution.py:835
  52.9 4.6 %collective-permute-start.12 = (bf16[16,2688]{1,0:T(8,128)(2,1)S(1)}, bf16[16,2688]{1,0:T(8,128)(2,1)S(1)}, u32[]{:S(2)}, u32[]{:S(2)}) collective-permute-start(bf16[16,2688]{1,0:T(8,128)(2,1)S(1)} %get-tuple-element.76), channel_id=1, source_target_pairs={{0,4},{4,8},{8,12},{1,5},{5,9},{9,13},{2,6},{6,10},{10,14},{3,7},{... | collective-permute-start | bytes 258056 | tf_op jit(solution)/shard_map/ppermute | solution.py:836
  58.0 3.0 %collective-permute-done.12.qedge = bf16[16,2688]{1,0:T(8,128)(2,1)S(1)} collective-permute-done((bf16[16,2688]{1,0:T(8,128)(2,1)S(1)}, bf16[16,2688]{1,0:T(8,128)(2,1)S(1)}, u32[]{:S(2)}, u32[]{:S(2)}) %collective-permute-start.12) | collective-permute-done | bytes 86048 | tf_op jit(solution)/shard_map/ppermute | solution.py:836
  61.7 1.3 %collective-permute-start.16 = (bf16[224,1280]{1,0:T(8,128)(2,1)S(1)}, bf16[224,1280]{1,0:T(8,128)(2,1)S(1)}, u32[]{:S(2)}, u32[]{:S(2)}) collective-permute-start(bf16[224,1280]{1,0:T(8,128)(2,1)S(1)} %get-tuple-element.87), channel_id=1, source_target_pairs={{4,0},{8,12},{5,1},{9,13},{6,2},{10,14},{7,3},{11,15},{20,16},{24,... | collective-permute-start | bytes 1720328 | tf_op jit(solution)/shard_map/ppermute | solution.py:841
  63.0 4.3 %near_pairs.1 = (bf16[224,2560]{1,0:T(8,128)(2,1)S(1)}, bf16[224,1280]{1,0:T(8,128)(2,1)S(1)}, bf16[224,1280]{1,0:T(8,128)(2,1)S(1)}, bf16[16,2560]{1,0:T(8,128)(2,1)S(1)}, bf16[16,1280]{1,0:T(8,128)(2,1)S(1)}) custom-call(bf16[224,1408]{1,0:T(8,128)(2,1)S(1)} %bitcast.9, bf16[224,1280]{1,0:T(8,128)(2,1)S(1)} %bitcast.13, bf16[224,2560]{1,0:T(8,128)(2,1)S(1)} %bitcast.15, ...), custom_call_target="tpu_custom_call" | custom-call | flops 642252800 | bytes 4587520 | tf_op jit(solution)/shard_map/near_pairs/pallas_call | solution.py:607
  67.3 15.9 %collective-permute-start.17 = (bf16[16,2560]{1,0:T(8,128)(2,1)S(1)}, bf16[16,2560]{1,0:T(8,128)(2,1)S(1)}, u32[]{:S(2)}, u32[]{:S(2)}) collective-permute-start(bf16[16,2560]{1,0:T(8,128)(2,1)S(1)} %get-tuple-element.88), channel_id=1, source_target_pairs={{0,4},{4,8},{8,12},{1,5},{5,9},{9,13},{2,6},{6,10},{10,14},{3,7},{... | collective-permute-start | bytes 245768 | tf_op jit(solution)/shard_map/ppermute | solution.py:842
  83.2 1.3 %collective-permute-start.18 = (bf16[16,1280]{1,0:T(8,128)(2,1)S(1)}, bf16[16,1280]{1,0:T(8,128)(2,1)S(1)}, u32[]{:S(2)}, u32[]{:S(2)}) collective-permute-start(bf16[16,1280]{1,0:T(8,128)(2,1)S(1)} %get-tuple-element.89), channel_id=1, source_target_pairs={{4,0},{8,4},{12,8},{5,1},{9,5},{13,9},{6,2},{10,6},{14,10},{7,3},{... | collective-permute-start | bytes 122888 | tf_op jit(solution)/shard_map/ppermute | solution.py:843
  84.5 5.1 %collective-permute-done.18.dq = bf16[16,1280]{1,0:T(8,128)(2,1)S(1)} collective-permute-done((bf16[16,1280]{1,0:T(8,128)(2,1)S(1)}, bf16[16,1280]{1,0:T(8,128)(2,1)S(1)}, u32[]{:S(2)}, u32[]{:S(2)}) %collective-permute-start.18) | collective-permute-done | bytes 40992 | tf_op jit(solution)/shard_map/ppermute | solution.py:843
  89.8 1.3 %collective-permute-start.20 = (bf16[224,1280]{1,0:T(8,128)(2,1)S(1)}, bf16[224,1280]{1,0:T(8,128)(2,1)S(1)}, u32[]{:S(2)}, u32[]{:S(2)}) collective-permute-start(bf16[224,1280]{1,0:T(8,128)(2,1)S(1)} %add_convert_fusion), channel_id=1, source_target_pairs={{4,0},{8,12},{5,1},{9,13},{6,2},{10,14},{7,3},{11,15},{20,16},{24,... | collective-permute-start | bytes 1720328 | tf_op jit(solution)/shard_map/ppermute | solution.py:846
  92.7 1.4 %collective-permute-start.24 = (bf16[56,2560]{1,0:T(8,128)(2,1)S(1)}, bf16[56,2560]{1,0:T(8,128)(2,1)S(1)}, u32[]{:S(2)}, u32[]{:S(2)}) collective-permute-start(bf16[56,2560]{1,0:T(8,128)(2,1)S(1)} %get-tuple-element.105), channel_id=1, source_target_pairs={{0,1},{1,0},{2,3},{3,2},{4,5},{5,4},{6,7},{7,6},{8,9},{9,8},{10,11... | collective-permute-start | bytes 860168 | tf_op jit(solution)/shard_map/ppermute | solution.py:820
  94.0 1.3 %collective-permute-start.25 = (bf16[56,2560]{1,0:T(8,128)(2,1)S(1)}, bf16[56,2560]{1,0:T(8,128)(2,1)S(1)}, u32[]{:S(2)}, u32[]{:S(2)}) collective-permute-start(bf16[56,2560]{1,0:T(8,128)(2,1)S(1)} %get-tuple-element.106), channel_id=1, source_target_pairs={{0,2},{1,3},{2,0},{3,1},{4,6},{5,7},{6,4},{7,5},{8,10},{9,11},{10,... | collective-permute-start | bytes 860168 | tf_op jit(solution)/shard_map/ppermute | solution.py:820
  96.2 5.1 %collective-permute-done.20.out2 = bf16[224,1280]{1,0:T(8,128)(2,1)S(1)} collective-permute-done((bf16[224,1280]{1,0:T(8,128)(2,1)S(1)}, bf16[224,1280]{1,0:T(8,128)(2,1)S(1)}, u32[]{:S(2)}, u32[]{:S(2)}) %collective-permute-start.20) | collective-permute-done | bytes 573472 | tf_op jit(solution)/shard_map/ppermute | solution.py:846
  101.4 1.1 finish_second.1
  102.4 1.4 %collective-permute-start.21 = (bf16[56,1280]{1,0:T(8,128)(2,1)S(1)}, bf16[56,1280]{1,0:T(8,128)(2,1)S(1)}, u32[]{:S(2)}, u32[]{:S(2)}) collective-permute-start(bf16[56,1280]{1,0:T(8,128)(2,1)S(1)} %get-tuple-element.101), channel_id=1, source_target_pairs={{0,1},{1,0},{2,3},{3,2},{4,5},{5,4},{6,7},{7,6},{8,9},{9,8},{10,11... | collective-permute-start | bytes 430088 | tf_op jit(solution)/shard_map/ppermute | solution.py:820
  103.8 1.6 %collective-permute-start.22 = (bf16[56,1280]{1,0:T(8,128)(2,1)S(1)}, bf16[56,1280]{1,0:T(8,128)(2,1)S(1)}, u32[]{:S(2)}, u32[]{:S(2)}) collective-permute-start(bf16[56,1280]{1,0:T(8,128)(2,1)S(1)} %get-tuple-element.102), channel_id=1, source_target_pairs={{0,2},{1,3},{2,0},{3,1},{4,6},{5,7},{6,4},{7,5},{8,10},{9,11},{10,... | collective-permute-start | bytes 430088 | tf_op jit(solution)/shard_map/ppermute | solution.py:820
  106.8 1.5 %unpack_early.1 = (bf16[56,5120]{1,0:T(8,128)(2,1)}, bf16[56,5120]{1,0:T(8,128)(2,1)}, bf16[56,5120]{1,0:T(8,128)(2,1)}) custom-call(bf16[56,2560]{1,0:T(8,128)(2,1)S(1)} %get-tuple-element.104.refs_0_, bf16[56,2560]{1,0:T(8,128)(2,1)S(1)} %collective-permute-done.24.refs_1_, bf16[56,2560]{1,0:T(8,128)(2,1)S(1)} %collective-permute-done.25.refs_2_, ...), custom_call_target="tpu_custom_call" | custom-call | bytes 2867200 | tf_op jit(solution)/shard_map/unpack_early/pallas_call | solution.py:756
  108.9 2.5 %collective-permute-done.23.refs_3_ = bf16[56,1280]{1,0:T(8,128)(2,1)S(1)} collective-permute-done((bf16[56,1280]{1,0:T(8,128)(2,1)S(1)}, bf16[56,1280]{1,0:T(8,128)(2,1)S(1)}, u32[]{:S(2)}, u32[]{:S(2)}) %collective-permute-start.23) | collective-permute-done | bytes 143392 | tf_op jit(solution)/shard_map/ppermute | solution.py:820
  111.4 1.6 %unpack_late.1 = (bf16[56,5120]{1,0:T(8,128)(2,1)}, bf16[56,5120]{1,0:T(8,128)(2,1)}, bf16[56,5120]{1,0:T(8,128)(2,1)}) custom-call(bf16[56,1280]{1,0:T(8,128)(2,1)S(1)} %get-tuple-element.100.refs_0_, bf16[56,1280]{1,0:T(8,128)(2,1)S(1)} %collective-permute-done.21.refs_1_, ...), custom_call_target="tpu_custom_call", output_to_operand_aliasing={{0}: (4, {}), {1}: (5, {}), {2}: (6, {})} | custom-call | bytes 2293760 | tf_op jit(solution)/shard_map/unpack_late/pallas_call | solution.py:797
  (47 shorter events, 12.6 us)
Async XLA Ops:
  0.6 16.0 %copy-start.3 = (f32[224,10]{0,1:T(8,128)S(1)}, f32[224,10]{0,1:T(8,128)}, u32[]{:S(2)}) copy-start(f32[224,10]{0,1:T(8,128)} %param.12) | copy-start | bytes 26884
  4.6 8.0 %collective-permute-start = (bf16[56,1408]{1,0:T(8,128)(2,1)}, bf16[56,1408]{1,0:T(8,128)(2,1)S(1)}, u32[]{:S(2)}, u32[]{:S(2)}) collective-permute-start(bf16[56,1408]{1,0:T(8,128)(2,1)} %get-tuple-element.58), channel_id=1, source_target_pairs={{0,1},{1,0},{2,3},{3,2},{4,5},{5,4},{6,7},{7,6},{8,9},{9,8},{10,11... | collective-permute-start | bytes 473096 | tf_op jit(solution)/shard_map/ppermute | solution.py:820
  7.6 9.1 %collective-permute-start.1 = (bf16[56,1408]{1,0:T(8,128)(2,1)}, bf16[56,1408]{1,0:T(8,128)(2,1)S(1)}, u32[]{:S(2)}, u32[]{:S(2)}) collective-permute-start(bf16[56,1408]{1,0:T(8,128)(2,1)} %get-tuple-element.59), channel_id=1, source_target_pairs={{0,2},{1,3},{2,0},{3,1},{4,6},{5,7},{6,4},{7,5},{8,10},{9,11},{10,... | collective-permute-start | bytes 473096 | tf_op jit(solution)/shard_map/ppermute | solution.py:820
  9.1 7.6 %collective-permute-start.2 = (bf16[56,1408]{1,0:T(8,128)(2,1)}, bf16[56,1408]{1,0:T(8,128)(2,1)S(1)}, u32[]{:S(2)}, u32[]{:S(2)}) collective-permute-start(bf16[56,1408]{1,0:T(8,128)(2,1)} %get-tuple-element.60), channel_id=1, source_target_pairs={{0,3},{1,2},{2,1},{3,0},{4,7},{5,6},{6,5},{7,4},{8,11},{9,10},{10,... | collective-permute-start | bytes 473096 | tf_op jit(solution)/shard_map/ppermute | solution.py:820
  17.6 15.7 %copy-start.5 = (bf16[56,2560]{1,0:T(8,128)(2,1)S(1)}, bf16[56,2560]{1,0:T(8,128)(2,1)}, u32[]{:S(2)}) copy-start(bf16[56,2560]{1,0:T(8,128)(2,1)} %get-tuple-element.67) | copy-start | bytes 860164
  17.6 18.6 %copy-start.4 = (bf16[56,2560]{1,0:T(8,128)(2,1)S(1)}, bf16[56,2560]{1,0:T(8,128)(2,1)}, u32[]{:S(2)}) copy-start(bf16[56,2560]{1,0:T(8,128)(2,1)} %get-tuple-element.68) | copy-start | bytes 860164
  17.6 19.6 %copy-start.2 = (bf16[56,1280]{1,0:T(8,128)(2,1)S(1)}, bf16[56,1280]{1,0:T(8,128)(2,1)}, u32[]{:S(2)}) copy-start(bf16[56,1280]{1,0:T(8,128)(2,1)} %get-tuple-element.61.refs_0_) | copy-start | bytes 430084
  17.6 33.6 %copy-start = (bf16[56,2560]{1,0:T(8,128)(2,1)S(1)}, bf16[56,2560]{1,0:T(8,128)(2,1)}, u32[]{:S(2)}) copy-start(bf16[56,2560]{1,0:T(8,128)(2,1)} %get-tuple-element.70.refs_0_) | copy-start | bytes 860164
  18.7 28.6 %collective-permute-start.7 = (bf16[224,1408]{1,0:T(8,128)(2,1)S(1)}, bf16[224,1408]{1,0:T(8,128)(2,1)S(1)}, u32[]{:S(2)}, u32[]{:S(2)}) collective-permute-start(bf16[224,1408]{1,0:T(8,128)(2,1)S(1)} %bitcast.5), channel_id=1, source_target_pairs={{4,8},{8,4},{5,9},{9,5},{6,10},{10,6},{7,11},{11,7},{20,24},{24,20... | collective-permute-start | bytes 1892360 | tf_op jit(solution)/shard_map/ppermute | solution.py:827
  19.4 27.9 %collective-permute-start.6 = (bf16[224,1408]{1,0:T(8,128)(2,1)S(1)}, bf16[224,1408]{1,0:T(8,128)(2,1)S(1)}, u32[]{:S(2)}, u32[]{:S(2)}) collective-permute-start(bf16[224,1408]{1,0:T(8,128)(2,1)S(1)} %bitcast.6), channel_id=1, source_target_pairs={{0,4},{12,8},{1,5},{13,9},{2,6},{14,10},{3,7},{15,11},{16,20},{28,... | collective-permute-start | bytes 1892360 | tf_op jit(solution)/shard_map/ppermute | solution.py:826
  25.7 6.9 %collective-permute-start.3 = (bf16[56,1280]{1,0:T(8,128)(2,1)}, bf16[56,1280]{1,0:T(8,128)(2,1)S(1)}, u32[]{:S(2)}, u32[]{:S(2)}) collective-permute-start(bf16[56,1280]{1,0:T(8,128)(2,1)} %get-tuple-element.62), channel_id=1, source_target_pairs={{0,1},{1,0},{2,3},{3,2},{4,5},{5,4},{6,7},{7,6},{8,9},{9,8},{10,11... | collective-permute-start | bytes 430088 | tf_op jit(solution)/shard_map/ppermute | solution.py:820
  27.0 6.2 %collective-permute-start.4 = (bf16[56,1280]{1,0:T(8,128)(2,1)}, bf16[56,1280]{1,0:T(8,128)(2,1)S(1)}, u32[]{:S(2)}, u32[]{:S(2)}) collective-permute-start(bf16[56,1280]{1,0:T(8,128)(2,1)} %get-tuple-element.63), channel_id=1, source_target_pairs={{0,2},{1,3},{2,0},{3,1},{4,6},{5,7},{6,4},{7,5},{8,10},{9,11},{10,... | collective-permute-start | bytes 430088 | tf_op jit(solution)/shard_map/ppermute | solution.py:820
  27.9 8.3 %collective-permute-start.5 = (bf16[56,1280]{1,0:T(8,128)(2,1)S(1)}, bf16[56,1280]{1,0:T(8,128)(2,1)S(1)}, u32[]{:S(2)}, u32[]{:S(2)}) collective-permute-start(bf16[56,1280]{1,0:T(8,128)(2,1)S(1)} %copy-done.6), channel_id=1, source_target_pairs={{0,3},{1,2},{2,1},{3,0},{4,7},{5,6},{6,5},{7,4},{8,11},{9,10},{10,... | collective-permute-start | bytes 430088 | tf_op jit(solution)/shard_map/ppermute | solution.py:820
  32.6 10.0 %collective-permute-start.8 = (bf16[56,2560]{1,0:T(8,128)(2,1)}, bf16[56,2560]{1,0:T(8,128)(2,1)S(1)}, u32[]{:S(2)}, u32[]{:S(2)}) collective-permute-start(bf16[56,2560]{1,0:T(8,128)(2,1)} %get-tuple-element.66), channel_id=1, source_target_pairs={{0,1},{1,0},{2,3},{3,2},{4,5},{5,4},{6,7},{7,6},{8,9},{9,8},{10,11... | collective-permute-start | bytes 860168 | tf_op jit(solution)/shard_map/ppermute | solution.py:820
  33.2 14.1 %collective-permute-start.9 = (bf16[56,2560]{1,0:T(8,128)(2,1)S(1)}, bf16[56,2560]{1,0:T(8,128)(2,1)S(1)}, u32[]{:S(2)}, u32[]{:S(2)}) collective-permute-start(bf16[56,2560]{1,0:T(8,128)(2,1)S(1)} %copy-done.5), channel_id=1, source_target_pairs={{0,2},{1,3},{2,0},{3,1},{4,6},{5,7},{6,4},{7,5},{8,10},{9,11},{10,... | collective-permute-start | bytes 860168 | tf_op jit(solution)/shard_map/ppermute | solution.py:820
  36.2 11.2 %collective-permute-start.10 = (bf16[56,2560]{1,0:T(8,128)(2,1)S(1)}, bf16[56,2560]{1,0:T(8,128)(2,1)S(1)}, u32[]{:S(2)}, u32[]{:S(2)}) collective-permute-start(bf16[56,2560]{1,0:T(8,128)(2,1)S(1)} %copy-done.4), channel_id=1, source_target_pairs={{0,3},{1,2},{2,1},{3,0},{4,7},{5,6},{6,5},{7,4},{8,11},{9,10},{10,... | collective-permute-start | bytes 860168 | tf_op jit(solution)/shard_map/ppermute | solution.py:820
  47.4 13.6 %collective-permute-start.14 = (bf16[224,1408]{1,0:T(8,128)(2,1)S(1)}, bf16[224,1408]{1,0:T(8,128)(2,1)S(1)}, u32[]{:S(2)}, u32[]{:S(2)}) collective-permute-start(bf16[224,1408]{1,0:T(8,128)(2,1)S(1)} %collective-permute-done.6.r1), channel_id=1, source_target_pairs={{4,8},{8,4},{5,9},{9,5},{6,10},{10,6},{7,11},{11,7},{20,24},{24,20... | collective-permute-start | bytes 1892360 | tf_op jit(solution)/shard_map/ppermute | solution.py:833
  48.1 12.8 %collective-permute-start.13 = (bf16[224,1280]{1,0:T(8,128)(2,1)S(1)}, bf16[224,1280]{1,0:T(8,128)(2,1)S(1)}, u32[]{:S(2)}, u32[]{:S(2)}) collective-permute-start(bf16[224,1280]{1,0:T(8,128)(2,1)S(1)} %bitcast.10), channel_id=1, source_target_pairs={{0,4},{12,8},{1,5},{13,9},{2,6},{14,10},{3,7},{15,11},{16,20},{28,... | collective-permute-start | bytes 1720328 | tf_op jit(solution)/shard_map/ppermute | solution.py:832
  51.6 6.4 %collective-permute-start.11 = (bf16[16,2688]{1,0:T(8,128)(2,1)S(1)}, bf16[16,2688]{1,0:T(8,128)(2,1)S(1)}, u32[]{:S(2)}, u32[]{:S(2)}) collective-permute-start(bf16[16,2688]{1,0:T(8,128)(2,1)S(1)} %get-tuple-element.75), channel_id=1, source_target_pairs={{4,0},{8,4},{12,8},{5,1},{9,5},{13,9},{6,2},{10,6},{14,10},{7,3},{... | collective-permute-start | bytes 258056 | tf_op jit(solution)/shard_map/ppermute | solution.py:835
  52.9 8.0 %collective-permute-start.12 = (bf16[16,2688]{1,0:T(8,128)(2,1)S(1)}, bf16[16,2688]{1,0:T(8,128)(2,1)S(1)}, u32[]{:S(2)}, u32[]{:S(2)}) collective-permute-start(bf16[16,2688]{1,0:T(8,128)(2,1)S(1)} %get-tuple-element.76), channel_id=1, source_target_pairs={{0,4},{4,8},{8,12},{1,5},{5,9},{9,13},{2,6},{6,10},{10,14},{3,7},{... | collective-permute-start | bytes 258056 | tf_op jit(solution)/shard_map/ppermute | solution.py:836
  61.0 28.6 %collective-permute-start.15 = (bf16[224,1280]{1,0:T(8,128)(2,1)S(1)}, bf16[224,1280]{1,0:T(8,128)(2,1)S(1)}, u32[]{:S(2)}, u32[]{:S(2)}) collective-permute-start(bf16[224,1280]{1,0:T(8,128)(2,1)S(1)} %get-tuple-element.85), channel_id=1, source_target_pairs={{4,8},{8,4},{5,9},{9,5},{6,10},{10,6},{7,11},{11,7},{20,24},{24,20... | collective-permute-start | bytes 1720328 | tf_op jit(solution)/shard_map/ppermute | solution.py:840
  61.7 27.9 %collective-permute-start.16 = (bf16[224,1280]{1,0:T(8,128)(2,1)S(1)}, bf16[224,1280]{1,0:T(8,128)(2,1)S(1)}, u32[]{:S(2)}, u32[]{:S(2)}) collective-permute-start(bf16[224,1280]{1,0:T(8,128)(2,1)S(1)} %get-tuple-element.87), channel_id=1, source_target_pairs={{4,0},{8,12},{5,1},{9,13},{6,2},{10,14},{7,3},{11,15},{20,16},{24,... | collective-permute-start | bytes 1720328 | tf_op jit(solution)/shard_map/ppermute | solution.py:841
  67.3 22.3 %collective-permute-start.17 = (bf16[16,2560]{1,0:T(8,128)(2,1)S(1)}, bf16[16,2560]{1,0:T(8,128)(2,1)S(1)}, u32[]{:S(2)}, u32[]{:S(2)}) collective-permute-start(bf16[16,2560]{1,0:T(8,128)(2,1)S(1)} %get-tuple-element.88), channel_id=1, source_target_pairs={{0,4},{4,8},{8,12},{1,5},{5,9},{9,13},{2,6},{6,10},{10,14},{3,7},{... | collective-permute-start | bytes 245768 | tf_op jit(solution)/shard_map/ppermute | solution.py:842
  83.2 6.4 %collective-permute-start.18 = (bf16[16,1280]{1,0:T(8,128)(2,1)S(1)}, bf16[16,1280]{1,0:T(8,128)(2,1)S(1)}, u32[]{:S(2)}, u32[]{:S(2)}) collective-permute-start(bf16[16,1280]{1,0:T(8,128)(2,1)S(1)} %get-tuple-element.89), channel_id=1, source_target_pairs={{4,0},{8,4},{12,8},{5,1},{9,5},{13,9},{6,2},{10,6},{14,10},{7,3},{... | collective-permute-start | bytes 122888 | tf_op jit(solution)/shard_map/ppermute | solution.py:843
  89.8 11.6 %collective-permute-start.20 = (bf16[224,1280]{1,0:T(8,128)(2,1)S(1)}, bf16[224,1280]{1,0:T(8,128)(2,1)S(1)}, u32[]{:S(2)}, u32[]{:S(2)}) collective-permute-start(bf16[224,1280]{1,0:T(8,128)(2,1)S(1)} %add_convert_fusion), channel_id=1, source_target_pairs={{4,0},{8,12},{5,1},{9,13},{6,2},{10,14},{7,3},{11,15},{20,16},{24,... | collective-permute-start | bytes 1720328 | tf_op jit(solution)/shard_map/ppermute | solution.py:846
  91.1 10.3 %collective-permute-start.19 = (bf16[224,1280]{1,0:T(8,128)(2,1)S(1)}, bf16[224,1280]{1,0:T(8,128)(2,1)S(1)}, u32[]{:S(2)}, u32[]{:S(2)}) collective-permute-start(bf16[224,1280]{1,0:T(8,128)(2,1)S(1)} %get-tuple-element.90), channel_id=1, source_target_pairs={{4,8},{8,4},{5,9},{9,5},{6,10},{10,6},{7,11},{11,7},{20,24},{24,20... | collective-permute-start | bytes 1720328 | tf_op jit(solution)/shard_map/ppermute | solution.py:845
  92.7 12.8 %collective-permute-start.24 = (bf16[56,2560]{1,0:T(8,128)(2,1)S(1)}, bf16[56,2560]{1,0:T(8,128)(2,1)S(1)}, u32[]{:S(2)}, u32[]{:S(2)}) collective-permute-start(bf16[56,2560]{1,0:T(8,128)(2,1)S(1)} %get-tuple-element.105), channel_id=1, source_target_pairs={{0,1},{1,0},{2,3},{3,2},{4,5},{5,4},{6,7},{7,6},{8,9},{9,8},{10,11... | collective-permute-start | bytes 860168 | tf_op jit(solution)/shard_map/ppermute | solution.py:820
  94.0 12.0 %collective-permute-start.25 = (bf16[56,2560]{1,0:T(8,128)(2,1)S(1)}, bf16[56,2560]{1,0:T(8,128)(2,1)S(1)}, u32[]{:S(2)}, u32[]{:S(2)}) collective-permute-start(bf16[56,2560]{1,0:T(8,128)(2,1)S(1)} %get-tuple-element.106), channel_id=1, source_target_pairs={{0,2},{1,3},{2,0},{3,1},{4,6},{5,7},{6,4},{7,5},{8,10},{9,11},{10,... | collective-permute-start | bytes 860168 | tf_op jit(solution)/shard_map/ppermute | solution.py:820
  95.3 11.5 %collective-permute-start.26 = (bf16[56,2560]{1,0:T(8,128)(2,1)S(1)}, bf16[56,2560]{1,0:T(8,128)(2,1)S(1)}, u32[]{:S(2)}, u32[]{:S(2)}) collective-permute-start(bf16[56,2560]{1,0:T(8,128)(2,1)S(1)} %get-tuple-element.107), channel_id=1, source_target_pairs={{0,3},{1,2},{2,1},{3,0},{4,7},{5,6},{6,5},{7,4},{8,11},{9,10},{10,... | collective-permute-start | bytes 860168 | tf_op jit(solution)/shard_map/ppermute | solution.py:820
  102.4 5.9 %collective-permute-start.21 = (bf16[56,1280]{1,0:T(8,128)(2,1)S(1)}, bf16[56,1280]{1,0:T(8,128)(2,1)S(1)}, u32[]{:S(2)}, u32[]{:S(2)}) collective-permute-start(bf16[56,1280]{1,0:T(8,128)(2,1)S(1)} %get-tuple-element.101), channel_id=1, source_target_pairs={{0,1},{1,0},{2,3},{3,2},{4,5},{5,4},{6,7},{7,6},{8,9},{9,8},{10,11... | collective-permute-start | bytes 430088 | tf_op jit(solution)/shard_map/ppermute | solution.py:820
  103.8 5.1 %collective-permute-start.22 = (bf16[56,1280]{1,0:T(8,128)(2,1)S(1)}, bf16[56,1280]{1,0:T(8,128)(2,1)S(1)}, u32[]{:S(2)}, u32[]{:S(2)}) collective-permute-start(bf16[56,1280]{1,0:T(8,128)(2,1)S(1)} %get-tuple-element.102), channel_id=1, source_target_pairs={{0,2},{1,3},{2,0},{3,1},{4,6},{5,7},{6,4},{7,5},{8,10},{9,11},{10,... | collective-permute-start | bytes 430088 | tf_op jit(solution)/shard_map/ppermute | solution.py:820
  105.4 6.0 %collective-permute-start.23 = (bf16[56,1280]{1,0:T(8,128)(2,1)S(1)}, bf16[56,1280]{1,0:T(8,128)(2,1)S(1)}, u32[]{:S(2)}, u32[]{:S(2)}) collective-permute-start(bf16[56,1280]{1,0:T(8,128)(2,1)S(1)} %get-tuple-element.103), channel_id=1, source_target_pairs={{0,3},{1,2},{2,1},{3,0},{4,7},{5,6},{6,5},{7,4},{8,11},{9,10},{10,... | collective-permute-start | bytes 430088 | tf_op jit(solution)/shard_map/ppermute | solution.py:820
  (2 other events, 11.2 us)

commit v5 on v4

--- a/solution.py
+++ b/solution.py
@@ -16,9 +16,8 @@
 BF16 = jnp.bfloat16
 F32 = jnp.float32
 
-INWARD = ((0, 1), (3, 2))
+PAIRS = ((0, 1), (1, 0), (2, 3), (3, 2))
 SWAP = ((1, 2), (2, 1))
-OUTWARD = ((1, 0), (2, 3))
 DOWN = ((1, 0), (2, 1), (3, 2))
 UP = ((0, 1), (1, 2), (2, 3))
 
@@ -561,7 +560,10 @@
         key_ids = jnp.sum(jnp.where(id_lane, kmeta[...].astype(F32), 0.0), axis=1, keepdims=True)
         at_key = lax.broadcasted_iota(jnp.int32, (total, total), 0)
         at_query = lax.broadcasted_iota(jnp.int32, (total, total), 1)
+        last_key = jnp.where(lax.axis_index("ctx") < 3, total, rows)
+        last_query = jnp.where(lax.axis_index("ctx") > 0, total, rows)
         visible = (key_ids <= info[2 * heads : 2 * heads + 1, :]) & ((at_key < rows) | (at_query < rows - EDGE))
+        visible = visible & (at_key < last_key) & (at_query < last_query)
         for i in range(2):
 
             def step(c, carry, i=i):
@@ -643,12 +645,13 @@
         here = lax.axis_index("head")
         z = lax.axis_index("ctx")
         low, middle = z < 2, (z == 1) | (z == 2)
+        after_first, before_last = z > 0, z < 3
 
         def own(cols):
             return dw[:, cols].astype(F32) + jnp.where(middle, l1[:, cols].astype(F32), 0.0)
 
         def second(cols):
-            return dy2[:, cols].astype(F32) + jnp.where(middle, l2[:, cols].astype(F32), 0.0) + out1[:, cols].astype(F32)
+            return dy2[:, cols].astype(F32) + jnp.where(middle, l2[:, cols], out1[:, cols]).astype(F32)
 
         def put(dst, cols, total, first, last=None):
             end = total[rows - EDGE :] if last is None else total[rows - EDGE :] + last
@@ -657,10 +660,10 @@
                 dst[h, :, cols] = total[h * share : (h + 1) * share].astype(BF16)
 
         def key_edge(cols):
-            return dk[:, cols].astype(F32)
+            return jnp.where(after_first, dk[:, cols].astype(F32), 0.0)
 
         def query_edge(cols):
-            return dq[:, cols].astype(F32)
+            return jnp.where(before_last, dq[:, cols].astype(F32), 0.0)
 
         a, b = pl.ds(0, half), pl.ds(half, half)
         c, d = pl.ds(width, half), pl.ds(width + half, half)
@@ -693,7 +696,8 @@
 
     def body(dy1, swap2, out2, v, dk, dq, *refs):
         outs, e, sems = refs[:groups], *refs[groups:]
-        here, low = lax.axis_index("head"), lax.axis_index("ctx") < 2
+        here, z = lax.axis_index("head"), lax.axis_index("ctx")
+        low, middle = z < 2, (z == 1) | (z == 2)
 
         def put(cols, whole):
             for h in range(groups):
@@ -703,14 +707,14 @@
         end = pl.ds(width + half, half)
 
         def total(cols):
-            return dy1[:, cols].astype(F32) + swap2[:, cols].astype(F32) + out2[:, cols].astype(F32)
+            return dy1[:, cols].astype(F32) + jnp.where(middle, swap2[:, cols], out2[:, cols]).astype(F32)
 
         left = total(a)
-        first = left[:EDGE] + jnp.where(low, dk[:, b].astype(F32), 0.0)
-        last = left[rows - EDGE :] + jnp.where(low, 0.0, dq[:, a].astype(F32))
+        first = left[:EDGE] + jnp.where(z == 1, dk[:, b].astype(F32), 0.0)
+        last = left[rows - EDGE :] + jnp.where(z == 2, dq[:, a].astype(F32), 0.0)
         put(a, jnp.concatenate([first, left[EDGE : rows - EDGE], last], axis=0))
         right = total(b)
-        right = jnp.concatenate([right[:EDGE] + dk[:, end].astype(F32), right[EDGE:]], axis=0)
+        right = jnp.concatenate([right[:EDGE] + jnp.where(z > 0, dk[:, end].astype(F32), 0.0), right[EDGE:]], axis=0)
         put(b, jnp.where(low, right, v[...].astype(F32)))
         wait_all(run_copies([(e.at[here ^ m], outs[m]) for m in range(groups)], sems))
 
@@ -823,13 +827,13 @@
     x1, x2, x3 = pack(queries, keys_in, values_in, attn_out, out_grad, span_id.reshape(1, -1), groups, width)
     x1 = swapped(x1)
     y1 = join_first(x1, log_norm.T)
-    r1 = lax.ppermute(y1, "ctx", INWARD)
+    r1 = lax.ppermute(y1, "ctx", PAIRS)
     s1 = lax.ppermute(y1, "ctx", SWAP)
     x2 = swapped(x2)
     x3 = swapped(x3)
     y2 = join(x2)
     y2, r1, s1, x3 = lax.optimization_barrier((y2, r1, s1, x3))
-    r2 = lax.ppermute(y2, "ctx", INWARD)
+    r2 = lax.ppermute(y2, "ctx", PAIRS)
     s2 = lax.ppermute(r1, "ctx", SWAP)
     w, key_edge, query_edge = join_last(x3, y1, y2)
     key_edge = lax.ppermute(key_edge, "ctx", DOWN)
@@ -838,12 +842,12 @@
     swap1, out1, swap2, l1, l2, l3 = far_pairs(y1, y2, w, r1, r2, s1, s2)
     dw, dy1, dy2, dkedge, dqedge = near_pairs(y1, y2, w, after(key_edge, l3), query_edge)
     swap1 = lax.ppermute(swap1, "ctx", SWAP)
-    out1 = lax.ppermute(out1, "ctx", OUTWARD)
+    out1 = lax.ppermute(out1, "ctx", PAIRS)
     dkedge = lax.ppermute(dkedge, "ctx", UP)
     dqedge = lax.ppermute(dqedge, "ctx", DOWN)
     swap1, swap2, out1, dkedge, dqedge = lax.optimization_barrier((swap1, swap2, out1, dkedge, dqedge))
     swap2 = lax.ppermute(swap2, "ctx", SWAP)
-    out2 = lax.ppermute((swap1.astype(F32) + l3.astype(F32)).astype(BF16), "ctx", OUTWARD)
+    out2 = lax.ppermute((swap1.astype(F32) + l3.astype(F32)).astype(BF16), "ctx", PAIRS)
     *early, kept = finish_first(dw, l1, dy2, l2, out1, dkedge, dqedge, groups)
     early = swapped(early)
     late = swapped(finish_second(dy1, swap2, out2, kept, dkedge, dqedge, groups))

time: 114 us -> 108 us (0.947)
  starting transfers between devices: 55.4 us -> 50.5 us
    ppermute x1, starting transfers between devices: 15.9 us -> 1.93 us  [local_split(): dkedge = lax.ppermute(dkedge, 'ctx', UP)]
    ppermute x4, starting transfers between devices: 12 us -> 21.2 us  [the longest x1 13.1 us: local_split(): out1 = lax.ppermute(out1, 'ctx', PAIRS)]
    ppermute x1, waiting for transfers between devices: 0.52 us -> 4.23 us  [local_split(): key_edge = lax.ppermute(key_edge, 'ctx', DOWN)]
    ppermute x1, waiting for transfers between devices: 2.95 us -> 0.01 us  [local_split(): query_edge = lax.ppermute(query_edge, 'ctx', UP)]
    ppermute x4, waiting for transfers between devices: 5.16 us -> 3.4 us  [the longest x1 3.4 us: local_split(): lax.ppermute((swap1.astype(F32) + l3.astype(F32)).astype(BF16), 'ctx', PA...]
  transfers between devices with their start and end apart: 27 -> 27, of which waited for: 13 -> 12; matrix products, arithmetic and copies ran while one was open for 0% -> 0% of each run, Pallas kernels for 8% -> 8%
where the time goes in v5:
time: 108 us; the launch traced here: 107 us
  starting transfers between devices  50.5 us (47%)
  waiting for transfers between devices  39.4 us (36%)
  Pallas kernels  15.5 us (14%)
    ppermute x15, waiting for transfers between devices, swapped(): lax.ppermute(parts[m], 'head', [(i, i ^ m) for i in range(groups)])  26.6 us
    ppermute x15, starting transfers between devices, swapped(): lax.ppermute(parts[m], 'head', [(i, i ^ m) for i in range(groups)])  17.5 us
    ppermute x1, starting transfers between devices, local_split(): out1 = lax.ppermute(out1, 'ctx', PAIRS)  13.1 us
    ppermute x1, waiting for transfers between devices, local_split(): dqedge = lax.ppermute(dqedge, 'ctx', DOWN)  5.1 us
    ppermute x1, starting transfers between devices, local_split(): query_edge = lax.ppermute(query_edge, 'ctx', UP)  4.55 us
    ppermute x1, starting transfers between devices, local_split(): r1 = lax.ppermute(y1, 'ctx', PAIRS)  4.43 us
    pallas_call x1, Pallas kernels, near_pairs(): pl.pallas_call(body, out_shape=[jax.ShapeDtypeStruct((rows, 2 * width), B...  4.29 us
    ppermute x1, waiting for transfers between devices, local_split(): key_edge = lax.ppermute(key_edge, 'ctx', DOWN)  4.23 us
  transfers between devices with their start and end apart: 27, of which 12 were waited for; matrix products, arithmetic and copies ran while one was open for 0% of the time, Pallas kernels for 8%

profile of v5, /device:TPU:0, one launch (start us, length us, event | category | flops | bytes accessed | tf_op | source)
XLA Modules:
  0.0 107.4 jit_solution(6879117699531330371)
XLA Ops:
  0.6 3.9 %pack.1 = (bf16[56,1408]{1,0:T(8,128)(2,1)}, bf16[56,1408]{1,0:T(8,128)(2,1)}, bf16[56,1408]{1,0:T(8,128)(2,1)}, bf16[56,1408]{1,0:T(8,128)(2,1)}, bf16[56,1280]...) custom-call(bf16[56,5120]{1,0:T(8,128)(2,1)} %q.1, ...), custom_call_target="tpu_custom_call" | custom-call | bytes 5734400 | tf_op jit(solution)/shard_map/pack/pallas_call | solution.py:223
  4.6 3.0 %collective-permute-start = (bf16[56,1408]{1,0:T(8,128)(2,1)}, bf16[56,1408]{1,0:T(8,128)(2,1)S(1)}, u32[]{:S(2)}, u32[]{:S(2)}) collective-permute-start(bf16[56,1408]{1,0:T(8,128)(2,1)} %get-tuple-element.58), channel_id=1, source_target_pairs={{0,1},{1,0},{2,3},{3,2},{4,5},{5,4},{6,7},{7,6},{8,9},{9,8},{10,11... | collective-permute-start | bytes 473096 | tf_op jit(solution)/shard_map/ppermute | solution.py:824
  7.6 1.5 %collective-permute-start.1 = (bf16[56,1408]{1,0:T(8,128)(2,1)}, bf16[56,1408]{1,0:T(8,128)(2,1)S(1)}, u32[]{:S(2)}, u32[]{:S(2)}) collective-permute-start(bf16[56,1408]{1,0:T(8,128)(2,1)} %get-tuple-element.59), channel_id=1, source_target_pairs={{0,2},{1,3},{2,0},{3,1},{4,6},{5,7},{6,4},{7,5},{8,10},{9,11},{10,... | collective-permute-start | bytes 473096 | tf_op jit(solution)/shard_map/ppermute | solution.py:824
  9.1 3.4 %collective-permute-done.refs_1_ = bf16[56,1408]{1,0:T(8,128)(2,1)S(1)} collective-permute-done((bf16[56,1408]{1,0:T(8,128)(2,1)}, bf16[56,1408]{1,0:T(8,128)(2,1)S(1)}, u32[]{:S(2)}, u32[]{:S(2)}) %collective-permute-start) | collective-permute-done | bytes 157728 | tf_op jit(solution)/shard_map/ppermute | solution.py:824
  12.5 4.2 %collective-permute-done.1.refs_2_ = bf16[56,1408]{1,0:T(8,128)(2,1)S(1)} collective-permute-done((bf16[56,1408]{1,0:T(8,128)(2,1)}, bf16[56,1408]{1,0:T(8,128)(2,1)S(1)}, u32[]{:S(2)}, u32[]{:S(2)}) %collective-permute-start.1) | collective-permute-done | bytes 157728 | tf_op jit(solution)/shard_map/ppermute | solution.py:824
  17.6 1.1 %join_first.1 = bf16[4,56,1408]{2,1,0:T(8,128)(2,1)S(1)} custom-call(bf16[56,1408]{1,0:T(8,128)(2,1)S(1)} %copy-done.1, bf16[56,1408]{1,0:T(8,128)(2,1)S(1)} %collective-permute-done.refs_1_, bf16[56,1408]{1,0:T(8,128)(2,1)S(1)} %collective-permute-done.1.refs_2_, bf16[56,1408]{1,0:T(8,128)(2,1)S(1)} %collective-permute-done.2.refs_3_, f32[10,224]{1,0:T(8,128)S(1)} %bitcast.16), custom_call_target="tpu_custom_call" | custom-call | bytes 1261568 | tf_op jit(solution)/shard_map/join_first/pallas_call | solution.py:261
  19.4 4.4 %collective-permute-start.6 = (bf16[224,1408]{1,0:T(8,128)(2,1)S(1)}, bf16[224,1408]{1,0:T(8,128)(2,1)S(1)}, u32[]{:S(2)}, u32[]{:S(2)}) collective-permute-start(bf16[224,1408]{1,0:T(8,128)(2,1)S(1)} %bitcast.6), channel_id=1, source_target_pairs={{0,4},{4,0},{8,12},{12,8},{1,5},{5,1},{9,13},{13,9},{2,6},{6,2},{1... | collective-permute-start | bytes 1892360 | tf_op jit(solution)/shard_map/ppermute | solution.py:830
  23.9 1.2 %collective-permute-start.3 = (bf16[56,1280]{1,0:T(8,128)(2,1)}, bf16[56,1280]{1,0:T(8,128)(2,1)S(1)}, u32[]{:S(2)}, u32[]{:S(2)}) collective-permute-start(bf16[56,1280]{1,0:T(8,128)(2,1)} %get-tuple-element.62), channel_id=1, source_target_pairs={{0,1},{1,0},{2,3},{3,2},{4,5},{5,4},{6,7},{7,6},{8,9},{9,8},{10,11... | collective-permute-start | bytes 430088 | tf_op jit(solution)/shard_map/ppermute | solution.py:824
  25.9 1.4 %collective-permute-start.5 = (bf16[56,1280]{1,0:T(8,128)(2,1)S(1)}, bf16[56,1280]{1,0:T(8,128)(2,1)S(1)}, u32[]{:S(2)}, u32[]{:S(2)}) collective-permute-start(bf16[56,1280]{1,0:T(8,128)(2,1)S(1)} %copy-done.6), channel_id=1, source_target_pairs={{0,3},{1,2},{2,1},{3,0},{4,7},{5,6},{6,5},{7,4},{8,11},{9,10},{10,... | collective-permute-start | bytes 430088 | tf_op jit(solution)/shard_map/ppermute | solution.py:824
  27.4 3.2 %collective-permute-done.3.refs_1_ = bf16[56,1280]{1,0:T(8,128)(2,1)S(1)} collective-permute-done((bf16[56,1280]{1,0:T(8,128)(2,1)}, bf16[56,1280]{1,0:T(8,128)(2,1)S(1)}, u32[]{:S(2)}, u32[]{:S(2)}) %collective-permute-start.3) | collective-permute-done | bytes 143392 | tf_op jit(solution)/shard_map/ppermute | solution.py:824
  31.9 2.0 %collective-permute-done.5.refs_3_ = bf16[56,1280]{1,0:T(8,128)(2,1)S(1)} collective-permute-done((bf16[56,1280]{1,0:T(8,128)(2,1)S(1)}, bf16[56,1280]{1,0:T(8,128)(2,1)S(1)}, u32[]{:S(2)}, u32[]{:S(2)}) %collective-permute-start.5) | collective-permute-done | bytes 143392 | tf_op jit(solution)/shard_map/ppermute | solution.py:824
  33.9 1.1 collective-permute-start.10
  35.7 4.8 %collective-permute-done.8.refs_1_ = bf16[56,2560]{1,0:T(8,128)(2,1)S(1)} collective-permute-done((bf16[56,2560]{1,0:T(8,128)(2,1)}, bf16[56,2560]{1,0:T(8,128)(2,1)S(1)}, u32[]{:S(2)}, u32[]{:S(2)}) %collective-permute-start.8) | collective-permute-done | bytes 286752 | tf_op jit(solution)/shard_map/ppermute | solution.py:824
  40.5 4.7 %collective-permute-done.9.refs_2_ = bf16[56,2560]{1,0:T(8,128)(2,1)S(1)} collective-permute-done((bf16[56,2560]{1,0:T(8,128)(2,1)S(1)}, bf16[56,2560]{1,0:T(8,128)(2,1)S(1)}, u32[]{:S(2)}, u32[]{:S(2)}) %collective-permute-start.9) | collective-permute-done | bytes 286752 | tf_op jit(solution)/shard_map/ppermute | solution.py:824
  45.9 2.3 %collective-permute-start.13 = (bf16[224,1280]{1,0:T(8,128)(2,1)S(1)}, bf16[224,1280]{1,0:T(8,128)(2,1)S(1)}, u32[]{:S(2)}, u32[]{:S(2)}) collective-permute-start(bf16[224,1280]{1,0:T(8,128)(2,1)S(1)} %bitcast.10), channel_id=1, source_target_pairs={{0,4},{4,0},{8,12},{12,8},{1,5},{5,1},{9,13},{13,9},{2,6},{6,2},{1... | collective-permute-start | bytes 1720328 | tf_op jit(solution)/shard_map/ppermute | solution.py:836
  48.6 1.3 %collective-permute-start.11 = (bf16[16,2688]{1,0:T(8,128)(2,1)S(1)}, bf16[16,2688]{1,0:T(8,128)(2,1)S(1)}, u32[]{:S(2)}, u32[]{:S(2)}) collective-permute-start(bf16[16,2688]{1,0:T(8,128)(2,1)S(1)} %get-tuple-element.75), channel_id=1, source_target_pairs={{4,0},{8,4},{12,8},{5,1},{9,5},{13,9},{6,2},{10,6},{14,10},{7,3},{... | collective-permute-start | bytes 258056 | tf_op jit(solution)/shard_map/ppermute | solution.py:839
  49.9 4.6 %collective-permute-start.12 = (bf16[16,2688]{1,0:T(8,128)(2,1)S(1)}, bf16[16,2688]{1,0:T(8,128)(2,1)S(1)}, u32[]{:S(2)}, u32[]{:S(2)}) collective-permute-start(bf16[16,2688]{1,0:T(8,128)(2,1)S(1)} %get-tuple-element.76), channel_id=1, source_target_pairs={{0,4},{4,8},{8,12},{1,5},{5,9},{9,13},{2,6},{6,10},{10,14},{3,7},{... | collective-permute-start | bytes 258056 | tf_op jit(solution)/shard_map/ppermute | solution.py:840
  54.5 4.2 %collective-permute-done.11.kedge = bf16[16,2688]{1,0:T(8,128)(2,1)S(1)} collective-permute-done((bf16[16,2688]{1,0:T(8,128)(2,1)S(1)}, bf16[16,2688]{1,0:T(8,128)(2,1)S(1)}, u32[]{:S(2)}, u32[]{:S(2)}) %collective-permute-start.11) | collective-permute-done | bytes 86048 | tf_op jit(solution)/shard_map/ppermute | solution.py:839
  59.6 13.1 %collective-permute-start.16 = (bf16[224,1280]{1,0:T(8,128)(2,1)S(1)}, bf16[224,1280]{1,0:T(8,128)(2,1)S(1)}, u32[]{:S(2)}, u32[]{:S(2)}) collective-permute-start(bf16[224,1280]{1,0:T(8,128)(2,1)S(1)} %get-tuple-element.87), channel_id=1, source_target_pairs={{0,4},{4,0},{8,12},{12,8},{1,5},{5,1},{9,13},{13,9},{2,6},{6,2},{1... | collective-permute-start | bytes 1720328 | tf_op jit(solution)/shard_map/ppermute | solution.py:845
  72.7 4.3 %near_pairs.1 = (bf16[224,2560]{1,0:T(8,128)(2,1)S(1)}, bf16[224,1280]{1,0:T(8,128)(2,1)S(1)}, bf16[224,1280]{1,0:T(8,128)(2,1)S(1)}, bf16[16,2560]{1,0:T(8,128)(2,1)S(1)}, bf16[16,1280]{1,0:T(8,128)(2,1)S(1)}) custom-call(bf16[224,1408]{1,0:T(8,128)(2,1)S(1)} %bitcast.9, bf16[224,1280]{1,0:T(8,128)(2,1)S(1)} %bitcast.13, bf16[224,2560]{1,0:T(8,128)(2,1)S(1)} %bitcast.15, ...), custom_call_target="tpu_custom_call" | custom-call | flops 642252800 | bytes 4587520 | tf_op jit(solution)/shard_map/near_pairs/pallas_call | solution.py:609
  77.0 1.9 %collective-permute-start.17 = (bf16[16,2560]{1,0:T(8,128)(2,1)S(1)}, bf16[16,2560]{1,0:T(8,128)(2,1)S(1)}, u32[]{:S(2)}, u32[]{:S(2)}) collective-permute-start(bf16[16,2560]{1,0:T(8,128)(2,1)S(1)} %get-tuple-element.88), channel_id=1, source_target_pairs={{0,4},{4,8},{8,12},{1,5},{5,9},{9,13},{2,6},{6,10},{10,14},{3,7},{... | collective-permute-start | bytes 245768 | tf_op jit(solution)/shard_map/ppermute | solution.py:846
  79.0 1.3 %collective-permute-start.18 = (bf16[16,1280]{1,0:T(8,128)(2,1)S(1)}, bf16[16,1280]{1,0:T(8,128)(2,1)S(1)}, u32[]{:S(2)}, u32[]{:S(2)}) collective-permute-start(bf16[16,1280]{1,0:T(8,128)(2,1)S(1)} %get-tuple-element.89), channel_id=1, source_target_pairs={{4,0},{8,4},{12,8},{5,1},{9,5},{13,9},{6,2},{10,6},{14,10},{7,3},{... | collective-permute-start | bytes 122888 | tf_op jit(solution)/shard_map/ppermute | solution.py:847
  80.3 5.1 %collective-permute-done.18.dq = bf16[16,1280]{1,0:T(8,128)(2,1)S(1)} collective-permute-done((bf16[16,1280]{1,0:T(8,128)(2,1)S(1)}, bf16[16,1280]{1,0:T(8,128)(2,1)S(1)}, u32[]{:S(2)}, u32[]{:S(2)}) %collective-permute-start.18) | collective-permute-done | bytes 40992 | tf_op jit(solution)/shard_map/ppermute | solution.py:847
  85.5 1.3 %collective-permute-start.20 = (bf16[224,1280]{1,0:T(8,128)(2,1)S(1)}, bf16[224,1280]{1,0:T(8,128)(2,1)S(1)}, u32[]{:S(2)}, u32[]{:S(2)}) collective-permute-start(bf16[224,1280]{1,0:T(8,128)(2,1)S(1)} %add_convert_fusion), channel_id=1, source_target_pairs={{0,4},{4,0},{8,12},{12,8},{1,5},{5,1},{9,13},{13,9},{2,6},{6,2},{1... | collective-permute-start | bytes 1720328 | tf_op jit(solution)/shard_map/ppermute | solution.py:850
  88.3 1.5 %collective-permute-start.24 = (bf16[56,2560]{1,0:T(8,128)(2,1)S(1)}, bf16[56,2560]{1,0:T(8,128)(2,1)S(1)}, u32[]{:S(2)}, u32[]{:S(2)}) collective-permute-start(bf16[56,2560]{1,0:T(8,128)(2,1)S(1)} %get-tuple-element.105), channel_id=1, source_target_pairs={{0,1},{1,0},{2,3},{3,2},{4,5},{5,4},{6,7},{7,6},{8,9},{9,8},{10,11... | collective-permute-start | bytes 860168 | tf_op jit(solution)/shard_map/ppermute | solution.py:824
  91.9 3.4 %collective-permute-done.20.out2 = bf16[224,1280]{1,0:T(8,128)(2,1)S(1)} collective-permute-done((bf16[224,1280]{1,0:T(8,128)(2,1)S(1)}, bf16[224,1280]{1,0:T(8,128)(2,1)S(1)}, u32[]{:S(2)}, u32[]{:S(2)}) %collective-permute-start.20) | collective-permute-done | bytes 573472 | tf_op jit(solution)/shard_map/ppermute | solution.py:850
  96.3 1.5 %collective-permute-start.21 = (bf16[56,1280]{1,0:T(8,128)(2,1)S(1)}, bf16[56,1280]{1,0:T(8,128)(2,1)S(1)}, u32[]{:S(2)}, u32[]{:S(2)}) collective-permute-start(bf16[56,1280]{1,0:T(8,128)(2,1)S(1)} %get-tuple-element.101), channel_id=1, source_target_pairs={{0,1},{1,0},{2,3},{3,2},{4,5},{5,4},{6,7},{7,6},{8,9},{9,8},{10,11... | collective-permute-start | bytes 430088 | tf_op jit(solution)/shard_map/ppermute | solution.py:824
  97.8 1.9 %collective-permute-start.22 = (bf16[56,1280]{1,0:T(8,128)(2,1)S(1)}, bf16[56,1280]{1,0:T(8,128)(2,1)S(1)}, u32[]{:S(2)}, u32[]{:S(2)}) collective-permute-start(bf16[56,1280]{1,0:T(8,128)(2,1)S(1)} %get-tuple-element.102), channel_id=1, source_target_pairs={{0,2},{1,3},{2,0},{3,1},{4,6},{5,7},{6,4},{7,5},{8,10},{9,11},{10,... | collective-permute-start | bytes 430088 | tf_op jit(solution)/shard_map/ppermute | solution.py:824
  99.9 2.6 %collective-permute-done.25.refs_2_ = bf16[56,2560]{1,0:T(8,128)(2,1)S(1)} collective-permute-done((bf16[56,2560]{1,0:T(8,128)(2,1)S(1)}, bf16[56,2560]{1,0:T(8,128)(2,1)S(1)}, u32[]{:S(2)}, u32[]{:S(2)}) %collective-permute-start.25) | collective-permute-done | bytes 286752 | tf_op jit(solution)/shard_map/ppermute | solution.py:824
  102.4 1.5 %unpack_early.1 = (bf16[56,5120]{1,0:T(8,128)(2,1)}, bf16[56,5120]{1,0:T(8,128)(2,1)}, bf16[56,5120]{1,0:T(8,128)(2,1)}) custom-call(bf16[56,2560]{1,0:T(8,128)(2,1)S(1)} %get-tuple-element.104.refs_0_, bf16[56,2560]{1,0:T(8,128)(2,1)S(1)} %collective-permute-done.24.refs_1_, bf16[56,2560]{1,0:T(8,128)(2,1)S(1)} %collective-permute-done.25.refs_2_, ...), custom_call_target="tpu_custom_call" | custom-call | bytes 2867200 | tf_op jit(solution)/shard_map/unpack_early/pallas_call | solution.py:760
  104.4 1.3 %collective-permute-done.23.refs_3_ = bf16[56,1280]{1,0:T(8,128)(2,1)S(1)} collective-permute-done((bf16[56,1280]{1,0:T(8,128)(2,1)S(1)}, bf16[56,1280]{1,0:T(8,128)(2,1)S(1)}, u32[]{:S(2)}, u32[]{:S(2)}) %collective-permute-start.23) | collective-permute-done | bytes 143392 | tf_op jit(solution)/shard_map/ppermute | solution.py:824
  105.7 1.6 %unpack_late.1 = (bf16[56,5120]{1,0:T(8,128)(2,1)}, bf16[56,5120]{1,0:T(8,128)(2,1)}, bf16[56,5120]{1,0:T(8,128)(2,1)}) custom-call(bf16[56,1280]{1,0:T(8,128)(2,1)S(1)} %get-tuple-element.100.refs_0_, bf16[56,1280]{1,0:T(8,128)(2,1)S(1)} %collective-permute-done.21.refs_1_, ...), custom_call_target="tpu_custom_call", output_to_operand_aliasing={{0}: (4, {}), {1}: (5, {}), {2}: (6, {})} | custom-call | bytes 2293760 | tf_op jit(solution)/shard_map/unpack_late/pallas_call | solution.py:801
  (47 shorter events, 11.8 us)
Async XLA Ops:
  0.6 16.0 %copy-start.3 = (f32[224,10]{0,1:T(8,128)S(1)}, f32[224,10]{0,1:T(8,128)}, u32[]{:S(2)}) copy-start(f32[224,10]{0,1:T(8,128)} %param.12) | copy-start | bytes 26884
  4.6 8.0 %collective-permute-start = (bf16[56,1408]{1,0:T(8,128)(2,1)}, bf16[56,1408]{1,0:T(8,128)(2,1)S(1)}, u32[]{:S(2)}, u32[]{:S(2)}) collective-permute-start(bf16[56,1408]{1,0:T(8,128)(2,1)} %get-tuple-element.58), channel_id=1, source_target_pairs={{0,1},{1,0},{2,3},{3,2},{4,5},{5,4},{6,7},{7,6},{8,9},{9,8},{10,11... | collective-permute-start | bytes 473096 | tf_op jit(solution)/shard_map/ppermute | solution.py:824
  7.6 9.1 %collective-permute-start.1 = (bf16[56,1408]{1,0:T(8,128)(2,1)}, bf16[56,1408]{1,0:T(8,128)(2,1)S(1)}, u32[]{:S(2)}, u32[]{:S(2)}) collective-permute-start(bf16[56,1408]{1,0:T(8,128)(2,1)} %get-tuple-element.59), channel_id=1, source_target_pairs={{0,2},{1,3},{2,0},{3,1},{4,6},{5,7},{6,4},{7,5},{8,10},{9,11},{10,... | collective-permute-start | bytes 473096 | tf_op jit(solution)/shard_map/ppermute | solution.py:824
  9.1 7.6 %collective-permute-start.2 = (bf16[56,1408]{1,0:T(8,128)(2,1)}, bf16[56,1408]{1,0:T(8,128)(2,1)S(1)}, u32[]{:S(2)}, u32[]{:S(2)}) collective-permute-start(bf16[56,1408]{1,0:T(8,128)(2,1)} %get-tuple-element.60), channel_id=1, source_target_pairs={{0,3},{1,2},{2,1},{3,0},{4,7},{5,6},{6,5},{7,4},{8,11},{9,10},{10,... | collective-permute-start | bytes 473096 | tf_op jit(solution)/shard_map/ppermute | solution.py:824
  17.6 13.4 %copy-start.5 = (bf16[56,2560]{1,0:T(8,128)(2,1)S(1)}, bf16[56,2560]{1,0:T(8,128)(2,1)}, u32[]{:S(2)}) copy-start(bf16[56,2560]{1,0:T(8,128)(2,1)} %get-tuple-element.67) | copy-start | bytes 860164
  17.6 16.3 %copy-start.4 = (bf16[56,2560]{1,0:T(8,128)(2,1)S(1)}, bf16[56,2560]{1,0:T(8,128)(2,1)}, u32[]{:S(2)}) copy-start(bf16[56,2560]{1,0:T(8,128)(2,1)} %get-tuple-element.68) | copy-start | bytes 860164
  17.6 17.4 %copy-start.2 = (bf16[56,1280]{1,0:T(8,128)(2,1)S(1)}, bf16[56,1280]{1,0:T(8,128)(2,1)}, u32[]{:S(2)}) copy-start(bf16[56,1280]{1,0:T(8,128)(2,1)} %get-tuple-element.61.refs_0_) | copy-start | bytes 430084
  17.6 30.6 %copy-start = (bf16[56,2560]{1,0:T(8,128)(2,1)S(1)}, bf16[56,2560]{1,0:T(8,128)(2,1)}, u32[]{:S(2)}) copy-start(bf16[56,2560]{1,0:T(8,128)(2,1)} %get-tuple-element.70.refs_0_) | copy-start | bytes 860164
  18.7 26.5 %collective-permute-start.7 = (bf16[224,1408]{1,0:T(8,128)(2,1)S(1)}, bf16[224,1408]{1,0:T(8,128)(2,1)S(1)}, u32[]{:S(2)}, u32[]{:S(2)}) collective-permute-start(bf16[224,1408]{1,0:T(8,128)(2,1)S(1)} %bitcast.5), channel_id=1, source_target_pairs={{4,8},{8,4},{5,9},{9,5},{6,10},{10,6},{7,11},{11,7},{20,24},{24,20... | collective-permute-start | bytes 1892360 | tf_op jit(solution)/shard_map/ppermute | solution.py:831
  19.4 25.8 %collective-permute-start.6 = (bf16[224,1408]{1,0:T(8,128)(2,1)S(1)}, bf16[224,1408]{1,0:T(8,128)(2,1)S(1)}, u32[]{:S(2)}, u32[]{:S(2)}) collective-permute-start(bf16[224,1408]{1,0:T(8,128)(2,1)S(1)} %bitcast.6), channel_id=1, source_target_pairs={{0,4},{4,0},{8,12},{12,8},{1,5},{5,1},{9,13},{13,9},{2,6},{6,2},{1... | collective-permute-start | bytes 1892360 | tf_op jit(solution)/shard_map/ppermute | solution.py:830
  23.9 6.7 %collective-permute-start.3 = (bf16[56,1280]{1,0:T(8,128)(2,1)}, bf16[56,1280]{1,0:T(8,128)(2,1)S(1)}, u32[]{:S(2)}, u32[]{:S(2)}) collective-permute-start(bf16[56,1280]{1,0:T(8,128)(2,1)} %get-tuple-element.62), channel_id=1, source_target_pairs={{0,1},{1,0},{2,3},{3,2},{4,5},{5,4},{6,7},{7,6},{8,9},{9,8},{10,11... | collective-permute-start | bytes 430088 | tf_op jit(solution)/shard_map/ppermute | solution.py:824
  25.1 5.9 %collective-permute-start.4 = (bf16[56,1280]{1,0:T(8,128)(2,1)}, bf16[56,1280]{1,0:T(8,128)(2,1)S(1)}, u32[]{:S(2)}, u32[]{:S(2)}) collective-permute-start(bf16[56,1280]{1,0:T(8,128)(2,1)} %get-tuple-element.63), channel_id=1, source_target_pairs={{0,2},{1,3},{2,0},{3,1},{4,6},{5,7},{6,4},{7,5},{8,10},{9,11},{10,... | collective-permute-start | bytes 430088 | tf_op jit(solution)/shard_map/ppermute | solution.py:824
  25.9 8.0 %collective-permute-start.5 = (bf16[56,1280]{1,0:T(8,128)(2,1)S(1)}, bf16[56,1280]{1,0:T(8,128)(2,1)S(1)}, u32[]{:S(2)}, u32[]{:S(2)}) collective-permute-start(bf16[56,1280]{1,0:T(8,128)(2,1)S(1)} %copy-done.6), channel_id=1, source_target_pairs={{0,3},{1,2},{2,1},{3,0},{4,7},{5,6},{6,5},{7,4},{8,11},{9,10},{10,... | collective-permute-start | bytes 430088 | tf_op jit(solution)/shard_map/ppermute | solution.py:824
  30.6 10.0 %collective-permute-start.8 = (bf16[56,2560]{1,0:T(8,128)(2,1)}, bf16[56,2560]{1,0:T(8,128)(2,1)S(1)}, u32[]{:S(2)}, u32[]{:S(2)}) collective-permute-start(bf16[56,2560]{1,0:T(8,128)(2,1)} %get-tuple-element.66), channel_id=1, source_target_pairs={{0,1},{1,0},{2,3},{3,2},{4,5},{5,4},{6,7},{7,6},{8,9},{9,8},{10,11... | collective-permute-start | bytes 860168 | tf_op jit(solution)/shard_map/ppermute | solution.py:824
  31.0 14.2 %collective-permute-start.9 = (bf16[56,2560]{1,0:T(8,128)(2,1)S(1)}, bf16[56,2560]{1,0:T(8,128)(2,1)S(1)}, u32[]{:S(2)}, u32[]{:S(2)}) collective-permute-start(bf16[56,2560]{1,0:T(8,128)(2,1)S(1)} %copy-done.5), channel_id=1, source_target_pairs={{0,2},{1,3},{2,0},{3,1},{4,6},{5,7},{6,4},{7,5},{8,10},{9,11},{10,... | collective-permute-start | bytes 860168 | tf_op jit(solution)/shard_map/ppermute | solution.py:824
  33.9 11.3 %collective-permute-start.10 = (bf16[56,2560]{1,0:T(8,128)(2,1)S(1)}, bf16[56,2560]{1,0:T(8,128)(2,1)S(1)}, u32[]{:S(2)}, u32[]{:S(2)}) collective-permute-start(bf16[56,2560]{1,0:T(8,128)(2,1)S(1)} %copy-done.4), channel_id=1, source_target_pairs={{0,3},{1,2},{2,1},{3,0},{4,7},{5,6},{6,5},{7,4},{8,11},{9,10},{10,... | collective-permute-start | bytes 860168 | tf_op jit(solution)/shard_map/ppermute | solution.py:824
  45.2 13.5 %collective-permute-start.14 = (bf16[224,1408]{1,0:T(8,128)(2,1)S(1)}, bf16[224,1408]{1,0:T(8,128)(2,1)S(1)}, u32[]{:S(2)}, u32[]{:S(2)}) collective-permute-start(bf16[224,1408]{1,0:T(8,128)(2,1)S(1)} %collective-permute-done.6.r1), channel_id=1, source_target_pairs={{4,8},{8,4},{5,9},{9,5},{6,10},{10,6},{7,11},{11,7},{20,24},{24,20... | collective-permute-start | bytes 1892360 | tf_op jit(solution)/shard_map/ppermute | solution.py:837
  45.9 12.8 %collective-permute-start.13 = (bf16[224,1280]{1,0:T(8,128)(2,1)S(1)}, bf16[224,1280]{1,0:T(8,128)(2,1)S(1)}, u32[]{:S(2)}, u32[]{:S(2)}) collective-permute-start(bf16[224,1280]{1,0:T(8,128)(2,1)S(1)} %bitcast.10), channel_id=1, source_target_pairs={{0,4},{4,0},{8,12},{12,8},{1,5},{5,1},{9,13},{13,9},{2,6},{6,2},{1... | collective-permute-start | bytes 1720328 | tf_op jit(solution)/shard_map/ppermute | solution.py:836
  48.6 10.1 %collective-permute-start.11 = (bf16[16,2688]{1,0:T(8,128)(2,1)S(1)}, bf16[16,2688]{1,0:T(8,128)(2,1)S(1)}, u32[]{:S(2)}, u32[]{:S(2)}) collective-permute-start(bf16[16,2688]{1,0:T(8,128)(2,1)S(1)} %get-tuple-element.75), channel_id=1, source_target_pairs={{4,0},{8,4},{12,8},{5,1},{9,5},{13,9},{6,2},{10,6},{14,10},{7,3},{... | collective-permute-start | bytes 258056 | tf_op jit(solution)/shard_map/ppermute | solution.py:839
  49.9 8.8 %collective-permute-start.12 = (bf16[16,2688]{1,0:T(8,128)(2,1)S(1)}, bf16[16,2688]{1,0:T(8,128)(2,1)S(1)}, u32[]{:S(2)}, u32[]{:S(2)}) collective-permute-start(bf16[16,2688]{1,0:T(8,128)(2,1)S(1)} %get-tuple-element.76), channel_id=1, source_target_pairs={{0,4},{4,8},{8,12},{1,5},{5,9},{9,13},{2,6},{6,10},{10,14},{3,7},{... | collective-permute-start | bytes 258056 | tf_op jit(solution)/shard_map/ppermute | solution.py:840
  58.9 26.5 %collective-permute-start.15 = (bf16[224,1280]{1,0:T(8,128)(2,1)S(1)}, bf16[224,1280]{1,0:T(8,128)(2,1)S(1)}, u32[]{:S(2)}, u32[]{:S(2)}) collective-permute-start(bf16[224,1280]{1,0:T(8,128)(2,1)S(1)} %get-tuple-element.85), channel_id=1, source_target_pairs={{4,8},{8,4},{5,9},{9,5},{6,10},{10,6},{7,11},{11,7},{20,24},{24,20... | collective-permute-start | bytes 1720328 | tf_op jit(solution)/shard_map/ppermute | solution.py:844
  59.6 25.8 %collective-permute-start.16 = (bf16[224,1280]{1,0:T(8,128)(2,1)S(1)}, bf16[224,1280]{1,0:T(8,128)(2,1)S(1)}, u32[]{:S(2)}, u32[]{:S(2)}) collective-permute-start(bf16[224,1280]{1,0:T(8,128)(2,1)S(1)} %get-tuple-element.87), channel_id=1, source_target_pairs={{0,4},{4,0},{8,12},{12,8},{1,5},{5,1},{9,13},{13,9},{2,6},{6,2},{1... | collective-permute-start | bytes 1720328 | tf_op jit(solution)/shard_map/ppermute | solution.py:845
  77.0 8.3 %collective-permute-start.17 = (bf16[16,2560]{1,0:T(8,128)(2,1)S(1)}, bf16[16,2560]{1,0:T(8,128)(2,1)S(1)}, u32[]{:S(2)}, u32[]{:S(2)}) collective-permute-start(bf16[16,2560]{1,0:T(8,128)(2,1)S(1)} %get-tuple-element.88), channel_id=1, source_target_pairs={{0,4},{4,8},{8,12},{1,5},{5,9},{9,13},{2,6},{6,10},{10,14},{3,7},{... | collective-permute-start | bytes 245768 | tf_op jit(solution)/shard_map/ppermute | solution.py:846
  79.0 6.4 %collective-permute-start.18 = (bf16[16,1280]{1,0:T(8,128)(2,1)S(1)}, bf16[16,1280]{1,0:T(8,128)(2,1)S(1)}, u32[]{:S(2)}, u32[]{:S(2)}) collective-permute-start(bf16[16,1280]{1,0:T(8,128)(2,1)S(1)} %get-tuple-element.89), channel_id=1, source_target_pairs={{4,0},{8,4},{12,8},{5,1},{9,5},{13,9},{6,2},{10,6},{14,10},{7,3},{... | collective-permute-start | bytes 122888 | tf_op jit(solution)/shard_map/ppermute | solution.py:847
  85.5 9.8 %collective-permute-start.20 = (bf16[224,1280]{1,0:T(8,128)(2,1)S(1)}, bf16[224,1280]{1,0:T(8,128)(2,1)S(1)}, u32[]{:S(2)}, u32[]{:S(2)}) collective-permute-start(bf16[224,1280]{1,0:T(8,128)(2,1)S(1)} %add_convert_fusion), channel_id=1, source_target_pairs={{0,4},{4,0},{8,12},{12,8},{1,5},{5,1},{9,13},{13,9},{2,6},{6,2},{1... | collective-permute-start | bytes 1720328 | tf_op jit(solution)/shard_map/ppermute | solution.py:850
  86.8 8.5 %collective-permute-start.19 = (bf16[224,1280]{1,0:T(8,128)(2,1)S(1)}, bf16[224,1280]{1,0:T(8,128)(2,1)S(1)}, u32[]{:S(2)}, u32[]{:S(2)}) collective-permute-start(bf16[224,1280]{1,0:T(8,128)(2,1)S(1)} %get-tuple-element.90), channel_id=1, source_target_pairs={{4,8},{8,4},{5,9},{9,5},{6,10},{10,6},{7,11},{11,7},{20,24},{24,20... | collective-permute-start | bytes 1720328 | tf_op jit(solution)/shard_map/ppermute | solution.py:849
  88.3 11.4 %collective-permute-start.24 = (bf16[56,2560]{1,0:T(8,128)(2,1)S(1)}, bf16[56,2560]{1,0:T(8,128)(2,1)S(1)}, u32[]{:S(2)}, u32[]{:S(2)}) collective-permute-start(bf16[56,2560]{1,0:T(8,128)(2,1)S(1)} %get-tuple-element.105), channel_id=1, source_target_pairs={{0,1},{1,0},{2,3},{3,2},{4,5},{5,4},{6,7},{7,6},{8,9},{9,8},{10,11... | collective-permute-start | bytes 860168 | tf_op jit(solution)/shard_map/ppermute | solution.py:824
  89.8 12.6 %collective-permute-start.25 = (bf16[56,2560]{1,0:T(8,128)(2,1)S(1)}, bf16[56,2560]{1,0:T(8,128)(2,1)S(1)}, u32[]{:S(2)}, u32[]{:S(2)}) collective-permute-start(bf16[56,2560]{1,0:T(8,128)(2,1)S(1)} %get-tuple-element.106), channel_id=1, source_target_pairs={{0,2},{1,3},{2,0},{3,1},{4,6},{5,7},{6,4},{7,5},{8,10},{9,11},{10,... | collective-permute-start | bytes 860168 | tf_op jit(solution)/shard_map/ppermute | solution.py:824
  90.9 11.6 %collective-permute-start.26 = (bf16[56,2560]{1,0:T(8,128)(2,1)S(1)}, bf16[56,2560]{1,0:T(8,128)(2,1)S(1)}, u32[]{:S(2)}, u32[]{:S(2)}) collective-permute-start(bf16[56,2560]{1,0:T(8,128)(2,1)S(1)} %get-tuple-element.107), channel_id=1, source_target_pairs={{0,3},{1,2},{2,1},{3,0},{4,7},{5,6},{6,5},{7,4},{8,11},{9,10},{10,... | collective-permute-start | bytes 860168 | tf_op jit(solution)/shard_map/ppermute | solution.py:824
  96.3 7.6 %collective-permute-start.21 = (bf16[56,1280]{1,0:T(8,128)(2,1)S(1)}, bf16[56,1280]{1,0:T(8,128)(2,1)S(1)}, u32[]{:S(2)}, u32[]{:S(2)}) collective-permute-start(bf16[56,1280]{1,0:T(8,128)(2,1)S(1)} %get-tuple-element.101), channel_id=1, source_target_pairs={{0,1},{1,0},{2,3},{3,2},{4,5},{5,4},{6,7},{7,6},{8,9},{9,8},{10,11... | collective-permute-start | bytes 430088 | tf_op jit(solution)/shard_map/ppermute | solution.py:824
  97.8 6.6 %collective-permute-start.22 = (bf16[56,1280]{1,0:T(8,128)(2,1)S(1)}, bf16[56,1280]{1,0:T(8,128)(2,1)S(1)}, u32[]{:S(2)}, u32[]{:S(2)}) collective-permute-start(bf16[56,1280]{1,0:T(8,128)(2,1)S(1)} %get-tuple-element.102), channel_id=1, source_target_pairs={{0,2},{1,3},{2,0},{3,1},{4,6},{5,7},{6,4},{7,5},{8,10},{9,11},{10,... | collective-permute-start | bytes 430088 | tf_op jit(solution)/shard_map/ppermute | solution.py:824
  99.7 6.0 %collective-permute-start.23 = (bf16[56,1280]{1,0:T(8,128)(2,1)S(1)}, bf16[56,1280]{1,0:T(8,128)(2,1)S(1)}, u32[]{:S(2)}, u32[]{:S(2)}) collective-permute-start(bf16[56,1280]{1,0:T(8,128)(2,1)S(1)} %get-tuple-element.103), channel_id=1, source_target_pairs={{0,3},{1,2},{2,1},{3,0},{4,7},{5,6},{6,5},{7,4},{8,11},{9,10},{10,... | collective-permute-start | bytes 430088 | tf_op jit(solution)/shard_map/ppermute | solution.py:824
  (2 other events, 9.2 us)

commit v6 on v5

--- a/solution.py
+++ b/solution.py
@@ -369,137 +369,88 @@
     return w.reshape(rows, 2 * width), key_edge, query_edge
 
 
+def in_vmem(count):
+    return [pl.BlockSpec(memory_space=pltpu.VMEM)] * count
+
+
 def far_pairs(y1, y2, w, r1, r2, s1, s2):
-    rows, width = r2.shape
+    rows, width = y2.shape
     half = width // 2
     count = half // LANES
     heads = 2 * count
 
-    def body(y1, y2, w, r1, r2, s1, s2, swap1, out1, swap2, l1, l2, l3, buf, grads, meta, info, sems):
+    def body(y1, y2, w, r1, r2, s1, s2, swap1, out1, swap2, l1, l2, l3, info):
         z = lax.axis_index("ctx")
-        one = z == 1
-
-        def pick(a, b):
-            return jnp.where(one, a, b)
-
-        @pl.when((z == 1) | (z == 2))
-        def _():
-            near = pl.multiple_of(pick(0, half), LANES)
-            other = pl.multiple_of(pick(half, 0), LANES)
-            main = pl.ds(0, width)
-            tail = pl.ds(width, LANES)
-            left, right = pl.ds(0, half), pl.ds(half, half)
-            made = run_copies(
-                [
-                    (y1.at[:, tail], meta.at[pick(2, 0)]),
-                    (s1.at[:, tail], meta.at[pick(0, 3)]),
-                    (s2.at[:, tail], meta.at[pick(1, 4)]),
-                    (r1.at[:, tail], meta.at[pick(3, 1)]),
-                    (s1.at[:, main], buf.at[pick(0, 3)]),
-                    (s2.at[:, main], buf.at[pick(1, 2)]),
-                    (r2, buf.at[pick(2, 1)]),
-                    (y2, buf.at[pick(3, 0)]),
-                    (w.at[:, pl.ds(near, half)], buf.at[4, :, left]),
-                    (w.at[:, pl.ds(width + near, half)], buf.at[4, :, right]),
-                    (w.at[:, pl.ds(other, half)], buf.at[5, :, left]),
-                    (w.at[:, pl.ds(width + other, half)], buf.at[5, :, right]),
-                    (r1.at[:, main], buf.at[6]),
-                ],
-                sems,
+
+        def both(ref, at=0, gap=half):
+            return lambda c: (
+                ref[:, at + c * LANES : at + (c + 1) * LANES],
+                ref[:, at + gap + c * LANES : at + gap + (c + 1) * LANES],
             )
-            wait_all(made)
-            for i in range(3):
-                info[i] = token_rows(meta[i], heads)
-            first_active = pick(0, count)
-            first_other = pick(count, 0)
-            zero = jnp.zeros((rows, LANES), BF16)
-
-            def single(q_slot, k_slot, c, head):
-                a = pl.ds(pl.multiple_of(c * LANES, LANES), LANES)
-                b = pl.ds(pl.multiple_of(half + c * LANES, LANES), LANES)
-                own = pick(2, 1)
-                return pair_terms(
-                    buf[q_slot, :, a],
-                    buf[q_slot, :, b],
-                    buf[k_slot, :, a],
-                    buf[k_slot, :, b],
-                    info[own, pl.ds(head, 1), :],
-                    info[own, pl.ds(heads + head, 1), :],
-                )
-
-            def step(c, carry):
-                a = pl.ds(pl.multiple_of(c * LANES, LANES), LANES)
-                b = pl.ds(pl.multiple_of(half + c * LANES, LANES), LANES)
-                head = first_active + c
-                extra_q, extra_k, extra_v = single(pick(4, 1), pick(2, 4), c, head)
-                key = buf[2:4, :, a].reshape(2 * rows, LANES)
-                value = buf[2:4, :, b].reshape(2 * rows, LANES)
-                key_sum, value_sum = None, None
-                for i in range(2):
-                    query_term, key_term, value_term = pair_terms(
-                        buf[i, :, a],
-                        buf[i, :, b],
-                        key,
-                        value,
-                        info[i, pl.ds(head, 1), :],
-                        info[i, pl.ds(heads + head, 1), :],
-                    )
-                    if i == 1:
-                        query_term += jnp.where(one, 0.0, extra_q)
-                    grads[i, :, a] = query_term.astype(BF16)
-                    grads[i, :, b] = zero
-                    key_sum = key_term if i == 0 else key_sum + key_term
-                    value_sum = value_term if i == 0 else value_sum + value_term
-                grads[2, :, a] = (key_sum[:rows] + jnp.where(one, extra_k, 0.0)).astype(BF16)
-                grads[2, :, b] = (value_sum[:rows] + jnp.where(one, extra_v, 0.0)).astype(BF16)
-                grads[3, :, a] = key_sum[rows:].astype(BF16)
-                grads[3, :, b] = value_sum[rows:].astype(BF16)
-                grads[4, :, a] = jnp.where(one, extra_q, extra_k).astype(BF16)
-                grads[4, :, b] = jnp.where(one, 0.0, extra_v).astype(BF16)
-                extra_q, extra_k, extra_v = single(pick(5, 6), pick(6, 5), c, first_other + c)
-                grads[5, :, a] = jnp.where(one, extra_q, extra_k).astype(BF16)
-                grads[5, :, b] = jnp.where(one, 0.0, extra_v).astype(BF16)
-                grads[6, :, a] = jnp.where(one, extra_k, extra_q).astype(BF16)
-                grads[6, :, b] = jnp.where(one, extra_v, 0.0).astype(BF16)
-                return carry
-
-            lax.fori_loop(0, count, step, 0, unroll=True)
-            made = run_copies(
-                [
-                    (grads.at[pick(1, 2)], swap1),
-                    (grads.at[pick(2, 1)], out1),
-                    (grads.at[pick(0, 3)], swap2),
-                    (grads.at[pick(3, 0)], l2),
-                    (grads.at[6], l3),
-                    (grads.at[4, :, left], l1.at[:, pl.ds(near, half)]),
-                    (grads.at[4, :, right], l1.at[:, pl.ds(width + near, half)]),
-                    (grads.at[5, :, left], l1.at[:, pl.ds(other, half)]),
-                    (grads.at[5, :, right], l1.at[:, pl.ds(width + other, half)]),
-                ],
-                sems,
-            )
-            wait_all(made)
-
-    single_shape = jax.ShapeDtypeStruct((rows, width), BF16)
+
+        def put(ref, at, value):
+            ref[:, at : at + LANES] = value.astype(BF16)
+
+        def scalars(slot, head):
+            return info[slot, head : head + 1, :], info[slot, heads + head : heads + head + 1, :]
+
+        def square(query_2, query_3, key_0, key_1, c, head):
+            keys, values = zip(key_0(c), key_1(c))
+            key, value = jnp.concatenate(keys, axis=0), jnp.concatenate(values, axis=0)
+            first = pair_terms(*query_2(c), key, value, *scalars(0, head))
+            second = pair_terms(*query_3(c), key, value, *scalars(1, head))
+            return first[0], second[0], first[1] + second[1], first[2] + second[2]
+
+        tail = pl.ds(width, LANES)
+
+        @pl.when(z == 1)
+        def _():
+            for slot, ref in enumerate((s1, s2, y1)):
+                info[slot] = token_rows(ref[:, tail], heads)
+            for c in range(count):
+                a, b = c * LANES, half + c * LANES
+                own = pair_terms(*both(w, 0, width)(c), *both(r2)(c), *scalars(2, c))
+                query_2, query_3, key, value = square(both(s1), both(s2), both(r2), both(y2), c, c)
+                put(swap1, a, query_3)
+                put(swap2, a, query_2)
+                put(out1, a, key[:rows] + own[1])
+                put(out1, b, value[:rows] + own[2])
+                put(l2, a, key[rows:])
+                put(l2, b, value[rows:])
+                put(l1, a, own[0])
+                own = pair_terms(*both(w, half, width)(c), *both(r1)(c), *scalars(2, count + c))
+                put(l1, half + a, own[0])
+                put(l3, a, own[1])
+                put(l3, b, own[2])
+
+        @pl.when(z == 2)
+        def _():
+            for slot, ref in enumerate((y1, r1)):
+                info[slot] = token_rows(ref[:, tail], heads)
+            for c in range(count):
+                a, b = c * LANES, half + c * LANES
+                own = pair_terms(*both(r2)(c), *both(w, half, width)(c), *scalars(1, count + c))
+                query_2, query_3, key, value = square(both(y2), both(r2), both(s2), both(s1), c, count + c)
+                put(swap1, a, key[:rows])
+                put(swap1, b, value[:rows])
+                put(swap2, a, key[rows:])
+                put(swap2, b, value[rows:])
+                put(out1, a, query_3 + own[0])
+                put(l2, a, query_2)
+                put(l1, b, own[1])
+                put(l1, width + b, own[2])
+                own = pair_terms(*both(r1)(c), *both(w, 0, width)(c), *scalars(1, c))
+                put(l1, a, own[1])
+                put(l1, width + a, own[2])
+                put(l3, a, own[0])
+
+    single = jax.ShapeDtypeStruct((rows, width), BF16)
     return pl.pallas_call(
         body,
-        out_shape=[
-            single_shape,
-            single_shape,
-            single_shape,
-            jax.ShapeDtypeStruct((rows, 2 * width), BF16),
-            single_shape,
-            single_shape,
-        ],
-        in_specs=anywhere(7),
-        out_specs=anywhere(6),
-        scratch_shapes=[
-            pltpu.VMEM((7, rows, width), BF16),
-            pltpu.VMEM((7, rows, width), BF16),
-            pltpu.VMEM((5, rows, LANES), BF16),
-            pltpu.VMEM((3, 32, rows), F32),
-            pltpu.SemaphoreType.DMA((13,)),
-        ],
+        out_shape=[single, single, single, jax.ShapeDtypeStruct((rows, 2 * width), BF16), single, single],
+        in_specs=in_vmem(7),
+        out_specs=in_vmem(6),
+        scratch_shapes=[pltpu.VMEM((3, 32, rows), F32)],
         compiler_params=pltpu.CompilerParams(vmem_limit_bytes=VMEM_LIMIT),
         cost_estimate=pl.CostEstimate(
             flops=30 * 10 * rows * rows * LANES, bytes_accessed=30 * rows * width, transcendentals=30 * rows * rows
@@ -515,96 +466,60 @@
     heads = 2 * count
     total = rows + EDGE
 
-    def body(y1, y2, w, kedge, qedge, dw, dy1, dy2, dkedge, dqedge, qbuf, kbuf, dq, dk, kmeta, qmeta, info, sems):
-        low = lax.axis_index("ctx") < 2
-        left, right = pl.ds(0, half), pl.ds(half, half)
-        own, past = pl.ds(0, rows), pl.ds(rows, EDGE)
-        main = pl.ds(0, width)
-
-        def halves(array, there, back=False, parts=2):
-            todo = []
-            for i in range(2):
-                for j in range(parts):
-                    wide = array.at[:, pl.ds(j * width + i * half, half)]
-                    narrow = there(i, right if j else left)
-                    todo.append((narrow, wide) if back else (wide, narrow))
-            return todo
-
-        shared = run_copies(
-            [
-                (y1.at[:, pl.ds(width, LANES)], kmeta.at[own]),
-                (y1.at[:, pl.ds(width, LANES)], qmeta.at[own]),
-                (kedge.at[:, pl.ds(2 * width, LANES)], kmeta.at[past]),
-                (qedge.at[:, pl.ds(2 * width, LANES)], qmeta.at[past]),
-            ]
-            + halves(kedge, lambda i, cols: kbuf.at[i, past, cols])
-            + halves(qedge, lambda i, cols: qbuf.at[i, past, cols]),
-            sems,
-        )
-
-        @pl.when(low)
-        def _():
-            todo = halves(w, lambda i, cols: qbuf.at[i, own, cols])
-            todo += [(y2, kbuf.at[0, own]), (y1.at[:, main], kbuf.at[1, own])]
-            wait_all(run_copies(todo, sems, 12))
-
-        @pl.when(jnp.logical_not(low))
-        def _():
-            todo = halves(w, lambda i, cols: kbuf.at[i, own, cols])
-            todo += [(y1.at[:, main], qbuf.at[0, own]), (y2, qbuf.at[1, own])]
-            wait_all(run_copies(todo, sems, 12))
-
-        wait_all(shared)
-        info[...] = token_rows(qmeta[...], heads)
+    def body(y1, y2, w, kedge, qedge, dw, dy1, dy2, dkedge, dqedge, info):
+        z = lax.axis_index("ctx")
+        tail, end = pl.ds(width, LANES), pl.ds(2 * width, LANES)
+        info[...] = token_rows(jnp.concatenate([y1[:, tail], qedge[:, end]], axis=0), heads)
+        key_meta = jnp.concatenate([y1[:, tail], kedge[:, end]], axis=0).astype(F32)
         id_lane = lax.broadcasted_iota(jnp.int32, (total, LANES), 1) == 3 * heads
-        key_ids = jnp.sum(jnp.where(id_lane, kmeta[...].astype(F32), 0.0), axis=1, keepdims=True)
+        key_ids = jnp.sum(jnp.where(id_lane, key_meta, 0.0), axis=1, keepdims=True)
         at_key = lax.broadcasted_iota(jnp.int32, (total, total), 0)
         at_query = lax.broadcasted_iota(jnp.int32, (total, total), 1)
-        last_key = jnp.where(lax.axis_index("ctx") < 3, total, rows)
-        last_query = jnp.where(lax.axis_index("ctx") > 0, total, rows)
+        last_key = jnp.where(z < 3, total, rows)
+        last_query = jnp.where(z > 0, total, rows)
         visible = (key_ids <= info[2 * heads : 2 * heads + 1, :]) & ((at_key < rows) | (at_query < rows - EDGE))
         visible = visible & (at_key < last_key) & (at_query < last_query)
-        for i in range(2):
-
-            def step(c, carry, i=i):
-                a = pl.ds(pl.multiple_of(c * LANES, LANES), LANES)
-                b = pl.ds(pl.multiple_of(half + c * LANES, LANES), LANES)
-                head = i * count + c
-                query_term, key_term, value_term = pair_terms(
-                    qbuf[i, :, a],
-                    qbuf[i, :, b],
-                    kbuf[i, :, a],
-                    kbuf[i, :, b],
-                    info[pl.ds(head, 1), :],
-                    info[pl.ds(heads + head, 1), :],
-                    visible,
-                )
-                dq[i, :, a] = query_term.astype(BF16)
-                dk[i, :, a] = key_term.astype(BF16)
-                dk[i, :, b] = value_term.astype(BF16)
-                return carry
-
-            lax.fori_loop(0, count, step, 0, unroll=True)
-
-        made = run_copies(
-            halves(dkedge, lambda i, cols: dk.at[i, past, cols], back=True)
-            + halves(dqedge, lambda i, cols: dq.at[i, past, cols], back=True, parts=1),
-            sems,
-        )
-
-        @pl.when(low)
-        def _():
-            todo = [(dq.at[0, own], dw.at[:, left]), (dq.at[1, own], dw.at[:, right])]
-            todo += [(dk.at[0, own], dy2), (dk.at[1, own], dy1)]
-            wait_all(run_copies(todo, sems, 12))
-
-        @pl.when(jnp.logical_not(low))
-        def _():
-            todo = halves(dw, lambda i, cols: dk.at[i, own, cols], back=True)
-            todo += [(dq.at[0, own], dy1.at[:, left]), (dq.at[1, own], dy2.at[:, left])]
-            wait_all(run_copies(todo, sems, 12))
-
-        wait_all(made)
+
+        def head_terms(i, c, payload):
+            a, b = i * half + c * LANES, width + i * half + c * LANES
+            small, large = c * LANES, half + c * LANES
+            wide = w[:, a : a + LANES], w[:, b : b + LANES]
+            narrow = payload[:, small : small + LANES], payload[:, large : large + LANES]
+            edge_k, edge_q = (
+                (edge[:, a : a + LANES], edge[:, b : b + LANES]) for edge in (kedge, qedge)
+            )
+
+            def terms(queries, keys):
+                query, grad = (jnp.concatenate(x, axis=0) for x in zip(queries, edge_q))
+                key, value = (jnp.concatenate(x, axis=0) for x in zip(keys, edge_k))
+                scalars = info[i * count + c : i * count + c + 1, :], info[heads + i * count + c : heads + i * count + c + 1, :]
+                made = [x.astype(BF16) for x in pair_terms(query, grad, key, value, *scalars, visible)]
+                dqedge[:, a : a + LANES] = made[0][rows:]
+                dkedge[:, a : a + LANES] = made[1][rows:]
+                dkedge[:, b : b + LANES] = made[2][rows:]
+                return [x[:rows] for x in made]
+
+            return a, b, small, large, wide, narrow, terms
+
+        @pl.when(z < 2)
+        def _():
+            for i, (payload, result) in enumerate(((y2, dy2), (y1, dy1))):
+                for c in range(count):
+                    a, b, small, large, wide, narrow, terms = head_terms(i, c, payload)
+                    query_term, key_term, value_term = terms(wide, narrow)
+                    dw[:, a : a + LANES] = query_term
+                    result[:, small : small + LANES] = key_term
+                    result[:, large : large + LANES] = value_term
+
+        @pl.when(z >= 2)
+        def _():
+            for i, (payload, result) in enumerate(((y1, dy1), (y2, dy2))):
+                for c in range(count):
+                    a, b, small, large, wide, narrow, terms = head_terms(i, c, payload)
+                    query_term, key_term, value_term = terms(narrow, wide)
+                    result[:, small : small + LANES] = query_term
+                    dw[:, a : a + LANES] = key_term
+                    dw[:, b : b + LANES] = value_term
 
     return pl.pallas_call(
         body,
@@ -615,18 +530,9 @@
             jax.ShapeDtypeStruct((EDGE, 2 * width), BF16),
             jax.ShapeDtypeStruct((EDGE, width), BF16),
         ],
-        in_specs=anywhere(5),
-        out_specs=anywhere(5),
-        scratch_shapes=[
-            pltpu.VMEM((2, total, width), BF16),
-            pltpu.VMEM((2, total, width), BF16),
-            pltpu.VMEM((2, total, half), BF16),
-            pltpu.VMEM((2, total, width), BF16),
-            pltpu.VMEM((total, LANES), BF16),
-            pltpu.VMEM((total, LANES), BF16),
-            pltpu.VMEM((32, total), F32),
-            pltpu.SemaphoreType.DMA((18,)),
-        ],
+        in_specs=in_vmem(5),
+        out_specs=in_vmem(5),
+        scratch_shapes=[pltpu.VMEM((32, total), F32)],
         compiler_params=pltpu.CompilerParams(vmem_limit_bytes=VMEM_LIMIT),
         cost_estimate=pl.CostEstimate(
             flops=10 * 10 * rows * rows * LANES, bytes_accessed=16 * rows * width, transcendentals=10 * rows * rows
@@ -825,11 +731,11 @@
         ]
 
     x1, x2, x3 = pack(queries, keys_in, values_in, attn_out, out_grad, span_id.reshape(1, -1), groups, width)
-    x1 = swapped(x1)
+    x1, x2 = swapped(x1), swapped(x2)
     y1 = join_first(x1, log_norm.T)
+    y1, x2[1], x2[2] = lax.optimization_barrier((y1, x2[1], x2[2]))
     r1 = lax.ppermute(y1, "ctx", PAIRS)
     s1 = lax.ppermute(y1, "ctx", SWAP)
-    x2 = swapped(x2)
     x3 = swapped(x3)
     y2 = join(x2)
     y2, r1, s1, x3 = lax.optimization_barrier((y2, r1, s1, x3))

time: 108 us -> 105 us (0.972)
  waiting for transfers between devices: 39.4 us -> 34.9 us
  starting transfers between devices: 50.5 us -> 52.9 us
    ppermute x15, waiting for transfers between devices: 26.6 us -> 19.9 us  [swapped(): lax.ppermute(parts[m], 'head', [(i, i ^ m) for i in range(groups)])]
    ppermute x15, starting transfers between devices: 17.5 us -> 20.2 us  [swapped(): lax.ppermute(parts[m], 'head', [(i, i ^ m) for i in range(groups)])]
    ppermute x1, waiting for transfers between devices: 4.23 us -> 6.45 us  [local_split(): key_edge = lax.ppermute(key_edge, 'ctx', DOWN)]
    ppermute x1, starting transfers between devices: 13.1 us -> 11.9 us  [local_split(): out1 = lax.ppermute(out1, 'ctx', PAIRS)]
    ppermute x1, starting transfers between devices: 1.3 us -> 2.55 us  [local_split(): lax.ppermute((swap1.astype(F32) + l3.astype(F32)).astype(BF16), 'ctx', PA...]
  transfers between devices with their start and end apart: 27 -> 27, of which waited for: 12 -> 12; matrix products, arithmetic and copies ran while one was open for 0% -> 0% of each run, Pallas kernels for 8% -> 9%
where the time goes in v6:
time: 105 us
  starting transfers between devices  52.9 us (50%)
  waiting for transfers between devices  34.9 us (33%)
  Pallas kernels  14.7 us (14%)
    ppermute x15, starting transfers between devices, swapped(): lax.ppermute(parts[m], 'head', [(i, i ^ m) for i in range(groups)])  20.2 us
    ppermute x15, waiting for transfers between devices, swapped(): lax.ppermute(parts[m], 'head', [(i, i ^ m) for i in range(groups)])  19.9 us
    ppermute x1, starting transfers between devices, local_split(): out1 = lax.ppermute(out1, 'ctx', PAIRS)  11.9 us
    ppermute x1, waiting for transfers between devices, local_split(): key_edge = lax.ppermute(key_edge, 'ctx', DOWN)  6.45 us
    ppermute x1, waiting for transfers between devices, local_split(): dqedge = lax.ppermute(dqedge, 'ctx', DOWN)  4.99 us
    ppermute x1, starting transfers between devices, local_split(): query_edge = lax.ppermute(query_edge, 'ctx', UP)  4.55 us
    ppermute x1, starting transfers between devices, local_split(): r1 = lax.ppermute(y1, 'ctx', PAIRS)  4.43 us
    pallas_call x1, Pallas kernels, pack(): pl.pallas_call(body, out_shape=[jax.ShapeDtypeStruct((rows, size), BF16)...  3.9 us
  transfers between devices with their start and end apart: 27, of which 12 were waited for; matrix products, arithmetic and copies ran while one was open for 0% of the time, Pallas kernels for 9%

profile of v6, /device:TPU:0, one launch (start us, length us, event | category | flops | bytes accessed | tf_op | source)
XLA Modules:
  0.0 104.7 jit_solution(10159611985071008746)
XLA Ops:
  0.6 3.9 %pack.1 = (bf16[56,1408]{1,0:T(8,128)(2,1)}, bf16[56,1408]{1,0:T(8,128)(2,1)}, bf16[56,1408]{1,0:T(8,128)(2,1)}, bf16[56,1408]{1,0:T(8,128)(2,1)}, bf16[56,1280]...) custom-call(bf16[56,5120]{1,0:T(8,128)(2,1)} %q.1, ...), custom_call_target="tpu_custom_call" | custom-call | bytes 5734400 | tf_op jit(solution)/shard_map/pack/pallas_call | solution.py:223
  4.6 3.0 %collective-permute-start = (bf16[56,1408]{1,0:T(8,128)(2,1)}, bf16[56,1408]{1,0:T(8,128)(2,1)S(1)}, u32[]{:S(2)}, u32[]{:S(2)}) collective-permute-start(bf16[56,1408]{1,0:T(8,128)(2,1)} %get-tuple-element.61), channel_id=1, source_target_pairs={{0,1},{1,0},{2,3},{3,2},{4,5},{5,4},{6,7},{7,6},{8,9},{9,8},{10,11... | collective-permute-start | bytes 473096 | tf_op jit(solution)/shard_map/ppermute | solution.py:730
  7.6 1.5 %collective-permute-start.1 = (bf16[56,1408]{1,0:T(8,128)(2,1)}, bf16[56,1408]{1,0:T(8,128)(2,1)S(1)}, u32[]{:S(2)}, u32[]{:S(2)}) collective-permute-start(bf16[56,1408]{1,0:T(8,128)(2,1)} %get-tuple-element.62), channel_id=1, source_target_pairs={{0,2},{1,3},{2,0},{3,1},{4,6},{5,7},{6,4},{7,5},{8,10},{9,11},{10,... | collective-permute-start | bytes 473096 | tf_op jit(solution)/shard_map/ppermute | solution.py:730
  9.1 1.9 %collective-permute-start.3 = (bf16[56,1280]{1,0:T(8,128)(2,1)}, bf16[56,1280]{1,0:T(8,128)(2,1)S(1)}, u32[]{:S(2)}, u32[]{:S(2)}) collective-permute-start(bf16[56,1280]{1,0:T(8,128)(2,1)} %get-tuple-element.64), channel_id=1, source_target_pairs={{0,1},{1,0},{2,3},{3,2},{4,5},{5,4},{6,7},{7,6},{8,9},{9,8},{10,11... | collective-permute-start | bytes 430088 | tf_op jit(solution)/shard_map/ppermute | solution.py:730
  11.0 1.5 %collective-permute-start.4 = (bf16[56,1280]{1,0:T(8,128)(2,1)}, bf16[56,1280]{1,0:T(8,128)(2,1)S(1)}, u32[]{:S(2)}, u32[]{:S(2)}) collective-permute-start(bf16[56,1280]{1,0:T(8,128)(2,1)} %get-tuple-element.65), channel_id=1, source_target_pairs={{0,2},{1,3},{2,0},{3,1},{4,6},{5,7},{6,4},{7,5},{8,10},{9,11},{10,... | collective-permute-start | bytes 430088 | tf_op jit(solution)/shard_map/ppermute | solution.py:730
  12.6 5.0 %collective-permute-done.1.refs_2_ = bf16[56,1408]{1,0:T(8,128)(2,1)S(1)} collective-permute-done((bf16[56,1408]{1,0:T(8,128)(2,1)}, bf16[56,1408]{1,0:T(8,128)(2,1)S(1)}, u32[]{:S(2)}, u32[]{:S(2)}) %collective-permute-start.1) | collective-permute-done | bytes 157728 | tf_op jit(solution)/shard_map/ppermute | solution.py:730
  20.4 4.4 %collective-permute-start.6 = (bf16[224,1408]{1,0:T(8,128)(2,1)S(1)}, bf16[224,1408]{1,0:T(8,128)(2,1)S(1)}, u32[]{:S(2)}, u32[]{:S(2)}) collective-permute-start(bf16[224,1408]{1,0:T(8,128)(2,1)S(1)} %bitcast.6), channel_id=1, source_target_pairs={{0,4},{4,0},{8,12},{12,8},{1,5},{5,1},{9,13},{13,9},{2,6},{6,2},{1... | collective-permute-start | bytes 1892360 | tf_op jit(solution)/shard_map/ppermute | solution.py:737
  24.9 1.6 %collective-permute-start.5 = (bf16[56,1280]{1,0:T(8,128)(2,1)S(1)}, bf16[56,1280]{1,0:T(8,128)(2,1)S(1)}, u32[]{:S(2)}, u32[]{:S(2)}) collective-permute-start(bf16[56,1280]{1,0:T(8,128)(2,1)S(1)} %copy-done.6), channel_id=1, source_target_pairs={{0,3},{1,2},{2,1},{3,0},{4,7},{5,6},{6,5},{7,4},{8,11},{9,10},{10,... | collective-permute-start | bytes 430088 | tf_op jit(solution)/shard_map/ppermute | solution.py:730
  26.4 1.8 %collective-permute-start.8 = (bf16[56,2560]{1,0:T(8,128)(2,1)}, bf16[56,2560]{1,0:T(8,128)(2,1)S(1)}, u32[]{:S(2)}, u32[]{:S(2)}) collective-permute-start(bf16[56,2560]{1,0:T(8,128)(2,1)} %get-tuple-element.72), channel_id=1, source_target_pairs={{0,1},{1,0},{2,3},{3,2},{4,5},{5,4},{6,7},{7,6},{8,9},{9,8},{10,11... | collective-permute-start | bytes 860168 | tf_op jit(solution)/shard_map/ppermute | solution.py:730
  28.4 4.1 %collective-permute-done.5.refs_3_ = bf16[56,1280]{1,0:T(8,128)(2,1)S(1)} collective-permute-done((bf16[56,1280]{1,0:T(8,128)(2,1)S(1)}, bf16[56,1280]{1,0:T(8,128)(2,1)S(1)}, u32[]{:S(2)}, u32[]{:S(2)}) %collective-permute-start.5) | collective-permute-done | bytes 143392 | tf_op jit(solution)/shard_map/ppermute | solution.py:730
  32.5 1.6 %collective-permute-start.10 = (bf16[56,2560]{1,0:T(8,128)(2,1)S(1)}, bf16[56,2560]{1,0:T(8,128)(2,1)S(1)}, u32[]{:S(2)}, u32[]{:S(2)}) collective-permute-start(bf16[56,2560]{1,0:T(8,128)(2,1)S(1)} %copy-done.4), channel_id=1, source_target_pairs={{0,3},{1,2},{2,1},{3,0},{4,7},{5,6},{6,5},{7,4},{8,11},{9,10},{10,... | collective-permute-start | bytes 860168 | tf_op jit(solution)/shard_map/ppermute | solution.py:730
  34.8 4.1 %collective-permute-done.8.refs_1_ = bf16[56,2560]{1,0:T(8,128)(2,1)S(1)} collective-permute-done((bf16[56,2560]{1,0:T(8,128)(2,1)}, bf16[56,2560]{1,0:T(8,128)(2,1)S(1)}, u32[]{:S(2)}, u32[]{:S(2)}) %collective-permute-start.8) | collective-permute-done | bytes 286752 | tf_op jit(solution)/shard_map/ppermute | solution.py:730
  38.9 3.4 %collective-permute-done.10.refs_3_ = bf16[56,2560]{1,0:T(8,128)(2,1)S(1)} collective-permute-done((bf16[56,2560]{1,0:T(8,128)(2,1)S(1)}, bf16[56,2560]{1,0:T(8,128)(2,1)S(1)}, u32[]{:S(2)}, u32[]{:S(2)}) %collective-permute-start.10) | collective-permute-done | bytes 286752 | tf_op jit(solution)/shard_map/ppermute | solution.py:730
  43.0 2.1 %collective-permute-start.13 = (bf16[224,1280]{1,0:T(8,128)(2,1)S(1)}, bf16[224,1280]{1,0:T(8,128)(2,1)S(1)}, u32[]{:S(2)}, u32[]{:S(2)}) collective-permute-start(bf16[224,1280]{1,0:T(8,128)(2,1)S(1)} %bitcast.10), channel_id=1, source_target_pairs={{0,4},{4,0},{8,12},{12,8},{1,5},{5,1},{9,13},{13,9},{2,6},{6,2},{1... | collective-permute-start | bytes 1720328 | tf_op jit(solution)/shard_map/ppermute | solution.py:742
  45.5 1.3 %collective-permute-start.11 = (bf16[16,2688]{1,0:T(8,128)(2,1)S(1)}, bf16[16,2688]{1,0:T(8,128)(2,1)S(1)}, u32[]{:S(2)}, u32[]{:S(2)}) collective-permute-start(bf16[16,2688]{1,0:T(8,128)(2,1)S(1)} %get-tuple-element.81), channel_id=1, source_target_pairs={{4,0},{8,4},{12,8},{5,1},{9,5},{13,9},{6,2},{10,6},{14,10},{7,3},{... | collective-permute-start | bytes 258056 | tf_op jit(solution)/shard_map/ppermute | solution.py:745
  46.8 4.6 %collective-permute-start.12 = (bf16[16,2688]{1,0:T(8,128)(2,1)S(1)}, bf16[16,2688]{1,0:T(8,128)(2,1)S(1)}, u32[]{:S(2)}, u32[]{:S(2)}) collective-permute-start(bf16[16,2688]{1,0:T(8,128)(2,1)S(1)} %get-tuple-element.82), channel_id=1, source_target_pairs={{0,4},{4,8},{8,12},{1,5},{5,9},{9,13},{2,6},{6,10},{10,14},{3,7},{... | collective-permute-start | bytes 258056 | tf_op jit(solution)/shard_map/ppermute | solution.py:746
  51.4 6.5 %collective-permute-done.11.kedge = bf16[16,2688]{1,0:T(8,128)(2,1)S(1)} collective-permute-done((bf16[16,2688]{1,0:T(8,128)(2,1)S(1)}, bf16[16,2688]{1,0:T(8,128)(2,1)S(1)}, u32[]{:S(2)}, u32[]{:S(2)}) %collective-permute-start.11) | collective-permute-done | bytes 86048 | tf_op jit(solution)/shard_map/ppermute | solution.py:745
  58.7 11.9 %collective-permute-start.16 = (bf16[224,1280]{1,0:T(8,128)(2,1)S(1)}, bf16[224,1280]{1,0:T(8,128)(2,1)S(1)}, u32[]{:S(2)}, u32[]{:S(2)}) collective-permute-start(bf16[224,1280]{1,0:T(8,128)(2,1)S(1)} %get-tuple-element.93), channel_id=1, source_target_pairs={{0,4},{4,0},{8,12},{12,8},{1,5},{5,1},{9,13},{13,9},{2,6},{6,2},{1... | collective-permute-start | bytes 1720328 | tf_op jit(solution)/shard_map/ppermute | solution.py:751
  70.6 3.5 %near_pairs.1 = (bf16[224,2560]{1,0:T(8,128)(2,1)S(1)}, bf16[224,1280]{1,0:T(8,128)(2,1)S(1)}, bf16[224,1280]{1,0:T(8,128)(2,1)S(1)}, bf16[16,2560]{1,0:T(8,128)(2,1)S(1)}, bf16[16,1280]{1,0:T(8,128)(2,1)S(1)}) custom-call(bf16[224,1408]{1,0:T(8,128)(2,1)S(1)} %bitcast.9, bf16[224,1280]{1,0:T(8,128)(2,1)S(1)} %bitcast.13, bf16[224,2560]{1,0:T(8,128)(2,1)S(1)} %bitcast.15, ...), custom_call_target="tpu_custom_call" | custom-call | flops 642252800 | bytes 4587520 | tf_op jit(solution)/shard_map/near_pairs/pallas_call | solution.py:524
  74.1 1.9 %collective-permute-start.17 = (bf16[16,2560]{1,0:T(8,128)(2,1)S(1)}, bf16[16,2560]{1,0:T(8,128)(2,1)S(1)}, u32[]{:S(2)}, u32[]{:S(2)}) collective-permute-start(bf16[16,2560]{1,0:T(8,128)(2,1)S(1)} %get-tuple-element.94), channel_id=1, source_target_pairs={{0,4},{4,8},{8,12},{1,5},{5,9},{9,13},{2,6},{6,10},{10,14},{3,7},{... | collective-permute-start | bytes 245768 | tf_op jit(solution)/shard_map/ppermute | solution.py:752
  76.1 1.3 %collective-permute-start.18 = (bf16[16,1280]{1,0:T(8,128)(2,1)S(1)}, bf16[16,1280]{1,0:T(8,128)(2,1)S(1)}, u32[]{:S(2)}, u32[]{:S(2)}) collective-permute-start(bf16[16,1280]{1,0:T(8,128)(2,1)S(1)} %get-tuple-element.95), channel_id=1, source_target_pairs={{4,0},{8,4},{12,8},{5,1},{9,5},{13,9},{6,2},{10,6},{14,10},{7,3},{... | collective-permute-start | bytes 122888 | tf_op jit(solution)/shard_map/ppermute | solution.py:753
  77.4 5.0 %collective-permute-done.18.dq = bf16[16,1280]{1,0:T(8,128)(2,1)S(1)} collective-permute-done((bf16[16,1280]{1,0:T(8,128)(2,1)S(1)}, bf16[16,1280]{1,0:T(8,128)(2,1)S(1)}, u32[]{:S(2)}, u32[]{:S(2)}) %collective-permute-start.18) | collective-permute-done | bytes 40992 | tf_op jit(solution)/shard_map/ppermute | solution.py:753
  82.9 2.5 %collective-permute-start.20 = (bf16[224,1280]{1,0:T(8,128)(2,1)S(1)}, bf16[224,1280]{1,0:T(8,128)(2,1)S(1)}, u32[]{:S(2)}, u32[]{:S(2)}) collective-permute-start(bf16[224,1280]{1,0:T(8,128)(2,1)S(1)} %add_convert_fusion), channel_id=1, source_target_pairs={{0,4},{4,0},{8,12},{12,8},{1,5},{5,1},{9,13},{13,9},{2,6},{6,2},{1... | collective-permute-start | bytes 1720328 | tf_op jit(solution)/shard_map/ppermute | solution.py:756
  87.0 1.5 %collective-permute-start.25 = (bf16[56,2560]{1,0:T(8,128)(2,1)S(1)}, bf16[56,2560]{1,0:T(8,128)(2,1)S(1)}, u32[]{:S(2)}, u32[]{:S(2)}) collective-permute-start(bf16[56,2560]{1,0:T(8,128)(2,1)S(1)} %get-tuple-element.112), channel_id=1, source_target_pairs={{0,2},{1,3},{2,0},{3,1},{4,6},{5,7},{6,4},{7,5},{8,10},{9,11},{10,... | collective-permute-start | bytes 860168 | tf_op jit(solution)/shard_map/ppermute | solution.py:730
  88.6 2.0 %collective-permute-start.26 = (bf16[56,2560]{1,0:T(8,128)(2,1)S(1)}, bf16[56,2560]{1,0:T(8,128)(2,1)S(1)}, u32[]{:S(2)}, u32[]{:S(2)}) collective-permute-start(bf16[56,2560]{1,0:T(8,128)(2,1)S(1)} %get-tuple-element.113), channel_id=1, source_target_pairs={{0,3},{1,2},{2,1},{3,0},{4,7},{5,6},{6,5},{7,4},{8,11},{9,10},{10,... | collective-permute-start | bytes 860168 | tf_op jit(solution)/shard_map/ppermute | solution.py:730
  90.5 3.2 %collective-permute-done.20.out2 = bf16[224,1280]{1,0:T(8,128)(2,1)S(1)} collective-permute-done((bf16[224,1280]{1,0:T(8,128)(2,1)S(1)}, bf16[224,1280]{1,0:T(8,128)(2,1)S(1)}, u32[]{:S(2)}, u32[]{:S(2)}) %collective-permute-start.20) | collective-permute-done | bytes 573472 | tf_op jit(solution)/shard_map/ppermute | solution.py:756
  94.8 1.5 %collective-permute-start.22 = (bf16[56,1280]{1,0:T(8,128)(2,1)S(1)}, bf16[56,1280]{1,0:T(8,128)(2,1)S(1)}, u32[]{:S(2)}, u32[]{:S(2)}) collective-permute-start(bf16[56,1280]{1,0:T(8,128)(2,1)S(1)} %get-tuple-element.108), channel_id=1, source_target_pairs={{0,2},{1,3},{2,0},{3,1},{4,6},{5,7},{6,4},{7,5},{8,10},{9,11},{10,... | collective-permute-start | bytes 430088 | tf_op jit(solution)/shard_map/ppermute | solution.py:730
  96.3 2.0 %collective-permute-start.23 = (bf16[56,1280]{1,0:T(8,128)(2,1)S(1)}, bf16[56,1280]{1,0:T(8,128)(2,1)S(1)}, u32[]{:S(2)}, u32[]{:S(2)}) collective-permute-start(bf16[56,1280]{1,0:T(8,128)(2,1)S(1)} %get-tuple-element.109), channel_id=1, source_target_pairs={{0,3},{1,2},{2,1},{3,0},{4,7},{5,6},{6,5},{7,4},{8,11},{9,10},{10,... | collective-permute-start | bytes 430088 | tf_op jit(solution)/shard_map/ppermute | solution.py:730
  98.3 1.3 %collective-permute-done.25.refs_2_ = bf16[56,2560]{1,0:T(8,128)(2,1)S(1)} collective-permute-done((bf16[56,2560]{1,0:T(8,128)(2,1)S(1)}, bf16[56,2560]{1,0:T(8,128)(2,1)S(1)}, u32[]{:S(2)}, u32[]{:S(2)}) %collective-permute-start.25) | collective-permute-done | bytes 286752 | tf_op jit(solution)/shard_map/ppermute | solution.py:730
  99.6 1.5 %unpack_early.1 = (bf16[56,5120]{1,0:T(8,128)(2,1)}, bf16[56,5120]{1,0:T(8,128)(2,1)}, bf16[56,5120]{1,0:T(8,128)(2,1)}) custom-call(bf16[56,2560]{1,0:T(8,128)(2,1)S(1)} %get-tuple-element.110.refs_0_, bf16[56,2560]{1,0:T(8,128)(2,1)S(1)} %collective-permute-done.24.refs_1_, bf16[56,2560]{1,0:T(8,128)(2,1)S(1)} %collective-permute-done.25.refs_2_, ...), custom_call_target="tpu_custom_call" | custom-call | bytes 2867200 | tf_op jit(solution)/shard_map/unpack_early/pallas_call | solution.py:666
  101.4 1.6 %collective-permute-done.22.refs_2_ = bf16[56,1280]{1,0:T(8,128)(2,1)S(1)} collective-permute-done((bf16[56,1280]{1,0:T(8,128)(2,1)S(1)}, bf16[56,1280]{1,0:T(8,128)(2,1)S(1)}, u32[]{:S(2)}, u32[]{:S(2)}) %collective-permute-start.22) | collective-permute-done | bytes 143392 | tf_op jit(solution)/shard_map/ppermute | solution.py:730
  103.0 1.6 %unpack_late.1 = (bf16[56,5120]{1,0:T(8,128)(2,1)}, bf16[56,5120]{1,0:T(8,128)(2,1)}, bf16[56,5120]{1,0:T(8,128)(2,1)}) custom-call(bf16[56,1280]{1,0:T(8,128)(2,1)S(1)} %get-tuple-element.106.refs_0_, bf16[56,1280]{1,0:T(8,128)(2,1)S(1)} %collective-permute-done.21.refs_1_, ...), custom_call_target="tpu_custom_call", output_to_operand_aliasing={{0}: (4, {}), {1}: (5, {}), {2}: (6, {})} | custom-call | bytes 2293760 | tf_op jit(solution)/shard_map/unpack_late/pallas_call | solution.py:707
  (47 shorter events, 9.2 us)
Async XLA Ops:
  0.6 17.0 %copy-start.3 = (f32[224,10]{0,1:T(8,128)S(1)}, f32[224,10]{0,1:T(8,128)}, u32[]{:S(2)}) copy-start(f32[224,10]{0,1:T(8,128)} %param.12) | copy-start | bytes 26884
  4.6 8.0 %collective-permute-start = (bf16[56,1408]{1,0:T(8,128)(2,1)}, bf16[56,1408]{1,0:T(8,128)(2,1)S(1)}, u32[]{:S(2)}, u32[]{:S(2)}) collective-permute-start(bf16[56,1408]{1,0:T(8,128)(2,1)} %get-tuple-element.61), channel_id=1, source_target_pairs={{0,1},{1,0},{2,3},{3,2},{4,5},{5,4},{6,7},{7,6},{8,9},{9,8},{10,11... | collective-permute-start | bytes 473096 | tf_op jit(solution)/shard_map/ppermute | solution.py:730
  7.6 10.1 %collective-permute-start.1 = (bf16[56,1408]{1,0:T(8,128)(2,1)}, bf16[56,1408]{1,0:T(8,128)(2,1)S(1)}, u32[]{:S(2)}, u32[]{:S(2)}) collective-permute-start(bf16[56,1408]{1,0:T(8,128)(2,1)} %get-tuple-element.62), channel_id=1, source_target_pairs={{0,2},{1,3},{2,0},{3,1},{4,6},{5,7},{6,4},{7,5},{8,10},{9,11},{10,... | collective-permute-start | bytes 473096 | tf_op jit(solution)/shard_map/ppermute | solution.py:730
  9.1 8.5 %collective-permute-start.2 = (bf16[56,1408]{1,0:T(8,128)(2,1)}, bf16[56,1408]{1,0:T(8,128)(2,1)S(1)}, u32[]{:S(2)}, u32[]{:S(2)}) collective-permute-start(bf16[56,1408]{1,0:T(8,128)(2,1)} %get-tuple-element.63), channel_id=1, source_target_pairs={{0,3},{1,2},{2,1},{3,0},{4,7},{5,6},{6,5},{7,4},{8,11},{9,10},{10,... | collective-permute-start | bytes 473096 | tf_op jit(solution)/shard_map/ppermute | solution.py:730
  9.1 10.6 %collective-permute-start.3 = (bf16[56,1280]{1,0:T(8,128)(2,1)}, bf16[56,1280]{1,0:T(8,128)(2,1)S(1)}, u32[]{:S(2)}, u32[]{:S(2)}) collective-permute-start(bf16[56,1280]{1,0:T(8,128)(2,1)} %get-tuple-element.64), channel_id=1, source_target_pairs={{0,1},{1,0},{2,3},{3,2},{4,5},{5,4},{6,7},{7,6},{8,9},{9,8},{10,11... | collective-permute-start | bytes 430088 | tf_op jit(solution)/shard_map/ppermute | solution.py:730
  11.0 8.7 %collective-permute-start.4 = (bf16[56,1280]{1,0:T(8,128)(2,1)}, bf16[56,1280]{1,0:T(8,128)(2,1)S(1)}, u32[]{:S(2)}, u32[]{:S(2)}) collective-permute-start(bf16[56,1280]{1,0:T(8,128)(2,1)} %get-tuple-element.65), channel_id=1, source_target_pairs={{0,2},{1,3},{2,0},{3,1},{4,6},{5,7},{6,4},{7,5},{8,10},{9,11},{10,... | collective-permute-start | bytes 430088 | tf_op jit(solution)/shard_map/ppermute | solution.py:730
  18.5 9.7 %copy-start.5 = (bf16[56,2560]{1,0:T(8,128)(2,1)S(1)}, bf16[56,2560]{1,0:T(8,128)(2,1)}, u32[]{:S(2)}) copy-start(bf16[56,2560]{1,0:T(8,128)(2,1)} %get-tuple-element.73) | copy-start | bytes 860164
  18.5 13.9 %copy-start.4 = (bf16[56,2560]{1,0:T(8,128)(2,1)S(1)}, bf16[56,2560]{1,0:T(8,128)(2,1)}, u32[]{:S(2)}) copy-start(bf16[56,2560]{1,0:T(8,128)(2,1)} %get-tuple-element.74) | copy-start | bytes 860164
  18.5 15.5 %copy-start.2 = (bf16[56,1280]{1,0:T(8,128)(2,1)S(1)}, bf16[56,1280]{1,0:T(8,128)(2,1)}, u32[]{:S(2)}) copy-start(bf16[56,1280]{1,0:T(8,128)(2,1)} %get-tuple-element.67.refs_0_) | copy-start | bytes 430084
  18.5 26.6 %copy-start = (bf16[56,2560]{1,0:T(8,128)(2,1)S(1)}, bf16[56,2560]{1,0:T(8,128)(2,1)}, u32[]{:S(2)}) copy-start(bf16[56,2560]{1,0:T(8,128)(2,1)} %get-tuple-element.76.refs_0_) | copy-start | bytes 860164
  19.7 22.6 %collective-permute-start.7 = (bf16[224,1408]{1,0:T(8,128)(2,1)S(1)}, bf16[224,1408]{1,0:T(8,128)(2,1)S(1)}, u32[]{:S(2)}, u32[]{:S(2)}) collective-permute-start(bf16[224,1408]{1,0:T(8,128)(2,1)S(1)} %bitcast.5), channel_id=1, source_target_pairs={{4,8},{8,4},{5,9},{9,5},{6,10},{10,6},{7,11},{11,7},{20,24},{24,20... | collective-permute-start | bytes 1892360 | tf_op jit(solution)/shard_map/ppermute | solution.py:738
  20.4 21.9 %collective-permute-start.6 = (bf16[224,1408]{1,0:T(8,128)(2,1)S(1)}, bf16[224,1408]{1,0:T(8,128)(2,1)S(1)}, u32[]{:S(2)}, u32[]{:S(2)}) collective-permute-start(bf16[224,1408]{1,0:T(8,128)(2,1)S(1)} %bitcast.6), channel_id=1, source_target_pairs={{0,4},{4,0},{8,12},{12,8},{1,5},{5,1},{9,13},{13,9},{2,6},{6,2},{1... | collective-permute-start | bytes 1892360 | tf_op jit(solution)/shard_map/ppermute | solution.py:737
  24.9 7.6 %collective-permute-start.5 = (bf16[56,1280]{1,0:T(8,128)(2,1)S(1)}, bf16[56,1280]{1,0:T(8,128)(2,1)S(1)}, u32[]{:S(2)}, u32[]{:S(2)}) collective-permute-start(bf16[56,1280]{1,0:T(8,128)(2,1)S(1)} %copy-done.6), channel_id=1, source_target_pairs={{0,3},{1,2},{2,1},{3,0},{4,7},{5,6},{6,5},{7,4},{8,11},{9,10},{10,... | collective-permute-start | bytes 430088 | tf_op jit(solution)/shard_map/ppermute | solution.py:730
  26.4 12.5 %collective-permute-start.8 = (bf16[56,2560]{1,0:T(8,128)(2,1)}, bf16[56,2560]{1,0:T(8,128)(2,1)S(1)}, u32[]{:S(2)}, u32[]{:S(2)}) collective-permute-start(bf16[56,2560]{1,0:T(8,128)(2,1)} %get-tuple-element.72), channel_id=1, source_target_pairs={{0,1},{1,0},{2,3},{3,2},{4,5},{5,4},{6,7},{7,6},{8,9},{9,8},{10,11... | collective-permute-start | bytes 860168 | tf_op jit(solution)/shard_map/ppermute | solution.py:730
  28.2 10.7 %collective-permute-start.9 = (bf16[56,2560]{1,0:T(8,128)(2,1)S(1)}, bf16[56,2560]{1,0:T(8,128)(2,1)S(1)}, u32[]{:S(2)}, u32[]{:S(2)}) collective-permute-start(bf16[56,2560]{1,0:T(8,128)(2,1)S(1)} %copy-done.5), channel_id=1, source_target_pairs={{0,2},{1,3},{2,0},{3,1},{4,6},{5,7},{6,4},{7,5},{8,10},{9,11},{10,... | collective-permute-start | bytes 860168 | tf_op jit(solution)/shard_map/ppermute | solution.py:730
  32.5 9.9 %collective-permute-start.10 = (bf16[56,2560]{1,0:T(8,128)(2,1)S(1)}, bf16[56,2560]{1,0:T(8,128)(2,1)S(1)}, u32[]{:S(2)}, u32[]{:S(2)}) collective-permute-start(bf16[56,2560]{1,0:T(8,128)(2,1)S(1)} %copy-done.4), channel_id=1, source_target_pairs={{0,3},{1,2},{2,1},{3,0},{4,7},{5,6},{6,5},{7,4},{8,11},{9,10},{10,... | collective-permute-start | bytes 860168 | tf_op jit(solution)/shard_map/ppermute | solution.py:730
  42.3 15.5 %collective-permute-start.14 = (bf16[224,1408]{1,0:T(8,128)(2,1)S(1)}, bf16[224,1408]{1,0:T(8,128)(2,1)S(1)}, u32[]{:S(2)}, u32[]{:S(2)}) collective-permute-start(bf16[224,1408]{1,0:T(8,128)(2,1)S(1)} %collective-permute-done.6.r1), channel_id=1, source_target_pairs={{4,8},{8,4},{5,9},{9,5},{6,10},{10,6},{7,11},{11,7},{20,24},{24,20... | collective-permute-start | bytes 1892360 | tf_op jit(solution)/shard_map/ppermute | solution.py:743
  43.0 14.8 %collective-permute-start.13 = (bf16[224,1280]{1,0:T(8,128)(2,1)S(1)}, bf16[224,1280]{1,0:T(8,128)(2,1)S(1)}, u32[]{:S(2)}, u32[]{:S(2)}) collective-permute-start(bf16[224,1280]{1,0:T(8,128)(2,1)S(1)} %bitcast.10), channel_id=1, source_target_pairs={{0,4},{4,0},{8,12},{12,8},{1,5},{5,1},{9,13},{13,9},{2,6},{6,2},{1... | collective-permute-start | bytes 1720328 | tf_op jit(solution)/shard_map/ppermute | solution.py:742
  45.5 12.3 %collective-permute-start.11 = (bf16[16,2688]{1,0:T(8,128)(2,1)S(1)}, bf16[16,2688]{1,0:T(8,128)(2,1)S(1)}, u32[]{:S(2)}, u32[]{:S(2)}) collective-permute-start(bf16[16,2688]{1,0:T(8,128)(2,1)S(1)} %get-tuple-element.81), channel_id=1, source_target_pairs={{4,0},{8,4},{12,8},{5,1},{9,5},{13,9},{6,2},{10,6},{14,10},{7,3},{... | collective-permute-start | bytes 258056 | tf_op jit(solution)/shard_map/ppermute | solution.py:745
  46.8 11.0 %collective-permute-start.12 = (bf16[16,2688]{1,0:T(8,128)(2,1)S(1)}, bf16[16,2688]{1,0:T(8,128)(2,1)S(1)}, u32[]{:S(2)}, u32[]{:S(2)}) collective-permute-start(bf16[16,2688]{1,0:T(8,128)(2,1)S(1)} %get-tuple-element.82), channel_id=1, source_target_pairs={{0,4},{4,8},{8,12},{1,5},{5,9},{9,13},{2,6},{6,10},{10,14},{3,7},{... | collective-permute-start | bytes 258056 | tf_op jit(solution)/shard_map/ppermute | solution.py:746
  58.0 24.7 %collective-permute-start.15 = (bf16[224,1280]{1,0:T(8,128)(2,1)S(1)}, bf16[224,1280]{1,0:T(8,128)(2,1)S(1)}, u32[]{:S(2)}, u32[]{:S(2)}) collective-permute-start(bf16[224,1280]{1,0:T(8,128)(2,1)S(1)} %get-tuple-element.91), channel_id=1, source_target_pairs={{4,8},{8,4},{5,9},{9,5},{6,10},{10,6},{7,11},{11,7},{20,24},{24,20... | collective-permute-start | bytes 1720328 | tf_op jit(solution)/shard_map/ppermute | solution.py:750
  58.7 24.0 %collective-permute-start.16 = (bf16[224,1280]{1,0:T(8,128)(2,1)S(1)}, bf16[224,1280]{1,0:T(8,128)(2,1)S(1)}, u32[]{:S(2)}, u32[]{:S(2)}) collective-permute-start(bf16[224,1280]{1,0:T(8,128)(2,1)S(1)} %get-tuple-element.93), channel_id=1, source_target_pairs={{0,4},{4,0},{8,12},{12,8},{1,5},{5,1},{9,13},{13,9},{2,6},{6,2},{1... | collective-permute-start | bytes 1720328 | tf_op jit(solution)/shard_map/ppermute | solution.py:751
  74.1 8.6 %collective-permute-start.17 = (bf16[16,2560]{1,0:T(8,128)(2,1)S(1)}, bf16[16,2560]{1,0:T(8,128)(2,1)S(1)}, u32[]{:S(2)}, u32[]{:S(2)}) collective-permute-start(bf16[16,2560]{1,0:T(8,128)(2,1)S(1)} %get-tuple-element.94), channel_id=1, source_target_pairs={{0,4},{4,8},{8,12},{1,5},{5,9},{9,13},{2,6},{6,10},{10,14},{3,7},{... | collective-permute-start | bytes 245768 | tf_op jit(solution)/shard_map/ppermute | solution.py:752
  76.1 6.3 %collective-permute-start.18 = (bf16[16,1280]{1,0:T(8,128)(2,1)S(1)}, bf16[16,1280]{1,0:T(8,128)(2,1)S(1)}, u32[]{:S(2)}, u32[]{:S(2)}) collective-permute-start(bf16[16,1280]{1,0:T(8,128)(2,1)S(1)} %get-tuple-element.95), channel_id=1, source_target_pairs={{4,0},{8,4},{12,8},{5,1},{9,5},{13,9},{6,2},{10,6},{14,10},{7,3},{... | collective-permute-start | bytes 122888 | tf_op jit(solution)/shard_map/ppermute | solution.py:753
  82.9 10.8 %collective-permute-start.20 = (bf16[224,1280]{1,0:T(8,128)(2,1)S(1)}, bf16[224,1280]{1,0:T(8,128)(2,1)S(1)}, u32[]{:S(2)}, u32[]{:S(2)}) collective-permute-start(bf16[224,1280]{1,0:T(8,128)(2,1)S(1)} %add_convert_fusion), channel_id=1, source_target_pairs={{0,4},{4,0},{8,12},{12,8},{1,5},{5,1},{9,13},{13,9},{2,6},{6,2},{1... | collective-permute-start | bytes 1720328 | tf_op jit(solution)/shard_map/ppermute | solution.py:756
  85.4 8.3 %collective-permute-start.19 = (bf16[224,1280]{1,0:T(8,128)(2,1)S(1)}, bf16[224,1280]{1,0:T(8,128)(2,1)S(1)}, u32[]{:S(2)}, u32[]{:S(2)}) collective-permute-start(bf16[224,1280]{1,0:T(8,128)(2,1)S(1)} %get-tuple-element.96), channel_id=1, source_target_pairs={{4,8},{8,4},{5,9},{9,5},{6,10},{10,6},{7,11},{11,7},{20,24},{24,20... | collective-permute-start | bytes 1720328 | tf_op jit(solution)/shard_map/ppermute | solution.py:755
  87.0 9.4 %collective-permute-start.24 = (bf16[56,2560]{1,0:T(8,128)(2,1)S(1)}, bf16[56,2560]{1,0:T(8,128)(2,1)S(1)}, u32[]{:S(2)}, u32[]{:S(2)}) collective-permute-start(bf16[56,2560]{1,0:T(8,128)(2,1)S(1)} %get-tuple-element.111), channel_id=1, source_target_pairs={{0,1},{1,0},{2,3},{3,2},{4,5},{5,4},{6,7},{7,6},{8,9},{9,8},{10,11... | collective-permute-start | bytes 860168 | tf_op jit(solution)/shard_map/ppermute | solution.py:730
  87.0 12.5 %collective-permute-start.25 = (bf16[56,2560]{1,0:T(8,128)(2,1)S(1)}, bf16[56,2560]{1,0:T(8,128)(2,1)S(1)}, u32[]{:S(2)}, u32[]{:S(2)}) collective-permute-start(bf16[56,2560]{1,0:T(8,128)(2,1)S(1)} %get-tuple-element.112), channel_id=1, source_target_pairs={{0,2},{1,3},{2,0},{3,1},{4,6},{5,7},{6,4},{7,5},{8,10},{9,11},{10,... | collective-permute-start | bytes 860168 | tf_op jit(solution)/shard_map/ppermute | solution.py:730
  88.6 11.0 %collective-permute-start.26 = (bf16[56,2560]{1,0:T(8,128)(2,1)S(1)}, bf16[56,2560]{1,0:T(8,128)(2,1)S(1)}, u32[]{:S(2)}, u32[]{:S(2)}) collective-permute-start(bf16[56,2560]{1,0:T(8,128)(2,1)S(1)} %get-tuple-element.113), channel_id=1, source_target_pairs={{0,3},{1,2},{2,1},{3,0},{4,7},{5,6},{6,5},{7,4},{8,11},{9,10},{10,... | collective-permute-start | bytes 860168 | tf_op jit(solution)/shard_map/ppermute | solution.py:730
  94.7 6.7 %collective-permute-start.21 = (bf16[56,1280]{1,0:T(8,128)(2,1)S(1)}, bf16[56,1280]{1,0:T(8,128)(2,1)S(1)}, u32[]{:S(2)}, u32[]{:S(2)}) collective-permute-start(bf16[56,1280]{1,0:T(8,128)(2,1)S(1)} %get-tuple-element.107), channel_id=1, source_target_pairs={{0,1},{1,0},{2,3},{3,2},{4,5},{5,4},{6,7},{7,6},{8,9},{9,8},{10,11... | collective-permute-start | bytes 430088 | tf_op jit(solution)/shard_map/ppermute | solution.py:730
  94.8 8.1 %collective-permute-start.22 = (bf16[56,1280]{1,0:T(8,128)(2,1)S(1)}, bf16[56,1280]{1,0:T(8,128)(2,1)S(1)}, u32[]{:S(2)}, u32[]{:S(2)}) collective-permute-start(bf16[56,1280]{1,0:T(8,128)(2,1)S(1)} %get-tuple-element.108), channel_id=1, source_target_pairs={{0,2},{1,3},{2,0},{3,1},{4,6},{5,7},{6,4},{7,5},{8,10},{9,11},{10,... | collective-permute-start | bytes 430088 | tf_op jit(solution)/shard_map/ppermute | solution.py:730
  96.3 6.6 %collective-permute-start.23 = (bf16[56,1280]{1,0:T(8,128)(2,1)S(1)}, bf16[56,1280]{1,0:T(8,128)(2,1)S(1)}, u32[]{:S(2)}, u32[]{:S(2)}) collective-permute-start(bf16[56,1280]{1,0:T(8,128)(2,1)S(1)} %get-tuple-element.109), channel_id=1, source_target_pairs={{0,3},{1,2},{2,1},{3,0},{4,7},{5,6},{6,5},{7,4},{8,11},{9,10},{10,... | collective-permute-start | bytes 430088 | tf_op jit(solution)/shard_map/ppermute | solution.py:730
  (2 other events, 7.3 us)

commit v7 on v6

--- a/solution.py
+++ b/solution.py
@@ -18,8 +18,6 @@
 
 PAIRS = ((0, 1), (1, 0), (2, 3), (3, 2))
 SWAP = ((1, 2), (2, 1))
-DOWN = ((1, 0), (2, 1), (3, 2))
-UP = ((0, 1), (1, 2), (2, 3))
 
 
 def tile_terms(query_blk, grad_blk, norm_blk, delta_blk, query_ids, key_blk, value_blk, key_ids):
@@ -321,7 +319,7 @@
     half = width // 2
 
     def body(*refs):
-        y1, y2, w, kedge, qedge, sems = refs[groups:]
+        y1, y2, w, pairs, swap, kedge, qedge, sems = refs[groups:]
         here, low = lax.axis_index("head"), lax.axis_index("ctx") < 2
         top, bottom, tail = pl.ds(0, EDGE), pl.ds(rows - EDGE, EDGE), pl.ds(width, LANES)
         whole, end = pl.ds(0, 2 * width), pl.ds(2 * width, LANES)
@@ -354,54 +352,117 @@
             kedge[:, whole] = w[0, :EDGE, :]
 
         wait_all(made)
+        even = lax.axis_index("ctx") % 2 == 0
+        pairs[...] = jnp.where(even, qedge[...], kedge[...])
+        swap[...] = jnp.where(even, kedge[...], qedge[...])
 
     edge = jax.ShapeDtypeStruct((EDGE, 2 * width + LANES), BF16)
-    w, key_edge, query_edge = pl.pallas_call(
+    w, for_pairs, for_swap = pl.pallas_call(
         body,
         out_shape=[jax.ShapeDtypeStruct((groups, share, 2 * width), BF16), edge, edge],
         in_specs=anywhere(groups + 2),
         out_specs=[pl.BlockSpec(memory_space=pltpu.VMEM)] * 3,
-        scratch_shapes=[pltpu.SemaphoreType.DMA((6 + groups,))],
+        scratch_shapes=[pltpu.VMEM(edge.shape, BF16)] * 2 + [pltpu.SemaphoreType.DMA((6 + groups,))],
         compiler_params=pltpu.CompilerParams(vmem_limit_bytes=VMEM_SMALL),
         cost_estimate=pl.CostEstimate(flops=0, bytes_accessed=8 * rows * width, transcendentals=0),
         name="join_last",
     )(*parts, y1, y2)
-    return w.reshape(rows, 2 * width), key_edge, query_edge
+    return w.reshape(rows, 2 * width), for_pairs, for_swap
 
 
 def in_vmem(count):
     return [pl.BlockSpec(memory_space=pltpu.VMEM)] * count
 
 
-def far_pairs(y1, y2, w, r1, r2, s1, s2):
+def both(ref, at, gap):
+    return lambda c: (
+        ref[:, at + c * LANES : at + (c + 1) * LANES],
+        ref[:, at + gap + c * LANES : at + gap + (c + 1) * LANES],
+    )
+
+
+def put(ref, at, value):
+    ref[:, at : at + LANES] = value.astype(BF16)
+
+
+def far_early(y1, y2, w, r1, s1):
     rows, width = y2.shape
     half = width // 2
     count = half // LANES
     heads = 2 * count
 
-    def body(y1, y2, w, r1, r2, s1, s2, swap1, out1, swap2, l1, l2, l3, info):
+    def body(y1, y2, w, r1, s1, pq, pk, lo, l3, info):
         z = lax.axis_index("ctx")
-
-        def both(ref, at=0, gap=half):
-            return lambda c: (
-                ref[:, at + c * LANES : at + (c + 1) * LANES],
-                ref[:, at + gap + c * LANES : at + gap + (c + 1) * LANES],
-            )
-
-        def put(ref, at, value):
-            ref[:, at : at + LANES] = value.astype(BF16)
+        tail = pl.ds(width, LANES)
 
         def scalars(slot, head):
             return info[slot, head : head + 1, :], info[slot, heads + head : heads + head + 1, :]
 
-        def square(query_2, query_3, key_0, key_1, c, head):
-            keys, values = zip(key_0(c), key_1(c))
-            key, value = jnp.concatenate(keys, axis=0), jnp.concatenate(values, axis=0)
-            first = pair_terms(*query_2(c), key, value, *scalars(0, head))
-            second = pair_terms(*query_3(c), key, value, *scalars(1, head))
-            return first[0], second[0], first[1] + second[1], first[2] + second[2]
-
+        @pl.when(z == 1)
+        def _():
+            info[0] = token_rows(s1[:, tail], heads)
+            info[1] = token_rows(y1[:, tail], heads)
+            for c in range(count):
+                a, b = c * LANES, half + c * LANES
+                made = pair_terms(*both(s1, 0, half)(c), *both(y2, 0, half)(c), *scalars(0, c))
+                own = pair_terms(*both(w, half, width)(c), *both(r1, 0, half)(c), *scalars(1, count + c))
+                for ref, at, value in ((pq, a, made[0]), (pk, a, made[1]), (pk, b, made[2])):
+                    put(ref, at, value)
+                for ref, at, value in ((lo, a, own[0]), (l3, a, own[1]), (l3, b, own[2])):
+                    put(ref, at, value)
+
+        @pl.when(z == 2)
+        def _():
+            info[0] = token_rows(y1[:, tail], heads)
+            info[1] = token_rows(r1[:, tail], heads)
+            for c in range(count):
+                a, b = c * LANES, half + c * LANES
+                made = pair_terms(*both(y2, 0, half)(c), *both(s1, 0, half)(c), *scalars(0, count + c))
+                own = pair_terms(*both(r1, 0, half)(c), *both(w, 0, width)(c), *scalars(1, c))
+                for ref, at, value in ((pq, a, made[0]), (pk, a, made[1]), (pk, b, made[2])):
+                    put(ref, at, value)
+                for ref, at, value in ((l3, a, own[0]), (lo, a, own[1]), (lo, b, own[2])):
+                    put(ref, at, value)
+
+    single = jax.ShapeDtypeStruct((rows, width), BF16)
+    return pl.pallas_call(
+        body,
+        out_shape=[jax.ShapeDtypeStruct((rows, half), BF16), single, single, single],
+        in_specs=in_vmem(5),
+        out_specs=in_vmem(4),
+        scratch_shapes=[pltpu.VMEM((2, 32, rows), F32)],
+        compiler_params=pltpu.CompilerParams(vmem_limit_bytes=VMEM_LIMIT),
+        cost_estimate=pl.CostEstimate(
+            flops=10 * 10 * rows * rows * LANES, bytes_accessed=10 * rows * width, transcendentals=10 * rows * rows
+        ),
+        name="far_early",
+    )(y1, y2, w, r1, s1)
+
+
+def far_pairs(y1, y2, w, r1, r2, s1, s2, pq, pk):
+    rows, width = y2.shape
+    half = width // 2
+    count = half // LANES
+    heads = 2 * count
+
+    def body(y1, y2, w, r1, r2, s1, s2, pq, pk, swap1, out1, swap2, la, l2, info):
+        z = lax.axis_index("ctx")
         tail = pl.ds(width, LANES)
+
+        def scalars(slot, head):
+            return info[slot, head : head + 1, :], info[slot, heads + head : heads + head + 1, :]
+
+        def before(ref, at):
+            return ref[:, at : at + LANES].astype(F32)
+
+        def corner(query_2, query_3, key_0, key_1, c, head):
+            first, other = both(key_0, 0, half)(c), both(key_1, 0, half)(c)
+            key, value = (jnp.concatenate(x, axis=0) for x in zip(first, other))
+            third = pair_terms(*both(query_3, 0, half)(c), key, value, *scalars(1, head))
+            second = pair_terms(*both(query_2, 0, half)(c), *first, *scalars(0, head))
+            key_1_terms = third[1][rows:] + before(pk, c * LANES), third[2][rows:] + before(pk, half + c * LANES)
+            key_0_terms = third[1][:rows] + second[1], third[2][:rows] + second[2]
+            return second[0] + before(pq, c * LANES), third[0], key_0_terms, key_1_terms
 
         @pl.when(z == 1)
         def _():
@@ -409,19 +470,15 @@
                 info[slot] = token_rows(ref[:, tail], heads)
             for c in range(count):
                 a, b = c * LANES, half + c * LANES
-                own = pair_terms(*both(w, 0, width)(c), *both(r2)(c), *scalars(2, c))
-                query_2, query_3, key, value = square(both(s1), both(s2), both(r2), both(y2), c, c)
+                own = pair_terms(*both(w, 0, width)(c), *both(r2, 0, half)(c), *scalars(2, c))
+                query_2, query_3, key_0, key_1 = corner(s1, s2, r2, y2, c, c)
                 put(swap1, a, query_3)
                 put(swap2, a, query_2)
-                put(out1, a, key[:rows] + own[1])
-                put(out1, b, value[:rows] + own[2])
-                put(l2, a, key[rows:])
-                put(l2, b, value[rows:])
-                put(l1, a, own[0])
-                own = pair_terms(*both(w, half, width)(c), *both(r1)(c), *scalars(2, count + c))
-                put(l1, half + a, own[0])
-                put(l3, a, own[1])
-                put(l3, b, own[2])
+                put(out1, a, key_0[0] + own[1])
+                put(out1, b, key_0[1] + own[2])
+                put(l2, a, key_1[0])
+                put(l2, b, key_1[1])
+                put(la, a, own[0])
 
         @pl.when(z == 2)
         def _():
@@ -429,48 +486,51 @@
                 info[slot] = token_rows(ref[:, tail], heads)
             for c in range(count):
                 a, b = c * LANES, half + c * LANES
-                own = pair_terms(*both(r2)(c), *both(w, half, width)(c), *scalars(1, count + c))
-                query_2, query_3, key, value = square(both(y2), both(r2), both(s2), both(s1), c, count + c)
-                put(swap1, a, key[:rows])
-                put(swap1, b, value[:rows])
-                put(swap2, a, key[rows:])
-                put(swap2, b, value[rows:])
+                own = pair_terms(*both(r2, 0, half)(c), *both(w, half, width)(c), *scalars(1, count + c))
+                query_2, query_3, key_0, key_1 = corner(y2, r2, s2, s1, c, count + c)
+                put(swap1, a, key_0[0])
+                put(swap1, b, key_0[1])
+                put(swap2, a, key_1[0])
+                put(swap2, b, key_1[1])
                 put(out1, a, query_3 + own[0])
                 put(l2, a, query_2)
-                put(l1, b, own[1])
-                put(l1, width + b, own[2])
-                own = pair_terms(*both(r1)(c), *both(w, 0, width)(c), *scalars(1, c))
-                put(l1, a, own[1])
-                put(l1, width + a, own[2])
-                put(l3, a, own[0])
+                put(la, a, own[1])
+                put(la, b, own[2])
 
     single = jax.ShapeDtypeStruct((rows, width), BF16)
     return pl.pallas_call(
         body,
-        out_shape=[single, single, single, jax.ShapeDtypeStruct((rows, 2 * width), BF16), single, single],
-        in_specs=in_vmem(7),
-        out_specs=in_vmem(6),
+        out_shape=[single] * 5,
+        in_specs=in_vmem(9),
+        out_specs=in_vmem(5),
         scratch_shapes=[pltpu.VMEM((3, 32, rows), F32)],
         compiler_params=pltpu.CompilerParams(vmem_limit_bytes=VMEM_LIMIT),
         cost_estimate=pl.CostEstimate(
-            flops=30 * 10 * rows * rows * LANES, bytes_accessed=30 * rows * width, transcendentals=30 * rows * rows
+            flops=20 * 10 * rows * rows * LANES, bytes_accessed=30 * rows * width, transcendentals=20 * rows * rows
         ),
         name="far_pairs",
-    )(y1, y2, w, r1, r2, s1, s2)
-
-
-def near_pairs(y1, y2, w, key_edge, query_edge):
+    )(y1, y2, w, r1, r2, s1, s2, pq, pk)
+
+
+def near_pairs(y1, y2, w, from_pair, from_swap):
     rows, width = y2.shape
     half = width // 2
     count = half // LANES
     heads = 2 * count
     total = rows + EDGE
 
-    def body(y1, y2, w, kedge, qedge, dw, dy1, dy2, dkedge, dqedge, info):
+    def body(y1, y2, w, from_pair, from_swap, dw, dy1, dy2, to_pair, to_swap, info):
         z = lax.axis_index("ctx")
-        tail, end = pl.ds(width, LANES), pl.ds(2 * width, LANES)
-        info[...] = token_rows(jnp.concatenate([y1[:, tail], qedge[:, end]], axis=0), heads)
-        key_meta = jnp.concatenate([y1[:, tail], kedge[:, end]], axis=0).astype(F32)
+        even = z % 2 == 0
+
+        def edge_part(at):
+            pair, swap = from_pair[:, at : at + LANES], from_swap[:, at : at + LANES]
+            return jnp.where(even, pair, swap), jnp.where(even, swap, pair)
+
+        tail = pl.ds(width, LANES)
+        key_tail, query_tail = edge_part(2 * width)
+        info[...] = token_rows(jnp.concatenate([y1[:, tail], query_tail], axis=0), heads)
+        key_meta = jnp.concatenate([y1[:, tail], key_tail], axis=0).astype(F32)
         id_lane = lax.broadcasted_iota(jnp.int32, (total, LANES), 1) == 3 * heads
         key_ids = jnp.sum(jnp.where(id_lane, key_meta, 0.0), axis=1, keepdims=True)
         at_key = lax.broadcasted_iota(jnp.int32, (total, total), 0)
@@ -485,18 +545,18 @@
             small, large = c * LANES, half + c * LANES
             wide = w[:, a : a + LANES], w[:, b : b + LANES]
             narrow = payload[:, small : small + LANES], payload[:, large : large + LANES]
-            edge_k, edge_q = (
-                (edge[:, a : a + LANES], edge[:, b : b + LANES]) for edge in (kedge, qedge)
-            )
+            edge_k, edge_q = zip(edge_part(a), edge_part(b))
 
             def terms(queries, keys):
                 query, grad = (jnp.concatenate(x, axis=0) for x in zip(queries, edge_q))
                 key, value = (jnp.concatenate(x, axis=0) for x in zip(keys, edge_k))
                 scalars = info[i * count + c : i * count + c + 1, :], info[heads + i * count + c : heads + i * count + c + 1, :]
                 made = [x.astype(BF16) for x in pair_terms(query, grad, key, value, *scalars, visible)]
-                dqedge[:, a : a + LANES] = made[0][rows:]
-                dkedge[:, a : a + LANES] = made[1][rows:]
-                dkedge[:, b : b + LANES] = made[2][rows:]
+                query_end, key_end, value_end = (x[rows:] for x in made)
+                to_pair[:, a : a + LANES] = jnp.where(even, key_end, query_end)
+                to_swap[:, a : a + LANES] = jnp.where(even, query_end, key_end)
+                to_pair[:, b : b + LANES] = value_end
+                to_swap[:, b : b + LANES] = value_end
                 return [x[:rows] for x in made]
 
             return a, b, small, large, wide, narrow, terms
@@ -528,7 +588,7 @@
             jax.ShapeDtypeStruct((rows, width), BF16),
             jax.ShapeDtypeStruct((rows, width), BF16),
             jax.ShapeDtypeStruct((EDGE, 2 * width), BF16),
-            jax.ShapeDtypeStruct((EDGE, width), BF16),
+            jax.ShapeDtypeStruct((EDGE, 2 * width), BF16),
         ],
         in_specs=in_vmem(5),
         out_specs=in_vmem(5),
@@ -538,23 +598,26 @@
             flops=10 * 10 * rows * rows * LANES, bytes_accessed=16 * rows * width, transcendentals=10 * rows * rows
         ),
         name="near_pairs",
-    )(y1, y2, w, key_edge, query_edge)
-
-
-def finish_first(dw, l1, dy2, l2, out1, dkedge, dqedge, groups):
+    )(y1, y2, w, from_pair, from_swap)
+
+
+def finish_first(dw, la, lo, dy2, l2, out1, from_pair, from_swap, groups):
     rows, width = dy2.shape
     half = width // 2
     share = rows // groups
 
-    def body(dw, l1, dy2, l2, out1, dk, dq, *refs):
+    def body(dw, la, lo, dy2, l2, out1, dp, ds, *refs):
         outs, v, e, sems = refs[:groups], *refs[groups:]
         here = lax.axis_index("head")
         z = lax.axis_index("ctx")
         low, middle = z < 2, (z == 1) | (z == 2)
-        after_first, before_last = z > 0, z < 3
-
-        def own(cols):
-            return dw[:, cols].astype(F32) + jnp.where(middle, l1[:, cols].astype(F32), 0.0)
+        after_first, before_last, odd = z > 0, z < 3, z % 2 == 1
+
+        def own(i):
+            at, there = pl.ds(i * half, half), pl.ds(i // 2 * half, half)
+            active, other = la[:, there].astype(F32), lo[:, there].astype(F32)
+            one, two = (active, other) if i % 2 == 0 else (other, active)
+            return dw[:, at].astype(F32) + jnp.where(middle, jnp.where(z == 1, one, two), 0.0)
 
         def second(cols):
             return dy2[:, cols].astype(F32) + jnp.where(middle, l2[:, cols], out1[:, cols]).astype(F32)
@@ -566,19 +629,19 @@
                 dst[h, :, cols] = total[h * share : (h + 1) * share].astype(BF16)
 
         def key_edge(cols):
-            return jnp.where(after_first, dk[:, cols].astype(F32), 0.0)
+            return jnp.where(after_first, jnp.where(odd, dp[:, cols], ds[:, cols]).astype(F32), 0.0)
 
         def query_edge(cols):
-            return jnp.where(before_last, dq[:, cols].astype(F32), 0.0)
+            return jnp.where(before_last, jnp.where(odd, ds[:, cols], dp[:, cols]).astype(F32), 0.0)
 
         a, b = pl.ds(0, half), pl.ds(half, half)
         c, d = pl.ds(width, half), pl.ds(width + half, half)
-        for cols in (a, b):
-            put(e, cols, own(cols), jnp.where(low, 0.0, key_edge(cols)), jnp.where(low, query_edge(cols), 0.0))
+        for i, cols in enumerate((a, b)):
+            put(e, cols, own(i), jnp.where(low, 0.0, key_edge(cols)), jnp.where(low, query_edge(cols), 0.0))
         put(e, c, second(a), jnp.where(low, key_edge(a), 0.0), jnp.where(low, 0.0, query_edge(b)))
-        put(e, d, jnp.where(low, second(b), own(c)), key_edge(c))
+        put(e, d, jnp.where(low, second(b), own(2)), key_edge(c))
         made = run_copies([(e.at[here ^ m], outs[m]) for m in range(groups)], sems)
-        left_over = own(d)
+        left_over = own(3)
         left_over = jnp.concatenate([left_over[:EDGE] + key_edge(d), left_over[EDGE:]], axis=0)
         v[...] = left_over.astype(BF16)
         wait_all(made)
@@ -586,21 +649,21 @@
     return pl.pallas_call(
         body,
         out_shape=[jax.ShapeDtypeStruct((share, 2 * width), BF16)] * groups + [jax.ShapeDtypeStruct((rows, half), BF16)],
-        in_specs=[pl.BlockSpec(memory_space=pltpu.VMEM)] * 7,
+        in_specs=in_vmem(8),
         out_specs=anywhere(groups) + [pl.BlockSpec(memory_space=pltpu.VMEM)],
         scratch_shapes=[pltpu.VMEM((groups, share, 2 * width), BF16), pltpu.SemaphoreType.DMA((groups,))],
         compiler_params=pltpu.CompilerParams(vmem_limit_bytes=VMEM_SMALL),
         cost_estimate=pl.CostEstimate(flops=0, bytes_accessed=16 * rows * width, transcendentals=0),
         name="finish_first",
-    )(dw, l1, dy2, l2, out1, dkedge, dqedge)
-
-
-def finish_second(dy1, swap2, out2, v, dkedge, dqedge, groups):
+    )(dw, la, lo, dy2, l2, out1, from_pair, from_swap)
+
+
+def finish_second(dy1, swap2, out2, v, from_pair, from_swap, groups):
     rows, width = dy1.shape
     half = width // 2
     share = rows // groups
 
-    def body(dy1, swap2, out2, v, dk, dq, *refs):
+    def body(dy1, swap2, out2, v, dp, ds, *refs):
         outs, e, sems = refs[:groups], *refs[groups:]
         here, z = lax.axis_index("head"), lax.axis_index("ctx")
         low, middle = z < 2, (z == 1) | (z == 2)
@@ -616,11 +679,11 @@
             return dy1[:, cols].astype(F32) + jnp.where(middle, swap2[:, cols], out2[:, cols]).astype(F32)
 
         left = total(a)
-        first = left[:EDGE] + jnp.where(z == 1, dk[:, b].astype(F32), 0.0)
-        last = left[rows - EDGE :] + jnp.where(z == 2, dq[:, a].astype(F32), 0.0)
+        first = left[:EDGE] + jnp.where(z == 1, dp[:, b].astype(F32), 0.0)
+        last = left[rows - EDGE :] + jnp.where(z == 2, dp[:, a].astype(F32), 0.0)
         put(a, jnp.concatenate([first, left[EDGE : rows - EDGE], last], axis=0))
         right = total(b)
-        right = jnp.concatenate([right[:EDGE] + jnp.where(z > 0, dk[:, end].astype(F32), 0.0), right[EDGE:]], axis=0)
+        right = jnp.concatenate([right[:EDGE] + jnp.where(z == 1, dp[:, end].astype(F32), 0.0), right[EDGE:]], axis=0)
         put(b, jnp.where(low, right, v[...].astype(F32)))
         wait_all(run_copies([(e.at[here ^ m], outs[m]) for m in range(groups)], sems))
 
@@ -633,7 +696,7 @@
         compiler_params=pltpu.CompilerParams(vmem_limit_bytes=VMEM_SMALL),
         cost_estimate=pl.CostEstimate(flops=0, bytes_accessed=9 * rows * width, transcendentals=0),
         name="finish_second",
-    )(dy1, swap2, out2, v, dkedge, dqedge)
+    )(dy1, swap2, out2, v, from_pair, from_swap)
 
 
 def unpack_early(parts):
@@ -738,25 +801,26 @@
     s1 = lax.ppermute(y1, "ctx", SWAP)
     x3 = swapped(x3)
     y2 = join(x2)
-    y2, r1, s1, x3 = lax.optimization_barrier((y2, r1, s1, x3))
+    y2, r1, s1, x3[:-1] = lax.optimization_barrier((y2, r1, s1, x3[:-1]))
     r2 = lax.ppermute(y2, "ctx", PAIRS)
     s2 = lax.ppermute(r1, "ctx", SWAP)
-    w, key_edge, query_edge = join_last(x3, y1, y2)
-    key_edge = lax.ppermute(key_edge, "ctx", DOWN)
-    query_edge = lax.ppermute(query_edge, "ctx", UP)
-    w, key_edge, query_edge = lax.optimization_barrier((w, key_edge, query_edge))
-    swap1, out1, swap2, l1, l2, l3 = far_pairs(y1, y2, w, r1, r2, s1, s2)
-    dw, dy1, dy2, dkedge, dqedge = near_pairs(y1, y2, w, after(key_edge, l3), query_edge)
+    w, from_pair, from_swap = join_last(x3, y1, y2)
+    from_pair = lax.ppermute(from_pair, "ctx", PAIRS)
+    from_swap = lax.ppermute(from_swap, "ctx", SWAP)
+    pq, pk, lo, l3 = far_early(y1, y2, w, r1, s1)
+    w, from_pair, from_swap = lax.optimization_barrier((w, from_pair, from_swap))
+    swap1, out1, swap2, la, l2 = far_pairs(y1, y2, w, r1, r2, s1, s2, pq, pk)
+    dw, dy1, dy2, to_pair, to_swap = near_pairs(y1, y2, w, after(from_pair, l2), from_swap)
     swap1 = lax.ppermute(swap1, "ctx", SWAP)
     out1 = lax.ppermute(out1, "ctx", PAIRS)
-    dkedge = lax.ppermute(dkedge, "ctx", UP)
-    dqedge = lax.ppermute(dqedge, "ctx", DOWN)
-    swap1, swap2, out1, dkedge, dqedge = lax.optimization_barrier((swap1, swap2, out1, dkedge, dqedge))
+    to_pair = lax.ppermute(to_pair, "ctx", PAIRS)
+    to_swap = lax.ppermute(to_swap, "ctx", SWAP)
+    swap1, swap2, out1, to_pair, to_swap = lax.optimization_barrier((swap1, swap2, out1, to_pair, to_swap))
     swap2 = lax.ppermute(swap2, "ctx", SWAP)
     out2 = lax.ppermute((swap1.astype(F32) + l3.astype(F32)).astype(BF16), "ctx", PAIRS)
-    *early, kept = finish_first(dw, l1, dy2, l2, out1, dkedge, dqedge, groups)
+    *early, kept = finish_first(dw, la, lo, dy2, l2, out1, to_pair, to_swap, groups)
     early = swapped(early)
-    late = swapped(finish_second(dy1, swap2, out2, kept, dkedge, dqedge, groups))
+    late = swapped(finish_second(dy1, swap2, out2, kept, to_pair, to_swap, groups))
     return tuple(unpack_late(late, *unpack_early(early)))
 
 

time: 105 us -> 102 us (0.971)
  starting transfers between devices: 52.9 us -> 45.2 us
  waiting for transfers between devices: 34.9 us -> 38.8 us
    ppermute x4, starting transfers between devices: 9.07 us -> 1.55 us  [the longest x1 0.67 us: local_split(): to_swap = lax.ppermute(to_swap, 'ctx', SWAP)]
    ppermute x15, waiting for transfers between devices: 19.9 us -> 22.4 us  [swapped(): lax.ppermute(parts[m], 'head', [(i, i ^ m) for i in range(groups)])]
    ppermute x1, starting transfers between devices: 2.09 us -> 3.46 us  [local_split(): r2 = lax.ppermute(y2, 'ctx', PAIRS)]
    ppermute x1, waiting for transfers between devices: 0.01 us -> 1.28 us  [local_split(): r1 = lax.ppermute(y1, 'ctx', PAIRS)]
  transfers between devices with their start and end apart: 27 -> 27, of which waited for: 12 -> 10; matrix products, arithmetic and copies ran while one was open for 0% -> 0% of each run, Pallas kernels for 9% -> 9%
where the time goes in v7:
time: 102 us; the launch traced here: 101 us
  starting transfers between devices  45.2 us (44%)
  waiting for transfers between devices  38.8 us (38%)
  Pallas kernels  15.2 us (15%)
  between operations  1.05 us (1%)
    ppermute x15, waiting for transfers between devices, swapped(): lax.ppermute(parts[m], 'head', [(i, i ^ m) for i in range(groups)])  22.4 us
    ppermute x15, starting transfers between devices, swapped(): lax.ppermute(parts[m], 'head', [(i, i ^ m) for i in range(groups)])  20 us
    ppermute x1, starting transfers between devices, local_split(): out1 = lax.ppermute(out1, 'ctx', PAIRS)  11 us
    ppermute x1, waiting for transfers between devices, local_split(): to_pair = lax.ppermute(to_pair, 'ctx', PAIRS)  8.17 us
    ppermute x1, starting transfers between devices, local_split(): r1 = lax.ppermute(y1, 'ctx', PAIRS)  4.43 us
    ppermute x1, waiting for transfers between devices, local_split(): from_pair = lax.ppermute(from_pair, 'ctx', PAIRS)  3.94 us
    pallas_call x1, Pallas kernels, pack(): pl.pallas_call(body, out_shape=[jax.ShapeDtypeStruct((rows, size), BF16)...  3.9 us
    pallas_call x1, Pallas kernels, near_pairs(): pl.pallas_call(body, out_shape=[jax.ShapeDtypeStruct((rows, 2 * width), B...  3.73 us
  transfers between devices with their start and end apart: 27, of which 10 were waited for; matrix products, arithmetic and copies ran while one was open for 0% of the time, Pallas kernels for 9%

profile of v7, /device:TPU:0, one launch (start us, length us, event | category | flops | bytes accessed | tf_op | source)
XLA Modules:
  0.0 101.3 jit_solution(4052025896763856750)
XLA Ops:
  0.6 3.9 %pack.1 = (bf16[56,1408]{1,0:T(8,128)(2,1)}, bf16[56,1408]{1,0:T(8,128)(2,1)}, bf16[56,1408]{1,0:T(8,128)(2,1)}, bf16[56,1408]{1,0:T(8,128)(2,1)}, bf16[56,1280]...) custom-call(bf16[56,5120]{1,0:T(8,128)(2,1)} %q.1, ...), custom_call_target="tpu_custom_call" | custom-call | bytes 5734400 | tf_op jit(solution)/shard_map/pack/pallas_call | solution.py:221
  4.5 3.0 %collective-permute-start = (bf16[56,1408]{1,0:T(8,128)(2,1)}, bf16[56,1408]{1,0:T(8,128)(2,1)S(1)}, u32[]{:S(2)}, u32[]{:S(2)}) collective-permute-start(bf16[56,1408]{1,0:T(8,128)(2,1)} %get-tuple-element.63), channel_id=1, source_target_pairs={{0,1},{1,0},{2,3},{3,2},{4,5},{5,4},{6,7},{7,6},{8,9},{9,8},{10,11... | collective-permute-start | bytes 473096 | tf_op jit(solution)/shard_map/ppermute | solution.py:793
  7.6 1.5 %collective-permute-start.1 = (bf16[56,1408]{1,0:T(8,128)(2,1)}, bf16[56,1408]{1,0:T(8,128)(2,1)S(1)}, u32[]{:S(2)}, u32[]{:S(2)}) collective-permute-start(bf16[56,1408]{1,0:T(8,128)(2,1)} %get-tuple-element.64), channel_id=1, source_target_pairs={{0,2},{1,3},{2,0},{3,1},{4,6},{5,7},{6,4},{7,5},{8,10},{9,11},{10,... | collective-permute-start | bytes 473096 | tf_op jit(solution)/shard_map/ppermute | solution.py:793
  9.1 1.9 %collective-permute-start.3 = (bf16[56,1280]{1,0:T(8,128)(2,1)}, bf16[56,1280]{1,0:T(8,128)(2,1)S(1)}, u32[]{:S(2)}, u32[]{:S(2)}) collective-permute-start(bf16[56,1280]{1,0:T(8,128)(2,1)} %get-tuple-element.66), channel_id=1, source_target_pairs={{0,1},{1,0},{2,3},{3,2},{4,5},{5,4},{6,7},{7,6},{8,9},{9,8},{10,11... | collective-permute-start | bytes 430088 | tf_op jit(solution)/shard_map/ppermute | solution.py:793
  11.0 1.5 %collective-permute-start.4 = (bf16[56,1280]{1,0:T(8,128)(2,1)}, bf16[56,1280]{1,0:T(8,128)(2,1)S(1)}, u32[]{:S(2)}, u32[]{:S(2)}) collective-permute-start(bf16[56,1280]{1,0:T(8,128)(2,1)} %get-tuple-element.67), channel_id=1, source_target_pairs={{0,2},{1,3},{2,0},{3,1},{4,6},{5,7},{6,4},{7,5},{8,10},{9,11},{10,... | collective-permute-start | bytes 430088 | tf_op jit(solution)/shard_map/ppermute | solution.py:793
  12.6 5.0 %collective-permute-done.1.refs_2_ = bf16[56,1408]{1,0:T(8,128)(2,1)S(1)} collective-permute-done((bf16[56,1408]{1,0:T(8,128)(2,1)}, bf16[56,1408]{1,0:T(8,128)(2,1)S(1)}, u32[]{:S(2)}, u32[]{:S(2)}) %collective-permute-start.1) | collective-permute-done | bytes 157728 | tf_op jit(solution)/shard_map/ppermute | solution.py:793
  17.6 0.9 copy-done.1
  18.5 1.1 %join_first.1 = bf16[4,56,1408]{2,1,0:T(8,128)(2,1)S(1)} custom-call(bf16[56,1408]{1,0:T(8,128)(2,1)S(1)} %copy-done.1, bf16[56,1408]{1,0:T(8,128)(2,1)S(1)} %collective-permute-done.refs_1_, bf16[56,1408]{1,0:T(8,128)(2,1)S(1)} %collective-permute-done.1.refs_2_, bf16[56,1408]{1,0:T(8,128)(2,1)S(1)} %collective-permute-done.2.refs_3_, f32[10,224]{1,0:T(8,128)S(1)} %bitcast.19), custom_call_target="tpu_custom_call" | custom-call | bytes 1261568 | tf_op jit(solution)/shard_map/join_first/pallas_call | solution.py:259
  20.4 4.4 %collective-permute-start.6 = (bf16[224,1408]{1,0:T(8,128)(2,1)S(1)}, bf16[224,1408]{1,0:T(8,128)(2,1)S(1)}, u32[]{:S(2)}, u32[]{:S(2)}) collective-permute-start(bf16[224,1408]{1,0:T(8,128)(2,1)S(1)} %bitcast.6), channel_id=1, source_target_pairs={{0,4},{4,0},{8,12},{12,8},{1,5},{5,1},{9,13},{13,9},{2,6},{6,2},{1... | collective-permute-start | bytes 1892360 | tf_op jit(solution)/shard_map/ppermute | solution.py:800
  24.9 1.4 %collective-permute-start.8 = (bf16[56,2560]{1,0:T(8,128)(2,1)}, bf16[56,2560]{1,0:T(8,128)(2,1)S(1)}, u32[]{:S(2)}, u32[]{:S(2)}) collective-permute-start(bf16[56,2560]{1,0:T(8,128)(2,1)} %get-tuple-element.74), channel_id=1, source_target_pairs={{0,1},{1,0},{2,3},{3,2},{4,5},{5,4},{6,7},{7,6},{8,9},{9,8},{10,11... | collective-permute-start | bytes 860168 | tf_op jit(solution)/shard_map/ppermute | solution.py:793
  27.0 1.4 %collective-permute-start.5 = (bf16[56,1280]{1,0:T(8,128)(2,1)S(1)}, bf16[56,1280]{1,0:T(8,128)(2,1)S(1)}, u32[]{:S(2)}, u32[]{:S(2)}) collective-permute-start(bf16[56,1280]{1,0:T(8,128)(2,1)S(1)} %copy-done.6), channel_id=1, source_target_pairs={{0,3},{1,2},{2,1},{3,0},{4,7},{5,6},{6,5},{7,4},{8,11},{9,10},{10,... | collective-permute-start | bytes 430088 | tf_op jit(solution)/shard_map/ppermute | solution.py:793
  28.4 7.7 %collective-permute-done.5.refs_3_ = bf16[56,1280]{1,0:T(8,128)(2,1)S(1)} collective-permute-done((bf16[56,1280]{1,0:T(8,128)(2,1)S(1)}, bf16[56,1280]{1,0:T(8,128)(2,1)S(1)}, u32[]{:S(2)}, u32[]{:S(2)}) %collective-permute-start.5) | collective-permute-done | bytes 143392 | tf_op jit(solution)/shard_map/ppermute | solution.py:793
  36.9 1.3 %collective-permute-done.6.r1 = bf16[224,1408]{1,0:T(8,128)(2,1)S(1)} collective-permute-done((bf16[224,1408]{1,0:T(8,128)(2,1)S(1)}, bf16[224,1408]{1,0:T(8,128)(2,1)S(1)}, u32[]{:S(2)}, u32[]{:S(2)}) %collective-permute-start.6) | collective-permute-done | bytes 630816 | tf_op jit(solution)/shard_map/ppermute | solution.py:800
  38.8 3.5 %collective-permute-start.13 = (bf16[224,1280]{1,0:T(8,128)(2,1)S(1)}, bf16[224,1280]{1,0:T(8,128)(2,1)S(1)}, u32[]{:S(2)}, u32[]{:S(2)}) collective-permute-start(bf16[224,1280]{1,0:T(8,128)(2,1)S(1)} %bitcast.11), channel_id=1, source_target_pairs={{0,4},{4,0},{8,12},{12,8},{1,5},{5,1},{9,13},{13,9},{2,6},{6,2},{1... | collective-permute-start | bytes 1720328 | tf_op jit(solution)/shard_map/ppermute | solution.py:805
  42.3 1.4 %collective-permute-start.10 = (bf16[56,2560]{1,0:T(8,128)(2,1)S(1)}, bf16[56,2560]{1,0:T(8,128)(2,1)S(1)}, u32[]{:S(2)}, u32[]{:S(2)}) collective-permute-start(bf16[56,2560]{1,0:T(8,128)(2,1)S(1)} %copy-done.4), channel_id=1, source_target_pairs={{0,3},{1,2},{2,1},{3,0},{4,7},{5,6},{6,5},{7,4},{8,11},{9,10},{10,... | collective-permute-start | bytes 860168 | tf_op jit(solution)/shard_map/ppermute | solution.py:793
  43.7 6.2 %collective-permute-done.10.refs_3_ = bf16[56,2560]{1,0:T(8,128)(2,1)S(1)} collective-permute-done((bf16[56,2560]{1,0:T(8,128)(2,1)S(1)}, bf16[56,2560]{1,0:T(8,128)(2,1)S(1)}, u32[]{:S(2)}, u32[]{:S(2)}) %collective-permute-start.10) | collective-permute-done | bytes 286752 | tf_op jit(solution)/shard_map/ppermute | solution.py:793
  51.1 3.9 %collective-permute-done.11.from_pair = bf16[16,2688]{1,0:T(8,128)(2,1)S(1)} collective-permute-done((bf16[16,2688]{1,0:T(8,128)(2,1)S(1)}, bf16[16,2688]{1,0:T(8,128)(2,1)S(1)}, u32[]{:S(2)}, u32[]{:S(2)}) %collective-permute-start.11) | collective-permute-done | bytes 86048 | tf_op jit(solution)/shard_map/ppermute | solution.py:808
  55.9 11.0 %collective-permute-start.16 = (bf16[224,1280]{1,0:T(8,128)(2,1)S(1)}, bf16[224,1280]{1,0:T(8,128)(2,1)S(1)}, u32[]{:S(2)}, u32[]{:S(2)}) collective-permute-start(bf16[224,1280]{1,0:T(8,128)(2,1)S(1)} %get-tuple-element.96), channel_id=1, source_target_pairs={{0,4},{4,0},{8,12},{12,8},{1,5},{5,1},{9,13},{13,9},{2,6},{6,2},{1... | collective-permute-start | bytes 1720328 | tf_op jit(solution)/shard_map/ppermute | solution.py:815
  67.0 3.7 %near_pairs.1 = (bf16[224,2560]{1,0:T(8,128)(2,1)S(1)}, bf16[224,1280]{1,0:T(8,128)(2,1)S(1)}, bf16[224,1280]{1,0:T(8,128)(2,1)S(1)}, bf16[16,2560]{1,0:T(8,128)(2,1)S(1)}, bf16[16,2560]{1,0:T(8,128)(2,1)S(1)}) custom-call(bf16[224,1408]{1,0:T(8,128)(2,1)S(1)} %bitcast.10, bf16[224,1280]{1,0:T(8,128)(2,1)S(1)} %bitcast.15, bf16[224,2560]{1,0:T(8,128)(2,1)S(1)} %bitcast.18, ...), custom_call_target="tpu_custom_call" | custom-call | flops 642252800 | bytes 4587520 | tf_op jit(solution)/shard_map/near_pairs/pallas_call | solution.py:584
  71.5 8.2 %collective-permute-done.17.dp = bf16[16,2560]{1,0:T(8,128)(2,1)S(1)} collective-permute-done((bf16[16,2560]{1,0:T(8,128)(2,1)S(1)}, bf16[16,2560]{1,0:T(8,128)(2,1)S(1)}, u32[]{:S(2)}, u32[]{:S(2)}) %collective-permute-start.17) | collective-permute-done | bytes 81952 | tf_op jit(solution)/shard_map/ppermute | solution.py:816
  79.8 2.0 %collective-permute-start.20 = (bf16[224,1280]{1,0:T(8,128)(2,1)S(1)}, bf16[224,1280]{1,0:T(8,128)(2,1)S(1)}, u32[]{:S(2)}, u32[]{:S(2)}) collective-permute-start(bf16[224,1280]{1,0:T(8,128)(2,1)S(1)} %add_convert_fusion), channel_id=1, source_target_pairs={{0,4},{4,0},{8,12},{12,8},{1,5},{5,1},{9,13},{13,9},{2,6},{6,2},{1... | collective-permute-start | bytes 1720328 | tf_op jit(solution)/shard_map/ppermute | solution.py:820
  82.5 1.0 finish_first.1
  83.6 1.6 %collective-permute-start.25 = (bf16[56,2560]{1,0:T(8,128)(2,1)S(1)}, bf16[56,2560]{1,0:T(8,128)(2,1)S(1)}, u32[]{:S(2)}, u32[]{:S(2)}) collective-permute-start(bf16[56,2560]{1,0:T(8,128)(2,1)S(1)} %get-tuple-element.116), channel_id=1, source_target_pairs={{0,2},{1,3},{2,0},{3,1},{4,6},{5,7},{6,4},{7,5},{8,10},{9,11},{10,... | collective-permute-start | bytes 860168 | tf_op jit(solution)/shard_map/ppermute | solution.py:793
  85.3 1.8 %collective-permute-start.26 = (bf16[56,2560]{1,0:T(8,128)(2,1)S(1)}, bf16[56,2560]{1,0:T(8,128)(2,1)S(1)}, u32[]{:S(2)}, u32[]{:S(2)}) collective-permute-start(bf16[56,2560]{1,0:T(8,128)(2,1)S(1)} %get-tuple-element.117), channel_id=1, source_target_pairs={{0,3},{1,2},{2,1},{3,0},{4,7},{5,6},{6,5},{7,4},{8,11},{9,10},{10,... | collective-permute-start | bytes 860168 | tf_op jit(solution)/shard_map/ppermute | solution.py:793
  87.0 3.0 %collective-permute-done.20.out2 = bf16[224,1280]{1,0:T(8,128)(2,1)S(1)} collective-permute-done((bf16[224,1280]{1,0:T(8,128)(2,1)S(1)}, bf16[224,1280]{1,0:T(8,128)(2,1)S(1)}, u32[]{:S(2)}, u32[]{:S(2)}) %collective-permute-start.20) | collective-permute-done | bytes 573472 | tf_op jit(solution)/shard_map/ppermute | solution.py:820
  90.0 1.0 finish_second.1
  91.2 1.6 %collective-permute-start.22 = (bf16[56,1280]{1,0:T(8,128)(2,1)S(1)}, bf16[56,1280]{1,0:T(8,128)(2,1)S(1)}, u32[]{:S(2)}, u32[]{:S(2)}) collective-permute-start(bf16[56,1280]{1,0:T(8,128)(2,1)S(1)} %get-tuple-element.112), channel_id=1, source_target_pairs={{0,2},{1,3},{2,0},{3,1},{4,6},{5,7},{6,4},{7,5},{8,10},{9,11},{10,... | collective-permute-start | bytes 430088 | tf_op jit(solution)/shard_map/ppermute | solution.py:793
  92.8 1.8 %collective-permute-start.23 = (bf16[56,1280]{1,0:T(8,128)(2,1)S(1)}, bf16[56,1280]{1,0:T(8,128)(2,1)S(1)}, u32[]{:S(2)}, u32[]{:S(2)}) collective-permute-start(bf16[56,1280]{1,0:T(8,128)(2,1)S(1)} %get-tuple-element.113), channel_id=1, source_target_pairs={{0,3},{1,2},{2,1},{3,0},{4,7},{5,6},{6,5},{7,4},{8,11},{9,10},{10,... | collective-permute-start | bytes 430088 | tf_op jit(solution)/shard_map/ppermute | solution.py:793
  94.6 1.9 %collective-permute-done.25.refs_2_ = bf16[56,2560]{1,0:T(8,128)(2,1)S(1)} collective-permute-done((bf16[56,2560]{1,0:T(8,128)(2,1)S(1)}, bf16[56,2560]{1,0:T(8,128)(2,1)S(1)}, u32[]{:S(2)}, u32[]{:S(2)}) %collective-permute-start.25) | collective-permute-done | bytes 286752 | tf_op jit(solution)/shard_map/ppermute | solution.py:793
  96.4 1.5 %unpack_early.1 = (bf16[56,5120]{1,0:T(8,128)(2,1)}, bf16[56,5120]{1,0:T(8,128)(2,1)}, bf16[56,5120]{1,0:T(8,128)(2,1)}) custom-call(bf16[56,2560]{1,0:T(8,128)(2,1)S(1)} %get-tuple-element.114.refs_0_, bf16[56,2560]{1,0:T(8,128)(2,1)S(1)} %collective-permute-done.24.refs_1_, bf16[56,2560]{1,0:T(8,128)(2,1)S(1)} %collective-permute-done.25.refs_2_, ...), custom_call_target="tpu_custom_call" | custom-call | bytes 2867200 | tf_op jit(solution)/shard_map/unpack_early/pallas_call | solution.py:729
  98.0 1.5 %collective-permute-done.22.refs_2_ = bf16[56,1280]{1,0:T(8,128)(2,1)S(1)} collective-permute-done((bf16[56,1280]{1,0:T(8,128)(2,1)S(1)}, bf16[56,1280]{1,0:T(8,128)(2,1)S(1)}, u32[]{:S(2)}, u32[]{:S(2)}) %collective-permute-start.22) | collective-permute-done | bytes 143392 | tf_op jit(solution)/shard_map/ppermute | solution.py:793
  99.5 1.6 %unpack_late.1 = (bf16[56,5120]{1,0:T(8,128)(2,1)}, bf16[56,5120]{1,0:T(8,128)(2,1)}, bf16[56,5120]{1,0:T(8,128)(2,1)}) custom-call(bf16[56,1280]{1,0:T(8,128)(2,1)S(1)} %get-tuple-element.110.refs_0_, bf16[56,1280]{1,0:T(8,128)(2,1)S(1)} %collective-permute-done.21.refs_1_, ...), custom_call_target="tpu_custom_call", output_to_operand_aliasing={{0}: (4, {}), {1}: (5, {}), {2}: (6, {})} | custom-call | bytes 2293760 | tf_op jit(solution)/shard_map/unpack_late/pallas_call | solution.py:770
  (48 shorter events, 7.0 us)
Async XLA Ops:
  0.6 17.0 %copy-start.3 = (f32[224,10]{0,1:T(8,128)S(1)}, f32[224,10]{0,1:T(8,128)}, u32[]{:S(2)}) copy-start(f32[224,10]{0,1:T(8,128)} %param.12) | copy-start | bytes 26884
  4.5 8.0 %collective-permute-start = (bf16[56,1408]{1,0:T(8,128)(2,1)}, bf16[56,1408]{1,0:T(8,128)(2,1)S(1)}, u32[]{:S(2)}, u32[]{:S(2)}) collective-permute-start(bf16[56,1408]{1,0:T(8,128)(2,1)} %get-tuple-element.63), channel_id=1, source_target_pairs={{0,1},{1,0},{2,3},{3,2},{4,5},{5,4},{6,7},{7,6},{8,9},{9,8},{10,11... | collective-permute-start | bytes 473096 | tf_op jit(solution)/shard_map/ppermute | solution.py:793
  7.6 10.1 %collective-permute-start.1 = (bf16[56,1408]{1,0:T(8,128)(2,1)}, bf16[56,1408]{1,0:T(8,128)(2,1)S(1)}, u32[]{:S(2)}, u32[]{:S(2)}) collective-permute-start(bf16[56,1408]{1,0:T(8,128)(2,1)} %get-tuple-element.64), channel_id=1, source_target_pairs={{0,2},{1,3},{2,0},{3,1},{4,6},{5,7},{6,4},{7,5},{8,10},{9,11},{10,... | collective-permute-start | bytes 473096 | tf_op jit(solution)/shard_map/ppermute | solution.py:793
  9.1 8.5 %collective-permute-start.2 = (bf16[56,1408]{1,0:T(8,128)(2,1)}, bf16[56,1408]{1,0:T(8,128)(2,1)S(1)}, u32[]{:S(2)}, u32[]{:S(2)}) collective-permute-start(bf16[56,1408]{1,0:T(8,128)(2,1)} %get-tuple-element.65), channel_id=1, source_target_pairs={{0,3},{1,2},{2,1},{3,0},{4,7},{5,6},{6,5},{7,4},{8,11},{9,10},{10,... | collective-permute-start | bytes 473096 | tf_op jit(solution)/shard_map/ppermute | solution.py:793
  9.1 10.6 %collective-permute-start.3 = (bf16[56,1280]{1,0:T(8,128)(2,1)}, bf16[56,1280]{1,0:T(8,128)(2,1)S(1)}, u32[]{:S(2)}, u32[]{:S(2)}) collective-permute-start(bf16[56,1280]{1,0:T(8,128)(2,1)} %get-tuple-element.66), channel_id=1, source_target_pairs={{0,1},{1,0},{2,3},{3,2},{4,5},{5,4},{6,7},{7,6},{8,9},{9,8},{10,11... | collective-permute-start | bytes 430088 | tf_op jit(solution)/shard_map/ppermute | solution.py:793
  11.0 8.7 %collective-permute-start.4 = (bf16[56,1280]{1,0:T(8,128)(2,1)}, bf16[56,1280]{1,0:T(8,128)(2,1)S(1)}, u32[]{:S(2)}, u32[]{:S(2)}) collective-permute-start(bf16[56,1280]{1,0:T(8,128)(2,1)} %get-tuple-element.67), channel_id=1, source_target_pairs={{0,2},{1,3},{2,0},{3,1},{4,6},{5,7},{6,4},{7,5},{8,10},{9,11},{10,... | collective-permute-start | bytes 430088 | tf_op jit(solution)/shard_map/ppermute | solution.py:793
  18.5 8.5 %copy-start.6 = (bf16[56,1280]{1,0:T(8,128)(2,1)S(1)}, bf16[56,1280]{1,0:T(8,128)(2,1)}, u32[]{:S(2)}) copy-start(bf16[56,1280]{1,0:T(8,128)(2,1)} %get-tuple-element.72) | copy-start | bytes 430084
  18.5 17.5 %copy-start.2 = (bf16[56,1280]{1,0:T(8,128)(2,1)S(1)}, bf16[56,1280]{1,0:T(8,128)(2,1)}, u32[]{:S(2)}) copy-start(bf16[56,1280]{1,0:T(8,128)(2,1)} %get-tuple-element.69.refs_0_) | copy-start | bytes 430084
  18.5 23.8 %copy-start.4 = (bf16[56,2560]{1,0:T(8,128)(2,1)S(1)}, bf16[56,2560]{1,0:T(8,128)(2,1)}, u32[]{:S(2)}) copy-start(bf16[56,2560]{1,0:T(8,128)(2,1)} %get-tuple-element.80) | copy-start | bytes 860164
  18.5 31.3 %copy-start = (bf16[56,2560]{1,0:T(8,128)(2,1)S(1)}, bf16[56,2560]{1,0:T(8,128)(2,1)}, u32[]{:S(2)}) copy-start(bf16[56,2560]{1,0:T(8,128)(2,1)} %get-tuple-element.77.refs_0_) | copy-start | bytes 860164
  19.7 17.1 %collective-permute-start.7 = (bf16[224,1408]{1,0:T(8,128)(2,1)S(1)}, bf16[224,1408]{1,0:T(8,128)(2,1)S(1)}, u32[]{:S(2)}, u32[]{:S(2)}) collective-permute-start(bf16[224,1408]{1,0:T(8,128)(2,1)S(1)} %bitcast.5), channel_id=1, source_target_pairs={{4,8},{8,4},{5,9},{9,5},{6,10},{10,6},{7,11},{11,7},{20,24},{24,20... | collective-permute-start | bytes 1892360 | tf_op jit(solution)/shard_map/ppermute | solution.py:801
  20.4 17.7 %collective-permute-start.6 = (bf16[224,1408]{1,0:T(8,128)(2,1)S(1)}, bf16[224,1408]{1,0:T(8,128)(2,1)S(1)}, u32[]{:S(2)}, u32[]{:S(2)}) collective-permute-start(bf16[224,1408]{1,0:T(8,128)(2,1)S(1)} %bitcast.6), channel_id=1, source_target_pairs={{0,4},{4,0},{8,12},{12,8},{1,5},{5,1},{9,13},{13,9},{2,6},{6,2},{1... | collective-permute-start | bytes 1892360 | tf_op jit(solution)/shard_map/ppermute | solution.py:800
  24.9 12.0 %collective-permute-start.8 = (bf16[56,2560]{1,0:T(8,128)(2,1)}, bf16[56,2560]{1,0:T(8,128)(2,1)S(1)}, u32[]{:S(2)}, u32[]{:S(2)}) collective-permute-start(bf16[56,2560]{1,0:T(8,128)(2,1)} %get-tuple-element.74), channel_id=1, source_target_pairs={{0,1},{1,0},{2,3},{3,2},{4,5},{5,4},{6,7},{7,6},{8,9},{9,8},{10,11... | collective-permute-start | bytes 860168 | tf_op jit(solution)/shard_map/ppermute | solution.py:793
  26.3 10.5 %collective-permute-start.9 = (bf16[56,2560]{1,0:T(8,128)(2,1)S(1)}, bf16[56,2560]{1,0:T(8,128)(2,1)S(1)}, u32[]{:S(2)}, u32[]{:S(2)}) collective-permute-start(bf16[56,2560]{1,0:T(8,128)(2,1)S(1)} %copy-done.5), channel_id=1, source_target_pairs={{0,2},{1,3},{2,0},{3,1},{4,6},{5,7},{6,4},{7,5},{8,10},{9,11},{10,... | collective-permute-start | bytes 860168 | tf_op jit(solution)/shard_map/ppermute | solution.py:793
  27.0 9.1 %collective-permute-start.5 = (bf16[56,1280]{1,0:T(8,128)(2,1)S(1)}, bf16[56,1280]{1,0:T(8,128)(2,1)S(1)}, u32[]{:S(2)}, u32[]{:S(2)}) collective-permute-start(bf16[56,1280]{1,0:T(8,128)(2,1)S(1)} %copy-done.6), channel_id=1, source_target_pairs={{0,3},{1,2},{2,1},{3,0},{4,7},{5,6},{6,5},{7,4},{8,11},{9,10},{10,... | collective-permute-start | bytes 430088 | tf_op jit(solution)/shard_map/ppermute | solution.py:793
  38.1 16.9 %collective-permute-start.14 = (bf16[224,1408]{1,0:T(8,128)(2,1)S(1)}, bf16[224,1408]{1,0:T(8,128)(2,1)S(1)}, u32[]{:S(2)}, u32[]{:S(2)}) collective-permute-start(bf16[224,1408]{1,0:T(8,128)(2,1)S(1)} %collective-permute-done.6.r1), channel_id=1, source_target_pairs={{4,8},{8,4},{5,9},{9,5},{6,10},{10,6},{7,11},{11,7},{20,24},{24,20... | collective-permute-start | bytes 1892360 | tf_op jit(solution)/shard_map/ppermute | solution.py:806
  38.8 16.2 %collective-permute-start.13 = (bf16[224,1280]{1,0:T(8,128)(2,1)S(1)}, bf16[224,1280]{1,0:T(8,128)(2,1)S(1)}, u32[]{:S(2)}, u32[]{:S(2)}) collective-permute-start(bf16[224,1280]{1,0:T(8,128)(2,1)S(1)} %bitcast.11), channel_id=1, source_target_pairs={{0,4},{4,0},{8,12},{12,8},{1,5},{5,1},{9,13},{13,9},{2,6},{6,2},{1... | collective-permute-start | bytes 1720328 | tf_op jit(solution)/shard_map/ppermute | solution.py:805
  42.3 7.5 %collective-permute-start.10 = (bf16[56,2560]{1,0:T(8,128)(2,1)S(1)}, bf16[56,2560]{1,0:T(8,128)(2,1)S(1)}, u32[]{:S(2)}, u32[]{:S(2)}) collective-permute-start(bf16[56,2560]{1,0:T(8,128)(2,1)S(1)} %copy-done.4), channel_id=1, source_target_pairs={{0,3},{1,2},{2,1},{3,0},{4,7},{5,6},{6,5},{7,4},{8,11},{9,10},{10,... | collective-permute-start | bytes 860168 | tf_op jit(solution)/shard_map/ppermute | solution.py:793
  50.2 4.8 %collective-permute-start.11 = (bf16[16,2688]{1,0:T(8,128)(2,1)S(1)}, bf16[16,2688]{1,0:T(8,128)(2,1)S(1)}, u32[]{:S(2)}, u32[]{:S(2)}) collective-permute-start(bf16[16,2688]{1,0:T(8,128)(2,1)S(1)} %get-tuple-element.82), channel_id=1, source_target_pairs={{0,4},{4,0},{8,12},{12,8},{1,5},{5,1},{9,13},{13,9},{2,6},{6,2},{1... | collective-permute-start | bytes 258056 | tf_op jit(solution)/shard_map/ppermute | solution.py:808
  50.4 4.6 %collective-permute-start.12 = (bf16[16,2688]{1,0:T(8,128)(2,1)S(1)}, bf16[16,2688]{1,0:T(8,128)(2,1)S(1)}, u32[]{:S(2)}, u32[]{:S(2)}) collective-permute-start(bf16[16,2688]{1,0:T(8,128)(2,1)S(1)} %get-tuple-element.83), channel_id=1, source_target_pairs={{4,8},{8,4},{5,9},{9,5},{6,10},{10,6},{7,11},{11,7},{20,24},{24,20... | collective-permute-start | bytes 258056 | tf_op jit(solution)/shard_map/ppermute | solution.py:809
  55.2 24.4 %collective-permute-start.15 = (bf16[224,1280]{1,0:T(8,128)(2,1)S(1)}, bf16[224,1280]{1,0:T(8,128)(2,1)S(1)}, u32[]{:S(2)}, u32[]{:S(2)}) collective-permute-start(bf16[224,1280]{1,0:T(8,128)(2,1)S(1)} %get-tuple-element.94), channel_id=1, source_target_pairs={{4,8},{8,4},{5,9},{9,5},{6,10},{10,6},{7,11},{11,7},{20,24},{24,20... | collective-permute-start | bytes 1720328 | tf_op jit(solution)/shard_map/ppermute | solution.py:814
  55.9 23.7 %collective-permute-start.16 = (bf16[224,1280]{1,0:T(8,128)(2,1)S(1)}, bf16[224,1280]{1,0:T(8,128)(2,1)S(1)}, u32[]{:S(2)}, u32[]{:S(2)}) collective-permute-start(bf16[224,1280]{1,0:T(8,128)(2,1)S(1)} %get-tuple-element.96), channel_id=1, source_target_pairs={{0,4},{4,0},{8,12},{12,8},{1,5},{5,1},{9,13},{13,9},{2,6},{6,2},{1... | collective-permute-start | bytes 1720328 | tf_op jit(solution)/shard_map/ppermute | solution.py:815
  70.7 8.9 %collective-permute-start.17 = (bf16[16,2560]{1,0:T(8,128)(2,1)S(1)}, bf16[16,2560]{1,0:T(8,128)(2,1)S(1)}, u32[]{:S(2)}, u32[]{:S(2)}) collective-permute-start(bf16[16,2560]{1,0:T(8,128)(2,1)S(1)} %get-tuple-element.97), channel_id=1, source_target_pairs={{0,4},{4,0},{8,12},{12,8},{1,5},{5,1},{9,13},{13,9},{2,6},{6,2},{1... | collective-permute-start | bytes 245768 | tf_op jit(solution)/shard_map/ppermute | solution.py:816
  70.8 8.8 %collective-permute-start.18 = (bf16[16,2560]{1,0:T(8,128)(2,1)S(1)}, bf16[16,2560]{1,0:T(8,128)(2,1)S(1)}, u32[]{:S(2)}, u32[]{:S(2)}) collective-permute-start(bf16[16,2560]{1,0:T(8,128)(2,1)S(1)} %get-tuple-element.98), channel_id=1, source_target_pairs={{4,8},{8,4},{5,9},{9,5},{6,10},{10,6},{7,11},{11,7},{20,24},{24,20... | collective-permute-start | bytes 245768 | tf_op jit(solution)/shard_map/ppermute | solution.py:817
  79.8 10.2 %collective-permute-start.20 = (bf16[224,1280]{1,0:T(8,128)(2,1)S(1)}, bf16[224,1280]{1,0:T(8,128)(2,1)S(1)}, u32[]{:S(2)}, u32[]{:S(2)}) collective-permute-start(bf16[224,1280]{1,0:T(8,128)(2,1)S(1)} %add_convert_fusion), channel_id=1, source_target_pairs={{0,4},{4,0},{8,12},{12,8},{1,5},{5,1},{9,13},{13,9},{2,6},{6,2},{1... | collective-permute-start | bytes 1720328 | tf_op jit(solution)/shard_map/ppermute | solution.py:820
  81.8 8.2 %collective-permute-start.19 = (bf16[224,1280]{1,0:T(8,128)(2,1)S(1)}, bf16[224,1280]{1,0:T(8,128)(2,1)S(1)}, u32[]{:S(2)}, u32[]{:S(2)}) collective-permute-start(bf16[224,1280]{1,0:T(8,128)(2,1)S(1)} %get-tuple-element.99), channel_id=1, source_target_pairs={{4,8},{8,4},{5,9},{9,5},{6,10},{10,6},{7,11},{11,7},{20,24},{24,20... | collective-permute-start | bytes 1720328 | tf_op jit(solution)/shard_map/ppermute | solution.py:819
  83.5 9.3 %collective-permute-start.24 = (bf16[56,2560]{1,0:T(8,128)(2,1)S(1)}, bf16[56,2560]{1,0:T(8,128)(2,1)S(1)}, u32[]{:S(2)}, u32[]{:S(2)}) collective-permute-start(bf16[56,2560]{1,0:T(8,128)(2,1)S(1)} %get-tuple-element.115), channel_id=1, source_target_pairs={{0,1},{1,0},{2,3},{3,2},{4,5},{5,4},{6,7},{7,6},{8,9},{9,8},{10,11... | collective-permute-start | bytes 860168 | tf_op jit(solution)/shard_map/ppermute | solution.py:793
  83.6 12.8 %collective-permute-start.25 = (bf16[56,2560]{1,0:T(8,128)(2,1)S(1)}, bf16[56,2560]{1,0:T(8,128)(2,1)S(1)}, u32[]{:S(2)}, u32[]{:S(2)}) collective-permute-start(bf16[56,2560]{1,0:T(8,128)(2,1)S(1)} %get-tuple-element.116), channel_id=1, source_target_pairs={{0,2},{1,3},{2,0},{3,1},{4,6},{5,7},{6,4},{7,5},{8,10},{9,11},{10,... | collective-permute-start | bytes 860168 | tf_op jit(solution)/shard_map/ppermute | solution.py:793
  85.3 11.2 %collective-permute-start.26 = (bf16[56,2560]{1,0:T(8,128)(2,1)S(1)}, bf16[56,2560]{1,0:T(8,128)(2,1)S(1)}, u32[]{:S(2)}, u32[]{:S(2)}) collective-permute-start(bf16[56,2560]{1,0:T(8,128)(2,1)S(1)} %get-tuple-element.117), channel_id=1, source_target_pairs={{0,3},{1,2},{2,1},{3,0},{4,7},{5,6},{6,5},{7,4},{8,11},{9,10},{10,... | collective-permute-start | bytes 860168 | tf_op jit(solution)/shard_map/ppermute | solution.py:793
  91.0 6.9 %collective-permute-start.21 = (bf16[56,1280]{1,0:T(8,128)(2,1)S(1)}, bf16[56,1280]{1,0:T(8,128)(2,1)S(1)}, u32[]{:S(2)}, u32[]{:S(2)}) collective-permute-start(bf16[56,1280]{1,0:T(8,128)(2,1)S(1)} %get-tuple-element.111), channel_id=1, source_target_pairs={{0,1},{1,0},{2,3},{3,2},{4,5},{5,4},{6,7},{7,6},{8,9},{9,8},{10,11... | collective-permute-start | bytes 430088 | tf_op jit(solution)/shard_map/ppermute | solution.py:793
  91.2 8.3 %collective-permute-start.22 = (bf16[56,1280]{1,0:T(8,128)(2,1)S(1)}, bf16[56,1280]{1,0:T(8,128)(2,1)S(1)}, u32[]{:S(2)}, u32[]{:S(2)}) collective-permute-start(bf16[56,1280]{1,0:T(8,128)(2,1)S(1)} %get-tuple-element.112), channel_id=1, source_target_pairs={{0,2},{1,3},{2,0},{3,1},{4,6},{5,7},{6,4},{7,5},{8,10},{9,11},{10,... | collective-permute-start | bytes 430088 | tf_op jit(solution)/shard_map/ppermute | solution.py:793
  92.8 6.7 %collective-permute-start.23 = (bf16[56,1280]{1,0:T(8,128)(2,1)S(1)}, bf16[56,1280]{1,0:T(8,128)(2,1)S(1)}, u32[]{:S(2)}, u32[]{:S(2)}) collective-permute-start(bf16[56,1280]{1,0:T(8,128)(2,1)S(1)} %get-tuple-element.113), channel_id=1, source_target_pairs={{0,3},{1,2},{2,1},{3,0},{4,7},{5,6},{6,5},{7,4},{8,11},{9,10},{10,... | collective-permute-start | bytes 430088 | tf_op jit(solution)/shard_map/ppermute | solution.py:793
  (2 other events, 8.7 us)

commit v8 on v7

--- a/solution.py
+++ b/solution.py
@@ -744,19 +744,16 @@
     half = width // 2
 
     def body(*refs):
-        dq, dk, dv, held, sems = refs[groups + 3 :]
+        dq, dk, dv, sems = refs[groups + 3 :]
         here, low = lax.axis_index("head"), lax.axis_index("ctx") < 2
-        loads = run_copies([(refs[m], held.at[m]) for m in range(groups)], sems)
 
         def moves(far, near):
             todo = []
             for m in range(groups):
                 base = pl.multiple_of((here ^ m) * width, LANES)
-                todo.append((held.at[m, :, pl.ds(0, half)], far.at[:, pl.ds(base + near, half)]))
-                todo.append((held.at[m, :, pl.ds(half, half)], dv.at[:, pl.ds(base + half, half)]))
+                todo.append((refs[m].at[:, pl.ds(0, half)], far.at[:, pl.ds(base + near, half)]))
+                todo.append((refs[m].at[:, pl.ds(half, half)], dv.at[:, pl.ds(base + half, half)]))
             return todo
-
-        wait_all(loads)
 
         @pl.when(low)
         def _():
@@ -770,9 +767,9 @@
     return pl.pallas_call(
         body,
         out_shape=[shape] * 3,
-        in_specs=anywhere(groups + 3),
+        in_specs=in_vmem(groups) + anywhere(3),
         out_specs=anywhere(3),
-        scratch_shapes=[pltpu.VMEM((groups, rows, width), BF16), pltpu.SemaphoreType.DMA((2 * groups,))],
+        scratch_shapes=[pltpu.SemaphoreType.DMA((2 * groups,))],
         input_output_aliases={groups: 0, groups + 1: 1, groups + 2: 2},
         compiler_params=pltpu.CompilerParams(vmem_limit_bytes=VMEM_SMALL),
         cost_estimate=pl.CostEstimate(flops=0, bytes_accessed=8 * rows * groups * width, transcendentals=0),

time: 102 us -> 101 us (level)
  no operation moved by 1% of the time
where the time goes in v8:
time: 101 us
  starting transfers between devices  45.2 us (45%)
  waiting for transfers between devices  38.8 us (38%)
  Pallas kernels  14.5 us (14%)
  between operations  1.05 us (1%)
    ppermute x15, waiting for transfers between devices, swapped(): lax.ppermute(parts[m], 'head', [(i, i ^ m) for i in range(groups)])  22.4 us
    ppermute x15, starting transfers between devices, swapped(): lax.ppermute(parts[m], 'head', [(i, i ^ m) for i in range(groups)])  20 us
    ppermute x1, starting transfers between devices, local_split(): out1 = lax.ppermute(out1, 'ctx', PAIRS)  11 us
    ppermute x1, waiting for transfers between devices, local_split(): to_pair = lax.ppermute(to_pair, 'ctx', PAIRS)  8.17 us
    ppermute x1, starting transfers between devices, local_split(): r1 = lax.ppermute(y1, 'ctx', PAIRS)  4.43 us
    ppermute x1, waiting for transfers between devices, local_split(): from_pair = lax.ppermute(from_pair, 'ctx', PAIRS)  3.94 us
    pallas_call x1, Pallas kernels, pack(): pl.pallas_call(body, out_shape=[jax.ShapeDtypeStruct((rows, size), BF16)...  3.9 us
    pallas_call x1, Pallas kernels, near_pairs(): pl.pallas_call(body, out_shape=[jax.ShapeDtypeStruct((rows, 2 * width), B...  3.73 us
  transfers between devices with their start and end apart: 27, of which 10 were waited for; matrix products, arithmetic and copies ran while one was open for 0% of the time, Pallas kernels for 9%

profile of v8, /device:TPU:0, one launch (start us, length us, event | category | flops | bytes accessed | tf_op | source)
XLA Modules:
  0.0 100.5 jit_solution(4449604551900563661)
XLA Ops:
  0.6 3.9 %pack.1 = (bf16[56,1408]{1,0:T(8,128)(2,1)}, bf16[56,1408]{1,0:T(8,128)(2,1)}, bf16[56,1408]{1,0:T(8,128)(2,1)}, bf16[56,1408]{1,0:T(8,128)(2,1)}, bf16[56,1280]...) custom-call(bf16[56,5120]{1,0:T(8,128)(2,1)} %q.1, ...), custom_call_target="tpu_custom_call" | custom-call | bytes 5734400 | tf_op jit(solution)/shard_map/pack/pallas_call | solution.py:221
  4.5 3.0 %collective-permute-start = (bf16[56,1408]{1,0:T(8,128)(2,1)}, bf16[56,1408]{1,0:T(8,128)(2,1)S(1)}, u32[]{:S(2)}, u32[]{:S(2)}) collective-permute-start(bf16[56,1408]{1,0:T(8,128)(2,1)} %get-tuple-element.63), channel_id=1, source_target_pairs={{0,1},{1,0},{2,3},{3,2},{4,5},{5,4},{6,7},{7,6},{8,9},{9,8},{10,11... | collective-permute-start | bytes 473096 | tf_op jit(solution)/shard_map/ppermute | solution.py:790
  7.6 1.5 %collective-permute-start.1 = (bf16[56,1408]{1,0:T(8,128)(2,1)}, bf16[56,1408]{1,0:T(8,128)(2,1)S(1)}, u32[]{:S(2)}, u32[]{:S(2)}) collective-permute-start(bf16[56,1408]{1,0:T(8,128)(2,1)} %get-tuple-element.64), channel_id=1, source_target_pairs={{0,2},{1,3},{2,0},{3,1},{4,6},{5,7},{6,4},{7,5},{8,10},{9,11},{10,... | collective-permute-start | bytes 473096 | tf_op jit(solution)/shard_map/ppermute | solution.py:790
  9.1 1.9 %collective-permute-start.3 = (bf16[56,1280]{1,0:T(8,128)(2,1)}, bf16[56,1280]{1,0:T(8,128)(2,1)S(1)}, u32[]{:S(2)}, u32[]{:S(2)}) collective-permute-start(bf16[56,1280]{1,0:T(8,128)(2,1)} %get-tuple-element.66), channel_id=1, source_target_pairs={{0,1},{1,0},{2,3},{3,2},{4,5},{5,4},{6,7},{7,6},{8,9},{9,8},{10,11... | collective-permute-start | bytes 430088 | tf_op jit(solution)/shard_map/ppermute | solution.py:790
  11.0 1.5 %collective-permute-start.4 = (bf16[56,1280]{1,0:T(8,128)(2,1)}, bf16[56,1280]{1,0:T(8,128)(2,1)S(1)}, u32[]{:S(2)}, u32[]{:S(2)}) collective-permute-start(bf16[56,1280]{1,0:T(8,128)(2,1)} %get-tuple-element.67), channel_id=1, source_target_pairs={{0,2},{1,3},{2,0},{3,1},{4,6},{5,7},{6,4},{7,5},{8,10},{9,11},{10,... | collective-permute-start | bytes 430088 | tf_op jit(solution)/shard_map/ppermute | solution.py:790
  12.6 5.0 %collective-permute-done.1.refs_2_ = bf16[56,1408]{1,0:T(8,128)(2,1)S(1)} collective-permute-done((bf16[56,1408]{1,0:T(8,128)(2,1)}, bf16[56,1408]{1,0:T(8,128)(2,1)S(1)}, u32[]{:S(2)}, u32[]{:S(2)}) %collective-permute-start.1) | collective-permute-done | bytes 157728 | tf_op jit(solution)/shard_map/ppermute | solution.py:790
  17.6 0.9 copy-done.1
  18.5 1.1 %join_first.1 = bf16[4,56,1408]{2,1,0:T(8,128)(2,1)S(1)} custom-call(bf16[56,1408]{1,0:T(8,128)(2,1)S(1)} %copy-done.1, bf16[56,1408]{1,0:T(8,128)(2,1)S(1)} %collective-permute-done.refs_1_, bf16[56,1408]{1,0:T(8,128)(2,1)S(1)} %collective-permute-done.1.refs_2_, bf16[56,1408]{1,0:T(8,128)(2,1)S(1)} %collective-permute-done.2.refs_3_, f32[10,224]{1,0:T(8,128)S(1)} %bitcast.19), custom_call_target="tpu_custom_call" | custom-call | bytes 1261568 | tf_op jit(solution)/shard_map/join_first/pallas_call | solution.py:259
  20.4 4.4 %collective-permute-start.6 = (bf16[224,1408]{1,0:T(8,128)(2,1)S(1)}, bf16[224,1408]{1,0:T(8,128)(2,1)S(1)}, u32[]{:S(2)}, u32[]{:S(2)}) collective-permute-start(bf16[224,1408]{1,0:T(8,128)(2,1)S(1)} %bitcast.6), channel_id=1, source_target_pairs={{0,4},{4,0},{8,12},{12,8},{1,5},{5,1},{9,13},{13,9},{2,6},{6,2},{1... | collective-permute-start | bytes 1892360 | tf_op jit(solution)/shard_map/ppermute | solution.py:797
  24.9 1.4 %collective-permute-start.8 = (bf16[56,2560]{1,0:T(8,128)(2,1)}, bf16[56,2560]{1,0:T(8,128)(2,1)S(1)}, u32[]{:S(2)}, u32[]{:S(2)}) collective-permute-start(bf16[56,2560]{1,0:T(8,128)(2,1)} %get-tuple-element.74), channel_id=1, source_target_pairs={{0,1},{1,0},{2,3},{3,2},{4,5},{5,4},{6,7},{7,6},{8,9},{9,8},{10,11... | collective-permute-start | bytes 860168 | tf_op jit(solution)/shard_map/ppermute | solution.py:790
  27.0 1.4 %collective-permute-start.5 = (bf16[56,1280]{1,0:T(8,128)(2,1)S(1)}, bf16[56,1280]{1,0:T(8,128)(2,1)S(1)}, u32[]{:S(2)}, u32[]{:S(2)}) collective-permute-start(bf16[56,1280]{1,0:T(8,128)(2,1)S(1)} %copy-done.6), channel_id=1, source_target_pairs={{0,3},{1,2},{2,1},{3,0},{4,7},{5,6},{6,5},{7,4},{8,11},{9,10},{10,... | collective-permute-start | bytes 430088 | tf_op jit(solution)/shard_map/ppermute | solution.py:790
  28.4 7.7 %collective-permute-done.5.refs_3_ = bf16[56,1280]{1,0:T(8,128)(2,1)S(1)} collective-permute-done((bf16[56,1280]{1,0:T(8,128)(2,1)S(1)}, bf16[56,1280]{1,0:T(8,128)(2,1)S(1)}, u32[]{:S(2)}, u32[]{:S(2)}) %collective-permute-start.5) | collective-permute-done | bytes 143392 | tf_op jit(solution)/shard_map/ppermute | solution.py:790
  36.9 1.3 %collective-permute-done.6.r1 = bf16[224,1408]{1,0:T(8,128)(2,1)S(1)} collective-permute-done((bf16[224,1408]{1,0:T(8,128)(2,1)S(1)}, bf16[224,1408]{1,0:T(8,128)(2,1)S(1)}, u32[]{:S(2)}, u32[]{:S(2)}) %collective-permute-start.6) | collective-permute-done | bytes 630816 | tf_op jit(solution)/shard_map/ppermute | solution.py:797
  38.8 3.5 %collective-permute-start.13 = (bf16[224,1280]{1,0:T(8,128)(2,1)S(1)}, bf16[224,1280]{1,0:T(8,128)(2,1)S(1)}, u32[]{:S(2)}, u32[]{:S(2)}) collective-permute-start(bf16[224,1280]{1,0:T(8,128)(2,1)S(1)} %bitcast.11), channel_id=1, source_target_pairs={{0,4},{4,0},{8,12},{12,8},{1,5},{5,1},{9,13},{13,9},{2,6},{6,2},{1... | collective-permute-start | bytes 1720328 | tf_op jit(solution)/shard_map/ppermute | solution.py:802
  42.3 1.4 %collective-permute-start.10 = (bf16[56,2560]{1,0:T(8,128)(2,1)S(1)}, bf16[56,2560]{1,0:T(8,128)(2,1)S(1)}, u32[]{:S(2)}, u32[]{:S(2)}) collective-permute-start(bf16[56,2560]{1,0:T(8,128)(2,1)S(1)} %copy-done.4), channel_id=1, source_target_pairs={{0,3},{1,2},{2,1},{3,0},{4,7},{5,6},{6,5},{7,4},{8,11},{9,10},{10,... | collective-permute-start | bytes 860168 | tf_op jit(solution)/shard_map/ppermute | solution.py:790
  43.7 6.2 %collective-permute-done.10.refs_3_ = bf16[56,2560]{1,0:T(8,128)(2,1)S(1)} collective-permute-done((bf16[56,2560]{1,0:T(8,128)(2,1)S(1)}, bf16[56,2560]{1,0:T(8,128)(2,1)S(1)}, u32[]{:S(2)}, u32[]{:S(2)}) %collective-permute-start.10) | collective-permute-done | bytes 286752 | tf_op jit(solution)/shard_map/ppermute | solution.py:790
  51.1 3.9 %collective-permute-done.11.from_pair = bf16[16,2688]{1,0:T(8,128)(2,1)S(1)} collective-permute-done((bf16[16,2688]{1,0:T(8,128)(2,1)S(1)}, bf16[16,2688]{1,0:T(8,128)(2,1)S(1)}, u32[]{:S(2)}, u32[]{:S(2)}) %collective-permute-start.11) | collective-permute-done | bytes 86048 | tf_op jit(solution)/shard_map/ppermute | solution.py:805
  55.9 11.0 %collective-permute-start.16 = (bf16[224,1280]{1,0:T(8,128)(2,1)S(1)}, bf16[224,1280]{1,0:T(8,128)(2,1)S(1)}, u32[]{:S(2)}, u32[]{:S(2)}) collective-permute-start(bf16[224,1280]{1,0:T(8,128)(2,1)S(1)} %get-tuple-element.96), channel_id=1, source_target_pairs={{0,4},{4,0},{8,12},{12,8},{1,5},{5,1},{9,13},{13,9},{2,6},{6,2},{1... | collective-permute-start | bytes 1720328 | tf_op jit(solution)/shard_map/ppermute | solution.py:812
  67.0 3.7 %near_pairs.1 = (bf16[224,2560]{1,0:T(8,128)(2,1)S(1)}, bf16[224,1280]{1,0:T(8,128)(2,1)S(1)}, bf16[224,1280]{1,0:T(8,128)(2,1)S(1)}, bf16[16,2560]{1,0:T(8,128)(2,1)S(1)}, bf16[16,2560]{1,0:T(8,128)(2,1)S(1)}) custom-call(bf16[224,1408]{1,0:T(8,128)(2,1)S(1)} %bitcast.10, bf16[224,1280]{1,0:T(8,128)(2,1)S(1)} %bitcast.15, bf16[224,2560]{1,0:T(8,128)(2,1)S(1)} %bitcast.18, ...), custom_call_target="tpu_custom_call" | custom-call | flops 642252800 | bytes 4587520 | tf_op jit(solution)/shard_map/near_pairs/pallas_call | solution.py:584
  71.5 8.2 %collective-permute-done.17.dp = bf16[16,2560]{1,0:T(8,128)(2,1)S(1)} collective-permute-done((bf16[16,2560]{1,0:T(8,128)(2,1)S(1)}, bf16[16,2560]{1,0:T(8,128)(2,1)S(1)}, u32[]{:S(2)}, u32[]{:S(2)}) %collective-permute-start.17) | collective-permute-done | bytes 81952 | tf_op jit(solution)/shard_map/ppermute | solution.py:813
  79.8 2.0 %collective-permute-start.20 = (bf16[224,1280]{1,0:T(8,128)(2,1)S(1)}, bf16[224,1280]{1,0:T(8,128)(2,1)S(1)}, u32[]{:S(2)}, u32[]{:S(2)}) collective-permute-start(bf16[224,1280]{1,0:T(8,128)(2,1)S(1)} %add_convert_fusion), channel_id=1, source_target_pairs={{0,4},{4,0},{8,12},{12,8},{1,5},{5,1},{9,13},{13,9},{2,6},{6,2},{1... | collective-permute-start | bytes 1720328 | tf_op jit(solution)/shard_map/ppermute | solution.py:817
  82.5 1.0 %finish_first.1 = (bf16[56,2560]{1,0:T(8,128)(2,1)S(1)}, bf16[56,2560]{1,0:T(8,128)(2,1)S(1)}, bf16[56,2560]{1,0:T(8,128)(2,1)S(1)}, bf16[56,2560]{1,0:T(8,128)(2,1)S(1)}, bf16[224,640]{1,0:T(8,128)(2,1)S(1)}) custom-call(bf16[224,2560]{1,0:T(8,128)(2,1)S(1)} %get-tuple-element.102.dw, bf16[224,1280]{1,0:T(8,128)(2,1)S(1)} %get-tuple-element.103.la, ...), custom_call_target="tpu_custom_call" | custom-call | bytes 4587520 | tf_op jit(solution)/shard_map/finish_first/pallas_call | solution.py:649
  83.6 1.6 %collective-permute-start.25 = (bf16[56,2560]{1,0:T(8,128)(2,1)S(1)}, bf16[56,2560]{1,0:T(8,128)(2,1)S(1)}, u32[]{:S(2)}, u32[]{:S(2)}) collective-permute-start(bf16[56,2560]{1,0:T(8,128)(2,1)S(1)} %get-tuple-element.116), channel_id=1, source_target_pairs={{0,2},{1,3},{2,0},{3,1},{4,6},{5,7},{6,4},{7,5},{8,10},{9,11},{10,... | collective-permute-start | bytes 860168 | tf_op jit(solution)/shard_map/ppermute | solution.py:790
  85.3 1.8 %collective-permute-start.26 = (bf16[56,2560]{1,0:T(8,128)(2,1)S(1)}, bf16[56,2560]{1,0:T(8,128)(2,1)S(1)}, u32[]{:S(2)}, u32[]{:S(2)}) collective-permute-start(bf16[56,2560]{1,0:T(8,128)(2,1)S(1)} %get-tuple-element.117), channel_id=1, source_target_pairs={{0,3},{1,2},{2,1},{3,0},{4,7},{5,6},{6,5},{7,4},{8,11},{9,10},{10,... | collective-permute-start | bytes 860168 | tf_op jit(solution)/shard_map/ppermute | solution.py:790
  87.0 3.0 %collective-permute-done.20.out2 = bf16[224,1280]{1,0:T(8,128)(2,1)S(1)} collective-permute-done((bf16[224,1280]{1,0:T(8,128)(2,1)S(1)}, bf16[224,1280]{1,0:T(8,128)(2,1)S(1)}, u32[]{:S(2)}, u32[]{:S(2)}) %collective-permute-start.20) | collective-permute-done | bytes 573472 | tf_op jit(solution)/shard_map/ppermute | solution.py:817
  90.0 1.0 finish_second.1
  91.2 1.6 %collective-permute-start.22 = (bf16[56,1280]{1,0:T(8,128)(2,1)S(1)}, bf16[56,1280]{1,0:T(8,128)(2,1)S(1)}, u32[]{:S(2)}, u32[]{:S(2)}) collective-permute-start(bf16[56,1280]{1,0:T(8,128)(2,1)S(1)} %get-tuple-element.112), channel_id=1, source_target_pairs={{0,2},{1,3},{2,0},{3,1},{4,6},{5,7},{6,4},{7,5},{8,10},{9,11},{10,... | collective-permute-start | bytes 430088 | tf_op jit(solution)/shard_map/ppermute | solution.py:790
  92.8 1.8 %collective-permute-start.23 = (bf16[56,1280]{1,0:T(8,128)(2,1)S(1)}, bf16[56,1280]{1,0:T(8,128)(2,1)S(1)}, u32[]{:S(2)}, u32[]{:S(2)}) collective-permute-start(bf16[56,1280]{1,0:T(8,128)(2,1)S(1)} %get-tuple-element.113), channel_id=1, source_target_pairs={{0,3},{1,2},{2,1},{3,0},{4,7},{5,6},{6,5},{7,4},{8,11},{9,10},{10,... | collective-permute-start | bytes 430088 | tf_op jit(solution)/shard_map/ppermute | solution.py:790
  94.6 1.9 %collective-permute-done.25.refs_2_ = bf16[56,2560]{1,0:T(8,128)(2,1)S(1)} collective-permute-done((bf16[56,2560]{1,0:T(8,128)(2,1)S(1)}, bf16[56,2560]{1,0:T(8,128)(2,1)S(1)}, u32[]{:S(2)}, u32[]{:S(2)}) %collective-permute-start.25) | collective-permute-done | bytes 286752 | tf_op jit(solution)/shard_map/ppermute | solution.py:790
  96.4 1.5 %unpack_early.1 = (bf16[56,5120]{1,0:T(8,128)(2,1)}, bf16[56,5120]{1,0:T(8,128)(2,1)}, bf16[56,5120]{1,0:T(8,128)(2,1)}) custom-call(bf16[56,2560]{1,0:T(8,128)(2,1)S(1)} %get-tuple-element.114.refs_0_, bf16[56,2560]{1,0:T(8,128)(2,1)S(1)} %collective-permute-done.24.refs_1_, bf16[56,2560]{1,0:T(8,128)(2,1)S(1)} %collective-permute-done.25.refs_2_, ...), custom_call_target="tpu_custom_call" | custom-call | bytes 2867200 | tf_op jit(solution)/shard_map/unpack_early/pallas_call | solution.py:729
  98.0 1.5 %collective-permute-done.22.refs_2_ = bf16[56,1280]{1,0:T(8,128)(2,1)S(1)} collective-permute-done((bf16[56,1280]{1,0:T(8,128)(2,1)S(1)}, bf16[56,1280]{1,0:T(8,128)(2,1)S(1)}, u32[]{:S(2)}, u32[]{:S(2)}) %collective-permute-start.22) | collective-permute-done | bytes 143392 | tf_op jit(solution)/shard_map/ppermute | solution.py:790
  99.5 0.9 unpack_late.1
  (48 shorter events, 7.0 us)
Async XLA Ops:
  0.6 17.0 %copy-start.3 = (f32[224,10]{0,1:T(8,128)S(1)}, f32[224,10]{0,1:T(8,128)}, u32[]{:S(2)}) copy-start(f32[224,10]{0,1:T(8,128)} %param.12) | copy-start | bytes 26884
  4.5 8.0 %collective-permute-start = (bf16[56,1408]{1,0:T(8,128)(2,1)}, bf16[56,1408]{1,0:T(8,128)(2,1)S(1)}, u32[]{:S(2)}, u32[]{:S(2)}) collective-permute-start(bf16[56,1408]{1,0:T(8,128)(2,1)} %get-tuple-element.63), channel_id=1, source_target_pairs={{0,1},{1,0},{2,3},{3,2},{4,5},{5,4},{6,7},{7,6},{8,9},{9,8},{10,11... | collective-permute-start | bytes 473096 | tf_op jit(solution)/shard_map/ppermute | solution.py:790
  7.6 10.1 %collective-permute-start.1 = (bf16[56,1408]{1,0:T(8,128)(2,1)}, bf16[56,1408]{1,0:T(8,128)(2,1)S(1)}, u32[]{:S(2)}, u32[]{:S(2)}) collective-permute-start(bf16[56,1408]{1,0:T(8,128)(2,1)} %get-tuple-element.64), channel_id=1, source_target_pairs={{0,2},{1,3},{2,0},{3,1},{4,6},{5,7},{6,4},{7,5},{8,10},{9,11},{10,... | collective-permute-start | bytes 473096 | tf_op jit(solution)/shard_map/ppermute | solution.py:790
  9.1 8.5 %collective-permute-start.2 = (bf16[56,1408]{1,0:T(8,128)(2,1)}, bf16[56,1408]{1,0:T(8,128)(2,1)S(1)}, u32[]{:S(2)}, u32[]{:S(2)}) collective-permute-start(bf16[56,1408]{1,0:T(8,128)(2,1)} %get-tuple-element.65), channel_id=1, source_target_pairs={{0,3},{1,2},{2,1},{3,0},{4,7},{5,6},{6,5},{7,4},{8,11},{9,10},{10,... | collective-permute-start | bytes 473096 | tf_op jit(solution)/shard_map/ppermute | solution.py:790
  9.1 10.6 %collective-permute-start.3 = (bf16[56,1280]{1,0:T(8,128)(2,1)}, bf16[56,1280]{1,0:T(8,128)(2,1)S(1)}, u32[]{:S(2)}, u32[]{:S(2)}) collective-permute-start(bf16[56,1280]{1,0:T(8,128)(2,1)} %get-tuple-element.66), channel_id=1, source_target_pairs={{0,1},{1,0},{2,3},{3,2},{4,5},{5,4},{6,7},{7,6},{8,9},{9,8},{10,11... | collective-permute-start | bytes 430088 | tf_op jit(solution)/shard_map/ppermute | solution.py:790
  11.0 8.7 %collective-permute-start.4 = (bf16[56,1280]{1,0:T(8,128)(2,1)}, bf16[56,1280]{1,0:T(8,128)(2,1)S(1)}, u32[]{:S(2)}, u32[]{:S(2)}) collective-permute-start(bf16[56,1280]{1,0:T(8,128)(2,1)} %get-tuple-element.67), channel_id=1, source_target_pairs={{0,2},{1,3},{2,0},{3,1},{4,6},{5,7},{6,4},{7,5},{8,10},{9,11},{10,... | collective-permute-start | bytes 430088 | tf_op jit(solution)/shard_map/ppermute | solution.py:790
  18.5 8.5 %copy-start.6 = (bf16[56,1280]{1,0:T(8,128)(2,1)S(1)}, bf16[56,1280]{1,0:T(8,128)(2,1)}, u32[]{:S(2)}) copy-start(bf16[56,1280]{1,0:T(8,128)(2,1)} %get-tuple-element.72) | copy-start | bytes 430084
  18.5 17.5 %copy-start.2 = (bf16[56,1280]{1,0:T(8,128)(2,1)S(1)}, bf16[56,1280]{1,0:T(8,128)(2,1)}, u32[]{:S(2)}) copy-start(bf16[56,1280]{1,0:T(8,128)(2,1)} %get-tuple-element.69.refs_0_) | copy-start | bytes 430084
  18.5 23.8 %copy-start.4 = (bf16[56,2560]{1,0:T(8,128)(2,1)S(1)}, bf16[56,2560]{1,0:T(8,128)(2,1)}, u32[]{:S(2)}) copy-start(bf16[56,2560]{1,0:T(8,128)(2,1)} %get-tuple-element.80) | copy-start | bytes 860164
  18.5 31.3 %copy-start = (bf16[56,2560]{1,0:T(8,128)(2,1)S(1)}, bf16[56,2560]{1,0:T(8,128)(2,1)}, u32[]{:S(2)}) copy-start(bf16[56,2560]{1,0:T(8,128)(2,1)} %get-tuple-element.77.refs_0_) | copy-start | bytes 860164
  19.7 17.1 %collective-permute-start.7 = (bf16[224,1408]{1,0:T(8,128)(2,1)S(1)}, bf16[224,1408]{1,0:T(8,128)(2,1)S(1)}, u32[]{:S(2)}, u32[]{:S(2)}) collective-permute-start(bf16[224,1408]{1,0:T(8,128)(2,1)S(1)} %bitcast.5), channel_id=1, source_target_pairs={{4,8},{8,4},{5,9},{9,5},{6,10},{10,6},{7,11},{11,7},{20,24},{24,20... | collective-permute-start | bytes 1892360 | tf_op jit(solution)/shard_map/ppermute | solution.py:798
  20.4 17.7 %collective-permute-start.6 = (bf16[224,1408]{1,0:T(8,128)(2,1)S(1)}, bf16[224,1408]{1,0:T(8,128)(2,1)S(1)}, u32[]{:S(2)}, u32[]{:S(2)}) collective-permute-start(bf16[224,1408]{1,0:T(8,128)(2,1)S(1)} %bitcast.6), channel_id=1, source_target_pairs={{0,4},{4,0},{8,12},{12,8},{1,5},{5,1},{9,13},{13,9},{2,6},{6,2},{1... | collective-permute-start | bytes 1892360 | tf_op jit(solution)/shard_map/ppermute | solution.py:797
  24.9 12.0 %collective-permute-start.8 = (bf16[56,2560]{1,0:T(8,128)(2,1)}, bf16[56,2560]{1,0:T(8,128)(2,1)S(1)}, u32[]{:S(2)}, u32[]{:S(2)}) collective-permute-start(bf16[56,2560]{1,0:T(8,128)(2,1)} %get-tuple-element.74), channel_id=1, source_target_pairs={{0,1},{1,0},{2,3},{3,2},{4,5},{5,4},{6,7},{7,6},{8,9},{9,8},{10,11... | collective-permute-start | bytes 860168 | tf_op jit(solution)/shard_map/ppermute | solution.py:790
  26.3 10.5 %collective-permute-start.9 = (bf16[56,2560]{1,0:T(8,128)(2,1)S(1)}, bf16[56,2560]{1,0:T(8,128)(2,1)S(1)}, u32[]{:S(2)}, u32[]{:S(2)}) collective-permute-start(bf16[56,2560]{1,0:T(8,128)(2,1)S(1)} %copy-done.5), channel_id=1, source_target_pairs={{0,2},{1,3},{2,0},{3,1},{4,6},{5,7},{6,4},{7,5},{8,10},{9,11},{10,... | collective-permute-start | bytes 860168 | tf_op jit(solution)/shard_map/ppermute | solution.py:790
  27.0 9.1 %collective-permute-start.5 = (bf16[56,1280]{1,0:T(8,128)(2,1)S(1)}, bf16[56,1280]{1,0:T(8,128)(2,1)S(1)}, u32[]{:S(2)}, u32[]{:S(2)}) collective-permute-start(bf16[56,1280]{1,0:T(8,128)(2,1)S(1)} %copy-done.6), channel_id=1, source_target_pairs={{0,3},{1,2},{2,1},{3,0},{4,7},{5,6},{6,5},{7,4},{8,11},{9,10},{10,... | collective-permute-start | bytes 430088 | tf_op jit(solution)/shard_map/ppermute | solution.py:790
  38.1 16.9 %collective-permute-start.14 = (bf16[224,1408]{1,0:T(8,128)(2,1)S(1)}, bf16[224,1408]{1,0:T(8,128)(2,1)S(1)}, u32[]{:S(2)}, u32[]{:S(2)}) collective-permute-start(bf16[224,1408]{1,0:T(8,128)(2,1)S(1)} %collective-permute-done.6.r1), channel_id=1, source_target_pairs={{4,8},{8,4},{5,9},{9,5},{6,10},{10,6},{7,11},{11,7},{20,24},{24,20... | collective-permute-start | bytes 1892360 | tf_op jit(solution)/shard_map/ppermute | solution.py:803
  38.8 16.2 %collective-permute-start.13 = (bf16[224,1280]{1,0:T(8,128)(2,1)S(1)}, bf16[224,1280]{1,0:T(8,128)(2,1)S(1)}, u32[]{:S(2)}, u32[]{:S(2)}) collective-permute-start(bf16[224,1280]{1,0:T(8,128)(2,1)S(1)} %bitcast.11), channel_id=1, source_target_pairs={{0,4},{4,0},{8,12},{12,8},{1,5},{5,1},{9,13},{13,9},{2,6},{6,2},{1... | collective-permute-start | bytes 1720328 | tf_op jit(solution)/shard_map/ppermute | solution.py:802
  42.3 7.5 %collective-permute-start.10 = (bf16[56,2560]{1,0:T(8,128)(2,1)S(1)}, bf16[56,2560]{1,0:T(8,128)(2,1)S(1)}, u32[]{:S(2)}, u32[]{:S(2)}) collective-permute-start(bf16[56,2560]{1,0:T(8,128)(2,1)S(1)} %copy-done.4), channel_id=1, source_target_pairs={{0,3},{1,2},{2,1},{3,0},{4,7},{5,6},{6,5},{7,4},{8,11},{9,10},{10,... | collective-permute-start | bytes 860168 | tf_op jit(solution)/shard_map/ppermute | solution.py:790
  50.2 4.8 %collective-permute-start.11 = (bf16[16,2688]{1,0:T(8,128)(2,1)S(1)}, bf16[16,2688]{1,0:T(8,128)(2,1)S(1)}, u32[]{:S(2)}, u32[]{:S(2)}) collective-permute-start(bf16[16,2688]{1,0:T(8,128)(2,1)S(1)} %get-tuple-element.82), channel_id=1, source_target_pairs={{0,4},{4,0},{8,12},{12,8},{1,5},{5,1},{9,13},{13,9},{2,6},{6,2},{1... | collective-permute-start | bytes 258056 | tf_op jit(solution)/shard_map/ppermute | solution.py:805
  50.4 4.6 %collective-permute-start.12 = (bf16[16,2688]{1,0:T(8,128)(2,1)S(1)}, bf16[16,2688]{1,0:T(8,128)(2,1)S(1)}, u32[]{:S(2)}, u32[]{:S(2)}) collective-permute-start(bf16[16,2688]{1,0:T(8,128)(2,1)S(1)} %get-tuple-element.83), channel_id=1, source_target_pairs={{4,8},{8,4},{5,9},{9,5},{6,10},{10,6},{7,11},{11,7},{20,24},{24,20... | collective-permute-start | bytes 258056 | tf_op jit(solution)/shard_map/ppermute | solution.py:806
  55.2 24.4 %collective-permute-start.15 = (bf16[224,1280]{1,0:T(8,128)(2,1)S(1)}, bf16[224,1280]{1,0:T(8,128)(2,1)S(1)}, u32[]{:S(2)}, u32[]{:S(2)}) collective-permute-start(bf16[224,1280]{1,0:T(8,128)(2,1)S(1)} %get-tuple-element.94), channel_id=1, source_target_pairs={{4,8},{8,4},{5,9},{9,5},{6,10},{10,6},{7,11},{11,7},{20,24},{24,20... | collective-permute-start | bytes 1720328 | tf_op jit(solution)/shard_map/ppermute | solution.py:811
  55.9 23.7 %collective-permute-start.16 = (bf16[224,1280]{1,0:T(8,128)(2,1)S(1)}, bf16[224,1280]{1,0:T(8,128)(2,1)S(1)}, u32[]{:S(2)}, u32[]{:S(2)}) collective-permute-start(bf16[224,1280]{1,0:T(8,128)(2,1)S(1)} %get-tuple-element.96), channel_id=1, source_target_pairs={{0,4},{4,0},{8,12},{12,8},{1,5},{5,1},{9,13},{13,9},{2,6},{6,2},{1... | collective-permute-start | bytes 1720328 | tf_op jit(solution)/shard_map/ppermute | solution.py:812
  70.7 8.9 %collective-permute-start.17 = (bf16[16,2560]{1,0:T(8,128)(2,1)S(1)}, bf16[16,2560]{1,0:T(8,128)(2,1)S(1)}, u32[]{:S(2)}, u32[]{:S(2)}) collective-permute-start(bf16[16,2560]{1,0:T(8,128)(2,1)S(1)} %get-tuple-element.97), channel_id=1, source_target_pairs={{0,4},{4,0},{8,12},{12,8},{1,5},{5,1},{9,13},{13,9},{2,6},{6,2},{1... | collective-permute-start | bytes 245768 | tf_op jit(solution)/shard_map/ppermute | solution.py:813
  70.8 8.8 %collective-permute-start.18 = (bf16[16,2560]{1,0:T(8,128)(2,1)S(1)}, bf16[16,2560]{1,0:T(8,128)(2,1)S(1)}, u32[]{:S(2)}, u32[]{:S(2)}) collective-permute-start(bf16[16,2560]{1,0:T(8,128)(2,1)S(1)} %get-tuple-element.98), channel_id=1, source_target_pairs={{4,8},{8,4},{5,9},{9,5},{6,10},{10,6},{7,11},{11,7},{20,24},{24,20... | collective-permute-start | bytes 245768 | tf_op jit(solution)/shard_map/ppermute | solution.py:814
  79.8 10.2 %collective-permute-start.20 = (bf16[224,1280]{1,0:T(8,128)(2,1)S(1)}, bf16[224,1280]{1,0:T(8,128)(2,1)S(1)}, u32[]{:S(2)}, u32[]{:S(2)}) collective-permute-start(bf16[224,1280]{1,0:T(8,128)(2,1)S(1)} %add_convert_fusion), channel_id=1, source_target_pairs={{0,4},{4,0},{8,12},{12,8},{1,5},{5,1},{9,13},{13,9},{2,6},{6,2},{1... | collective-permute-start | bytes 1720328 | tf_op jit(solution)/shard_map/ppermute | solution.py:817
  81.8 8.2 %collective-permute-start.19 = (bf16[224,1280]{1,0:T(8,128)(2,1)S(1)}, bf16[224,1280]{1,0:T(8,128)(2,1)S(1)}, u32[]{:S(2)}, u32[]{:S(2)}) collective-permute-start(bf16[224,1280]{1,0:T(8,128)(2,1)S(1)} %get-tuple-element.99), channel_id=1, source_target_pairs={{4,8},{8,4},{5,9},{9,5},{6,10},{10,6},{7,11},{11,7},{20,24},{24,20... | collective-permute-start | bytes 1720328 | tf_op jit(solution)/shard_map/ppermute | solution.py:816
  83.5 9.3 %collective-permute-start.24 = (bf16[56,2560]{1,0:T(8,128)(2,1)S(1)}, bf16[56,2560]{1,0:T(8,128)(2,1)S(1)}, u32[]{:S(2)}, u32[]{:S(2)}) collective-permute-start(bf16[56,2560]{1,0:T(8,128)(2,1)S(1)} %get-tuple-element.115), channel_id=1, source_target_pairs={{0,1},{1,0},{2,3},{3,2},{4,5},{5,4},{6,7},{7,6},{8,9},{9,8},{10,11... | collective-permute-start | bytes 860168 | tf_op jit(solution)/shard_map/ppermute | solution.py:790
  83.6 12.8 %collective-permute-start.25 = (bf16[56,2560]{1,0:T(8,128)(2,1)S(1)}, bf16[56,2560]{1,0:T(8,128)(2,1)S(1)}, u32[]{:S(2)}, u32[]{:S(2)}) collective-permute-start(bf16[56,2560]{1,0:T(8,128)(2,1)S(1)} %get-tuple-element.116), channel_id=1, source_target_pairs={{0,2},{1,3},{2,0},{3,1},{4,6},{5,7},{6,4},{7,5},{8,10},{9,11},{10,... | collective-permute-start | bytes 860168 | tf_op jit(solution)/shard_map/ppermute | solution.py:790
  85.3 11.2 %collective-permute-start.26 = (bf16[56,2560]{1,0:T(8,128)(2,1)S(1)}, bf16[56,2560]{1,0:T(8,128)(2,1)S(1)}, u32[]{:S(2)}, u32[]{:S(2)}) collective-permute-start(bf16[56,2560]{1,0:T(8,128)(2,1)S(1)} %get-tuple-element.117), channel_id=1, source_target_pairs={{0,3},{1,2},{2,1},{3,0},{4,7},{5,6},{6,5},{7,4},{8,11},{9,10},{10,... | collective-permute-start | bytes 860168 | tf_op jit(solution)/shard_map/ppermute | solution.py:790
  91.0 6.9 %collective-permute-start.21 = (bf16[56,1280]{1,0:T(8,128)(2,1)S(1)}, bf16[56,1280]{1,0:T(8,128)(2,1)S(1)}, u32[]{:S(2)}, u32[]{:S(2)}) collective-permute-start(bf16[56,1280]{1,0:T(8,128)(2,1)S(1)} %get-tuple-element.111), channel_id=1, source_target_pairs={{0,1},{1,0},{2,3},{3,2},{4,5},{5,4},{6,7},{7,6},{8,9},{9,8},{10,11... | collective-permute-start | bytes 430088 | tf_op jit(solution)/shard_map/ppermute | solution.py:790
  91.2 8.3 %collective-permute-start.22 = (bf16[56,1280]{1,0:T(8,128)(2,1)S(1)}, bf16[56,1280]{1,0:T(8,128)(2,1)S(1)}, u32[]{:S(2)}, u32[]{:S(2)}) collective-permute-start(bf16[56,1280]{1,0:T(8,128)(2,1)S(1)} %get-tuple-element.112), channel_id=1, source_target_pairs={{0,2},{1,3},{2,0},{3,1},{4,6},{5,7},{6,4},{7,5},{8,10},{9,11},{10,... | collective-permute-start | bytes 430088 | tf_op jit(solution)/shard_map/ppermute | solution.py:790
  92.8 6.7 %collective-permute-start.23 = (bf16[56,1280]{1,0:T(8,128)(2,1)S(1)}, bf16[56,1280]{1,0:T(8,128)(2,1)S(1)}, u32[]{:S(2)}, u32[]{:S(2)}) collective-permute-start(bf16[56,1280]{1,0:T(8,128)(2,1)S(1)} %get-tuple-element.113), channel_id=1, source_target_pairs={{0,3},{1,2},{2,1},{3,0},{4,7},{5,6},{6,5},{7,4},{8,11},{9,10},{10,... | collective-permute-start | bytes 430088 | tf_op jit(solution)/shard_map/ppermute | solution.py:790
  (2 other events, 8.7 us)
